TPU v7x, 1024 devices: a whole 4x8x16 slice. The times are simulated.
1024 devices in a mesh: dp: 128 (over z, y_lo, x), tensor: 8 (over y_hi, core).
Axes of the slice: x: 4, y: 8 (y_hi: 4, y_lo: 2; y = y_hi * 2 + y_lo), z: 16, core: 2. Of those that a mesh axis runs over, the one named last changes fastest.
Arguments:
- rollout_states: bfloat16 [32768, 4096], P('dp', 'tensor'), may hold values from -6 to 6
- lengths: int32 [128, 4], P('dp'), may hold values from 1 to 192, 256 in all within a row
- moved: int32 [128], P('dp'), may hold values from 0 to 3, as said below
- norm_gain: bfloat16 [4096], replicated, may hold values from 0.099609375 to 1.8984375
- qkv_weight: bfloat16 [4096, 6144], P('dp', 'tensor'), may hold values from -0.09375 to 0.09375
- qkv_bias: bfloat16 [6144], P('tensor'), may hold values from -5 to 5
Outputs:
- context: bfloat16 [65536, 4096], P('dp', 'tensor')
Inputs may be any that keep to these rules, and one draw needn't show every extreme that they name: `moved`: the last rollout group keeps all of its responses; every other group hands on at least one.
All inputs are finite; a program needn't handle non-finite values.
Results may differ from a plain program's by a relative error of at most 0.011.
Values may be sent and summed in bfloat16 or wider, within the bound.
No kernel may reach another device: no remote copies, remote signals or barrier semaphores. Data moves between devices by JAX's collectives and lax.ppermute only.
A program may use at most 32 MiB of HBM per device.

v0:
```python
import jax
import jax.numpy as jnp
from jax import lax
from jax.sharding import PartitionSpec as P

HEADS = 32
KV = 8
HEAD = 128


EPSILON = 1e-06
ROPE_BASE = 1000000.0


def shifted(value, axis, steps):
    count = lax.axis_size(axis)
    leading, last = (max(0, -steps), min(count, count - steps))
    return lax.ppermute(value, axis, [(source, source + steps) for source in range(leading, last)])


def token_layout(lengths_row, moved_count, slot_count):
    slot_ids = jnp.arange(slot_count, dtype=jnp.int32)
    samples = lengths_row.shape[0]
    starts = jnp.cumsum(lengths_row) - lengths_row
    owners = jnp.sum((starts[None, :] <= slot_ids[:, None]).astype(jnp.int32), axis=1) - 1
    onehot = owners[:, None] == jnp.arange(samples, dtype=jnp.int32)[None, :]
    positions = slot_ids - jnp.sum(jnp.where(onehot, starts[None, :], 0), axis=1)
    moving = jnp.arange(samples, dtype=jnp.int32) >= samples - moved_count
    tail_tokens = jnp.sum(jnp.where(moving, lengths_row, 0))
    return (owners, positions, tail_tokens)


def project(states, norm_gain, qkv_weight, qkv_bias):
    gathered = lax.all_gather(states, "tensor", axis=1, tiled=True)
    values = gathered.astype(jnp.float32)
    mean_square = jnp.mean(values * values, axis=1, keepdims=True)
    normed = (values * lax.rsqrt(mean_square + EPSILON) * norm_gain.astype(jnp.float32)).astype(
        jnp.bfloat16
    )
    projected = jnp.dot(
        normed,
        lax.all_gather(qkv_weight, "dp", axis=0, tiled=True),
        preferred_element_type=jnp.float32,
    )
    return projected + qkv_bias.astype(jnp.float32)


def rope_tables(positions):
    half_dim = HEAD // 2
    inv_freq = ROPE_BASE ** (-(2.0 * jnp.arange(half_dim, dtype=jnp.float32)) / HEAD)
    angles = positions.astype(jnp.float32)[:, None] * inv_freq[None, :]
    angles = jnp.concatenate([angles, angles], axis=1)
    return (jnp.cos(angles), jnp.sin(angles))


def rotary(values, cosine_table, sine_table):
    half_dim = values.shape[-1] // 2
    turned = jnp.concatenate([-values[..., half_dim:], values[..., :half_dim]], axis=-1)
    return values * cosine_table + turned * sine_table


def attend(projected, segments, positions):
    row_count = projected.shape[0]
    per_group = HEADS // KV
    groups = projected.shape[1] // ((per_group + 2) * HEAD)
    heads_view = projected.reshape(row_count, groups, per_group + 2, HEAD)
    cosine_table, sine_table = rope_tables(positions)
    query_heads = rotary(
        heads_view[:, :, :per_group], cosine_table[:, None, None, :], sine_table[:, None, None, :]
    ).astype(jnp.bfloat16)
    key_heads = rotary(
        heads_view[:, :, per_group], cosine_table[:, None, :], sine_table[:, None, :]
    ).astype(jnp.bfloat16)
    value_heads = heads_view[:, :, per_group + 1].astype(jnp.bfloat16)
    scores = jnp.einsum(
        "qgnd,kgd->gnqk", query_heads, key_heads, preferred_element_type=jnp.float32
    ) * HEAD ** (-0.5)
    slot_ids = jnp.arange(row_count, dtype=jnp.int32)
    allowed = (segments[:, None] == segments[None, :]) & (slot_ids[None, :] <= slot_ids[:, None])
    scores = jnp.where(allowed[None, None], scores, -1e30)
    row_max = jnp.max(scores, axis=-1, keepdims=True)
    exp_scores = jnp.exp(scores - row_max)
    weights = (exp_scores / jnp.sum(exp_scores, axis=-1, keepdims=True)).astype(jnp.bfloat16)
    context = jnp.einsum("gnqk,kgd->qgnd", weights, value_heads, preferred_element_type=jnp.float32)
    return context.reshape(row_count, groups * per_group * HEAD).astype(jnp.bfloat16)


def assemble(previous, current, incoming, outgoing, pad_value):
    slot_count = current.shape[0]
    filler = jnp.full(current.shape, pad_value, current.dtype)
    stacked = jnp.concatenate([previous, current, filler], axis=0)
    packed = lax.dynamic_slice_in_dim(
        stacked, (slot_count - incoming).astype(jnp.int32), 2 * slot_count, 0
    )
    keep_mask = jnp.arange(2 * slot_count, dtype=jnp.int32) < incoming + slot_count - outgoing
    keep_mask = keep_mask.reshape((2 * slot_count,) + (1,) * (current.ndim - 1))
    return jnp.where(keep_mask, packed, jnp.asarray(pad_value, current.dtype))


def local(rollout_states, lengths, moved, norm_gain, qkv_weight, qkv_bias):
    slot_count = rollout_states.shape[0]
    samples = lengths.shape[1]
    owners, positions, tail_tokens = token_layout(lengths[0], moved[0], slot_count)
    tail_box = tail_tokens.reshape((1,))
    layout = jnp.stack([owners, positions], axis=0)
    previous, previous_layout, previous_tail = shifted((rollout_states, layout, tail_box), "dp", 1)
    incoming = previous_tail[0]
    states = assemble(previous, rollout_states, incoming, tail_tokens, 0.0)
    segments = assemble(previous_layout[0], owners + samples, incoming, tail_tokens, -1)
    row_positions = assemble(previous_layout[1], positions, incoming, tail_tokens, 0)
    projected = project(states, norm_gain, qkv_weight, qkv_bias)
    context = attend(projected, segments, row_positions)
    result = jnp.where((segments >= 0)[:, None], context, jnp.zeros((), jnp.bfloat16))
    return result


def solution(mesh):
    return jax.shard_map(
        local,
        mesh=mesh,
        in_specs=(P("dp", "tensor"), P("dp", None), P("dp"), P(), P("dp", "tensor"), P("tensor")),
        out_specs=P("dp", "tensor"),
        check_vma=False,
    )
```

profile of v0, /device:TPU:16, one launch (start us, length us, event | category | flops | bytes accessed | tf_op | source)
XLA Modules:
  0.0 719.7 jit_solution(12218159517570061843)
XLA Ops:
  6.5 0.0 all-gather.3.cloned.1.call-start
  6.5 3.4 collective-permute-start.2
  10.6 1.3 fusion.43
  11.9 4.0 collective-permute-start
  15.8 0.9 collective-permute-done
  19.4 0.1 pad_dynamic-slice_fusion.2
  19.5 0.0 collective-permute-done.2
  19.5 2.1 fusion.23
  21.6 0.0 all-gather.3.cloned.1.call-update
  21.6 0.0 all-gather.5.cloned.1.call-start
  21.7 0.7 all-gather.5.cloned.1.call-update
  22.4 0.8 reduce-window_clone.1
  23.2 0.7 subtract_bitcast_fusion
  23.9 0.1 convert_reduce_fusion
  24.0 0.1 select_reduce_fusion
  24.1 4.1 collective-permute-start.1
  28.2 0.7 convert_element_type.54
  28.9 0.7 convert_element_type.56
  29.6 0.0 collective-permute-done.1
  29.6 0.1 select_convert_fusion
  29.7 0.1 broadcast_compare_fusion
  29.8 0.1 fusion.42
  29.9 1.7 fusion.36
  31.6 0.2 fusion.20
  31.8 60.8 %all-gather.3.cloned.1.call-done = bf16[512,4096]{1,0:T(8,128)(2,1)} async-done(((bf16[512,512]{1,0:T(8,128)(2,1)}), bf16[512,4096]{1,0:T(8,128)(2,1)}) %all-gather.3.cloned.1.call-update) | async-done | bytes 4194320 | tf_op jit(solution)/shard_map/all_gather | solution.py:34
  92.6 3.1 fusion
  95.7 602.9 %all-gather.5.cloned.1.call-done = bf16[4096,768]{1,0:T(8,128)(2,1)} async-done(((bf16[32,768]{1,0:T(8,128)(2,1)}), bf16[4096,768]{1,0:T(8,128)(2,1)}) %all-gather.5.cloned.1.call-update) | async-done | bytes 6291472 | tf_op jit(solution)/shard_map/all_gather | solution.py:42
  698.6 7.2 fusion.12
  705.8 0.5 copy.19
  706.2 0.1 slice_negate_fusion
  706.4 2.9 fusion.8
  709.3 0.9 fusion.7
  710.2 1.5 fusion.15
  711.7 0.2 copy.23
  711.9 0.9 broadcast_select_fusion
  (15 shorter events, 0.1 us)
Async XLA Ops:
  6.5 86.0 %all-gather.3.cloned.1.call-start = ((), (), s32[]{:S(2)}) async-start(), calls=%async_computation | async-start | bytes 4718592 | tf_op jit(solution)/shard_map/all_gather | solution.py:34
  6.5 13.0 %collective-permute-start.2 = (bf16[256,512]{1,0:T(8,128)(2,1)}, bf16[256,512]{1,0:T(8,128)(2,1)S(1)}, u32[]{:S(2)}, u32[]{:S(2)}) collective-permute-start(bf16[256,512]{1,0:T(8,128)(2,1)} %param.6), channel_id=1, source_target_pairs={{0,8},{8,16},{16,24},{24,32},{32,40},{40,48},{48,56},{56,64},{64,7... | collective-permute-start | bytes 786440 | tf_op jit(solution)/shard_map/ppermute | solution.py:18
  11.9 4.9 collective-permute-start
  21.6 676.9 %all-gather.5.cloned.1.call-start = ((), (), s32[]{:S(2)}) async-start(), calls=%async_computation.1 | async-start | bytes 6340608 | tf_op jit(solution)/shard_map/all_gather | solution.py:42
  24.1 5.5 collective-permute-start.1
Sparse Core Ops, SparseCore 0:
  21.7 70.7 all-gather.2
  95.2 603.2 all-gather.4
where the time goes:
time: 720 us
  waiting for transfers between devices  665 us (92%)
  between operations  16.8 us (2%)
  other arithmetic  13.7 us (2%)
  matrix products  11.6 us (2%)
  starting transfers between devices  11.5 us (2%)
    all_gather x1, waiting for transfers between devices, project(): lax.all_gather(qkv_weight, 'dp', axis=0, tiled=True)  603 us
    all_gather x1, waiting for transfers between devices, project(): gathered = lax.all_gather(states, 'tensor', axis=1, tiled=True)  60.8 us
  transfers between devices with their start and end apart: 5, of which 3 were waited for; matrix products, arithmetic and copies ran while one was open for 1% of the time, Pallas kernels for 0%

commit v1 on v0

v1 whole, which is shorter than its diff:
```python
import functools

import jax
import jax.numpy as jnp
from jax import lax
from jax.experimental import pallas as pl
from jax.experimental.pallas import tpu as pltpu
from jax.sharding import Mesh
from jax.sharding import PartitionSpec as P

HEADS = 32
KV = 8
HEAD = 128
PER = HEADS // KV
EPSILON = 1e-06
ROPE_BASE = 1000000.0

NZ, NYL, NX, NYH, NC = 16, 2, 4, 4, 2
DP = ("z", "yl", "x")
TP = ("yh", "c")
WROWS = 32
ROWS = 256
VMEM = 32 << 20


def whole(shape):
    return pl.BlockSpec(memory_space=pltpu.VMEM)


def call(kernel, out_shape, args, scalars=0, flops=0, nbytes=0, scratch=()):
    smem = pl.BlockSpec(memory_space=pltpu.SMEM)
    vmem = pl.BlockSpec(memory_space=pltpu.VMEM)
    return pl.pallas_call(
        kernel,
        out_shape=out_shape,
        in_specs=[smem] * scalars + [vmem] * (len(args) - scalars),
        out_specs=vmem if not isinstance(out_shape, (list, tuple)) else [vmem] * len(out_shape),
        scratch_shapes=list(scratch),
        compiler_params=pltpu.CompilerParams(vmem_limit_bytes=VMEM),
        cost_estimate=pl.CostEstimate(flops=flops, bytes_accessed=nbytes, transcendentals=0),
    )(*args)


def reorder_kernel(yl_ref, s_ref, o_ref):
    yl = yl_ref[0]
    source = lax.broadcasted_iota(jnp.int32, (512, 128), 0)
    r = lax.broadcasted_iota(jnp.int32, (512, 128), 1)
    rel, zz, k = lax.shift_right_logical(r, 6), lax.shift_right_logical(r, 5) & 1, r & 31
    base = zz * 256 + (rel ^ yl) * 128 + k
    for x in range(NX):
        perm = (source == base + x * 32).astype(jnp.bfloat16)
        o_ref[x] = jnp.dot(s_ref[...], perm, preferred_element_type=jnp.float32).astype(jnp.bfloat16)


def matmul_kernel(c_ref, own_ref, oth_ref, wown_ref, woth_ref, o_ref, w_ref):
    c = c_ref[0]
    for rel in range(NC):
        for yh in range(NYH):
            row = pl.multiple_of((yh * 4 + (c ^ rel) * 2) * WROWS, 64)
            at = (rel * NYH + yh) * 128
            w_ref[at : at + 64] = wown_ref[pl.ds(row, 64)]
            w_ref[at + 64 : at + 128] = woth_ref[pl.ds(row, 64)]

    def body(g, carry):
        rows = pl.ds(pl.multiple_of(g * ROWS, ROWS), ROWS)
        x = jnp.concatenate(
            [own_ref[yh, rows] for yh in range(NYH)] + [oth_ref[yh, rows] for yh in range(NYH)], axis=1
        )
        o_ref[g] = jnp.dot(x, w_ref[...], preferred_element_type=jnp.float32).astype(jnp.bfloat16)
        return carry

    lax.fori_loop(0, NX, body, 0)


def attend_kernel(len_ref, a_ref, b_ref, r_ref, bias_ref, cos_ref, sin_ref, o_ref):
    s1 = len_ref[0]
    s2 = s1 + len_ref[1]
    s3 = s2 + len_ref[2]
    i = lax.broadcasted_iota(jnp.int32, (ROWS, ROWS), 0)
    j = lax.broadcasted_iota(jnp.int32, (ROWS, ROWS), 1)
    start = jnp.where(i >= s3, s3, jnp.where(i >= s2, s2, jnp.where(i >= s1, s1, 0)))
    allowed = (j >= start) & (j <= i)
    r = r_ref[...]
    cos, sin = cos_ref[...], sin_ref[...]

    def head(n):
        ref, at = (a_ref, n * HEAD) if n < 3 else (b_ref, (n - 3) * HEAD)
        total = ref[0, :, at : at + HEAD].astype(jnp.float32)
        for k in range(1, NX):
            total = total + ref[k, :, at : at + HEAD].astype(jnp.float32)
        return total * r + bias_ref[:, n * HEAD : (n + 1) * HEAD]

    def rotate(v):
        return (v * cos + pltpu.roll(v, HEAD // 2, 1) * sin).astype(jnp.bfloat16)

    key = rotate(head(PER))
    value = head(PER + 1).astype(jnp.bfloat16)
    for h in range(PER):
        query = rotate(head(h))
        scores = lax.dot_general(query, key, (((1,), (1,)), ((), ())), preferred_element_type=jnp.float32)
        scores = jnp.where(allowed, scores * HEAD ** (-0.5), -1e30)
        e = jnp.exp(scores - jnp.max(scores, axis=1, keepdims=True))
        weights = (e / jnp.sum(e, axis=1, keepdims=True)).astype(jnp.bfloat16)
        o_ref[:, h * HEAD : (h + 1) * HEAD] = jnp.dot(
            weights, value, preferred_element_type=jnp.float32
        ).astype(jnp.bfloat16)


def pack_kernel(n_ref, prev_ref, own_ref, o_ref):
    incoming, tail = n_ref[0], n_ref[1]
    slot = lax.broadcasted_iota(jnp.int32, (2 * ROWS, ROWS), 0)
    row = lax.broadcasted_iota(jnp.int32, (2 * ROWS, ROWS), 1)
    first = ((slot < incoming) & (row == slot + (ROWS - incoming))).astype(jnp.bfloat16)
    second = ((row == slot - incoming) & (row < ROWS - tail)).astype(jnp.bfloat16)
    picked = jnp.dot(first, prev_ref[...], preferred_element_type=jnp.float32)
    picked = picked + jnp.dot(second, own_ref[...], preferred_element_type=jnp.float32)
    o_ref[...] = picked.astype(jnp.bfloat16)


def local(states, lengths, moved, norm_gain, qkv_weight, qkv_bias):
    yl, c = lax.axis_index("yl"), lax.axis_index("c")
    dp = lax.axis_index(DP)
    samples = lengths.shape[1]
    bf = lambda *shape: jax.ShapeDtypeStruct(shape, jnp.bfloat16)

    sent = call(reorder_kernel, bf(NX, ROWS, 128), (yl.reshape(1), states), 1, 2 * 256 * 512 * 512, 1 << 20)
    mine = lax.all_to_all(sent, "x", 0, 0, tiled=True).reshape(1, NX * ROWS, 128)
    spread = lax.all_to_all(jnp.broadcast_to(mine, (NYH, NX * ROWS, 128)), "yh", 0, 0, tiled=True)
    gain = lax.dynamic_slice_in_dim(norm_gain, dp * WROWS, WROWS, 0).astype(jnp.float32)
    scaled = (qkv_weight.astype(jnp.float32) * gain[:, None]).astype(jnp.bfloat16)
    scaled, sent_first = lax.optimization_barrier((scaled, mine))
    wown = lax.all_gather(scaled, "z", axis=0, tiled=True)
    spread, wown = lax.optimization_barrier((spread, wown))
    other = lax.ppermute(spread, "c", [(0, 1), (1, 0)])

    row_ids = jnp.arange(ROWS, dtype=jnp.int32)
    lens = lengths[0]
    starts = jnp.cumsum(lens) - lens
    begin = jnp.max(jnp.where(starts[None, :] <= row_ids[:, None], starts[None, :], 0), axis=1)
    positions = (row_ids - begin).astype(jnp.float32)
    inv_freq = ROPE_BASE ** (-(2.0 * jnp.arange(HEAD // 2, dtype=jnp.float32)) / HEAD)
    angles = positions[:, None] * inv_freq[None, :]
    cos, sin = jnp.cos(angles), jnp.sin(angles)
    cos = jnp.concatenate([cos, cos], axis=1)
    sin = jnp.concatenate([-sin, sin], axis=1)
    moving = jnp.arange(samples, dtype=jnp.int32) >= samples - moved[0]
    tail = jnp.sum(jnp.where(moving, lens, 0)).reshape(1)
    ndp = NZ * NYL * NX
    shift = [(i, i + 1) for i in range(ndp - 1)]
    incoming = lax.ppermute(tail, DP, shift)

    squares = jnp.sum(jnp.square(spread.astype(jnp.float32)), axis=(0, 2)) + jnp.sum(
        jnp.square(other.astype(jnp.float32)), axis=(0, 2)
    )
    squares = jnp.sum(lax.all_to_all(squares.reshape(NX, ROWS), "x", 0, 0, tiled=True), axis=0)
    scale = lax.rsqrt(squares / (NZ * NYL * NX * WROWS) + EPSILON).reshape(ROWS, 1)

    half = qkv_weight.shape[1] // 2
    parts = []
    for n in range(2):
        own = wown[:, n * half : (n + 1) * half]
        oth = lax.ppermute(own, "yl", [(0, 1), (1, 0)])
        partial = call(
            matmul_kernel,
            bf(NX, ROWS, half),
            (c.reshape(1), spread, other, own, oth),
            1,
            2 * NX * ROWS * 1024 * half,
            4 << 20,
            scratch=[pltpu.VMEM((1024, half), jnp.bfloat16)],
        )
        parts.append(lax.all_to_all(partial, "x", 0, 0, tiled=True))
    bias = qkv_bias.astype(jnp.float32)[None, :]
    context = call(
        attend_kernel, bf(ROWS, PER * HEAD), (lens, *parts, scale, bias, cos, sin), 1, 4 * 4 * ROWS * ROWS * HEAD, 3 << 20
    )
    previous = lax.ppermute(context, DP, shift)
    counts = jnp.concatenate([incoming, tail])
    return call(
        pack_kernel, bf(2 * ROWS, PER * HEAD), (counts, previous, context), 1, 4 * 512 * 256 * 512, 1 << 20
    )


def solution(mesh):
    fine = Mesh(mesh.devices.reshape(NZ, NYL, NX, NYH, NC), DP + TP)
    return jax.shard_map(
        local,
        mesh=fine,
        in_specs=(P(DP, TP), P(DP, None), P(DP), P(), P(DP, TP), P(TP)),
        out_specs=P(DP, TP),
        check_vma=False,
    )
```

time: 720 us -> 137 us (0.19)
  the two profiles are of different devices: /device:TPU:16 before, /device:TPU:40 now
where the time goes in v1:
time: 137 us
  blocking collectives  59.8 us (44%)
  starting transfers between devices  29.7 us (22%)
  waiting for transfers between devices  27.7 us (20%)
  Pallas kernels  8.68 us (6%)
  local copies, waits for them, and re-layouts  5.17 us (4%)
  other arithmetic  4.86 us (4%)
    all_gather x1, blocking collectives, local(): wown = lax.all_gather(scaled, 'z', axis=0, tiled=True)  49.1 us
    all_to_all x2, waiting for transfers between devices, local(): parts.append(lax.all_to_all(partial, 'x', 0, 0, tiled=True))  16.6 us
    all_to_all x1, blocking collectives, local(): lax.all_to_all(sent, 'x', 0, 0, tiled=True).reshape(1, NX * ROWS, 128)  10.8 us
    pallas_call x5, Pallas kernels, call(): pl.pallas_call(kernel, out_shape=out_shape, in_specs=[smem] * scalars + [...  8.68 us
    all_to_all x1, starting transfers between devices, local(): lax.all_to_all(jnp.broadcast_to(mine, (NYH, NX * ROWS, 128)), 'yh', 0, 0,...  7.33 us
    all_to_all x2, starting transfers between devices, local(): parts.append(lax.all_to_all(partial, 'x', 0, 0, tiled=True))  6.99 us
    ppermute x1, waiting for transfers between devices, local(): incoming = lax.ppermute(tail, DP, shift)  5.93 us
    ppermute x2, starting transfers between devices, local(): oth = lax.ppermute(own, 'yl', [(0, 1), (1, 0)])  5.83 us
  transfers between devices with their start and end apart: 9, of which 5 were waited for; matrix products, arithmetic and copies ran while one was open for 5% of the time, Pallas kernels for 3%

profile of v1, /device:TPU:40, one launch (start us, length us, event | category | flops | bytes accessed | tf_op | source)
XLA Modules:
  0.0 136.8 jit_solution(7094142739524345950)
XLA Ops:
  0.0 0.0 copy-start.2
  0.0 0.9 copy-done.2
  1.0 0.4 shard_map.64
  1.4 10.8 %all_to_all.26 = bf16[4,256,128]{2,1,0:T(8,128)(2,1)S(1)} all-to-all(bf16[4,256,128]{2,1,0:T(8,128)(2,1)S(1)} %shard_map.64), channel_id=1, replica_groups=mesh['z'=16,'yl'=2,'x'=4,'yh'=4,'c'=2] {'x'}, dimensions={0} | all-to-all | bytes 524288 | tf_op jit(solution)/shard_map/all_to_all | solution.py:127
  12.2 1.1 broadcast_in_dim.34
  13.3 0.0 copy-start.4
  13.3 7.3 %all-to-all-start.1 = ((bf16[4,1024,128]{2,1,0:T(8,128)(2,1)}), bf16[4,1024,128]{2,1,0:T(8,128)(2,1)S(1)}, u32[]{:S(2)}, u32[]{:S(2)}) async-start(bf16[4,1024,128]{2,1,0:T(8,128)(2,1)} %broadcast_in_dim.34), calls=%async_computation.1 | async-start | bytes 2097152 | tf_op jit(solution)/shard_map/all_to_all | solution.py:128
  20.6 0.8 dynamic-slice_convert_fusion
  21.3 0.0 copy-done.4
  21.3 0.1 multiply_convert_fusion
  21.4 0.0 copy-start.3
  21.4 49.1 %all_gather.3 = bf16[512,768]{1,0:T(8,128)(2,1)} all-gather(bf16[32,768]{1,0:T(8,128)(2,1)S(1)} %multiply_convert_fusion), channel_id=1, replica_groups=mesh['z'=16,'yl'=2,'x'=4,'yh'=4,'c'=2] {'z'}, dimensions={0}, use_global_device_ids=true | all-gather | bytes 835584 | tf_op jit(solution)/shard_map/all_gather | solution.py:132
  70.5 0.0 all-to-all-done.1.own_ref
  70.5 1.9 %collective-permute-start.1 = (bf16[4,1024,128]{2,1,0:T(8,128)(2,1)S(1)}, bf16[4,1024,128]{2,1,0:T(8,128)(2,1)S(1)}, u32[]{:S(2)}, u32[]{:S(2)}) collective-permute-start(bf16[4,1024,128]{2,1,0:T(8,128)(2,1)S(1)} %all-to-all-done.1.own_ref), channel_id=1, source_target_pairs={{0,1},{1,0},{2,3},{3,2},{4,5},{5,4},{6,7},{7,6},{8,9},{9,8},{10,11... | collective-permute-start | bytes 3145736 | tf_op jit(solution)/shard_map/ppermute | solution.py:134
  72.4 1.2 fusion.2
  73.6 3.6 %collective-permute-start.3 = (bf16[512,384]{1,0:T(8,128)(2,1)S(1)}, bf16[512,384]{1,0:T(8,128)(2,1)S(1)}, u32[]{:S(2)}, u32[]{:S(2)}) collective-permute-start(bf16[512,384]{1,0:T(8,128)(2,1)S(1)} %get-tuple-element.9.wown_ref), channel_id=1, source_target_pairs={{0,32},{32,0},{1,33},{33,1},{2,34},{34,2},{3,35},{35,3},{4,36},{36... | collective-permute-start | bytes 1179656 | tf_op jit(solution)/shard_map/ppermute | solution.py:162
  77.2 0.0 copy-done.3
  77.2 0.2 reduce-window_clone.1
  77.4 2.3 %collective-permute-start.2 = (bf16[512,384]{1,0:T(8,128)(2,1)S(1)}, bf16[512,384]{1,0:T(8,128)(2,1)}, u32[]{:S(2)}, u32[]{:S(2)}) collective-permute-start(bf16[512,384]{1,0:T(8,128)(2,1)S(1)} %get-tuple-element.10.wown_ref), channel_id=1, source_target_pairs={{0,32},{32,0},{1,33},{33,1},{2,34},{34,2},{3,35},{35,3},{4,36},{36... | collective-permute-start | bytes 1179656 | tf_op jit(solution)/shard_map/ppermute | solution.py:162
  79.7 0.3 multiply_reduce_fusion.1
  79.9 0.0 collective-permute-done.1.oth_ref
  79.9 0.3 multiply_reduce_fusion
  80.2 0.6 add.40
  80.8 3.2 %all-to-all-start.4 = ((f32[4,1,256]{2,1,0:T(1,128)}), f32[4,1,256]{2,1,0:T(1,128)S(1)}, u32[]{:S(2)}, u32[]{:S(2)}) async-start(f32[4,1,256]{2,1,0:T(1,128)} %bitcast.6), calls=%async_computation.4 | async-start | bytes 8192 | tf_op jit(solution)/shard_map/all_to_all | solution.py:155
  84.1 3.3 %collective-permute-done.3.woth_ref = bf16[512,384]{1,0:T(8,128)(2,1)S(1)} collective-permute-done((bf16[512,384]{1,0:T(8,128)(2,1)S(1)}, bf16[512,384]{1,0:T(8,128)(2,1)S(1)}, u32[]{:S(2)}, u32[]{:S(2)}) %collective-permute-start.3) | collective-permute-done | bytes 393248 | tf_op jit(solution)/shard_map/ppermute | solution.py:162
  87.4 1.8 %shard_map.66 = bf16[4,256,384]{2,1,0:T(8,128)(2,1)S(1)} custom-call(s32[1]{0:T(128)} %bitcast.3.c_ref, bf16[4,1024,128]{2,1,0:T(8,128)(2,1)S(1)} %all-to-all-done.1.own_ref, bf16[4,1024,128]{2,1,0:T(8,128)(2,1)S(1)} %collective-permute-done.1.oth_ref, bf16[512,384]{1,0:T(8,128)(2,1)S(1)} %get-tuple-element.9.wown_ref, ...), custom_call_target="tpu_custom_call" | custom-call | flops 805306368 | bytes 4194304 | tf_op jit(solution)/shard_map/pallas_call | solution.py:33
  89.3 0.0 copy-start.1
  89.3 0.9 copy-done.1
  90.2 0.0 all-to-all-done.4
  90.2 3.5 %all-to-all-start.3 = ((bf16[4,256,384]{2,1,0:T(8,128)(2,1)}), bf16[4,256,384]{2,1,0:T(8,128)(2,1)S(1)}, u32[]{:S(2)}, u32[]{:S(2)}) async-start(bf16[4,256,384]{2,1,0:T(8,128)(2,1)} %copy-done.1), calls=%async_computation.3 | async-start | bytes 1572864 | tf_op jit(solution)/shard_map/all_to_all | solution.py:172
  93.7 0.1 select_reduce_fusion
  93.8 1.8 %collective-permute-done.2.woth_ref = bf16[512,384]{1,0:T(8,128)(2,1)} collective-permute-done((bf16[512,384]{1,0:T(8,128)(2,1)S(1)}, bf16[512,384]{1,0:T(8,128)(2,1)}, u32[]{:S(2)}, u32[]{:S(2)}) %collective-permute-start.2) | collective-permute-done | bytes 393248 | tf_op jit(solution)/shard_map/ppermute | solution.py:162
  95.6 2.8 %shard_map.65 = bf16[4,256,384]{2,1,0:T(8,128)(2,1)S(1)} custom-call(s32[1]{0:T(128)} %bitcast.3.c_ref, bf16[4,1024,128]{2,1,0:T(8,128)(2,1)S(1)} %all-to-all-done.1.own_ref, bf16[4,1024,128]{2,1,0:T(8,128)(2,1)S(1)} %collective-permute-done.1.oth_ref, bf16[512,384]{1,0:T(8,128)(2,1)S(1)} %get-tuple-element.10.wown_ref, ...), custom_call_target="tpu_custom_call" | custom-call | flops 805306368 | bytes 4194304 | tf_op jit(solution)/shard_map/pallas_call | solution.py:33
  98.4 0.0 copy-start
  98.4 0.9 copy-done
  99.3 0.0 copy-start.5
  99.3 6.4 %all-to-all-done.3.b_ref = bf16[4,256,384]{2,1,0:T(8,128)(2,1)S(1)} async-done(((bf16[4,256,384]{2,1,0:T(8,128)(2,1)}), bf16[4,256,384]{2,1,0:T(8,128)(2,1)S(1)}, u32[]{:S(2)}, u32[]{:S(2)}) %all-to-all-start.3) | async-done | bytes 786464 | tf_op jit(solution)/shard_map/all_to_all | solution.py:172
  105.7 3.5 %all-to-all-start.2 = ((bf16[4,256,384]{2,1,0:T(8,128)(2,1)}), bf16[4,256,384]{2,1,0:T(8,128)(2,1)S(1)}, u32[]{:S(2)}, u32[]{:S(2)}) async-start(bf16[4,256,384]{2,1,0:T(8,128)(2,1)} %copy-done), calls=%async_computation.2 | async-start | bytes 1572864 | tf_op jit(solution)/shard_map/all_to_all | solution.py:172
  109.2 0.0 copy-done.5
  109.2 0.5 fusion
  109.8 0.1 pad_maximum_fusion
  109.9 0.1 copy.10.r_ref
  110.1 10.2 %all-to-all-done.2.a_ref = bf16[4,256,384]{2,1,0:T(8,128)(2,1)S(1)} async-done(((bf16[4,256,384]{2,1,0:T(8,128)(2,1)}), bf16[4,256,384]{2,1,0:T(8,128)(2,1)S(1)}, u32[]{:S(2)}, u32[]{:S(2)}) %all-to-all-start.2) | async-done | bytes 786464 | tf_op jit(solution)/shard_map/all_to_all | solution.py:172
  120.3 1.8 %shard_map.67.own_ref = bf16[256,512]{1,0:T(8,128)(2,1)S(1)} custom-call(s32[4]{0:T(128)S(1)} %bitcast.11, bf16[4,256,384]{2,1,0:T(8,128)(2,1)S(1)} %all-to-all-done.2.a_ref, bf16[4,256,384]{2,1,0:T(8,128)(2,1)S(1)} %all-to-all-done.3.b_ref, f32[256,1]{1,0:T(8,128)S(1)} %copy.10.r_ref, f32[1,768]{1,0:T(1,128)S(1)} %reshape.80.bias_ref, ...), custom_call_target="tpu_custom_call" | custom-call | flops 134217728 | bytes 3145728 | tf_op jit(solution)/shard_map/pallas_call | solution.py:33
  122.1 2.5 %collective-permute-start.4 = (bf16[256,512]{1,0:T(8,128)(2,1)S(1)}, bf16[256,512]{1,0:T(8,128)(2,1)S(1)}, u32[]{:S(2)}, u32[]{:S(2)}) collective-permute-start(bf16[256,512]{1,0:T(8,128)(2,1)S(1)} %shard_map.67.own_ref), channel_id=1, source_target_pairs={{0,8},{8,16},{16,24},{24,32},{32,40},{40,48},{48,56},{56,64},{64,7... | collective-permute-start | bytes 786440 | tf_op jit(solution)/shard_map/ppermute | solution.py:177
  125.3 0.6 fusion.1
  125.9 1.9 %collective-permute-start = (s32[1]{0:T(128)}, s32[1]{0:T(128)}, u32[]{:S(2)}, u32[]{:S(2)}) collective-permute-start(s32[1]{0:T(128)} %bitcast.2), channel_id=1, source_target_pairs={{0,8},{8,16},{16,24},{24,32},{32,40},{40,48},{48,56},{56,64},{64,7... | collective-permute-start | bytes 20 | tf_op jit(solution)/shard_map/ppermute | solution.py:150
  127.8 5.9 %collective-permute-done = s32[1]{0:T(128)} collective-permute-done((s32[1]{0:T(128)}, s32[1]{0:T(128)}, u32[]{:S(2)}, u32[]{:S(2)}) %collective-permute-start) | collective-permute-done | bytes 36 | tf_op jit(solution)/shard_map/ppermute | solution.py:150
  133.7 1.2 pad_add_fusion.n_ref
  135.0 0.0 collective-permute-done.4.prev_ref
  135.0 1.8 %shard_map.68 = bf16[512,512]{1,0:T(8,128)(2,1)} custom-call(s32[2]{0:T(128)S(1)} %pad_add_fusion.n_ref, bf16[256,512]{1,0:T(8,128)(2,1)S(1)} %collective-permute-done.4.prev_ref, bf16[256,512]{1,0:T(8,128)(2,1)S(1)} %shard_map.67.own_ref), custom_call_target="tpu_custom_call" | custom-call | flops 268435456 | bytes 1048576 | tf_op jit(solution)/shard_map/pallas_call | solution.py:33
  (6 shorter events, 0.1 us)
Async XLA Ops:
  0.0 0.9 copy-start.2
  13.3 8.1 %copy-start.4 = (bf16[32,768]{1,0:T(8,128)(2,1)S(1)}, bf16[32,768]{1,0:T(8,128)(2,1)}, u32[]{:S(2)}) copy-start(bf16[32,768]{1,0:T(8,128)(2,1)} %param.10) | copy-start | bytes 147460
  13.3 57.2 %all-to-all-start.1 = ((bf16[4,1024,128]{2,1,0:T(8,128)(2,1)}), bf16[4,1024,128]{2,1,0:T(8,128)(2,1)S(1)}, u32[]{:S(2)}, u32[]{:S(2)}) async-start(bf16[4,1024,128]{2,1,0:T(8,128)(2,1)} %broadcast_in_dim.34), calls=%async_computation.1 | async-start | bytes 2097152 | tf_op jit(solution)/shard_map/all_to_all | solution.py:128
  21.4 55.8 %copy-start.3 = (s32[1,4]{1,0:T(1,128)S(1)}, s32[1,4]{1,0:T(1,128)}, u32[]{:S(2)}) copy-start(s32[1,4]{1,0:T(1,128)} %param.7) | copy-start | bytes 52
  70.5 9.4 %collective-permute-start.1 = (bf16[4,1024,128]{2,1,0:T(8,128)(2,1)S(1)}, bf16[4,1024,128]{2,1,0:T(8,128)(2,1)S(1)}, u32[]{:S(2)}, u32[]{:S(2)}) collective-permute-start(bf16[4,1024,128]{2,1,0:T(8,128)(2,1)S(1)} %all-to-all-done.1.own_ref), channel_id=1, source_target_pairs={{0,1},{1,0},{2,3},{3,2},{4,5},{5,4},{6,7},{7,6},{8,9},{9,8},{10,11... | collective-permute-start | bytes 3145736 | tf_op jit(solution)/shard_map/ppermute | solution.py:134
  73.6 13.8 %collective-permute-start.3 = (bf16[512,384]{1,0:T(8,128)(2,1)S(1)}, bf16[512,384]{1,0:T(8,128)(2,1)S(1)}, u32[]{:S(2)}, u32[]{:S(2)}) collective-permute-start(bf16[512,384]{1,0:T(8,128)(2,1)S(1)} %get-tuple-element.9.wown_ref), channel_id=1, source_target_pairs={{0,32},{32,0},{1,33},{33,1},{2,34},{34,2},{3,35},{35,3},{4,36},{36... | collective-permute-start | bytes 1179656 | tf_op jit(solution)/shard_map/ppermute | solution.py:162
  77.4 18.2 %collective-permute-start.2 = (bf16[512,384]{1,0:T(8,128)(2,1)S(1)}, bf16[512,384]{1,0:T(8,128)(2,1)}, u32[]{:S(2)}, u32[]{:S(2)}) collective-permute-start(bf16[512,384]{1,0:T(8,128)(2,1)S(1)} %get-tuple-element.10.wown_ref), channel_id=1, source_target_pairs={{0,32},{32,0},{1,33},{33,1},{2,34},{34,2},{3,35},{35,3},{4,36},{36... | collective-permute-start | bytes 1179656 | tf_op jit(solution)/shard_map/ppermute | solution.py:162
  80.8 9.3 %all-to-all-start.4 = ((f32[4,1,256]{2,1,0:T(1,128)}), f32[4,1,256]{2,1,0:T(1,128)S(1)}, u32[]{:S(2)}, u32[]{:S(2)}) async-start(f32[4,1,256]{2,1,0:T(1,128)} %bitcast.6), calls=%async_computation.4 | async-start | bytes 8192 | tf_op jit(solution)/shard_map/all_to_all | solution.py:155
  89.3 0.9 copy-start.1
  90.2 15.5 %all-to-all-start.3 = ((bf16[4,256,384]{2,1,0:T(8,128)(2,1)}), bf16[4,256,384]{2,1,0:T(8,128)(2,1)S(1)}, u32[]{:S(2)}, u32[]{:S(2)}) async-start(bf16[4,256,384]{2,1,0:T(8,128)(2,1)} %copy-done.1), calls=%async_computation.3 | async-start | bytes 1572864 | tf_op jit(solution)/shard_map/all_to_all | solution.py:172
  98.4 0.9 copy-start
  99.3 9.9 %copy-start.5 = (bf16[768]{0:T(1024)(128)(2,1)S(1)}, bf16[768]{0:T(1024)(128)(2,1)}, u32[]{:S(2)}) copy-start(bf16[768]{0:T(1024)(128)(2,1)} %param.11) | copy-start | bytes 4612
  105.7 14.6 %all-to-all-start.2 = ((bf16[4,256,384]{2,1,0:T(8,128)(2,1)}), bf16[4,256,384]{2,1,0:T(8,128)(2,1)S(1)}, u32[]{:S(2)}, u32[]{:S(2)}) async-start(bf16[4,256,384]{2,1,0:T(8,128)(2,1)} %copy-done), calls=%async_computation.2 | async-start | bytes 1572864 | tf_op jit(solution)/shard_map/all_to_all | solution.py:172
  122.1 12.9 %collective-permute-start.4 = (bf16[256,512]{1,0:T(8,128)(2,1)S(1)}, bf16[256,512]{1,0:T(8,128)(2,1)S(1)}, u32[]{:S(2)}, u32[]{:S(2)}) collective-permute-start(bf16[256,512]{1,0:T(8,128)(2,1)S(1)} %shard_map.67.own_ref), channel_id=1, source_target_pairs={{0,8},{8,16},{16,24},{24,32},{32,40},{40,48},{48,56},{56,64},{64,7... | collective-permute-start | bytes 786440 | tf_op jit(solution)/shard_map/ppermute | solution.py:177
  125.9 7.8 %collective-permute-start = (s32[1]{0:T(128)}, s32[1]{0:T(128)}, u32[]{:S(2)}, u32[]{:S(2)}) collective-permute-start(s32[1]{0:T(128)} %bitcast.2), channel_id=1, source_target_pairs={{0,8},{8,16},{16,24},{24,32},{32,40},{40,48},{48,56},{56,64},{64,7... | collective-permute-start | bytes 20 | tf_op jit(solution)/shard_map/ppermute | solution.py:150

commit v2 on v1

v2 whole, which is shorter than its diff:
```python
import jax
import jax.numpy as jnp
from jax import lax
from jax.experimental import pallas as pl
from jax.experimental.pallas import tpu as pltpu
from jax.sharding import Mesh
from jax.sharding import PartitionSpec as P

HEADS = 32
KV = 8
HEAD = 128
PER = HEADS // KV
EPSILON = 1e-06
ROPE_BASE = 1000000.0

NZ, NYL, NX, NYH, NC = 16, 2, 4, 4, 2
DP = ("z", "yl", "x")
TP = ("yh", "c")
WROWS = 32
ROWS = 256
VMEM = 32 << 20


def call(kernel, out_shape, args, scalars=0, flops=0, nbytes=0, scratch=()):
    smem = pl.BlockSpec(memory_space=pltpu.SMEM)
    vmem = pl.BlockSpec(memory_space=pltpu.VMEM)
    return pl.pallas_call(
        kernel,
        out_shape=out_shape,
        in_specs=[smem] * scalars + [vmem] * (len(args) - scalars),
        out_specs=vmem if not isinstance(out_shape, (list, tuple)) else [vmem] * len(out_shape),
        scratch_shapes=list(scratch),
        compiler_params=pltpu.CompilerParams(vmem_limit_bytes=VMEM),
        cost_estimate=pl.CostEstimate(flops=flops, bytes_accessed=nbytes, transcendentals=0),
    )(*args)


def prepare_kernel(at_ref, s_ref, w_ref, gain_ref, o_ref, ow_ref):
    yl, dp = at_ref[0], at_ref[1]
    feature = lax.broadcasted_iota(jnp.int32, (WROWS, gain_ref.shape[1]), 1)
    row = lax.broadcasted_iota(jnp.int32, (WROWS, gain_ref.shape[1]), 0)
    gain = jnp.where(feature == dp * WROWS + row, gain_ref[...].astype(jnp.float32), 0.0)
    gain = jnp.sum(gain, axis=1, keepdims=True)
    ow_ref[...] = (w_ref[...].astype(jnp.float32) * gain).astype(jnp.bfloat16)
    source = lax.broadcasted_iota(jnp.int32, (512, 128), 0)
    r = lax.broadcasted_iota(jnp.int32, (512, 128), 1)
    rel, zz, k = lax.shift_right_logical(r, 6), lax.shift_right_logical(r, 5) & 1, r & 31
    base = zz * 256 + (rel ^ yl) * 128 + k
    for x in range(NX):
        perm = (source == base + x * 32).astype(jnp.bfloat16)
        picked = jnp.dot(s_ref[...], perm, preferred_element_type=jnp.float32).astype(jnp.bfloat16)
        for yh in range(NYH):
            o_ref[yh, x] = picked


def matmul_kernel(c_ref, own_ref, oth0_ref, oth1_ref, wown_ref, woth_ref, o_ref, w_ref):
    c = c_ref[0]
    for rel in range(NC):
        for yh in range(NYH):
            row = pl.multiple_of((yh * 4 + (c ^ rel) * 2) * WROWS, 64)
            at = (rel * NYH + yh) * 128
            w_ref[at : at + 64] = wown_ref[pl.ds(row, 64)]
            w_ref[at + 64 : at + 128] = woth_ref[pl.ds(row, 64)]

    for n, oth_ref in enumerate((oth0_ref, oth1_ref)):
        for k in range(2):
            g = n * 2 + k
            x = jnp.concatenate([own_ref[g, yh] for yh in range(NYH)] + [oth_ref[k, yh] for yh in range(NYH)], axis=1)
            o_ref[g] = jnp.dot(x, w_ref[...], preferred_element_type=jnp.float32).astype(jnp.bfloat16)


def attend_kernel(len_ref, p_ref, r_ref, bias_ref, cos_ref, sin_ref, o_ref):
    s1 = len_ref[0]
    s2 = s1 + len_ref[1]
    s3 = s2 + len_ref[2]
    i = lax.broadcasted_iota(jnp.int32, (ROWS, ROWS), 0)
    j = lax.broadcasted_iota(jnp.int32, (ROWS, ROWS), 1)
    start = jnp.where(i >= s3, s3, jnp.where(i >= s2, s2, jnp.where(i >= s1, s1, 0)))
    allowed = (j >= start) & (j <= i)
    r = r_ref[...]
    cos, sin = cos_ref[...], sin_ref[...]

    def head(n):
        at = n * HEAD
        total = p_ref[0, :, at : at + HEAD].astype(jnp.float32)
        for k in range(1, NX):
            total = total + p_ref[k, :, at : at + HEAD].astype(jnp.float32)
        return total * r + bias_ref[:, n * HEAD : (n + 1) * HEAD]

    def rotate(v):
        return (v * cos + pltpu.roll(v, HEAD // 2, 1) * sin).astype(jnp.bfloat16)

    key = rotate(head(PER))
    value = head(PER + 1).astype(jnp.bfloat16)
    for h in range(PER):
        query = rotate(head(h))
        scores = lax.dot_general(query, key, (((1,), (1,)), ((), ())), preferred_element_type=jnp.float32)
        scores = jnp.where(allowed, scores * HEAD ** (-0.5), -1e30)
        e = jnp.exp(scores - jnp.max(scores, axis=1, keepdims=True))
        weights = (e / jnp.sum(e, axis=1, keepdims=True)).astype(jnp.bfloat16)
        o_ref[:, h * HEAD : (h + 1) * HEAD] = jnp.dot(
            weights, value, preferred_element_type=jnp.float32
        ).astype(jnp.bfloat16)


def pack_kernel(n_ref, prev_ref, own_ref, o_ref):
    incoming, tail = n_ref[0], n_ref[1]
    slot = lax.broadcasted_iota(jnp.int32, (2 * ROWS, ROWS), 0)
    row = lax.broadcasted_iota(jnp.int32, (2 * ROWS, ROWS), 1)
    first = ((slot < incoming) & (row == slot + (ROWS - incoming))).astype(jnp.bfloat16)
    second = ((row == slot - incoming) & (row < ROWS - tail)).astype(jnp.bfloat16)
    picked = jnp.dot(first, prev_ref[...], preferred_element_type=jnp.float32)
    picked = picked + jnp.dot(second, own_ref[...], preferred_element_type=jnp.float32)
    o_ref[...] = picked.astype(jnp.bfloat16)


def local(states, lengths, moved, norm_gain, qkv_weight, qkv_bias):
    yl, c = lax.axis_index("yl"), lax.axis_index("c")
    dp = lax.axis_index(DP)
    bf = lambda *shape: jax.ShapeDtypeStruct(shape, jnp.bfloat16)

    columns = qkv_weight.shape[1]
    sent, scaled = call(
        prepare_kernel,
        (bf(NYH, NX, ROWS, 128), bf(WROWS, columns)),
        (jnp.stack([yl, dp]), states, qkv_weight, norm_gain.reshape(1, -1)),
        1,
        2 * 256 * 512 * 512,
        1 << 20,
    )
    raw = lax.all_to_all(sent, "yh", 0, 0, tiled=True)
    wown = lax.all_gather(scaled, "z", axis=0, tiled=True)
    raw, wown, lens_early = lax.optimization_barrier((raw, wown, lengths))

    woth = lax.ppermute(wown, "yl", [(0, 1), (1, 0)])
    spread = lax.all_to_all(raw.transpose(1, 0, 2, 3), "x", 0, 0, tiled=True)
    others = [lax.ppermute(spread[n * 2 : n * 2 + 2], "c", [(0, 1), (1, 0)]) for n in range(2)]

    lens = lens_early[0]
    ids = jnp.arange(ROWS, dtype=jnp.int32)
    s1 = lens[0]
    s2 = s1 + lens[1]
    s3 = s2 + lens[2]
    begin = jnp.where(ids >= s3, s3, jnp.where(ids >= s2, s2, jnp.where(ids >= s1, s1, 0)))
    positions = (ids - begin).astype(jnp.float32)
    inv_freq = ROPE_BASE ** (-(2.0 * jnp.arange(HEAD // 2, dtype=jnp.float32)) / HEAD)
    angles = positions[:, None] * inv_freq[None, :]
    cos, sin = jnp.cos(angles), jnp.sin(angles)
    cos = jnp.concatenate([cos, cos], axis=1)
    sin = jnp.concatenate([-sin, sin], axis=1)
    bias = qkv_bias.astype(jnp.float32)[None, :]
    woth, cos, sin, bias = lax.optimization_barrier((woth, cos, sin, bias))

    partial = call(
        matmul_kernel,
        bf(NX, ROWS, columns),
        (c.reshape(1), spread, *others, wown, woth),
        1,
        2 * NX * ROWS * 1024 * columns,
        6 << 20,
        scratch=[pltpu.VMEM((1024, columns), jnp.bfloat16)],
    )
    partial, raw, lengths, moved = lax.optimization_barrier((partial, raw, lengths, moved))
    summed = lax.all_to_all(partial, "x", 0, 0, tiled=True)

    squares = jnp.sum(jnp.square(raw.astype(jnp.float32)), axis=(0, 1, 3))
    squares = squares + lax.ppermute(squares, "c", [(0, 1), (1, 0)])
    scale = lax.rsqrt(squares / (NZ * NYL * NX * WROWS) + EPSILON).reshape(ROWS, 1)
    samples = lengths.shape[1]
    moving = jnp.arange(samples, dtype=jnp.int32) >= samples - moved[0]
    tail = jnp.sum(jnp.where(moving, lengths[0], 0)).reshape(1)
    shift = [(i, i + 1) for i in range(NZ * NYL * NX - 1)]
    counts = jnp.concatenate([lax.ppermute(tail, DP, shift), tail])
    summed, counts, scale = lax.optimization_barrier((summed, counts, scale))

    context = call(
        attend_kernel, bf(ROWS, PER * HEAD), (lens, summed, scale, bias, cos, sin), 1, 4 * 4 * ROWS * ROWS * HEAD, 3 << 20
    )
    previous = lax.ppermute(context, DP, shift)
    return call(
        pack_kernel, bf(2 * ROWS, PER * HEAD), (counts, previous, context), 1, 4 * 512 * 256 * 512, 1 << 20
    )


def solution(mesh):
    fine = Mesh(mesh.devices.reshape(NZ, NYL, NX, NYH, NC), DP + TP)
    return jax.shard_map(
        local,
        mesh=fine,
        in_specs=(P(DP, TP), P(DP, None), P(DP), P(), P(DP, TP), P(TP)),
        out_specs=P(DP, TP),
        check_vma=False,
    )
```

time: 137 us -> 129 us (0.942)
  blocking collectives: 59.8 us -> 46.9 us
  between operations: 0.85 us -> 2.72 us
    all_to_all x1 -> x0, blocking collectives: 10.8 us -> none  [local(): lax.all_to_all(sent, 'x', 0, 0, tiled=True).reshape(1, NX * ROWS, 128)]
    ppermute x1, waiting for transfers between devices: 0.01 us -> 8.9 us  [local(): previous = lax.ppermute(context, DP, shift)]
    all_to_all x4 -> x3, waiting for transfers between devices: 16.6 us -> 9.75 us  [the longest x1 7.6 us: local(): spread = lax.all_to_all(raw.transpose(1, 0, 2, 3), 'x', 0, 0, tiled=True)]
    ppermute x4 -> x5, starting transfers between devices: 9.65 us -> 13.4 us  [the longest x2 4.32 us: local(): lax.ppermute(spread[n * 2:n * 2 + 2], 'c', [(0, 1), (1, 0)])]
    all_to_all x4 -> x3, starting transfers between devices: 17.6 us -> 15.2 us  [the longest x1 7.2 us: local(): raw = lax.all_to_all(sent, 'yh', 0, 0, tiled=True)]
    all_gather x1, blocking collectives: 49.1 us -> 46.9 us  [local(): wown = lax.all_gather(scaled, 'z', axis=0, tiled=True)]
    ppermute x4 -> x5, waiting for transfers between devices: 11.1 us -> 10.1 us  [the longest x1 10.1 us: local(): counts = jnp.concatenate([lax.ppermute(tail, DP, shift), tail])]
    pallas_call x5 -> x4, Pallas kernels: 8.68 us -> 9.62 us  [call(): pl.pallas_call(kernel, out_shape=out_shape, in_specs=[smem] * scalars + [...]
  transfers between devices with their start and end apart: 9 -> 9, of which waited for: 5 -> 4; matrix products, arithmetic and copies ran while one was open for 5% -> 4% of each run, Pallas kernels for 3% -> 0%
where the time goes in v2:
time: 129 us; the launch traced here: 128 us
  blocking collectives  46.9 us (36%)
  starting transfers between devices  31 us (24%)
  waiting for transfers between devices  28.8 us (22%)
  Pallas kernels  9.62 us (7%)
  local copies, waits for them, and re-layouts  5.65 us (4%)
  other arithmetic  3.78 us (3%)
  between operations  2.72 us (2%)
    all_gather x1, blocking collectives, local(): wown = lax.all_gather(scaled, 'z', axis=0, tiled=True)  46.9 us
    ppermute x1, waiting for transfers between devices, local(): counts = jnp.concatenate([lax.ppermute(tail, DP, shift), tail])  10.1 us
    pallas_call x4, Pallas kernels, call(): pl.pallas_call(kernel, out_shape=out_shape, in_specs=[smem] * scalars + [...  9.62 us
    ppermute x1, waiting for transfers between devices, local(): previous = lax.ppermute(context, DP, shift)  8.9 us
    all_to_all x1, waiting for transfers between devices, local(): spread = lax.all_to_all(raw.transpose(1, 0, 2, 3), 'x', 0, 0, tiled=True)  7.6 us
    all_to_all x1, starting transfers between devices, local(): raw = lax.all_to_all(sent, 'yh', 0, 0, tiled=True)  7.2 us
    ppermute x2, starting transfers between devices, local(): lax.ppermute(spread[n * 2:n * 2 + 2], 'c', [(0, 1), (1, 0)])  4.32 us
    all_to_all x1, starting transfers between devices, local(): spread = lax.all_to_all(raw.transpose(1, 0, 2, 3), 'x', 0, 0, tiled=True)  4.29 us
  transfers between devices with their start and end apart: 9, of which 4 were waited for; matrix products, arithmetic and copies ran while one was open for 4% of the time, Pallas kernels for 0%

profile of v2, /device:TPU:40, one launch (start us, length us, event | category | flops | bytes accessed | tf_op | source)
XLA Modules:
  0.0 128.5 jit_solution(7371983105408093332)
XLA Ops:
  0.0 0.7 reshape.42.gain_ref
  0.7 0.1 pad_add_fusion.at_ref
  0.8 0.0 copy-start.1
  0.8 0.9 copy-done.1
  1.7 0.0 copy-start.2
  1.8 0.8 copy-done.2
  2.5 2.0 %shard_map.64 = (bf16[4,4,256,128]{3,2,1,0:T(8,128)(2,1)}, bf16[32,768]{1,0:T(8,128)(2,1)S(1)}) custom-call(s32[2]{0:T(128)S(1)} %pad_add_fusion.at_ref, bf16[256,512]{1,0:T(8,128)(2,1)S(1)} %copy-done.1, bf16[32,768]{1,0:T(8,128)(2,1)S(1)} %copy-done.2, bf16[1,4096]{1,0:T(2,128)(2,1)S(1)} %reshape.42.gain_ref), custom_call_target="tpu_custom_call" | custom-call | flops 134217728 | bytes 1048576 | tf_op jit(solution)/shard_map/pallas_call | solution.py:27
  4.5 7.2 %all-to-all-start = ((bf16[4,4,256,128]{3,2,1,0:T(8,128)(2,1)}), bf16[4,4,256,128]{3,2,1,0:T(8,128)(2,1)S(1)}, u32[]{:S(2)}, u32[]{:S(2)}) async-start(bf16[4,4,256,128]{3,2,1,0:T(8,128)(2,1)} %get-tuple-element.21), calls=%async_computation | async-start | bytes 2097152 | tf_op jit(solution)/shard_map/all_to_all | solution.py:131
  11.7 46.9 %all_gather.3.wown_ref = bf16[512,768]{1,0:T(8,128)(2,1)S(1)} all-gather(bf16[32,768]{1,0:T(8,128)(2,1)S(1)} %get-tuple-element.22), channel_id=1, replica_groups=mesh['z'=16,'yl'=2,'x'=4,'yh'=4,'c'=2] {'z'}, dimensions={0}, use_global_device_ids=true | all-gather | bytes 835584 | tf_op jit(solution)/shard_map/all_gather | solution.py:132
  58.6 0.0 all-to-all-done
  58.6 0.0 copy-start.3
  58.6 1.1 copy.13
  59.7 0.0 copy-start.5
  59.7 0.2 copy-done.3
  60.0 4.3 %all-to-all-start.1 = ((bf16[4,4,256,128]{3,2,1,0:T(8,128)(2,1)}), bf16[4,4,256,128]{3,2,1,0:T(8,128)(2,1)S(1)}, u32[]{:S(2)}, u32[]{:S(2)}) async-start(bf16[4,4,256,128]{3,2,1,0:T(8,128)(2,1)} %bitcast.16), calls=%async_computation.1 | async-start | bytes 2097152 | tf_op jit(solution)/shard_map/all_to_all | solution.py:136
  64.3 0.0 copy-start
  64.3 0.0 copy-done.5
  64.3 3.3 %collective-permute-start.2 = (bf16[512,768]{1,0:T(8,128)(2,1)S(1)}, bf16[512,768]{1,0:T(8,128)(2,1)S(1)}, u32[]{:S(2)}, u32[]{:S(2)}) collective-permute-start(bf16[512,768]{1,0:T(8,128)(2,1)S(1)} %all_gather.3.wown_ref), channel_id=1, source_target_pairs={{0,32},{32,0},{1,33},{33,1},{2,34},{34,2},{3,35},{35,3},{4,36},{36... | collective-permute-start | bytes 2359304 | tf_op jit(solution)/shard_map/ppermute | solution.py:135
  67.6 7.6 %all-to-all-done.1.own_ref = bf16[4,4,256,128]{3,2,1,0:T(8,128)(2,1)S(1)} async-done(((bf16[4,4,256,128]{3,2,1,0:T(8,128)(2,1)}), bf16[4,4,256,128]{3,2,1,0:T(8,128)(2,1)S(1)}, u32[]{:S(2)}, u32[]{:S(2)}) %all-to-all-start.1) | async-done | bytes 1048608 | tf_op jit(solution)/shard_map/all_to_all | solution.py:136
  75.2 1.0 fusion.4
  76.2 1.9 %collective-permute-start = (bf16[2,4,256,128]{3,2,1,0:T(8,128)(2,1)}, bf16[2,4,256,128]{3,2,1,0:T(8,128)(2,1)S(1)}, u32[]{:S(2)}, u32[]{:S(2)}) collective-permute-start(bf16[2,4,256,128]{3,2,1,0:T(8,128)(2,1)} %get-tuple-element.38), channel_id=1, source_target_pairs={{0,1},{1,0},{2,3},{3,2},{4,5},{5,4},{6,7},{7,6},{8,9},{9,8},{10,11... | collective-permute-start | bytes 1572872 | tf_op jit(solution)/shard_map/ppermute | solution.py:137
  78.1 2.4 %collective-permute-start.1 = (bf16[2,4,256,128]{3,2,1,0:T(8,128)(2,1)}, bf16[2,4,256,128]{3,2,1,0:T(8,128)(2,1)}, u32[]{:S(2)}, u32[]{:S(2)}) collective-permute-start(bf16[2,4,256,128]{3,2,1,0:T(8,128)(2,1)} %get-tuple-element.37), channel_id=1, source_target_pairs={{0,1},{1,0},{2,3},{3,2},{4,5},{5,4},{6,7},{7,6},{8,9},{9,8},{10,11... | collective-permute-start | bytes 1572872 | tf_op jit(solution)/shard_map/ppermute | solution.py:137
  80.5 0.0 copy-done
  80.5 0.6 fusion.5
  83.1 0.6 fusion.2
  83.7 0.5 fusion
  84.3 0.1 pad_maximum_fusion
  84.4 0.0 collective-permute-done.2.woth_ref
  84.4 0.0 collective-permute-done.oth0_ref
  84.4 0.0 collective-permute-done.1.oth1_ref
  84.4 4.0 %shard_map.65 = bf16[4,256,768]{2,1,0:T(8,128)(2,1)} custom-call(s32[1]{0:T(128)} %bitcast.c_ref, bf16[4,4,256,128]{3,2,1,0:T(8,128)(2,1)S(1)} %all-to-all-done.1.own_ref, bf16[2,4,256,128]{3,2,1,0:T(8,128)(2,1)S(1)} %collective-permute-done.oth0_ref, bf16[2,4,256,128]{3,2,1,0:T(8,128)(2,1)} %collective-permute-done.1.oth1_ref, ...), custom_call_target="tpu_custom_call" | custom-call | flops 1610612736 | bytes 6291456 | tf_op jit(solution)/shard_map/pallas_call | solution.py:27
  88.5 0.0 copy-start.4
  88.5 3.7 %all-to-all-start.2 = ((bf16[4,256,768]{2,1,0:T(8,128)(2,1)}), bf16[4,256,768]{2,1,0:T(8,128)(2,1)S(1)}, u32[]{:S(2)}, u32[]{:S(2)}) async-start(bf16[4,256,768]{2,1,0:T(8,128)(2,1)} %shard_map.65), calls=%async_computation.2 | async-start | bytes 3145728 | tf_op jit(solution)/shard_map/all_to_all | solution.py:164
  92.8 0.0 copy-done.4
  92.8 0.3 multiply_reduce_fusion
  93.1 1.9 %collective-permute-start.4 = (f32[256]{0:T(256)S(1)}, f32[256]{0:T(256)S(1)}, u32[]{:S(2)}, u32[]{:S(2)}) collective-permute-start(f32[256]{0:T(256)S(1)} %multiply_reduce_fusion), channel_id=1, source_target_pairs={{0,1},{1,0},{2,3},{3,2},{4,5},{5,4},{6,7},{7,6},{8,9},{9,8},{10,11... | collective-permute-start | bytes 3080 | tf_op jit(solution)/shard_map/ppermute | solution.py:167
  95.0 0.7 fusion.3
  95.8 3.9 %collective-permute-start.3 = (s32[1]{0:T(128)}, s32[1]{0:T(128)}, u32[]{:S(2)}, u32[]{:S(2)}) collective-permute-start(s32[1]{0:T(128)} %bitcast.9), channel_id=1, source_target_pairs={{0,8},{8,16},{16,24},{24,32},{32,40},{40,48},{48,56},{56,64},{64,7... | collective-permute-start | bytes 20 | tf_op jit(solution)/shard_map/ppermute | solution.py:173
  99.7 10.1 %collective-permute-done.3 = s32[1]{0:T(128)} collective-permute-done((s32[1]{0:T(128)}, s32[1]{0:T(128)}, u32[]{:S(2)}, u32[]{:S(2)}) %collective-permute-start.3) | collective-permute-done | bytes 36 | tf_op jit(solution)/shard_map/ppermute | solution.py:173
  109.8 1.4 %pad_add_fusion.1.n_ref = s32[2]{0:T(128)S(1)} fusion(s32[1]{0:T(128)} %bitcast.9, s32[1]{0:T(128)} %collective-permute-done.3), kind=kLoop, calls=%fused_computation.16 | loop fusion | flops 2 | bytes 16 | tf_op jit(solution)/shard_map/concatenate | solution.py:173
  111.2 0.0 collective-permute-done.4
  111.2 2.1 %all-to-all-done.2.p_ref = bf16[4,256,768]{2,1,0:T(8,128)(2,1)S(1)} async-done(((bf16[4,256,768]{2,1,0:T(8,128)(2,1)}), bf16[4,256,768]{2,1,0:T(8,128)(2,1)S(1)}, u32[]{:S(2)}, u32[]{:S(2)}) %all-to-all-start.2) | async-done | bytes 1572896 | tf_op jit(solution)/shard_map/all_to_all | solution.py:164
  113.3 0.1 copy.11.r_ref
  113.5 1.9 %shard_map.66.own_ref = bf16[256,512]{1,0:T(8,128)(2,1)S(1)} custom-call(s32[4]{0:T(128)S(1)} %bitcast.15, bf16[4,256,768]{2,1,0:T(8,128)(2,1)S(1)} %all-to-all-done.2.p_ref, f32[256,1]{1,0:T(8,128)S(1)} %copy.11.r_ref, f32[1,768]{1,0:T(1,128)S(1)} %reshape.45.bias_ref, f32[256,128]{1,0:T(8,128)S(1)} %get-tuple-element.35.cos_ref, ...), custom_call_target="tpu_custom_call" | custom-call | flops 134217728 | bytes 3145728 | tf_op jit(solution)/shard_map/pallas_call | solution.py:27
  115.3 2.5 %collective-permute-start.5 = (bf16[256,512]{1,0:T(8,128)(2,1)S(1)}, bf16[256,512]{1,0:T(8,128)(2,1)S(1)}, u32[]{:S(2)}, u32[]{:S(2)}) collective-permute-start(bf16[256,512]{1,0:T(8,128)(2,1)S(1)} %shard_map.66.own_ref), channel_id=1, source_target_pairs={{0,8},{8,16},{16,24},{24,32},{32,40},{40,48},{48,56},{56,64},{64,7... | collective-permute-start | bytes 786440 | tf_op jit(solution)/shard_map/ppermute | solution.py:179
  117.8 8.9 %collective-permute-done.5.prev_ref = bf16[256,512]{1,0:T(8,128)(2,1)S(1)} collective-permute-done((bf16[256,512]{1,0:T(8,128)(2,1)S(1)}, bf16[256,512]{1,0:T(8,128)(2,1)S(1)}, u32[]{:S(2)}, u32[]{:S(2)}) %collective-permute-start.5) | collective-permute-done | bytes 262176 | tf_op jit(solution)/shard_map/ppermute | solution.py:179
  126.7 1.8 %shard_map.67 = bf16[512,512]{1,0:T(8,128)(2,1)} custom-call(s32[2]{0:T(128)S(1)} %pad_add_fusion.1.n_ref, bf16[256,512]{1,0:T(8,128)(2,1)S(1)} %collective-permute-done.5.prev_ref, bf16[256,512]{1,0:T(8,128)(2,1)S(1)} %shard_map.66.own_ref), custom_call_target="tpu_custom_call" | custom-call | flops 268435456 | bytes 1048576 | tf_op jit(solution)/shard_map/pallas_call | solution.py:27
  (3 shorter events, 0.0 us)
Async XLA Ops:
  0.8 1.0 copy-start.1
  1.7 0.8 copy-start.2
  4.5 54.1 %all-to-all-start = ((bf16[4,4,256,128]{3,2,1,0:T(8,128)(2,1)}), bf16[4,4,256,128]{3,2,1,0:T(8,128)(2,1)S(1)}, u32[]{:S(2)}, u32[]{:S(2)}) async-start(bf16[4,4,256,128]{3,2,1,0:T(8,128)(2,1)} %get-tuple-element.21), calls=%async_computation | async-start | bytes 2097152 | tf_op jit(solution)/shard_map/all_to_all | solution.py:131
  58.6 1.4 %copy-start.3 = (bf16[4,4,256,128]{3,2,1,0:T(8,128)(2,1)}, bf16[4,4,256,128]{3,2,1,0:T(8,128)(2,1)S(1)}, u32[]{:S(2)}) copy-start(bf16[4,4,256,128]{3,2,1,0:T(8,128)(2,1)S(1)} %all-to-all-done) | copy-start | bytes 3145732
  59.7 4.5 %copy-start.5 = (bf16[768]{0:T(1024)(128)(2,1)S(1)}, bf16[768]{0:T(1024)(128)(2,1)}, u32[]{:S(2)}) copy-start(bf16[768]{0:T(1024)(128)(2,1)} %param.11) | copy-start | bytes 4612
  60.0 15.2 %all-to-all-start.1 = ((bf16[4,4,256,128]{3,2,1,0:T(8,128)(2,1)}), bf16[4,4,256,128]{3,2,1,0:T(8,128)(2,1)S(1)}, u32[]{:S(2)}, u32[]{:S(2)}) async-start(bf16[4,4,256,128]{3,2,1,0:T(8,128)(2,1)} %bitcast.16), calls=%async_computation.1 | async-start | bytes 2097152 | tf_op jit(solution)/shard_map/all_to_all | solution.py:136
  64.3 16.3 %copy-start = (s32[1,4]{1,0:T(1,128)S(1)}, s32[1,4]{1,0:T(1,128)}, u32[]{:S(2)}) copy-start(s32[1,4]{1,0:T(1,128)} %param.7) | copy-start | bytes 52
  64.3 20.1 %collective-permute-start.2 = (bf16[512,768]{1,0:T(8,128)(2,1)S(1)}, bf16[512,768]{1,0:T(8,128)(2,1)S(1)}, u32[]{:S(2)}, u32[]{:S(2)}) collective-permute-start(bf16[512,768]{1,0:T(8,128)(2,1)S(1)} %all_gather.3.wown_ref), channel_id=1, source_target_pairs={{0,32},{32,0},{1,33},{33,1},{2,34},{34,2},{3,35},{35,3},{4,36},{36... | collective-permute-start | bytes 2359304 | tf_op jit(solution)/shard_map/ppermute | solution.py:135
  76.2 8.2 %collective-permute-start = (bf16[2,4,256,128]{3,2,1,0:T(8,128)(2,1)}, bf16[2,4,256,128]{3,2,1,0:T(8,128)(2,1)S(1)}, u32[]{:S(2)}, u32[]{:S(2)}) collective-permute-start(bf16[2,4,256,128]{3,2,1,0:T(8,128)(2,1)} %get-tuple-element.38), channel_id=1, source_target_pairs={{0,1},{1,0},{2,3},{3,2},{4,5},{5,4},{6,7},{7,6},{8,9},{9,8},{10,11... | collective-permute-start | bytes 1572872 | tf_op jit(solution)/shard_map/ppermute | solution.py:137
  78.1 6.3 %collective-permute-start.1 = (bf16[2,4,256,128]{3,2,1,0:T(8,128)(2,1)}, bf16[2,4,256,128]{3,2,1,0:T(8,128)(2,1)}, u32[]{:S(2)}, u32[]{:S(2)}) collective-permute-start(bf16[2,4,256,128]{3,2,1,0:T(8,128)(2,1)} %get-tuple-element.37), channel_id=1, source_target_pairs={{0,1},{1,0},{2,3},{3,2},{4,5},{5,4},{6,7},{7,6},{8,9},{9,8},{10,11... | collective-permute-start | bytes 1572872 | tf_op jit(solution)/shard_map/ppermute | solution.py:137
  88.5 4.4 %copy-start.4 = (bf16[4,4,256,128]{3,2,1,0:T(8,128)(2,1)S(1)}, bf16[4,4,256,128]{3,2,1,0:T(8,128)(2,1)}, u32[]{:S(2)}) copy-start(bf16[4,4,256,128]{3,2,1,0:T(8,128)(2,1)} %copy-done.3) | copy-start | bytes 3145732
  88.5 24.8 %all-to-all-start.2 = ((bf16[4,256,768]{2,1,0:T(8,128)(2,1)}), bf16[4,256,768]{2,1,0:T(8,128)(2,1)S(1)}, u32[]{:S(2)}, u32[]{:S(2)}) async-start(bf16[4,256,768]{2,1,0:T(8,128)(2,1)} %shard_map.65), calls=%async_computation.2 | async-start | bytes 3145728 | tf_op jit(solution)/shard_map/all_to_all | solution.py:164
  93.1 18.0 %collective-permute-start.4 = (f32[256]{0:T(256)S(1)}, f32[256]{0:T(256)S(1)}, u32[]{:S(2)}, u32[]{:S(2)}) collective-permute-start(f32[256]{0:T(256)S(1)} %multiply_reduce_fusion), channel_id=1, source_target_pairs={{0,1},{1,0},{2,3},{3,2},{4,5},{5,4},{6,7},{7,6},{8,9},{9,8},{10,11... | collective-permute-start | bytes 3080 | tf_op jit(solution)/shard_map/ppermute | solution.py:167
  95.8 14.0 %collective-permute-start.3 = (s32[1]{0:T(128)}, s32[1]{0:T(128)}, u32[]{:S(2)}, u32[]{:S(2)}) collective-permute-start(s32[1]{0:T(128)} %bitcast.9), channel_id=1, source_target_pairs={{0,8},{8,16},{16,24},{24,32},{32,40},{40,48},{48,56},{56,64},{64,7... | collective-permute-start | bytes 20 | tf_op jit(solution)/shard_map/ppermute | solution.py:173
  115.3 11.4 %collective-permute-start.5 = (bf16[256,512]{1,0:T(8,128)(2,1)S(1)}, bf16[256,512]{1,0:T(8,128)(2,1)S(1)}, u32[]{:S(2)}, u32[]{:S(2)}) collective-permute-start(bf16[256,512]{1,0:T(8,128)(2,1)S(1)} %shard_map.66.own_ref), channel_id=1, source_target_pairs={{0,8},{8,16},{16,24},{24,32},{32,40},{40,48},{48,56},{56,64},{64,7... | collective-permute-start | bytes 786440 | tf_op jit(solution)/shard_map/ppermute | solution.py:179

commit v3 on v2

v3 whole, which is shorter than its diff:
```python
import jax
import jax.numpy as jnp
from jax import lax
from jax.experimental import pallas as pl
from jax.experimental.pallas import tpu as pltpu
from jax.sharding import Mesh
from jax.sharding import PartitionSpec as P

HEADS = 32
KV = 8
HEAD = 128
PER = HEADS // KV
EPSILON = 1e-06
ROPE_BASE = 1000000.0

NZ, NYL, NX, NYH, NC = 16, 2, 4, 4, 2
DP = ("z", "yl", "x")
TP = ("yh", "c")
WROWS = 32
ROWS = 256
SAMPLES = 4
EXTRA = 16
VMEM = 32 << 20


def call(kernel, out_shape, args, scalars=0, hbm=0, flops=0, nbytes=0, scratch=(), vmem_bytes=VMEM):
    smem = pl.BlockSpec(memory_space=pltpu.SMEM)
    vmem = pl.BlockSpec(memory_space=pltpu.VMEM)
    far = pl.BlockSpec(memory_space=pltpu.HBM)
    return pl.pallas_call(
        kernel,
        out_shape=out_shape,
        in_specs=[smem] * scalars + [far] * hbm + [vmem] * (len(args) - scalars - hbm),
        out_specs=[far] * len(out_shape) if isinstance(out_shape, list) else vmem,
        scratch_shapes=list(scratch),
        compiler_params=pltpu.CompilerParams(vmem_limit_bytes=vmem_bytes),
        cost_estimate=pl.CostEstimate(flops=flops, bytes_accessed=nbytes, transcendentals=0),
    )(*args)


def prepare_kernel(at_ref, s_hbm, w_hbm, gain_ref, o_hbm, ow_hbm, s_ref, w_ref, o_ref, sems):
    load_s = pltpu.make_async_copy(s_hbm, s_ref, sems.at[0])
    load_w = pltpu.make_async_copy(w_hbm, w_ref, sems.at[1])
    load_s.start()
    load_w.start()
    yl, dp = at_ref[0], at_ref[1]
    lines = gain_ref.shape[0]
    line = lax.broadcasted_iota(jnp.int32, (lines, 128), 0)
    gain = jnp.where(line == lax.shift_right_logical(dp, 2), gain_ref[...].astype(jnp.float32), 0.0)
    gain = jnp.sum(gain, axis=0, keepdims=True)
    row = lax.broadcasted_iota(jnp.int32, (WROWS, 128), 0)
    lane = lax.broadcasted_iota(jnp.int32, (WROWS, 128), 1)
    gain = jnp.sum(jnp.where(lane == (dp & 3) * WROWS + row, gain, 0.0), axis=1, keepdims=True)
    source = lax.broadcasted_iota(jnp.int32, (512, 128), 0)
    r = lax.broadcasted_iota(jnp.int32, (512, 128), 1)
    rel, zz, k = lax.shift_right_logical(r, 6), lax.shift_right_logical(r, 5) & 1, r & 31
    base = zz * 256 + (rel ^ yl) * 128 + k
    load_s.wait()
    stores = []
    for x in range(NX):
        perm = (source == base + x * 32).astype(jnp.bfloat16)
        o_ref[x] = jnp.dot(s_ref[...], perm, preferred_element_type=jnp.float32).astype(jnp.bfloat16)
        for yh in range(NYH):
            copy = pltpu.make_async_copy(o_ref.at[x], o_hbm.at[yh, x], sems.at[3 + x * NYH + yh])
            copy.start()
            stores.append(copy)
    load_w.wait()
    w_ref[...] = (w_ref[...].astype(jnp.float32) * gain).astype(jnp.bfloat16)
    copy = pltpu.make_async_copy(w_ref, ow_hbm, sems.at[2])
    copy.start()
    stores.append(copy)
    for copy in stores:
        copy.wait()


def matmul_kernel(c_ref, own_ref, oth0_ref, oth1_ref, wown_ref, woth_ref, o_ref, w_ref):
    c = c_ref[0]
    for rel in range(NC):
        for yh in range(NYH):
            row = pl.multiple_of((yh * 4 + (c ^ rel) * 2) * WROWS, 64)
            at = (rel * NYH + yh) * 128
            w_ref[at : at + 64] = wown_ref[pl.ds(row, 64)]
            w_ref[at + 64 : at + 128] = woth_ref[pl.ds(row, 64)]

    for n, oth_ref in enumerate((oth0_ref, oth1_ref)):
        for k in range(2):
            g = n * 2 + k
            x = jnp.concatenate([own_ref[g, yh] for yh in range(NYH)] + [oth_ref[k, yh] for yh in range(NYH)], axis=1)
            o_ref[g] = jnp.dot(x, w_ref[...], preferred_element_type=jnp.float32).astype(jnp.bfloat16)


def tail_of(lens, moved):
    return sum(jnp.where(n >= SAMPLES - moved, lens[n], 0) for n in range(SAMPLES))


def attend_kernel(len_ref, moved_ref, p_ref, sq_ref, sq2_ref, bias_ref, cos_ref, sin_ref, o_ref):
    s1 = len_ref[0]
    s2 = s1 + len_ref[1]
    s3 = s2 + len_ref[2]
    i = lax.broadcasted_iota(jnp.int32, (ROWS, ROWS), 0)
    j = lax.broadcasted_iota(jnp.int32, (ROWS, ROWS), 1)
    start = jnp.where(i >= s3, s3, jnp.where(i >= s2, s2, jnp.where(i >= s1, s1, 0)))
    allowed = (j >= start) & (j <= i)
    r = lax.rsqrt((sq_ref[...] + sq2_ref[...]) * (1.0 / (NZ * NYL * NX * WROWS)) + EPSILON)
    r = jnp.sum(jnp.where(i == j, r, 0.0), axis=1, keepdims=True)
    cos, sin = cos_ref[...], sin_ref[...]

    def head(n):
        at = n * HEAD
        total = p_ref[0, :, at : at + HEAD].astype(jnp.float32)
        for k in range(1, NX):
            total = total + p_ref[k, :, at : at + HEAD].astype(jnp.float32)
        return total * r + bias_ref[:, n * HEAD : (n + 1) * HEAD]

    def rotate(v):
        return (v * cos + pltpu.roll(v, HEAD // 2, 1) * sin).astype(jnp.bfloat16)

    key = rotate(head(PER))
    value = head(PER + 1).astype(jnp.bfloat16)
    for h in range(PER):
        query = rotate(head(h))
        scores = lax.dot_general(query, key, (((1,), (1,)), ((), ())), preferred_element_type=jnp.float32)
        scores = jnp.where(allowed, scores * HEAD ** (-0.5), -1e30)
        e = jnp.exp(scores - jnp.max(scores, axis=1, keepdims=True))
        weights = (e / jnp.sum(e, axis=1, keepdims=True)).astype(jnp.bfloat16)
        o_ref[:ROWS, h * HEAD : (h + 1) * HEAD] = jnp.dot(
            weights, value, preferred_element_type=jnp.float32
        ).astype(jnp.bfloat16)
    tail = tail_of(len_ref, moved_ref[0]).astype(jnp.float32)
    o_ref[ROWS:] = jnp.full((EXTRA, PER * HEAD), tail, jnp.float32).astype(jnp.bfloat16)


def pack_kernel(len_ref, moved_ref, prev_ref, own_ref, o_ref):
    tail = tail_of(len_ref, moved_ref[0])
    incoming = prev_ref[ROWS:, :HEAD].astype(jnp.float32)[:1, :1].astype(jnp.int32)
    slot = lax.broadcasted_iota(jnp.int32, (2 * ROWS, ROWS), 0)
    row = lax.broadcasted_iota(jnp.int32, (2 * ROWS, ROWS), 1)
    first = ((slot < incoming) & (row == slot + (ROWS - incoming))).astype(jnp.bfloat16)
    second = ((row == slot - incoming) & (row < ROWS - tail)).astype(jnp.bfloat16)
    picked = jnp.dot(first, prev_ref[:ROWS], preferred_element_type=jnp.float32)
    picked = picked + jnp.dot(second, own_ref[:ROWS], preferred_element_type=jnp.float32)
    o_ref[...] = picked.astype(jnp.bfloat16)


def local(states, lengths, moved, norm_gain, qkv_weight, qkv_bias):
    yl, c = lax.axis_index("yl"), lax.axis_index("c")
    dp = lax.axis_index(DP)
    bf = lambda *shape: jax.ShapeDtypeStruct(shape, jnp.bfloat16)

    columns = qkv_weight.shape[1]
    sent, scaled = call(
        prepare_kernel,
        [bf(NYH, NX, ROWS, 128), bf(WROWS, columns)],
        (jnp.stack([yl, dp]), states, qkv_weight, norm_gain.reshape(-1, 128)),
        1,
        2,
        flops=2 * 256 * 512 * 512,
        nbytes=1 << 20,
        scratch=[
            pltpu.VMEM((ROWS, 512), jnp.bfloat16),
            pltpu.VMEM((WROWS, columns), jnp.bfloat16),
            pltpu.VMEM((NX, ROWS, 128), jnp.bfloat16),
            pltpu.SemaphoreType.DMA((3 + NX * NYH,)),
        ],
        vmem_bytes=60 << 20,
    )
    raw = lax.all_to_all(sent, "yh", 0, 0, tiled=True)
    wown = lax.all_gather(scaled, "z", axis=0, tiled=True)
    raw, wown, lengths, moved, qkv_bias = lax.optimization_barrier((raw, wown, lengths, moved, qkv_bias))

    woth = lax.ppermute(wown, "yl", [(0, 1), (1, 0)])
    spread = lax.all_to_all(raw.transpose(1, 0, 2, 3), "x", 0, 0, tiled=True)

    squares = jnp.sum(jnp.square(raw.astype(jnp.float32)), axis=(0, 1, 3))
    lens = lengths[0]
    ids = jnp.arange(ROWS, dtype=jnp.int32)
    starts = [jnp.sum(lens[:n]) for n in range(SAMPLES)]
    begin = jnp.zeros_like(ids)
    for n in range(1, SAMPLES):
        begin = jnp.where(ids >= starts[n], starts[n], begin)
    positions = (ids - begin).astype(jnp.float32)
    inv_freq = ROPE_BASE ** (-(2.0 * jnp.arange(HEAD // 2, dtype=jnp.float32)) / HEAD)
    angles = positions[:, None] * inv_freq[None, :]
    cos, sin = jnp.cos(angles), jnp.sin(angles)
    cos = jnp.concatenate([cos, cos], axis=1)
    sin = jnp.concatenate([-sin, sin], axis=1)
    bias = qkv_bias.astype(jnp.float32)[None, :]
    spread, squares, bias, cos, sin = lax.optimization_barrier((spread, squares, bias, cos, sin))
    others = [lax.ppermute(spread[n * 2 : n * 2 + 2], "c", [(0, 1), (1, 0)]) for n in range(2)]

    partial = call(
        matmul_kernel,
        bf(NX, ROWS, columns),
        (c.reshape(1), spread, *others, wown, woth),
        1,
        flops=2 * NX * ROWS * 1024 * columns,
        nbytes=6 << 20,
        scratch=[pltpu.VMEM((1024, columns), jnp.bfloat16)],
    )
    partial, squares = lax.optimization_barrier((partial, squares))
    summed = lax.all_to_all(partial, "x", 0, 0, tiled=True)

    squares2 = lax.ppermute(squares, "c", [(0, 1), (1, 0)])
    context = call(
        attend_kernel,
        bf(ROWS + EXTRA, PER * HEAD),
        (lens, moved, summed, squares.reshape(1, ROWS), squares2.reshape(1, ROWS), bias, cos, sin),
        2,
        flops=4 * 4 * ROWS * ROWS * HEAD,
        nbytes=3 << 20,
    )
    previous = lax.ppermute(context, DP, [(i, i + 1) for i in range(NZ * NYL * NX - 1)])
    return call(
        pack_kernel,
        bf(2 * ROWS, PER * HEAD),
        (lens, moved, previous, context),
        2,
        flops=4 * 512 * 256 * 512,
        nbytes=1 << 20,
    )


def solution(mesh):
    fine = Mesh(mesh.devices.reshape(NZ, NYL, NX, NYH, NC), DP + TP)
    return jax.shard_map(
        local,
        mesh=fine,
        in_specs=(P(DP, TP), P(DP, None), P(DP), P(), P(DP, TP), P(TP)),
        out_specs=P(DP, TP),
        check_vma=False,
    )
```

time: 129 us -> 127 us (0.984)
  waiting for transfers between devices: 28.8 us -> 34 us
  starting transfers between devices: 31 us -> 27.5 us
  local copies, waits for them, and re-layouts: 5.65 us -> 2.36 us
  between operations: 2.72 us -> 0.79 us
    all_to_all x1, waiting for transfers between devices: 2.15 us -> 18.4 us  [local(): summed = lax.all_to_all(partial, 'x', 0, 0, tiled=True)]
    ppermute x3 -> x2, waiting for transfers between devices: 19 us -> 9.79 us  [the longest x1 9.64 us: local(): lax.ppermute(context, DP, [(i, i + 1) for i in range(NZ * NYL * NX - 1)])]
    all_to_all x1, waiting for transfers between devices: 7.6 us -> 3.95 us  [local(): spread = lax.all_to_all(raw.transpose(1, 0, 2, 3), 'x', 0, 0, tiled=True)]
    ppermute x3 -> x2, starting transfers between devices: 8.28 us -> 4.76 us  [the longest x1 2.47 us: local(): lax.ppermute(context, DP, [(i, i + 1) for i in range(NZ * NYL * NX - 1)])]
    ppermute x2, waiting for transfers between devices: 0.01 us -> 1.83 us  [local(): lax.ppermute(spread[n * 2:n * 2 + 2], 'c', [(0, 1), (1, 0)])]
    unnamed x12 -> x10, local copies, waits for them, and re-layouts: 1.99 us -> 0.21 us
    concatenate x1 -> x0, other arithmetic: 1.38 us -> none  [local(): counts = jnp.concatenate([lax.ppermute(tail, DP, shift), tail])]
  transfers between devices with their start and end apart: 9 -> 8, of which waited for: 4 -> 5; matrix products, arithmetic and copies ran while one was open for 4% -> 4% of each run, Pallas kernels for 0% -> 0%
where the time goes in v3:
time: 127 us; the launch traced here: 126 us
  blocking collectives  46.9 us (37%)
  waiting for transfers between devices  34 us (27%)
  starting transfers between devices  27.5 us (22%)
  Pallas kernels  10.7 us (8%)
  other arithmetic  4.24 us (3%)
  local copies, waits for them, and re-layouts  2.36 us (2%)
    all_gather x1, blocking collectives, local(): wown = lax.all_gather(scaled, 'z', axis=0, tiled=True)  46.9 us
    all_to_all x1, waiting for transfers between devices, local(): summed = lax.all_to_all(partial, 'x', 0, 0, tiled=True)  18.4 us
    pallas_call x4, Pallas kernels, call(): pl.pallas_call(kernel, out_shape=out_shape, in_specs=[smem] * scalars + [...  10.7 us
    ppermute x1, waiting for transfers between devices, local(): lax.ppermute(context, DP, [(i, i + 1) for i in range(NZ * NYL * NX - 1)])  9.64 us
    all_to_all x1, starting transfers between devices, local(): raw = lax.all_to_all(sent, 'yh', 0, 0, tiled=True)  7.34 us
    ppermute x2, starting transfers between devices, local(): lax.ppermute(spread[n * 2:n * 2 + 2], 'c', [(0, 1), (1, 0)])  4.32 us
    all_to_all x1, starting transfers between devices, local(): spread = lax.all_to_all(raw.transpose(1, 0, 2, 3), 'x', 0, 0, tiled=True)  4.29 us
    all_to_all x1, waiting for transfers between devices, local(): spread = lax.all_to_all(raw.transpose(1, 0, 2, 3), 'x', 0, 0, tiled=True)  3.95 us
  transfers between devices with their start and end apart: 8, of which 5 were waited for; matrix products, arithmetic and copies ran while one was open for 4% of the time, Pallas kernels for 0%

profile of v3, /device:TPU:40, one launch (start us, length us, event | category | flops | bytes accessed | tf_op | source)
XLA Modules:
  0.0 126.5 jit_solution(1790359981190774980)
XLA Ops:
  0.0 0.6 pad_add_fusion.at_ref
  0.6 3.0 %shard_map.64 = (bf16[4,4,256,128]{3,2,1,0:T(8,128)(2,1)}, bf16[32,768]{1,0:T(8,128)(2,1)}) custom-call(s32[2]{0:T(128)} %pad_add_fusion.at_ref, bf16[256,512]{1,0:T(8,128)(2,1)} %s_hbm.1, bf16[32,768]{1,0:T(8,128)(2,1)} %w_hbm.1, bf16[32,128]{1,0:T(8,128)(2,1)} %bitcast.17), custom_call_target="tpu_custom_call" | custom-call | flops 134217728 | bytes 1048576 | tf_op jit(solution)/shard_map/pallas_call | solution.py:30
  3.6 0.0 copy-start.3
  3.6 7.3 %all-to-all-start = ((bf16[4,4,256,128]{3,2,1,0:T(8,128)(2,1)}), bf16[4,4,256,128]{3,2,1,0:T(8,128)(2,1)S(1)}, u32[]{:S(2)}, u32[]{:S(2)}) async-start(bf16[4,4,256,128]{3,2,1,0:T(8,128)(2,1)} %get-tuple-element.19), calls=%async_computation | async-start | bytes 2097152 | tf_op jit(solution)/shard_map/all_to_all | solution.py:167
  11.0 0.0 copy-done.3
  11.0 46.9 %all_gather.3.wown_ref = bf16[512,768]{1,0:T(8,128)(2,1)S(1)} all-gather(bf16[32,768]{1,0:T(8,128)(2,1)S(1)} %copy-done.3), channel_id=1, replica_groups=mesh['z'=16,'yl'=2,'x'=4,'yh'=4,'c'=2] {'z'}, dimensions={0}, use_global_device_ids=true | all-gather | bytes 835584 | tf_op jit(solution)/shard_map/all_gather | solution.py:168
  57.9 0.0 all-to-all-done
  57.9 0.0 copy-start.1
  57.9 1.1 copy.10
  59.0 0.0 copy-start
  59.0 0.0 copy-start.4
  59.0 0.2 copy-done.1
  59.2 4.3 %all-to-all-start.1 = ((bf16[4,4,256,128]{3,2,1,0:T(8,128)(2,1)}), bf16[4,4,256,128]{3,2,1,0:T(8,128)(2,1)S(1)}, u32[]{:S(2)}, u32[]{:S(2)}) async-start(bf16[4,4,256,128]{3,2,1,0:T(8,128)(2,1)} %bitcast.10), calls=%async_computation.1 | async-start | bytes 2097152 | tf_op jit(solution)/shard_map/all_to_all | solution.py:172
  63.5 0.0 copy-done
  63.5 0.0 copy-start.2
  63.5 0.6 slice_reduce_fusion
  64.1 0.0 copy-done.4
  64.1 3.2 %collective-permute-start.2 = (bf16[512,768]{1,0:T(8,128)(2,1)S(1)}, bf16[512,768]{1,0:T(8,128)(2,1)S(1)}, u32[]{:S(2)}, u32[]{:S(2)}) collective-permute-start(bf16[512,768]{1,0:T(8,128)(2,1)S(1)} %all_gather.3.wown_ref), channel_id=1, source_target_pairs={{0,32},{32,0},{1,33},{33,1},{2,34},{34,2},{3,35},{35,3},{4,36},{36... | collective-permute-start | bytes 2359304 | tf_op jit(solution)/shard_map/ppermute | solution.py:171
  67.4 0.7 slice_reduce_fusion.1
  68.1 1.4 %fusion.2 = f32[256]{0:T(256)S(1)} fusion(s32[]{:T(128)S(1)} %bitcast.12, s32[]{:T(128)} %slice_reduce_fusion, s32[]{:T(128)} %slice_reduce_fusion.1), kind=kLoop, calls=%fused_computation.11 | loop fusion | flops 2048 | bytes 1036 | tf_op jit(solution)/shard_map/convert_element_type | solution.py:181
  69.4 0.5 fusion
  70.0 0.1 pad_maximum_fusion
  70.1 0.0 copy-done.2
  70.1 0.3 multiply_reduce_fusion
  70.4 3.9 %all-to-all-done.1.own_ref = bf16[4,4,256,128]{3,2,1,0:T(8,128)(2,1)S(1)} async-done(((bf16[4,4,256,128]{3,2,1,0:T(8,128)(2,1)}), bf16[4,4,256,128]{3,2,1,0:T(8,128)(2,1)S(1)}, u32[]{:S(2)}, u32[]{:S(2)}) %all-to-all-start.1) | async-done | bytes 1048608 | tf_op jit(solution)/shard_map/all_to_all | solution.py:172
  74.4 1.0 fusion.3
  75.4 1.9 %collective-permute-start = (bf16[2,4,256,128]{3,2,1,0:T(8,128)(2,1)}, bf16[2,4,256,128]{3,2,1,0:T(8,128)(2,1)S(1)}, u32[]{:S(2)}, u32[]{:S(2)}) collective-permute-start(bf16[2,4,256,128]{3,2,1,0:T(8,128)(2,1)} %get-tuple-element.34), channel_id=1, source_target_pairs={{0,1},{1,0},{2,3},{3,2},{4,5},{5,4},{6,7},{7,6},{8,9},{9,8},{10,11... | collective-permute-start | bytes 1572872 | tf_op jit(solution)/shard_map/ppermute | solution.py:189
  77.3 2.4 %collective-permute-start.1 = (bf16[2,4,256,128]{3,2,1,0:T(8,128)(2,1)}, bf16[2,4,256,128]{3,2,1,0:T(8,128)(2,1)}, u32[]{:S(2)}, u32[]{:S(2)}) collective-permute-start(bf16[2,4,256,128]{3,2,1,0:T(8,128)(2,1)} %get-tuple-element.33), channel_id=1, source_target_pairs={{0,1},{1,0},{2,3},{3,2},{4,5},{5,4},{6,7},{7,6},{8,9},{9,8},{10,11... | collective-permute-start | bytes 1572872 | tf_op jit(solution)/shard_map/ppermute | solution.py:189
  79.7 0.0 collective-permute-done.2.woth_ref
  79.7 0.0 collective-permute-done.oth0_ref
  79.8 1.8 %collective-permute-done.1.oth1_ref = bf16[2,4,256,128]{3,2,1,0:T(8,128)(2,1)} collective-permute-done((bf16[2,4,256,128]{3,2,1,0:T(8,128)(2,1)}, bf16[2,4,256,128]{3,2,1,0:T(8,128)(2,1)}, u32[]{:S(2)}, u32[]{:S(2)}) %collective-permute-start.1) | collective-permute-done | bytes 524320 | tf_op jit(solution)/shard_map/ppermute | solution.py:189
  81.6 4.0 %shard_map.65 = bf16[4,256,768]{2,1,0:T(8,128)(2,1)} custom-call(s32[1]{0:T(128)} %bitcast.4.c_ref, bf16[4,4,256,128]{3,2,1,0:T(8,128)(2,1)S(1)} %all-to-all-done.1.own_ref, bf16[2,4,256,128]{3,2,1,0:T(8,128)(2,1)S(1)} %collective-permute-done.oth0_ref, bf16[2,4,256,128]{3,2,1,0:T(8,128)(2,1)} %collective-permute-done.1.oth1_ref, ...), custom_call_target="tpu_custom_call" | custom-call | flops 1610612736 | bytes 6291456 | tf_op jit(solution)/shard_map/pallas_call | solution.py:30
  85.6 3.6 %all-to-all-start.2 = ((bf16[4,256,768]{2,1,0:T(8,128)(2,1)}), bf16[4,256,768]{2,1,0:T(8,128)(2,1)S(1)}, u32[]{:S(2)}, u32[]{:S(2)}) async-start(bf16[4,256,768]{2,1,0:T(8,128)(2,1)} %shard_map.65), calls=%async_computation.2 | async-start | bytes 3145728 | tf_op jit(solution)/shard_map/all_to_all | solution.py:201
  89.2 2.3 %collective-permute-start.3 = (f32[256]{0:T(256)S(1)}, f32[256]{0:T(256)S(1)}, u32[]{:S(2)}, u32[]{:S(2)}) collective-permute-start(f32[256]{0:T(256)S(1)} %multiply_reduce_fusion), channel_id=1, source_target_pairs={{0,1},{1,0},{2,3},{3,2},{4,5},{5,4},{6,7},{7,6},{8,9},{9,8},{10,11... | collective-permute-start | bytes 3080 | tf_op jit(solution)/shard_map/ppermute | solution.py:203
  92.1 0.1 collective-permute-done.3
  92.3 18.4 %all-to-all-done.2.p_ref = bf16[4,256,768]{2,1,0:T(8,128)(2,1)S(1)} async-done(((bf16[4,256,768]{2,1,0:T(8,128)(2,1)}), bf16[4,256,768]{2,1,0:T(8,128)(2,1)S(1)}, u32[]{:S(2)}, u32[]{:S(2)}) %all-to-all-start.2) | async-done | bytes 1572896 | tf_op jit(solution)/shard_map/all_to_all | solution.py:201
  110.7 1.9 %shard_map.66.own_ref = bf16[272,512]{1,0:T(8,128)(2,1)S(1)} custom-call(s32[4]{0:T(128)S(1)} %bitcast.13, s32[1]{0:T(128)S(6)} %copy.11.moved_ref, bf16[4,256,768]{2,1,0:T(8,128)(2,1)S(1)} %all-to-all-done.2.p_ref, f32[1,256]{1,0:T(1,128)S(1)} %bitcast.15, f32[1,256]{1,0:T(1,128)S(1)} %bitcast.16, f32[1,768]{1,0:T(1,128)S(1)} %reshape.42.bias_ref, ...), custom_call_target="tpu_custom_call" | custom-call | flops 134217728 | bytes 3145728 | tf_op jit(solution)/shard_map/pallas_call | solution.py:30
  112.6 2.5 %collective-permute-start.4 = (bf16[272,512]{1,0:T(8,128)(2,1)S(1)}, bf16[272,512]{1,0:T(8,128)(2,1)S(1)}, u32[]{:S(2)}, u32[]{:S(2)}) collective-permute-start(bf16[272,512]{1,0:T(8,128)(2,1)S(1)} %shard_map.66.own_ref), channel_id=1, source_target_pairs={{0,8},{8,16},{16,24},{24,32},{32,40},{40,48},{48,56},{56,64},{64,7... | collective-permute-start | bytes 835592 | tf_op jit(solution)/shard_map/ppermute | solution.py:212
  115.0 9.6 %collective-permute-done.4.prev_ref = bf16[272,512]{1,0:T(8,128)(2,1)S(1)} collective-permute-done((bf16[272,512]{1,0:T(8,128)(2,1)S(1)}, bf16[272,512]{1,0:T(8,128)(2,1)S(1)}, u32[]{:S(2)}, u32[]{:S(2)}) %collective-permute-start.4) | collective-permute-done | bytes 278560 | tf_op jit(solution)/shard_map/ppermute | solution.py:212
  124.7 1.8 %shard_map.67 = bf16[512,512]{1,0:T(8,128)(2,1)} custom-call(s32[4]{0:T(128)S(1)} %bitcast.14, s32[1]{0:T(128)S(6)} %copy.11.moved_ref, bf16[272,512]{1,0:T(8,128)(2,1)S(1)} %collective-permute-done.4.prev_ref, bf16[272,512]{1,0:T(8,128)(2,1)S(1)} %shard_map.66.own_ref), custom_call_target="tpu_custom_call" | custom-call | flops 268435456 | bytes 1048576 | tf_op jit(solution)/shard_map/pallas_call | solution.py:30
  (2 shorter events, 0.0 us)
Async XLA Ops:
  3.6 7.4 %copy-start.3 = (bf16[32,768]{1,0:T(8,128)(2,1)S(1)}, bf16[32,768]{1,0:T(8,128)(2,1)}, u32[]{:S(2)}) copy-start(bf16[32,768]{1,0:T(8,128)(2,1)} %get-tuple-element.20) | copy-start | bytes 147460
  3.6 54.3 %all-to-all-start = ((bf16[4,4,256,128]{3,2,1,0:T(8,128)(2,1)}), bf16[4,4,256,128]{3,2,1,0:T(8,128)(2,1)S(1)}, u32[]{:S(2)}, u32[]{:S(2)}) async-start(bf16[4,4,256,128]{3,2,1,0:T(8,128)(2,1)} %get-tuple-element.19), calls=%async_computation | async-start | bytes 2097152 | tf_op jit(solution)/shard_map/all_to_all | solution.py:167
  57.9 1.3 %copy-start.1 = (bf16[4,4,256,128]{3,2,1,0:T(8,128)(2,1)}, bf16[4,4,256,128]{3,2,1,0:T(8,128)(2,1)S(1)}, u32[]{:S(2)}) copy-start(bf16[4,4,256,128]{3,2,1,0:T(8,128)(2,1)S(1)} %all-to-all-done) | copy-start | bytes 3145732
  59.0 4.5 %copy-start = (s32[1,4]{1,0:T(1,128)S(1)}, s32[1,4]{1,0:T(1,128)}, u32[]{:S(2)}) copy-start(s32[1,4]{1,0:T(1,128)} %param.7) | copy-start | bytes 52
  59.0 5.1 %copy-start.4 = (bf16[768]{0:T(1024)(128)(2,1)S(1)}, bf16[768]{0:T(1024)(128)(2,1)}, u32[]{:S(2)}) copy-start(bf16[768]{0:T(1024)(128)(2,1)} %param.11) | copy-start | bytes 4612
  59.2 15.2 %all-to-all-start.1 = ((bf16[4,4,256,128]{3,2,1,0:T(8,128)(2,1)}), bf16[4,4,256,128]{3,2,1,0:T(8,128)(2,1)S(1)}, u32[]{:S(2)}, u32[]{:S(2)}) async-start(bf16[4,4,256,128]{3,2,1,0:T(8,128)(2,1)} %bitcast.10), calls=%async_computation.1 | async-start | bytes 2097152 | tf_op jit(solution)/shard_map/all_to_all | solution.py:172
  63.5 6.6 %copy-start.2 = (bf16[4,4,256,128]{3,2,1,0:T(8,128)(2,1)S(1)}, bf16[4,4,256,128]{3,2,1,0:T(8,128)(2,1)}, u32[]{:S(2)}) copy-start(bf16[4,4,256,128]{3,2,1,0:T(8,128)(2,1)} %copy-done.1) | copy-start | bytes 3145732
  64.1 15.6 %collective-permute-start.2 = (bf16[512,768]{1,0:T(8,128)(2,1)S(1)}, bf16[512,768]{1,0:T(8,128)(2,1)S(1)}, u32[]{:S(2)}, u32[]{:S(2)}) collective-permute-start(bf16[512,768]{1,0:T(8,128)(2,1)S(1)} %all_gather.3.wown_ref), channel_id=1, source_target_pairs={{0,32},{32,0},{1,33},{33,1},{2,34},{34,2},{3,35},{35,3},{4,36},{36... | collective-permute-start | bytes 2359304 | tf_op jit(solution)/shard_map/ppermute | solution.py:171
  75.4 4.3 %collective-permute-start = (bf16[2,4,256,128]{3,2,1,0:T(8,128)(2,1)}, bf16[2,4,256,128]{3,2,1,0:T(8,128)(2,1)S(1)}, u32[]{:S(2)}, u32[]{:S(2)}) collective-permute-start(bf16[2,4,256,128]{3,2,1,0:T(8,128)(2,1)} %get-tuple-element.34), channel_id=1, source_target_pairs={{0,1},{1,0},{2,3},{3,2},{4,5},{5,4},{6,7},{7,6},{8,9},{9,8},{10,11... | collective-permute-start | bytes 1572872 | tf_op jit(solution)/shard_map/ppermute | solution.py:189
  77.3 4.3 %collective-permute-start.1 = (bf16[2,4,256,128]{3,2,1,0:T(8,128)(2,1)}, bf16[2,4,256,128]{3,2,1,0:T(8,128)(2,1)}, u32[]{:S(2)}, u32[]{:S(2)}) collective-permute-start(bf16[2,4,256,128]{3,2,1,0:T(8,128)(2,1)} %get-tuple-element.33), channel_id=1, source_target_pairs={{0,1},{1,0},{2,3},{3,2},{4,5},{5,4},{6,7},{7,6},{8,9},{9,8},{10,11... | collective-permute-start | bytes 1572872 | tf_op jit(solution)/shard_map/ppermute | solution.py:189
  85.6 25.1 %all-to-all-start.2 = ((bf16[4,256,768]{2,1,0:T(8,128)(2,1)}), bf16[4,256,768]{2,1,0:T(8,128)(2,1)S(1)}, u32[]{:S(2)}, u32[]{:S(2)}) async-start(bf16[4,256,768]{2,1,0:T(8,128)(2,1)} %shard_map.65), calls=%async_computation.2 | async-start | bytes 3145728 | tf_op jit(solution)/shard_map/all_to_all | solution.py:201
  89.2 3.1 %collective-permute-start.3 = (f32[256]{0:T(256)S(1)}, f32[256]{0:T(256)S(1)}, u32[]{:S(2)}, u32[]{:S(2)}) collective-permute-start(f32[256]{0:T(256)S(1)} %multiply_reduce_fusion), channel_id=1, source_target_pairs={{0,1},{1,0},{2,3},{3,2},{4,5},{5,4},{6,7},{7,6},{8,9},{9,8},{10,11... | collective-permute-start | bytes 3080 | tf_op jit(solution)/shard_map/ppermute | solution.py:203
  112.6 12.1 %collective-permute-start.4 = (bf16[272,512]{1,0:T(8,128)(2,1)S(1)}, bf16[272,512]{1,0:T(8,128)(2,1)S(1)}, u32[]{:S(2)}, u32[]{:S(2)}) collective-permute-start(bf16[272,512]{1,0:T(8,128)(2,1)S(1)} %shard_map.66.own_ref), channel_id=1, source_target_pairs={{0,8},{8,16},{16,24},{24,32},{32,40},{40,48},{48,56},{56,64},{64,7... | collective-permute-start | bytes 835592 | tf_op jit(solution)/shard_map/ppermute | solution.py:212

commit v4 on v3

--- a/solution.py
+++ b/solution.py
@@ -20,7 +20,8 @@
 ROWS = 256
 SAMPLES = 4
 EXTRA = 16
-VMEM = 32 << 20
+NEAR = (1, 3, 0)
+VMEM = 16 << 20
 
 
 def call(kernel, out_shape, args, scalars=0, hbm=0, flops=0, nbytes=0, scratch=(), vmem_bytes=VMEM):
@@ -31,7 +32,7 @@
         kernel,
         out_shape=out_shape,
         in_specs=[smem] * scalars + [far] * hbm + [vmem] * (len(args) - scalars - hbm),
-        out_specs=[far] * len(out_shape) if isinstance(out_shape, list) else vmem,
+        out_specs=[far] * len(out_shape) if isinstance(out_shape, list) else jax.tree.map(lambda _: vmem, out_shape),
         scratch_shapes=list(scratch),
         compiler_params=pltpu.CompilerParams(vmem_limit_bytes=vmem_bytes),
         cost_estimate=pl.CostEstimate(flops=flops, bytes_accessed=nbytes, transcendentals=0),
@@ -73,27 +74,39 @@
         copy.wait()
 
 
-def matmul_kernel(c_ref, own_ref, oth0_ref, oth1_ref, wown_ref, woth_ref, o_ref, w_ref):
-    c = c_ref[0]
+def first_kernel(at_ref, own_ref, oth0_ref, oth1_ref, wown_ref, woth_ref, o_ref, w_ref, x_ref):
+    far, c = at_ref[0], at_ref[1]
     for rel in range(NC):
         for yh in range(NYH):
             row = pl.multiple_of((yh * 4 + (c ^ rel) * 2) * WROWS, 64)
             at = (rel * NYH + yh) * 128
             w_ref[at : at + 64] = wown_ref[pl.ds(row, 64)]
             w_ref[at + 64 : at + 128] = woth_ref[pl.ds(row, 64)]
-
-    for n, oth_ref in enumerate((oth0_ref, oth1_ref)):
-        for k in range(2):
-            g = n * 2 + k
-            x = jnp.concatenate([own_ref[g, yh] for yh in range(NYH)] + [oth_ref[k, yh] for yh in range(NYH)], axis=1)
-            o_ref[g] = jnp.dot(x, w_ref[...], preferred_element_type=jnp.float32).astype(jnp.bfloat16)
+    half = NYH // 2
+
+    def states(g):
+        return jnp.concatenate(
+            [own_ref[g, yh] for yh in range(NYH)]
+            + [oth0_ref[g, yh] for yh in range(half)]
+            + [oth1_ref[g, yh] for yh in range(half)],
+            axis=1,
+        )
+
+    o_ref[...] = jnp.dot(states(far), w_ref[...], preferred_element_type=jnp.float32).astype(jnp.bfloat16)
+    for n, step in enumerate(NEAR):
+        x_ref[n] = states((far + 2 + step) & 3)
+
+
+def second_kernel(x_ref, w_ref, o1_ref, o3_ref, own_ref):
+    for n, ref in enumerate((o1_ref, o3_ref, own_ref)):
+        ref[...] = jnp.dot(x_ref[n], w_ref[...], preferred_element_type=jnp.float32).astype(ref.dtype)
 
 
 def tail_of(lens, moved):
     return sum(jnp.where(n >= SAMPLES - moved, lens[n], 0) for n in range(SAMPLES))
 
 
-def attend_kernel(len_ref, moved_ref, p_ref, sq_ref, sq2_ref, bias_ref, cos_ref, sin_ref, o_ref):
+def attend_kernel(len_ref, moved_ref, p0_ref, p1_ref, p2_ref, sq_ref, sq2_ref, bias_ref, cos_ref, sin_ref, o_ref):
     s1 = len_ref[0]
     s2 = s1 + len_ref[1]
     s3 = s2 + len_ref[2]
@@ -107,9 +120,9 @@
 
     def head(n):
         at = n * HEAD
-        total = p_ref[0, :, at : at + HEAD].astype(jnp.float32)
-        for k in range(1, NX):
-            total = total + p_ref[k, :, at : at + HEAD].astype(jnp.float32)
+        total = p0_ref[:, at : at + HEAD]
+        for ref in (p1_ref, p2_ref):
+            total = total + ref[:, at : at + HEAD].astype(jnp.float32)
         return total * r + bias_ref[:, n * HEAD : (n + 1) * HEAD]
 
     def rotate(v):
@@ -186,25 +199,35 @@
     sin = jnp.concatenate([-sin, sin], axis=1)
     bias = qkv_bias.astype(jnp.float32)[None, :]
     spread, squares, bias, cos, sin = lax.optimization_barrier((spread, squares, bias, cos, sin))
-    others = [lax.ppermute(spread[n * 2 : n * 2 + 2], "c", [(0, 1), (1, 0)]) for n in range(2)]
-
-    partial = call(
-        matmul_kernel,
-        bf(NX, ROWS, columns),
-        (c.reshape(1), spread, *others, wown, woth),
+    others = [lax.ppermute(spread[:, n * 2 : n * 2 + 2], "c", [(0, 1), (1, 0)]) for n in range(2)]
+
+    x = lax.axis_index("x")
+    whole = lambda step, v: lax.ppermute(v, "x", [(i, (i + step) % NX) for i in range(NX)])
+    flops = 2 * ROWS * 1024 * columns
+    far, weights, near = call(
+        first_kernel,
+        (bf(ROWS, columns), bf(1024, columns), bf(3, ROWS, 1024)),
+        (jnp.stack([(x + 2) & 3, c]), spread, *others, wown, woth),
         1,
-        flops=2 * NX * ROWS * 1024 * columns,
+        flops=flops,
         nbytes=6 << 20,
-        scratch=[pltpu.VMEM((1024, columns), jnp.bfloat16)],
-    )
-    partial, squares = lax.optimization_barrier((partial, squares))
-    summed = lax.all_to_all(partial, "x", 0, 0, tiled=True)
-
+    )
+    far = whole(2, far)
+    right, left, own = call(
+        second_kernel,
+        (bf(ROWS, columns), bf(ROWS, columns), jax.ShapeDtypeStruct((ROWS, columns), jnp.float32)),
+        (near, weights),
+        flops=3 * flops,
+        nbytes=4 << 20,
+    )
+    right, left = whole(1, right), whole(3, left)
+    own, squares = lax.optimization_barrier((own, squares))
+    own = own + far.astype(jnp.float32)
     squares2 = lax.ppermute(squares, "c", [(0, 1), (1, 0)])
     context = call(
         attend_kernel,
         bf(ROWS + EXTRA, PER * HEAD),
-        (lens, moved, summed, squares.reshape(1, ROWS), squares2.reshape(1, ROWS), bias, cos, sin),
+        (lens, moved, own, right, left, squares.reshape(1, ROWS), squares2.reshape(1, ROWS), bias, cos, sin),
         2,
         flops=4 * 4 * ROWS * ROWS * HEAD,
         nbytes=3 << 20,

time: 127 us -> 124 us (0.976)
  waiting for transfers between devices: 34 us -> 25.6 us
  starting transfers between devices: 27.5 us -> 33.1 us
    all_to_all x1 -> x0, waiting for transfers between devices: 18.4 us -> none  [local(): summed = lax.all_to_all(partial, 'x', 0, 0, tiled=True)]
    ppermute x2 -> x5, waiting for transfers between devices: 1.83 us -> 11.4 us  [the longest x3 9.61 us: local(): lax.ppermute(v, 'x', [(i, (i + step) % NX) for i in range(NX)])]
    ppermute x2 -> x5, starting transfers between devices: 4.32 us -> 13.9 us  [the longest x3 9.54 us: local(): lax.ppermute(v, 'x', [(i, (i + step) % NX) for i in range(NX)])]
    all_to_all x1 -> x0, starting transfers between devices: 3.56 us -> none  [local(): summed = lax.all_to_all(partial, 'x', 0, 0, tiled=True)]
    pallas_call x4 -> x5, Pallas kernels: 10.7 us -> 9.92 us  [call(): pl.pallas_call(kernel, out_shape=out_shape, in_specs=[smem] * scalars + [...]
  transfers between devices with their start and end apart: 8 -> 10, of which waited for: 5 -> 5; matrix products, arithmetic and copies ran while one was open for 4% -> 4% of each run, Pallas kernels for 0% -> 1%
where the time goes in v4:
time: 124 us; the launch traced here: 123 us
  blocking collectives  46.9 us (38%)
  starting transfers between devices  33.1 us (27%)
  waiting for transfers between devices  25.6 us (21%)
  Pallas kernels  9.92 us (8%)
  other arithmetic  4.36 us (4%)
  local copies, waits for them, and re-layouts  2.39 us (2%)
    all_gather x1, blocking collectives, local(): wown = lax.all_gather(scaled, 'z', axis=0, tiled=True)  46.9 us
    ppermute x1, waiting for transfers between devices, local(): lax.ppermute(context, DP, [(i, i + 1) for i in range(NZ * NYL * NX - 1)])  10.1 us
    pallas_call x5, Pallas kernels, call(): pl.pallas_call(kernel, out_shape=out_shape, in_specs=[smem] * scalars + [...  9.92 us
    ppermute x3, waiting for transfers between devices, local(): lax.ppermute(v, 'x', [(i, (i + step) % NX) for i in range(NX)])  9.61 us
    ppermute x3, starting transfers between devices, local(): lax.ppermute(v, 'x', [(i, (i + step) % NX) for i in range(NX)])  9.54 us
    all_to_all x1, starting transfers between devices, local(): raw = lax.all_to_all(sent, 'yh', 0, 0, tiled=True)  7.34 us
    ppermute x2, starting transfers between devices, local(): lax.ppermute(spread[:, n * 2:n * 2 + 2], 'c', [(0, 1), (1, 0)])  4.32 us
    all_to_all x1, starting transfers between devices, local(): spread = lax.all_to_all(raw.transpose(1, 0, 2, 3), 'x', 0, 0, tiled=True)  4.29 us
  transfers between devices with their start and end apart: 10, of which 5 were waited for; matrix products, arithmetic and copies ran while one was open for 4% of the time, Pallas kernels for 1%

profile of v4, /device:TPU:40, one launch (start us, length us, event | category | flops | bytes accessed | tf_op | source)
XLA Modules:
  0.0 123.1 jit_solution(1252103569895165623)
XLA Ops:
  0.0 0.7 pad_add_fusion.at_ref
  0.7 3.0 %shard_map.64 = (bf16[4,4,256,128]{3,2,1,0:T(8,128)(2,1)}, bf16[32,768]{1,0:T(8,128)(2,1)}) custom-call(s32[2]{0:T(128)} %pad_add_fusion.at_ref, bf16[256,512]{1,0:T(8,128)(2,1)} %s_hbm.1, bf16[32,768]{1,0:T(8,128)(2,1)} %w_hbm.1, bf16[32,128]{1,0:T(8,128)(2,1)} %bitcast.18), custom_call_target="tpu_custom_call" | custom-call | flops 134217728 | bytes 1048576 | tf_op jit(solution)/shard_map/pallas_call | solution.py:31
  3.7 0.0 copy-start.3
  3.7 7.3 %all-to-all-start = ((bf16[4,4,256,128]{3,2,1,0:T(8,128)(2,1)}), bf16[4,4,256,128]{3,2,1,0:T(8,128)(2,1)S(1)}, u32[]{:S(2)}, u32[]{:S(2)}) async-start(bf16[4,4,256,128]{3,2,1,0:T(8,128)(2,1)} %get-tuple-element.25), calls=%async_computation | async-start | bytes 2097152 | tf_op jit(solution)/shard_map/all_to_all | solution.py:180
  11.1 0.0 copy-done.3
  11.1 46.9 %all_gather.3.wown_ref = bf16[512,768]{1,0:T(8,128)(2,1)S(1)} all-gather(bf16[32,768]{1,0:T(8,128)(2,1)S(1)} %copy-done.3), channel_id=1, replica_groups=mesh['z'=16,'yl'=2,'x'=4,'yh'=4,'c'=2] {'z'}, dimensions={0}, use_global_device_ids=true | all-gather | bytes 835584 | tf_op jit(solution)/shard_map/all_gather | solution.py:181
  58.0 0.0 all-to-all-done
  58.0 0.0 copy-start.1
  58.0 1.2 copy.10
  59.1 0.0 copy-start
  59.1 0.0 copy-start.4
  59.1 0.1 copy-done.1
  59.3 4.3 %all-to-all-start.1 = ((bf16[4,4,256,128]{3,2,1,0:T(8,128)(2,1)}), bf16[4,4,256,128]{3,2,1,0:T(8,128)(2,1)S(1)}, u32[]{:S(2)}, u32[]{:S(2)}) async-start(bf16[4,4,256,128]{3,2,1,0:T(8,128)(2,1)} %bitcast.11), calls=%async_computation.1 | async-start | bytes 2097152 | tf_op jit(solution)/shard_map/all_to_all | solution.py:185
  63.6 0.0 copy-done
  63.6 0.0 copy-start.2
  63.6 0.6 slice_reduce_fusion
  64.2 0.0 copy-done.4
  64.2 3.2 %collective-permute-start.2 = (bf16[512,768]{1,0:T(8,128)(2,1)S(1)}, bf16[512,768]{1,0:T(8,128)(2,1)S(1)}, u32[]{:S(2)}, u32[]{:S(2)}) collective-permute-start(bf16[512,768]{1,0:T(8,128)(2,1)S(1)} %all_gather.3.wown_ref), channel_id=1, source_target_pairs={{0,32},{32,0},{1,33},{33,1},{2,34},{34,2},{3,35},{35,3},{4,36},{36... | collective-permute-start | bytes 2359304 | tf_op jit(solution)/shard_map/ppermute | solution.py:184
  67.5 0.7 slice_reduce_fusion.1
  68.1 1.3 %fusion.2 = f32[256]{0:T(256)S(1)} fusion(s32[]{:T(128)S(1)} %bitcast.13, s32[]{:T(128)} %slice_reduce_fusion, s32[]{:T(128)} %slice_reduce_fusion.1), kind=kLoop, calls=%fused_computation.12 | loop fusion | flops 2048 | bytes 1036 | tf_op jit(solution)/shard_map/convert_element_type | solution.py:194
  69.4 0.5 fusion
  70.0 0.1 pad_maximum_fusion
  70.1 0.0 copy-done.2
  70.1 0.3 multiply_reduce_fusion
  70.4 4.1 %all-to-all-done.1.own_ref = bf16[4,4,256,128]{3,2,1,0:T(8,128)(2,1)S(1)} async-done(((bf16[4,4,256,128]{3,2,1,0:T(8,128)(2,1)}), bf16[4,4,256,128]{3,2,1,0:T(8,128)(2,1)S(1)}, u32[]{:S(2)}, u32[]{:S(2)}) %all-to-all-start.1) | async-done | bytes 1048608 | tf_op jit(solution)/shard_map/all_to_all | solution.py:185
  74.5 1.1 fusion.3
  75.5 1.9 %collective-permute-start = (bf16[4,2,256,128]{3,2,1,0:T(8,128)(2,1)}, bf16[4,2,256,128]{3,2,1,0:T(8,128)(2,1)S(1)}, u32[]{:S(2)}, u32[]{:S(2)}) collective-permute-start(bf16[4,2,256,128]{3,2,1,0:T(8,128)(2,1)} %get-tuple-element.46), channel_id=1, source_target_pairs={{0,1},{1,0},{2,3},{3,2},{4,5},{5,4},{6,7},{7,6},{8,9},{9,8},{10,11... | collective-permute-start | bytes 1572872 | tf_op jit(solution)/shard_map/ppermute | solution.py:202
  77.4 2.4 %collective-permute-start.1 = (bf16[4,2,256,128]{3,2,1,0:T(8,128)(2,1)}, bf16[4,2,256,128]{3,2,1,0:T(8,128)(2,1)}, u32[]{:S(2)}, u32[]{:S(2)}) collective-permute-start(bf16[4,2,256,128]{3,2,1,0:T(8,128)(2,1)} %get-tuple-element.45), channel_id=1, source_target_pairs={{0,1},{1,0},{2,3},{3,2},{4,5},{5,4},{6,7},{7,6},{8,9},{9,8},{10,11... | collective-permute-start | bytes 1572872 | tf_op jit(solution)/shard_map/ppermute | solution.py:202
  79.9 0.1 pad_add_fusion.1.at_ref
  79.9 0.0 collective-permute-done.2.woth_ref
  79.9 0.0 collective-permute-done.oth0_ref
  79.9 1.8 %collective-permute-done.1.oth1_ref = bf16[4,2,256,128]{3,2,1,0:T(8,128)(2,1)} collective-permute-done((bf16[4,2,256,128]{3,2,1,0:T(8,128)(2,1)}, bf16[4,2,256,128]{3,2,1,0:T(8,128)(2,1)}, u32[]{:S(2)}, u32[]{:S(2)}) %collective-permute-start.1) | collective-permute-done | bytes 524320 | tf_op jit(solution)/shard_map/ppermute | solution.py:202
  81.7 1.9 %shard_map.65 = (bf16[256,768]{1,0:T(8,128)(2,1)S(1)}, bf16[1024,768]{1,0:T(8,128)(2,1)S(1)}, bf16[3,256,1024]{2,1,0:T(8,128)(2,1)S(1)}) custom-call(s32[2]{0:T(128)S(1)} %pad_add_fusion.1.at_ref, bf16[4,4,256,128]{3,2,1,0:T(8,128)(2,1)S(1)} %all-to-all-done.1.own_ref, bf16[4,2,256,128]{3,2,1,0:T(8,128)(2,1)S(1)} %collective-permute-done.oth0_ref, ...), custom_call_target="tpu_custom_call" | custom-call | flops 402653184 | bytes 6291456 | tf_op jit(solution)/shard_map/pallas_call | solution.py:31
  83.6 2.5 %collective-permute-start.3 = (bf16[256,768]{1,0:T(8,128)(2,1)S(1)}, bf16[256,768]{1,0:T(8,128)(2,1)S(1)}, u32[]{:S(2)}, u32[]{:S(2)}) collective-permute-start(bf16[256,768]{1,0:T(8,128)(2,1)S(1)} %get-tuple-element.38), channel_id=1, source_target_pairs={{0,16},{8,24},{16,0},{24,8},{1,17},{9,25},{17,1},{25,9},{2,18},{10... | collective-permute-start | bytes 1179656 | tf_op jit(solution)/shard_map/ppermute | solution.py:205
  86.1 1.4 %shard_map.66 = (bf16[256,768]{1,0:T(8,128)(2,1)S(1)}, bf16[256,768]{1,0:T(8,128)(2,1)S(1)}, f32[256,768]{1,0:T(8,128)S(1)}) custom-call(bf16[3,256,1024]{2,1,0:T(8,128)(2,1)S(1)} %get-tuple-element.33.x_ref, bf16[1024,768]{1,0:T(8,128)(2,1)S(1)} %get-tuple-element.34.w_ref), custom_call_target="tpu_custom_call" | custom-call | flops 1207959552 | bytes 4194304 | tf_op jit(solution)/shard_map/pallas_call | solution.py:31
  87.5 3.4 %collective-permute-start.4 = (bf16[256,768]{1,0:T(8,128)(2,1)S(1)}, bf16[256,768]{1,0:T(8,128)(2,1)S(1)}, u32[]{:S(2)}, u32[]{:S(2)}) collective-permute-start(bf16[256,768]{1,0:T(8,128)(2,1)S(1)} %get-tuple-element.39), channel_id=1, source_target_pairs={{0,8},{8,16},{16,24},{24,0},{1,9},{9,17},{17,25},{25,1},{2,10},{10... | collective-permute-start | bytes 1179656 | tf_op jit(solution)/shard_map/ppermute | solution.py:205
  90.9 3.7 %collective-permute-start.5 = (bf16[256,768]{1,0:T(8,128)(2,1)S(1)}, bf16[256,768]{1,0:T(8,128)(2,1)S(1)}, u32[]{:S(2)}, u32[]{:S(2)}) collective-permute-start(bf16[256,768]{1,0:T(8,128)(2,1)S(1)} %get-tuple-element.40), channel_id=1, source_target_pairs={{0,24},{8,0},{16,8},{24,16},{1,25},{9,1},{17,9},{25,17},{2,26},{10... | collective-permute-start | bytes 1179656 | tf_op jit(solution)/shard_map/ppermute | solution.py:205
  95.2 1.9 %collective-permute-start.6 = (f32[256]{0:T(256)S(1)}, f32[256]{0:T(256)S(1)}, u32[]{:S(2)}, u32[]{:S(2)}) collective-permute-start(f32[256]{0:T(256)S(1)} %multiply_reduce_fusion), channel_id=1, source_target_pairs={{0,1},{1,0},{2,3},{3,2},{4,5},{5,4},{6,7},{7,6},{8,9},{9,8},{10,11... | collective-permute-start | bytes 3080 | tf_op jit(solution)/shard_map/ppermute | solution.py:226
  97.1 1.9 %collective-permute-done.3 = bf16[256,768]{1,0:T(8,128)(2,1)S(1)} collective-permute-done((bf16[256,768]{1,0:T(8,128)(2,1)S(1)}, bf16[256,768]{1,0:T(8,128)(2,1)S(1)}, u32[]{:S(2)}, u32[]{:S(2)}) %collective-permute-start.3) | collective-permute-done | bytes 393248 | tf_op jit(solution)/shard_map/ppermute | solution.py:205
  99.0 0.1 convert_add_fusion.p0_ref
  99.0 0.0 collective-permute-done.6
  99.1 7.8 %collective-permute-done.4.p1_ref = bf16[256,768]{1,0:T(8,128)(2,1)S(1)} collective-permute-done((bf16[256,768]{1,0:T(8,128)(2,1)S(1)}, bf16[256,768]{1,0:T(8,128)(2,1)S(1)}, u32[]{:S(2)}, u32[]{:S(2)}) %collective-permute-start.4) | collective-permute-done | bytes 393248 | tf_op jit(solution)/shard_map/ppermute | solution.py:205
  106.8 0.0 collective-permute-done.5.p2_ref
  106.8 1.9 %shard_map.67.own_ref = bf16[272,512]{1,0:T(8,128)(2,1)S(1)} custom-call(s32[4]{0:T(128)S(1)} %bitcast.14, s32[1]{0:T(128)S(6)} %copy.11.moved_ref, f32[256,768]{1,0:T(8,128)S(1)} %convert_add_fusion.p0_ref, bf16[256,768]{1,0:T(8,128)(2,1)S(1)} %collective-permute-done.4.p1_ref, bf16[256,768]{1,0:T(8,128)(2,1)S(1)} %collective-permute-done.5.p2_ref, ...), custom_call_target="tpu_custom_call" | custom-call | flops 134217728 | bytes 3145728 | tf_op jit(solution)/shard_map/pallas_call | solution.py:31
  108.7 2.5 %collective-permute-start.7 = (bf16[272,512]{1,0:T(8,128)(2,1)S(1)}, bf16[272,512]{1,0:T(8,128)(2,1)S(1)}, u32[]{:S(2)}, u32[]{:S(2)}) collective-permute-start(bf16[272,512]{1,0:T(8,128)(2,1)S(1)} %shard_map.67.own_ref), channel_id=1, source_target_pairs={{0,8},{8,16},{16,24},{24,32},{32,40},{40,48},{48,56},{56,64},{64,7... | collective-permute-start | bytes 835592 | tf_op jit(solution)/shard_map/ppermute | solution.py:235
  111.2 10.1 %collective-permute-done.7.prev_ref = bf16[272,512]{1,0:T(8,128)(2,1)S(1)} collective-permute-done((bf16[272,512]{1,0:T(8,128)(2,1)S(1)}, bf16[272,512]{1,0:T(8,128)(2,1)S(1)}, u32[]{:S(2)}, u32[]{:S(2)}) %collective-permute-start.7) | collective-permute-done | bytes 278560 | tf_op jit(solution)/shard_map/ppermute | solution.py:235
  121.3 1.8 %shard_map.68 = bf16[512,512]{1,0:T(8,128)(2,1)} custom-call(s32[4]{0:T(128)S(1)} %bitcast.15, s32[1]{0:T(128)S(6)} %copy.11.moved_ref, bf16[272,512]{1,0:T(8,128)(2,1)S(1)} %collective-permute-done.7.prev_ref, bf16[272,512]{1,0:T(8,128)(2,1)S(1)} %shard_map.67.own_ref), custom_call_target="tpu_custom_call" | custom-call | flops 268435456 | bytes 1048576 | tf_op jit(solution)/shard_map/pallas_call | solution.py:31
  (2 shorter events, 0.0 us)
Async XLA Ops:
  3.7 7.4 %copy-start.3 = (bf16[32,768]{1,0:T(8,128)(2,1)S(1)}, bf16[32,768]{1,0:T(8,128)(2,1)}, u32[]{:S(2)}) copy-start(bf16[32,768]{1,0:T(8,128)(2,1)} %get-tuple-element.26) | copy-start | bytes 147460
  3.7 54.3 %all-to-all-start = ((bf16[4,4,256,128]{3,2,1,0:T(8,128)(2,1)}), bf16[4,4,256,128]{3,2,1,0:T(8,128)(2,1)S(1)}, u32[]{:S(2)}, u32[]{:S(2)}) async-start(bf16[4,4,256,128]{3,2,1,0:T(8,128)(2,1)} %get-tuple-element.25), calls=%async_computation | async-start | bytes 2097152 | tf_op jit(solution)/shard_map/all_to_all | solution.py:180
  58.0 1.3 %copy-start.1 = (bf16[4,4,256,128]{3,2,1,0:T(8,128)(2,1)}, bf16[4,4,256,128]{3,2,1,0:T(8,128)(2,1)S(1)}, u32[]{:S(2)}) copy-start(bf16[4,4,256,128]{3,2,1,0:T(8,128)(2,1)S(1)} %all-to-all-done) | copy-start | bytes 3145732
  59.1 4.4 %copy-start = (s32[1,4]{1,0:T(1,128)S(1)}, s32[1,4]{1,0:T(1,128)}, u32[]{:S(2)}) copy-start(s32[1,4]{1,0:T(1,128)} %param.7) | copy-start | bytes 52
  59.1 5.1 %copy-start.4 = (bf16[768]{0:T(1024)(128)(2,1)S(1)}, bf16[768]{0:T(1024)(128)(2,1)}, u32[]{:S(2)}) copy-start(bf16[768]{0:T(1024)(128)(2,1)} %param.11) | copy-start | bytes 4612
  59.3 15.2 %all-to-all-start.1 = ((bf16[4,4,256,128]{3,2,1,0:T(8,128)(2,1)}), bf16[4,4,256,128]{3,2,1,0:T(8,128)(2,1)S(1)}, u32[]{:S(2)}, u32[]{:S(2)}) async-start(bf16[4,4,256,128]{3,2,1,0:T(8,128)(2,1)} %bitcast.11), calls=%async_computation.1 | async-start | bytes 2097152 | tf_op jit(solution)/shard_map/all_to_all | solution.py:185
  63.6 6.5 %copy-start.2 = (bf16[4,4,256,128]{3,2,1,0:T(8,128)(2,1)S(1)}, bf16[4,4,256,128]{3,2,1,0:T(8,128)(2,1)}, u32[]{:S(2)}) copy-start(bf16[4,4,256,128]{3,2,1,0:T(8,128)(2,1)} %copy-done.1) | copy-start | bytes 3145732
  64.2 15.7 %collective-permute-start.2 = (bf16[512,768]{1,0:T(8,128)(2,1)S(1)}, bf16[512,768]{1,0:T(8,128)(2,1)S(1)}, u32[]{:S(2)}, u32[]{:S(2)}) collective-permute-start(bf16[512,768]{1,0:T(8,128)(2,1)S(1)} %all_gather.3.wown_ref), channel_id=1, source_target_pairs={{0,32},{32,0},{1,33},{33,1},{2,34},{34,2},{3,35},{35,3},{4,36},{36... | collective-permute-start | bytes 2359304 | tf_op jit(solution)/shard_map/ppermute | solution.py:184
  75.5 4.4 %collective-permute-start = (bf16[4,2,256,128]{3,2,1,0:T(8,128)(2,1)}, bf16[4,2,256,128]{3,2,1,0:T(8,128)(2,1)S(1)}, u32[]{:S(2)}, u32[]{:S(2)}) collective-permute-start(bf16[4,2,256,128]{3,2,1,0:T(8,128)(2,1)} %get-tuple-element.46), channel_id=1, source_target_pairs={{0,1},{1,0},{2,3},{3,2},{4,5},{5,4},{6,7},{7,6},{8,9},{9,8},{10,11... | collective-permute-start | bytes 1572872 | tf_op jit(solution)/shard_map/ppermute | solution.py:202
  77.4 4.3 %collective-permute-start.1 = (bf16[4,2,256,128]{3,2,1,0:T(8,128)(2,1)}, bf16[4,2,256,128]{3,2,1,0:T(8,128)(2,1)}, u32[]{:S(2)}, u32[]{:S(2)}) collective-permute-start(bf16[4,2,256,128]{3,2,1,0:T(8,128)(2,1)} %get-tuple-element.45), channel_id=1, source_target_pairs={{0,1},{1,0},{2,3},{3,2},{4,5},{5,4},{6,7},{7,6},{8,9},{9,8},{10,11... | collective-permute-start | bytes 1572872 | tf_op jit(solution)/shard_map/ppermute | solution.py:202
  83.6 15.4 %collective-permute-start.3 = (bf16[256,768]{1,0:T(8,128)(2,1)S(1)}, bf16[256,768]{1,0:T(8,128)(2,1)S(1)}, u32[]{:S(2)}, u32[]{:S(2)}) collective-permute-start(bf16[256,768]{1,0:T(8,128)(2,1)S(1)} %get-tuple-element.38), channel_id=1, source_target_pairs={{0,16},{8,24},{16,0},{24,8},{1,17},{9,25},{17,1},{25,9},{2,18},{10... | collective-permute-start | bytes 1179656 | tf_op jit(solution)/shard_map/ppermute | solution.py:205
  87.5 19.3 %collective-permute-start.4 = (bf16[256,768]{1,0:T(8,128)(2,1)S(1)}, bf16[256,768]{1,0:T(8,128)(2,1)S(1)}, u32[]{:S(2)}, u32[]{:S(2)}) collective-permute-start(bf16[256,768]{1,0:T(8,128)(2,1)S(1)} %get-tuple-element.39), channel_id=1, source_target_pairs={{0,8},{8,16},{16,24},{24,0},{1,9},{9,17},{17,25},{25,1},{2,10},{10... | collective-permute-start | bytes 1179656 | tf_op jit(solution)/shard_map/ppermute | solution.py:205
  90.9 16.0 %collective-permute-start.5 = (bf16[256,768]{1,0:T(8,128)(2,1)S(1)}, bf16[256,768]{1,0:T(8,128)(2,1)S(1)}, u32[]{:S(2)}, u32[]{:S(2)}) collective-permute-start(bf16[256,768]{1,0:T(8,128)(2,1)S(1)} %get-tuple-element.40), channel_id=1, source_target_pairs={{0,24},{8,0},{16,8},{24,16},{1,25},{9,1},{17,9},{25,17},{2,26},{10... | collective-permute-start | bytes 1179656 | tf_op jit(solution)/shard_map/ppermute | solution.py:205
  95.2 3.9 %collective-permute-start.6 = (f32[256]{0:T(256)S(1)}, f32[256]{0:T(256)S(1)}, u32[]{:S(2)}, u32[]{:S(2)}) collective-permute-start(f32[256]{0:T(256)S(1)} %multiply_reduce_fusion), channel_id=1, source_target_pairs={{0,1},{1,0},{2,3},{3,2},{4,5},{5,4},{6,7},{7,6},{8,9},{9,8},{10,11... | collective-permute-start | bytes 3080 | tf_op jit(solution)/shard_map/ppermute | solution.py:226
  108.7 12.6 %collective-permute-start.7 = (bf16[272,512]{1,0:T(8,128)(2,1)S(1)}, bf16[272,512]{1,0:T(8,128)(2,1)S(1)}, u32[]{:S(2)}, u32[]{:S(2)}) collective-permute-start(bf16[272,512]{1,0:T(8,128)(2,1)S(1)} %shard_map.67.own_ref), channel_id=1, source_target_pairs={{0,8},{8,16},{16,24},{24,32},{32,40},{40,48},{48,56},{56,64},{64,7... | collective-permute-start | bytes 835592 | tf_op jit(solution)/shard_map/ppermute | solution.py:235

commit v5 on v4

v5 whole, which is shorter than its diff:
```python
import jax
import jax.numpy as jnp
from jax import lax
from jax.experimental import pallas as pl
from jax.experimental.pallas import tpu as pltpu
from jax.sharding import Mesh
from jax.sharding import PartitionSpec as P

HEADS = 32
KV = 8
HEAD = 128
PER = HEADS // KV
EPSILON = 1e-06
ROPE_BASE = 1000000.0

NZH, NQ, NX, NYH, NC = 8, 4, 4, 4, 2
Q = ("zl", "yl")
DP = ("zh",) + Q + ("x",)
TP = ("yh", "c")
NDP = NZH * NQ * NX
WROWS = 32
ROWS = 256
SAMPLES = 4
EXTRA = 16
FULL = ROWS + EXTRA
NEAR = (1, 2, 0)
VMEM = 16 << 20


def call(kernel, out_shape, args, scalars=0, hbm=0, flops=0, nbytes=0, scratch=(), vmem_bytes=VMEM):
    smem = pl.BlockSpec(memory_space=pltpu.SMEM)
    vmem = pl.BlockSpec(memory_space=pltpu.VMEM)
    far = pl.BlockSpec(memory_space=pltpu.HBM)
    return pl.pallas_call(
        kernel,
        out_shape=out_shape,
        in_specs=[smem] * scalars + [far] * hbm + [vmem] * (len(args) - scalars - hbm),
        out_specs=[far] * len(out_shape) if isinstance(out_shape, list) else jax.tree.map(lambda _: vmem, out_shape),
        scratch_shapes=list(scratch),
        compiler_params=pltpu.CompilerParams(vmem_limit_bytes=vmem_bytes),
        cost_estimate=pl.CostEstimate(flops=flops, bytes_accessed=nbytes, transcendentals=0),
    )(*args)


def prepare_kernel(dp_ref, s_hbm, w_hbm, gain_ref, o_hbm, ow_hbm, w_ref, sems):
    copies = []
    for q in range(NQ):
        copy = pltpu.make_async_copy(s_hbm.at[:, q * 128 : (q + 1) * 128], o_hbm.at[q], sems.at[2 + q])
        copy.start()
        copies.append(copy)
    load = pltpu.make_async_copy(w_hbm, w_ref, sems.at[0])
    load.start()
    dp = dp_ref[0]
    line = lax.broadcasted_iota(jnp.int32, (gain_ref.shape[0], 128), 0)
    gain = jnp.where(line == lax.shift_right_logical(dp, 2), gain_ref[...].astype(jnp.float32), 0.0)
    gain = jnp.sum(gain, axis=0, keepdims=True)
    row = lax.broadcasted_iota(jnp.int32, (WROWS, 128), 0)
    lane = lax.broadcasted_iota(jnp.int32, (WROWS, 128), 1)
    gain = jnp.sum(jnp.where(lane == (dp & 3) * WROWS + row, gain, 0.0), axis=1, keepdims=True)
    load.wait()
    w_ref[...] = (w_ref[...].astype(jnp.float32) * gain).astype(jnp.bfloat16)
    store = pltpu.make_async_copy(w_ref, ow_hbm, sems.at[1])
    store.start()
    copies.append(store)
    for copy in copies:
        copy.wait()


def product(x, w_ref, o_ref):
    o_ref[:ROWS] = jnp.dot(x, w_ref[...], preferred_element_type=jnp.float32).astype(o_ref.dtype)
    square = jnp.square(x.astype(jnp.float32))
    high = square.astype(jnp.bfloat16)
    low = (square - high.astype(jnp.float32)).astype(jnp.bfloat16)
    ones = jnp.ones((EXTRA, x.shape[1]), jnp.bfloat16)
    lanes = (((1,), (1,)), ((), ()))
    total = lax.dot_general(ones, high, lanes, preferred_element_type=jnp.float32)
    total = total + lax.dot_general(ones, low, lanes, preferred_element_type=jnp.float32)
    rounded = total.astype(jnp.bfloat16).astype(jnp.float32)
    row = lax.broadcasted_iota(jnp.int32, total.shape, 0)
    o_ref[ROWS:, :ROWS] = jnp.where(row < EXTRA // 2, rounded, total - rounded).astype(o_ref.dtype)
    o_ref[ROWS:, ROWS:] = jnp.zeros((EXTRA, o_ref.shape[1] - ROWS), o_ref.dtype)


def first_kernel(q_ref, x_at_ref, c_ref, own_ref, *refs):
    others, weights, (o_ref, w_ref, x_ref) = refs[:NYH], refs[NYH : NYH + NX], refs[NYH + NX :]
    q, c = q_ref[0], c_ref[0]
    for step, ref in enumerate(weights):
        source = (x_at_ref[0] + (NX - step)) & 3
        for rel in range(NC):
            for yh in range(NYH):
                row = pl.multiple_of((yh * NC + (c ^ rel)) * WROWS, WROWS)
                at = pl.multiple_of((rel * NYH + yh) * 128 + source * WROWS, WROWS)
                w_ref[pl.ds(at, WROWS)] = ref[pl.ds(row, WROWS)]

    def states(r):
        rows = pl.ds(pl.multiple_of((q ^ r) * ROWS, ROWS), ROWS)
        return jnp.concatenate([own_ref[yh, rows] for yh in range(NYH)] + [ref[rows] for ref in others], axis=1)

    product(states(3), w_ref, o_ref)
    for n, r in enumerate(NEAR):
        x_ref[n] = states(r)


def second_kernel(x_ref, w_ref, o1_ref, o2_ref, own_ref):
    for n, ref in enumerate((o1_ref, o2_ref, own_ref)):
        product(x_ref[n], w_ref, ref)


def tail_of(lens, moved):
    return sum(jnp.where(n >= SAMPLES - moved, lens[n], 0) for n in range(SAMPLES))


def attend_kernel(len_ref, moved_ref, p0_ref, p1_ref, p2_ref, bias_ref, cos_ref, sin_ref, o_ref):
    s1 = len_ref[0]
    s2 = s1 + len_ref[1]
    s3 = s2 + len_ref[2]
    i = lax.broadcasted_iota(jnp.int32, (ROWS, ROWS), 0)
    j = lax.broadcasted_iota(jnp.int32, (ROWS, ROWS), 1)
    start = jnp.where(i >= s3, s3, jnp.where(i >= s2, s2, jnp.where(i >= s1, s1, 0)))
    allowed = (j >= start) & (j <= i)
    squares = jnp.zeros((1, ROWS), jnp.float32)
    for ref in (p0_ref, p1_ref, p2_ref):
        for row in (0, EXTRA // 2):
            part = ref[ROWS:, :ROWS].astype(jnp.float32)
            squares = squares + part[row : row + 1]
    r = lax.rsqrt(squares * (1.0 / (NDP * WROWS)) + EPSILON)
    r = jnp.sum(jnp.where(i == j, r, 0.0), axis=1, keepdims=True)
    cos, sin = cos_ref[...], sin_ref[...]

    def head(n):
        at = n * HEAD
        total = p0_ref[:ROWS, at : at + HEAD]
        for ref in (p1_ref, p2_ref):
            total = total + ref[:ROWS, at : at + HEAD].astype(jnp.float32)
        return total * r + bias_ref[:, n * HEAD : (n + 1) * HEAD]

    def rotate(v):
        return (v * cos + pltpu.roll(v, HEAD // 2, 1) * sin).astype(jnp.bfloat16)

    key = rotate(head(PER))
    value = head(PER + 1).astype(jnp.bfloat16)
    for h in range(PER):
        query = rotate(head(h))
        scores = lax.dot_general(query, key, (((1,), (1,)), ((), ())), preferred_element_type=jnp.float32)
        scores = jnp.where(allowed, scores * HEAD ** (-0.5), -1e30)
        e = jnp.exp(scores - jnp.max(scores, axis=1, keepdims=True))
        weights = (e / jnp.sum(e, axis=1, keepdims=True)).astype(jnp.bfloat16)
        o_ref[:ROWS, h * HEAD : (h + 1) * HEAD] = jnp.dot(
            weights, value, preferred_element_type=jnp.float32
        ).astype(jnp.bfloat16)
    tail = tail_of(len_ref, moved_ref[0]).astype(jnp.float32)
    o_ref[ROWS:] = jnp.full((EXTRA, PER * HEAD), tail, jnp.float32).astype(jnp.bfloat16)


def pack_kernel(len_ref, moved_ref, prev_ref, own_ref, o_ref):
    tail = tail_of(len_ref, moved_ref[0])
    incoming = prev_ref[ROWS:, :HEAD].astype(jnp.float32)[:1, :1].astype(jnp.int32)
    slot = lax.broadcasted_iota(jnp.int32, (2 * ROWS, ROWS), 0)
    row = lax.broadcasted_iota(jnp.int32, (2 * ROWS, ROWS), 1)
    first = ((slot < incoming) & (row == slot + (ROWS - incoming))).astype(jnp.bfloat16)
    second = ((row == slot - incoming) & (row < ROWS - tail)).astype(jnp.bfloat16)
    picked = jnp.dot(first, prev_ref[:ROWS], preferred_element_type=jnp.float32)
    picked = picked + jnp.dot(second, own_ref[:ROWS], preferred_element_type=jnp.float32)
    o_ref[...] = picked.astype(jnp.bfloat16)


def local(states, lengths, moved, norm_gain, qkv_weight, qkv_bias):
    scalar = lambda v: v.astype(jnp.int32).reshape(1)
    at = {name: scalar(lax.axis_index(name)) for name in ("x", "c")}
    at["q"], at["dp"] = scalar(lax.axis_index(Q)), scalar(lax.axis_index(DP))
    bf = lambda *shape: jax.ShapeDtypeStruct(shape, jnp.bfloat16)
    columns = qkv_weight.shape[1]

    sent, scaled = call(
        prepare_kernel,
        [bf(NQ, ROWS, 128), bf(WROWS, columns)],
        (at["dp"], states, qkv_weight, norm_gain.reshape(-1, 128)),
        1,
        2,
        nbytes=1 << 20,
        scratch=[pltpu.VMEM((WROWS, columns), jnp.bfloat16), pltpu.SemaphoreType.DMA((2 + NQ,))],
        vmem_bytes=60 << 20,
    )
    mine = lax.all_to_all(sent, Q, 0, 0, tiled=True).reshape(1, NQ * ROWS, 128)
    mine, scaled = lax.optimization_barrier((mine, scaled))
    spread = lax.all_to_all(jnp.broadcast_to(mine, (NYH, NQ * ROWS, 128)), "yh", 0, 0, tiled=True)
    held = lax.all_gather(scaled, "zh", axis=0, tiled=True)
    held, lengths_late, qkv_bias = lax.optimization_barrier((held, lengths, qkv_bias))

    send = lambda v, axis, count, to: lax.ppermute(v, axis, [(i, to(i)) for i in range(count)])
    weights = {0: held}
    for step in (2, 1, 3):
        weights[step] = send(held, "x", NX, lambda i: (i + step) % NX)

    lens = lengths_late[0]
    ids = jnp.arange(ROWS, dtype=jnp.int32)
    starts = [jnp.sum(lens[:n]) for n in range(SAMPLES)]
    begin = jnp.zeros_like(ids)
    for n in range(1, SAMPLES):
        begin = jnp.where(ids >= starts[n], starts[n], begin)
    positions = (ids - begin).astype(jnp.float32)
    inv_freq = ROPE_BASE ** (-(2.0 * jnp.arange(HEAD // 2, dtype=jnp.float32)) / HEAD)
    angles = positions[:, None] * inv_freq[None, :]
    cos, sin = jnp.cos(angles), jnp.sin(angles)
    cos = jnp.concatenate([cos, cos], axis=1)
    sin = jnp.concatenate([-sin, sin], axis=1)
    bias = qkv_bias.astype(jnp.float32)[None, :]

    spread, bias, cos, sin = lax.optimization_barrier((spread, bias, cos, sin))
    others = [send(spread[n], "c", NC, lambda i: 1 - i) for n in range(NYH)]

    flops = 2 * ROWS * 1024 * columns
    far, packed, near = call(
        first_kernel,
        (bf(FULL, columns), bf(1024, columns), bf(3, ROWS, 1024)),
        (at["q"], at["x"], at["c"], spread, *others, *[weights[step] for step in range(NX)]),
        3,
        flops=flops,
        nbytes=6 << 20,
    )
    far = send(far, Q, NQ, lambda i: i ^ 3)
    one, two, own = call(
        second_kernel,
        (bf(FULL, columns), bf(FULL, columns), jax.ShapeDtypeStruct((FULL, columns), jnp.float32)),
        (near, packed),
        flops=3 * flops,
        nbytes=4 << 20,
    )
    one, two = send(one, Q, NQ, lambda i: i ^ 1), send(two, Q, NQ, lambda i: i ^ 2)
    own = own + far.astype(jnp.float32)
    context = call(
        attend_kernel,
        bf(FULL, PER * HEAD),
        (lens, moved, own, one, two, bias, cos, sin),
        2,
        flops=4 * 4 * ROWS * ROWS * HEAD,
        nbytes=3 << 20,
    )
    previous = lax.ppermute(context, DP, [(i, i + 1) for i in range(NDP - 1)])
    return call(
        pack_kernel,
        bf(2 * ROWS, PER * HEAD),
        (lens, moved, previous, context),
        2,
        flops=4 * 512 * 256 * 512,
        nbytes=1 << 20,
    )


def solution(mesh):
    fine = Mesh(mesh.devices.reshape(NZH, 2, 2, NX, NYH, NC), DP + TP)
    return jax.shard_map(
        local,
        mesh=fine,
        in_specs=(P(DP, TP), P(DP, None), P(DP), P(), P(DP, TP), P(TP)),
        out_specs=P(DP, TP),
        check_vma=False,
    )
```

time: 124 us -> 139 us (1.12)
  starting transfers between devices: 33.1 us -> 47.7 us
  Pallas kernels: 9.92 us -> 17.8 us
  blocking collectives: 46.9 us -> 43.1 us
  waiting for transfers between devices: 25.6 us -> 23 us
    all_gather x1, blocking collectives: 46.9 us -> 33.2 us  [local(): held = lax.all_gather(scaled, 'zh', axis=0, tiled=True)]
    ppermute x8 -> x11, starting transfers between devices: 21.5 us -> 31.9 us  [the longest x10 29.4 us: local(): lax.ppermute(v, axis, [(i, to(i)) for i in range(count)])]
    all_to_all x0 -> x1, blocking collectives: none -> 9.91 us  [local(): mine = lax.all_to_all(sent, Q, 0, 0, tiled=True).reshape(1, NQ * ROWS, 128)]
    pallas_call x5, Pallas kernels: 9.92 us -> 17.8 us  [call(): pl.pallas_call(kernel, out_shape=out_shape, in_specs=[smem] * scalars + [...]
    all_to_all x2 -> x1, starting transfers between devices: 11.6 us -> 15.8 us  [local(): lax.all_to_all(jnp.broadcast_to(mine, (NYH, NQ * ROWS, 128)), 'yh', 0, 0,...]
    all_to_all x2 -> x1, waiting for transfers between devices: 4.06 us -> 0.01 us  [local(): lax.all_to_all(jnp.broadcast_to(mine, (NYH, NQ * ROWS, 128)), 'yh', 0, 0,...]
    ppermute x8 -> x11, waiting for transfers between devices: 21.5 us -> 23 us  [the longest x10 12.9 us: local(): lax.ppermute(v, axis, [(i, to(i)) for i in range(count)])]
  transfers between devices with their start and end apart: 10 -> 12, of which waited for: 5 -> 4; matrix products, arithmetic and copies ran while one was open for 4% -> 3% of each run, Pallas kernels for 1% -> 2%
where the time goes in v5:
time: 139 us; the launch traced here: 138 us
  starting transfers between devices  47.7 us (34%)
  blocking collectives  43.1 us (31%)
  waiting for transfers between devices  23 us (17%)
  Pallas kernels  17.8 us (13%)
  other arithmetic  3.36 us (2%)
  local copies, waits for them, and re-layouts  2.13 us (2%)
    all_gather x1, blocking collectives, local(): held = lax.all_gather(scaled, 'zh', axis=0, tiled=True)  33.2 us
    ppermute x10, starting transfers between devices, local(): lax.ppermute(v, axis, [(i, to(i)) for i in range(count)])  29.4 us
    pallas_call x5, Pallas kernels, call(): pl.pallas_call(kernel, out_shape=out_shape, in_specs=[smem] * scalars + [...  17.8 us
    all_to_all x1, starting transfers between devices, local(): lax.all_to_all(jnp.broadcast_to(mine, (NYH, NQ * ROWS, 128)), 'yh', 0, 0,...  15.8 us
    ppermute x10, waiting for transfers between devices, local(): lax.ppermute(v, axis, [(i, to(i)) for i in range(count)])  12.9 us
    ppermute x1, waiting for transfers between devices, local(): previous = lax.ppermute(context, DP, [(i, i + 1) for i in range(NDP - 1)])  10.1 us
    all_to_all x1, blocking collectives, local(): mine = lax.all_to_all(sent, Q, 0, 0, tiled=True).reshape(1, NQ * ROWS, 128)  9.91 us
  transfers between devices with their start and end apart: 12, of which 4 were waited for; matrix products, arithmetic and copies ran while one was open for 3% of the time, Pallas kernels for 2%

profile of v5, /device:TPU:40, one launch (start us, length us, event | category | flops | bytes accessed | tf_op | source)
XLA Modules:
  0.0 137.9 jit_solution(17442146373251519053)
XLA Ops:
  0.0 9.8 %shard_map.64 = (bf16[4,256,128]{2,1,0:T(8,128)(2,1)}, bf16[32,768]{1,0:T(8,128)(2,1)}) custom-call(s32[1]{0:T(128)} %bitcast.dp_ref, bf16[256,512]{1,0:T(8,128)(2,1)} %s_hbm.1, bf16[32,768]{1,0:T(8,128)(2,1)} %w_hbm.1, bf16[32,128]{1,0:T(8,128)(2,1)} %bitcast.22), custom_call_target="tpu_custom_call" | custom-call | bytes 1048576 | tf_op jit(solution)/shard_map/pallas_call | solution.py:34
  9.8 9.9 %all_to_all.10 = bf16[4,256,128]{2,1,0:T(8,128)(2,1)S(1)} all-to-all(bf16[4,256,128]{2,1,0:T(8,128)(2,1)} %get-tuple-element.22), channel_id=1, replica_groups=mesh['zh'=8,'zl'=2,'yl'=2,'x'=4,'yh'=4,'c'=2] {'zl','yl'}, dimensions={0} | all-to-all | bytes 524288 | tf_op jit(solution)/shard_map/all_to_all | solution.py:184
  19.7 0.0 copy-start.1
  19.7 1.1 broadcast_in_dim.23
  20.8 0.0 copy-start
  20.8 0.0 copy-start.2
  20.8 15.8 %all-to-all-start.1 = ((bf16[4,1024,128]{2,1,0:T(8,128)(2,1)}), bf16[4,1024,128]{2,1,0:T(8,128)(2,1)S(1)}, u32[]{:S(2)}, u32[]{:S(2)}) async-start(bf16[4,1024,128]{2,1,0:T(8,128)(2,1)} %broadcast_in_dim.23), calls=%async_computation.1 | async-start | bytes 2097152 | tf_op jit(solution)/shard_map/all_to_all | solution.py:186
  36.7 0.0 copy-done.1
  36.7 33.2 %all_gather.3.refs_4_ = bf16[256,768]{1,0:T(8,128)(2,1)S(1)} all-gather(bf16[32,768]{1,0:T(8,128)(2,1)S(1)} %copy-done.1), channel_id=1, replica_groups=mesh['zh'=8,'zl'=2,'yl'=2,'x'=4,'yh'=4,'c'=2] {'zh'}, dimensions={0}, use_global_device_ids=true | all-gather | bytes 442368 | tf_op jit(solution)/shard_map/all_gather | solution.py:187
  69.9 3.5 %collective-permute-start.4 = (bf16[256,768]{1,0:T(8,128)(2,1)S(1)}, bf16[256,768]{1,0:T(8,128)(2,1)S(1)}, u32[]{:S(2)}, u32[]{:S(2)}) collective-permute-start(bf16[256,768]{1,0:T(8,128)(2,1)S(1)} %all_gather.3.refs_4_), channel_id=1, source_target_pairs={{0,8},{8,16},{16,24},{24,0},{1,9},{9,17},{17,25},{25,1},{2,10},{10... | collective-permute-start | bytes 1179656 | tf_op jit(solution)/shard_map/ppermute | solution.py:190
  73.4 4.6 %collective-permute-start.5 = (bf16[256,768]{1,0:T(8,128)(2,1)S(1)}, bf16[256,768]{1,0:T(8,128)(2,1)S(1)}, u32[]{:S(2)}, u32[]{:S(2)}) collective-permute-start(bf16[256,768]{1,0:T(8,128)(2,1)S(1)} %all_gather.3.refs_4_), channel_id=1, source_target_pairs={{0,16},{8,24},{16,0},{24,8},{1,17},{9,25},{17,1},{25,9},{2,18},{10... | collective-permute-start | bytes 1179656 | tf_op jit(solution)/shard_map/ppermute | solution.py:190
  78.0 3.3 %collective-permute-start.6 = (bf16[256,768]{1,0:T(8,128)(2,1)S(1)}, bf16[256,768]{1,0:T(8,128)(2,1)S(1)}, u32[]{:S(2)}, u32[]{:S(2)}) collective-permute-start(bf16[256,768]{1,0:T(8,128)(2,1)S(1)} %all_gather.3.refs_4_), channel_id=1, source_target_pairs={{0,24},{8,0},{16,8},{24,16},{1,25},{9,1},{17,9},{25,17},{2,26},{10... | collective-permute-start | bytes 1179656 | tf_op jit(solution)/shard_map/ppermute | solution.py:190
  81.4 0.0 copy-done
  81.4 0.6 slice_reduce_fusion
  82.0 0.6 slice_reduce_fusion.1
  82.7 1.3 fusion.2
  84.0 0.5 fusion
  84.5 0.0 copy-done.2
  84.6 0.1 pad_maximum_fusion
  84.7 0.0 all-to-all-done.1.own_ref
  84.7 1.0 slice_bitcast_fusion
  85.7 1.9 %collective-permute-start = (bf16[1024,128]{1,0:T(8,128)(2,1)}, bf16[1024,128]{1,0:T(8,128)(2,1)S(1)}, u32[]{:S(2)}, u32[]{:S(2)}) collective-permute-start(bf16[1024,128]{1,0:T(8,128)(2,1)} %get-tuple-element.42), channel_id=1, source_target_pairs={{0,1},{1,0},{2,3},{3,2},{4,5},{5,4},{6,7},{7,6},{8,9},{9,8},{10,11... | collective-permute-start | bytes 786440 | tf_op jit(solution)/shard_map/ppermute | solution.py:190
  87.6 2.4 %collective-permute-start.1 = (bf16[1024,128]{1,0:T(8,128)(2,1)}, bf16[1024,128]{1,0:T(8,128)(2,1)S(1)}, u32[]{:S(2)}, u32[]{:S(2)}) collective-permute-start(bf16[1024,128]{1,0:T(8,128)(2,1)} %get-tuple-element.41), channel_id=1, source_target_pairs={{0,1},{1,0},{2,3},{3,2},{4,5},{5,4},{6,7},{7,6},{8,9},{9,8},{10,11... | collective-permute-start | bytes 786440 | tf_op jit(solution)/shard_map/ppermute | solution.py:190
  90.0 0.0 collective-permute-done.4.refs_5_
  90.1 1.9 %collective-permute-start.2 = (bf16[1024,128]{1,0:T(8,128)(2,1)}, bf16[1024,128]{1,0:T(8,128)(2,1)}, u32[]{:S(2)}, u32[]{:S(2)}) collective-permute-start(bf16[1024,128]{1,0:T(8,128)(2,1)} %get-tuple-element.40), channel_id=1, source_target_pairs={{0,1},{1,0},{2,3},{3,2},{4,5},{5,4},{6,7},{7,6},{8,9},{9,8},{10,11... | collective-permute-start | bytes 786440 | tf_op jit(solution)/shard_map/ppermute | solution.py:190
  92.0 0.0 collective-permute-done.5.refs_6_
  92.0 2.4 %collective-permute-start.3 = (bf16[1024,128]{1,0:T(8,128)(2,1)}, bf16[1024,128]{1,0:T(8,128)(2,1)}, u32[]{:S(2)}, u32[]{:S(2)}) collective-permute-start(bf16[1024,128]{1,0:T(8,128)(2,1)} %get-tuple-element.39), channel_id=1, source_target_pairs={{0,1},{1,0},{2,3},{3,2},{4,5},{5,4},{6,7},{7,6},{8,9},{9,8},{10,11... | collective-permute-start | bytes 786440 | tf_op jit(solution)/shard_map/ppermute | solution.py:190
  94.4 0.0 collective-permute-done.6.refs_7_
  94.4 0.0 collective-permute-done.refs_0_
  94.4 0.0 collective-permute-done.1.refs_1_
  94.5 0.0 collective-permute-done.2.refs_2_
  94.5 1.4 %collective-permute-done.3.refs_3_ = bf16[1024,128]{1,0:T(8,128)(2,1)} collective-permute-done((bf16[1024,128]{1,0:T(8,128)(2,1)}, bf16[1024,128]{1,0:T(8,128)(2,1)}, u32[]{:S(2)}, u32[]{:S(2)}) %collective-permute-start.3) | collective-permute-done | bytes 262176 | tf_op jit(solution)/shard_map/ppermute | solution.py:190
  95.9 2.1 %shard_map.65 = (bf16[272,768]{1,0:T(8,128)(2,1)S(1)}, bf16[1024,768]{1,0:T(8,128)(2,1)S(1)}, bf16[3,256,1024]{2,1,0:T(8,128)(2,1)S(1)}) custom-call(s32[1]{0:T(128)} %bitcast.4.q_ref, s32[1]{0:T(128)} %bitcast.5.x_at_ref, s32[1]{0:T(128)} %bitcast.6.c_ref, bf16[4,1024,128]{2,1,0:T(8,128)(2,1)S(1)} %all-to-all-done.1.own_ref, ...), custom_call_target="tpu_custom_call" | custom-call | flops 402653184 | bytes 6291456 | tf_op jit(solution)/shard_map/pallas_call | solution.py:34
  98.0 2.9 %collective-permute-start.7 = (bf16[272,768]{1,0:T(8,128)(2,1)S(1)}, bf16[272,768]{1,0:T(8,128)(2,1)S(1)}, u32[]{:S(2)}, u32[]{:S(2)}) collective-permute-start(bf16[272,768]{1,0:T(8,128)(2,1)S(1)} %get-tuple-element.33), channel_id=1, source_target_pairs={{0,96},{32,64},{64,32},{96,0},{1,97},{33,65},{65,33},{97,1},{2,98}... | collective-permute-start | bytes 1253384 | tf_op jit(solution)/shard_map/ppermute | solution.py:190
  100.9 2.2 %shard_map.66 = (bf16[272,768]{1,0:T(8,128)(2,1)S(1)}, bf16[272,768]{1,0:T(8,128)(2,1)S(1)}, f32[272,768]{1,0:T(8,128)S(1)}) custom-call(bf16[3,256,1024]{2,1,0:T(8,128)(2,1)S(1)} %get-tuple-element.30.x_ref, bf16[1024,768]{1,0:T(8,128)(2,1)S(1)} %get-tuple-element.31.w_ref), custom_call_target="tpu_custom_call" | custom-call | flops 1207959552 | bytes 4194304 | tf_op jit(solution)/shard_map/pallas_call | solution.py:34
  103.1 2.7 %collective-permute-start.8 = (bf16[272,768]{1,0:T(8,128)(2,1)S(1)}, bf16[272,768]{1,0:T(8,128)(2,1)S(1)}, u32[]{:S(2)}, u32[]{:S(2)}) collective-permute-start(bf16[272,768]{1,0:T(8,128)(2,1)S(1)} %get-tuple-element.34), channel_id=1, source_target_pairs={{0,32},{32,0},{64,96},{96,64},{1,33},{33,1},{65,97},{97,65},{2,34}... | collective-permute-start | bytes 1253384 | tf_op jit(solution)/shard_map/ppermute | solution.py:190
  105.9 3.6 %collective-permute-start.9 = (bf16[272,768]{1,0:T(8,128)(2,1)S(1)}, bf16[272,768]{1,0:T(8,128)(2,1)S(1)}, u32[]{:S(2)}, u32[]{:S(2)}) collective-permute-start(bf16[272,768]{1,0:T(8,128)(2,1)S(1)} %get-tuple-element.35), channel_id=1, source_target_pairs={{0,64},{32,96},{64,0},{96,32},{1,65},{33,97},{65,1},{97,33},{2,66}... | collective-permute-start | bytes 1253384 | tf_op jit(solution)/shard_map/ppermute | solution.py:190
  110.1 3.2 %collective-permute-done.7 = bf16[272,768]{1,0:T(8,128)(2,1)S(1)} collective-permute-done((bf16[272,768]{1,0:T(8,128)(2,1)S(1)}, bf16[272,768]{1,0:T(8,128)(2,1)S(1)}, u32[]{:S(2)}, u32[]{:S(2)}) %collective-permute-start.7) | collective-permute-done | bytes 417824 | tf_op jit(solution)/shard_map/ppermute | solution.py:190
  113.3 0.1 convert_add_fusion.p0_ref
  113.4 8.3 %collective-permute-done.8.p1_ref = bf16[272,768]{1,0:T(8,128)(2,1)S(1)} collective-permute-done((bf16[272,768]{1,0:T(8,128)(2,1)S(1)}, bf16[272,768]{1,0:T(8,128)(2,1)S(1)}, u32[]{:S(2)}, u32[]{:S(2)}) %collective-permute-start.8) | collective-permute-done | bytes 417824 | tf_op jit(solution)/shard_map/ppermute | solution.py:190
  121.7 0.0 collective-permute-done.9.p2_ref
  121.7 1.9 %shard_map.67.own_ref = bf16[272,512]{1,0:T(8,128)(2,1)S(1)} custom-call(s32[4]{0:T(128)S(1)} %bitcast.19, s32[1]{0:T(128)S(6)} %copy.7.moved_ref, f32[272,768]{1,0:T(8,128)S(1)} %convert_add_fusion.p0_ref, bf16[272,768]{1,0:T(8,128)(2,1)S(1)} %collective-permute-done.8.p1_ref, bf16[272,768]{1,0:T(8,128)(2,1)S(1)} %collective-permute-done.9.p2_ref, ...), custom_call_target="tpu_custom_call" | custom-call | flops 134217728 | bytes 3145728 | tf_op jit(solution)/shard_map/pallas_call | solution.py:34
  123.6 2.5 %collective-permute-start.10 = (bf16[272,512]{1,0:T(8,128)(2,1)S(1)}, bf16[272,512]{1,0:T(8,128)(2,1)S(1)}, u32[]{:S(2)}, u32[]{:S(2)}) collective-permute-start(bf16[272,512]{1,0:T(8,128)(2,1)S(1)} %shard_map.67.own_ref), channel_id=1, source_target_pairs={{0,8},{8,16},{16,24},{24,32},{32,40},{40,48},{48,56},{56,64},{64,7... | collective-permute-start | bytes 835592 | tf_op jit(solution)/shard_map/ppermute | solution.py:239
  126.1 10.1 %collective-permute-done.10.prev_ref = bf16[272,512]{1,0:T(8,128)(2,1)S(1)} collective-permute-done((bf16[272,512]{1,0:T(8,128)(2,1)S(1)}, bf16[272,512]{1,0:T(8,128)(2,1)S(1)}, u32[]{:S(2)}, u32[]{:S(2)}) %collective-permute-start.10) | collective-permute-done | bytes 278560 | tf_op jit(solution)/shard_map/ppermute | solution.py:239
  136.2 1.8 %shard_map.68 = bf16[512,512]{1,0:T(8,128)(2,1)} custom-call(s32[4]{0:T(128)S(1)} %bitcast.20, s32[1]{0:T(128)S(6)} %copy.7.moved_ref, bf16[272,512]{1,0:T(8,128)(2,1)S(1)} %collective-permute-done.10.prev_ref, bf16[272,512]{1,0:T(8,128)(2,1)S(1)} %shard_map.67.own_ref), custom_call_target="tpu_custom_call" | custom-call | flops 268435456 | bytes 1048576 | tf_op jit(solution)/shard_map/pallas_call | solution.py:34
  (2 shorter events, 0.0 us)
Async XLA Ops:
  19.7 16.9 %copy-start.1 = (bf16[32,768]{1,0:T(8,128)(2,1)S(1)}, bf16[32,768]{1,0:T(8,128)(2,1)}, u32[]{:S(2)}) copy-start(bf16[32,768]{1,0:T(8,128)(2,1)} %get-tuple-element.24) | copy-start | bytes 147460
  20.8 60.6 %copy-start = (s32[1,4]{1,0:T(1,128)S(1)}, s32[1,4]{1,0:T(1,128)}, u32[]{:S(2)}) copy-start(s32[1,4]{1,0:T(1,128)} %param.7) | copy-start | bytes 52
  20.8 63.7 %copy-start.2 = (bf16[768]{0:T(1024)(128)(2,1)S(1)}, bf16[768]{0:T(1024)(128)(2,1)}, u32[]{:S(2)}) copy-start(bf16[768]{0:T(1024)(128)(2,1)} %param.11) | copy-start | bytes 4612
  20.8 63.9 %all-to-all-start.1 = ((bf16[4,1024,128]{2,1,0:T(8,128)(2,1)}), bf16[4,1024,128]{2,1,0:T(8,128)(2,1)S(1)}, u32[]{:S(2)}, u32[]{:S(2)}) async-start(bf16[4,1024,128]{2,1,0:T(8,128)(2,1)} %broadcast_in_dim.23), calls=%async_computation.1 | async-start | bytes 2097152 | tf_op jit(solution)/shard_map/all_to_all | solution.py:186
  69.9 20.2 %collective-permute-start.4 = (bf16[256,768]{1,0:T(8,128)(2,1)S(1)}, bf16[256,768]{1,0:T(8,128)(2,1)S(1)}, u32[]{:S(2)}, u32[]{:S(2)}) collective-permute-start(bf16[256,768]{1,0:T(8,128)(2,1)S(1)} %all_gather.3.refs_4_), channel_id=1, source_target_pairs={{0,8},{8,16},{16,24},{24,0},{1,9},{9,17},{17,25},{25,1},{2,10},{10... | collective-permute-start | bytes 1179656 | tf_op jit(solution)/shard_map/ppermute | solution.py:190
  73.4 18.6 %collective-permute-start.5 = (bf16[256,768]{1,0:T(8,128)(2,1)S(1)}, bf16[256,768]{1,0:T(8,128)(2,1)S(1)}, u32[]{:S(2)}, u32[]{:S(2)}) collective-permute-start(bf16[256,768]{1,0:T(8,128)(2,1)S(1)} %all_gather.3.refs_4_), channel_id=1, source_target_pairs={{0,16},{8,24},{16,0},{24,8},{1,17},{9,25},{17,1},{25,9},{2,18},{10... | collective-permute-start | bytes 1179656 | tf_op jit(solution)/shard_map/ppermute | solution.py:190
  78.0 16.4 %collective-permute-start.6 = (bf16[256,768]{1,0:T(8,128)(2,1)S(1)}, bf16[256,768]{1,0:T(8,128)(2,1)S(1)}, u32[]{:S(2)}, u32[]{:S(2)}) collective-permute-start(bf16[256,768]{1,0:T(8,128)(2,1)S(1)} %all_gather.3.refs_4_), channel_id=1, source_target_pairs={{0,24},{8,0},{16,8},{24,16},{1,25},{9,1},{17,9},{25,17},{2,26},{10... | collective-permute-start | bytes 1179656 | tf_op jit(solution)/shard_map/ppermute | solution.py:190
  85.7 8.7 %collective-permute-start = (bf16[1024,128]{1,0:T(8,128)(2,1)}, bf16[1024,128]{1,0:T(8,128)(2,1)S(1)}, u32[]{:S(2)}, u32[]{:S(2)}) collective-permute-start(bf16[1024,128]{1,0:T(8,128)(2,1)} %get-tuple-element.42), channel_id=1, source_target_pairs={{0,1},{1,0},{2,3},{3,2},{4,5},{5,4},{6,7},{7,6},{8,9},{9,8},{10,11... | collective-permute-start | bytes 786440 | tf_op jit(solution)/shard_map/ppermute | solution.py:190
  87.6 6.8 %collective-permute-start.1 = (bf16[1024,128]{1,0:T(8,128)(2,1)}, bf16[1024,128]{1,0:T(8,128)(2,1)S(1)}, u32[]{:S(2)}, u32[]{:S(2)}) collective-permute-start(bf16[1024,128]{1,0:T(8,128)(2,1)} %get-tuple-element.41), channel_id=1, source_target_pairs={{0,1},{1,0},{2,3},{3,2},{4,5},{5,4},{6,7},{7,6},{8,9},{9,8},{10,11... | collective-permute-start | bytes 786440 | tf_op jit(solution)/shard_map/ppermute | solution.py:190
  90.1 4.4 %collective-permute-start.2 = (bf16[1024,128]{1,0:T(8,128)(2,1)}, bf16[1024,128]{1,0:T(8,128)(2,1)}, u32[]{:S(2)}, u32[]{:S(2)}) collective-permute-start(bf16[1024,128]{1,0:T(8,128)(2,1)} %get-tuple-element.40), channel_id=1, source_target_pairs={{0,1},{1,0},{2,3},{3,2},{4,5},{5,4},{6,7},{7,6},{8,9},{9,8},{10,11... | collective-permute-start | bytes 786440 | tf_op jit(solution)/shard_map/ppermute | solution.py:190
  92.0 3.9 %collective-permute-start.3 = (bf16[1024,128]{1,0:T(8,128)(2,1)}, bf16[1024,128]{1,0:T(8,128)(2,1)}, u32[]{:S(2)}, u32[]{:S(2)}) collective-permute-start(bf16[1024,128]{1,0:T(8,128)(2,1)} %get-tuple-element.39), channel_id=1, source_target_pairs={{0,1},{1,0},{2,3},{3,2},{4,5},{5,4},{6,7},{7,6},{8,9},{9,8},{10,11... | collective-permute-start | bytes 786440 | tf_op jit(solution)/shard_map/ppermute | solution.py:190
  98.0 15.3 %collective-permute-start.7 = (bf16[272,768]{1,0:T(8,128)(2,1)S(1)}, bf16[272,768]{1,0:T(8,128)(2,1)S(1)}, u32[]{:S(2)}, u32[]{:S(2)}) collective-permute-start(bf16[272,768]{1,0:T(8,128)(2,1)S(1)} %get-tuple-element.33), channel_id=1, source_target_pairs={{0,96},{32,64},{64,32},{96,0},{1,97},{33,65},{65,33},{97,1},{2,98}... | collective-permute-start | bytes 1253384 | tf_op jit(solution)/shard_map/ppermute | solution.py:190
  103.1 18.6 %collective-permute-start.8 = (bf16[272,768]{1,0:T(8,128)(2,1)S(1)}, bf16[272,768]{1,0:T(8,128)(2,1)S(1)}, u32[]{:S(2)}, u32[]{:S(2)}) collective-permute-start(bf16[272,768]{1,0:T(8,128)(2,1)S(1)} %get-tuple-element.34), channel_id=1, source_target_pairs={{0,32},{32,0},{64,96},{96,64},{1,33},{33,1},{65,97},{97,65},{2,34}... | collective-permute-start | bytes 1253384 | tf_op jit(solution)/shard_map/ppermute | solution.py:190
  105.9 15.8 %collective-permute-start.9 = (bf16[272,768]{1,0:T(8,128)(2,1)S(1)}, bf16[272,768]{1,0:T(8,128)(2,1)S(1)}, u32[]{:S(2)}, u32[]{:S(2)}) collective-permute-start(bf16[272,768]{1,0:T(8,128)(2,1)S(1)} %get-tuple-element.35), channel_id=1, source_target_pairs={{0,64},{32,96},{64,0},{96,32},{1,65},{33,97},{65,1},{97,33},{2,66}... | collective-permute-start | bytes 1253384 | tf_op jit(solution)/shard_map/ppermute | solution.py:190
  123.6 12.6 %collective-permute-start.10 = (bf16[272,512]{1,0:T(8,128)(2,1)S(1)}, bf16[272,512]{1,0:T(8,128)(2,1)S(1)}, u32[]{:S(2)}, u32[]{:S(2)}) collective-permute-start(bf16[272,512]{1,0:T(8,128)(2,1)S(1)} %shard_map.67.own_ref), channel_id=1, source_target_pairs={{0,8},{8,16},{16,24},{24,32},{32,40},{40,48},{48,56},{56,64},{64,7... | collective-permute-start | bytes 835592 | tf_op jit(solution)/shard_map/ppermute | solution.py:239

commit v6 on v3

--- a/solution.py
+++ b/solution.py
@@ -20,7 +20,10 @@
 ROWS = 256
 SAMPLES = 4
 EXTRA = 16
-VMEM = 32 << 20
+FULL = ROWS + EXTRA
+FIRST = 512
+STEPS = (2, 1, 3, 0)
+VMEM = 16 << 20
 
 
 def call(kernel, out_shape, args, scalars=0, hbm=0, flops=0, nbytes=0, scratch=(), vmem_bytes=VMEM):
@@ -31,19 +34,19 @@
         kernel,
         out_shape=out_shape,
         in_specs=[smem] * scalars + [far] * hbm + [vmem] * (len(args) - scalars - hbm),
-        out_specs=[far] * len(out_shape) if isinstance(out_shape, list) else vmem,
+        out_specs=[far] * len(out_shape) if isinstance(out_shape, list) else jax.tree.map(lambda _: vmem, out_shape),
         scratch_shapes=list(scratch),
         compiler_params=pltpu.CompilerParams(vmem_limit_bytes=vmem_bytes),
         cost_estimate=pl.CostEstimate(flops=flops, bytes_accessed=nbytes, transcendentals=0),
     )(*args)
 
 
-def prepare_kernel(at_ref, s_hbm, w_hbm, gain_ref, o_hbm, ow_hbm, s_ref, w_ref, o_ref, sems):
+def prepare_kernel(yl_ref, dp_ref, s_hbm, w_hbm, gain_ref, o_hbm, ow_hbm, s_ref, w_ref, o_ref, sems):
     load_s = pltpu.make_async_copy(s_hbm, s_ref, sems.at[0])
     load_w = pltpu.make_async_copy(w_hbm, w_ref, sems.at[1])
     load_s.start()
     load_w.start()
-    yl, dp = at_ref[0], at_ref[1]
+    yl, dp = yl_ref[0], dp_ref[0]
     lines = gain_ref.shape[0]
     line = lax.broadcasted_iota(jnp.int32, (lines, 128), 0)
     gain = jnp.where(line == lax.shift_right_logical(dp, 2), gain_ref[...].astype(jnp.float32), 0.0)
@@ -55,26 +58,23 @@
     r = lax.broadcasted_iota(jnp.int32, (512, 128), 1)
     rel, zz, k = lax.shift_right_logical(r, 6), lax.shift_right_logical(r, 5) & 1, r & 31
     base = zz * 256 + (rel ^ yl) * 128 + k
-    load_s.wait()
-    stores = []
-    for x in range(NX):
-        perm = (source == base + x * 32).astype(jnp.bfloat16)
-        o_ref[x] = jnp.dot(s_ref[...], perm, preferred_element_type=jnp.float32).astype(jnp.bfloat16)
-        for yh in range(NYH):
-            copy = pltpu.make_async_copy(o_ref.at[x], o_hbm.at[yh, x], sems.at[3 + x * NYH + yh])
-            copy.start()
-            stores.append(copy)
     load_w.wait()
     w_ref[...] = (w_ref[...].astype(jnp.float32) * gain).astype(jnp.bfloat16)
     copy = pltpu.make_async_copy(w_ref, ow_hbm, sems.at[2])
     copy.start()
-    stores.append(copy)
+    stores = [copy]
+    load_s.wait()
+    for x in range(NX):
+        perm = (source == base + x * 32).astype(jnp.bfloat16)
+        o_ref[x] = jnp.dot(s_ref[...], perm, preferred_element_type=jnp.float32).astype(jnp.bfloat16)
+        copy = pltpu.make_async_copy(o_ref.at[x], o_hbm.at[x], sems.at[3 + x])
+        copy.start()
+        stores.append(copy)
     for copy in stores:
         copy.wait()
 
 
-def matmul_kernel(c_ref, own_ref, oth0_ref, oth1_ref, wown_ref, woth_ref, o_ref, w_ref):
-    c = c_ref[0]
+def arrange(c, wown_ref, woth_ref, w_ref):
     for rel in range(NC):
         for yh in range(NYH):
             row = pl.multiple_of((yh * 4 + (c ^ rel) * 2) * WROWS, 64)
@@ -82,18 +82,39 @@
             w_ref[at : at + 64] = wown_ref[pl.ds(row, 64)]
             w_ref[at + 64 : at + 128] = woth_ref[pl.ds(row, 64)]
 
-    for n, oth_ref in enumerate((oth0_ref, oth1_ref)):
-        for k in range(2):
-            g = n * 2 + k
-            x = jnp.concatenate([own_ref[g, yh] for yh in range(NYH)] + [oth_ref[k, yh] for yh in range(NYH)], axis=1)
-            o_ref[g] = jnp.dot(x, w_ref[...], preferred_element_type=jnp.float32).astype(jnp.bfloat16)
+
+def first_kernel(x_ref, c_ref, own_ref, oth_ref, wown_ref, woth_ref, o2_ref, o1_ref, o3_ref, o0_ref, s_ref, w_ref):
+    arrange(c_ref[0], wown_ref, woth_ref, w_ref)
+    for n, (step, o_ref) in enumerate(zip(STEPS, (o2_ref, o1_ref, o3_ref, o0_ref))):
+        rows = pl.ds(pl.multiple_of(((x_ref[0] + step) & 3) * ROWS, ROWS), ROWS)
+        x = jnp.concatenate([ref[yh, rows] for ref in (own_ref, oth_ref) for yh in range(NYH)], axis=1)
+        s_ref[n] = x
+        o_ref[:ROWS] = jnp.dot(x, w_ref[...], preferred_element_type=jnp.float32).astype(o_ref.dtype)
+        square = jnp.square(x.astype(jnp.float32))
+        high = square.astype(jnp.bfloat16)
+        low = (square - high.astype(jnp.float32)).astype(jnp.bfloat16)
+        ones = jnp.ones((EXTRA, x.shape[1]), jnp.bfloat16)
+        lanes = (((1,), (1,)), ((), ()))
+        total = lax.dot_general(ones, high, lanes, preferred_element_type=jnp.float32)
+        total = total + lax.dot_general(ones, low, lanes, preferred_element_type=jnp.float32)
+        rounded = total.astype(jnp.bfloat16).astype(jnp.float32)
+        row = lax.broadcasted_iota(jnp.int32, total.shape, 0)
+        o_ref[ROWS:, :ROWS] = jnp.where(row < EXTRA // 2, rounded, total - rounded).astype(o_ref.dtype)
+        o_ref[ROWS:, ROWS:] = jnp.zeros((EXTRA, o_ref.shape[1] - ROWS), o_ref.dtype)
+
+
+def second_kernel(c_ref, s_ref, wown_ref, woth_ref, o2_ref, o1_ref, o3_ref, o0_ref, w_ref):
+    arrange(c_ref[0], wown_ref, woth_ref, w_ref)
+    for n, o_ref in enumerate((o2_ref, o1_ref, o3_ref, o0_ref)):
+        o_ref[...] = jnp.dot(s_ref[n], w_ref[...], preferred_element_type=jnp.float32).astype(o_ref.dtype)
 
 
 def tail_of(lens, moved):
     return sum(jnp.where(n >= SAMPLES - moved, lens[n], 0) for n in range(SAMPLES))
 
 
-def attend_kernel(len_ref, moved_ref, p_ref, sq_ref, sq2_ref, bias_ref, cos_ref, sin_ref, o_ref):
+def attend_kernel(len_ref, moved_ref, bias_ref, cos_ref, sin_ref, *refs):
+    first, second, o_ref = refs[:NX], refs[NX : 2 * NX], refs[2 * NX]
     s1 = len_ref[0]
     s2 = s1 + len_ref[1]
     s3 = s2 + len_ref[2]
@@ -101,15 +122,19 @@
     j = lax.broadcasted_iota(jnp.int32, (ROWS, ROWS), 1)
     start = jnp.where(i >= s3, s3, jnp.where(i >= s2, s2, jnp.where(i >= s1, s1, 0)))
     allowed = (j >= start) & (j <= i)
-    r = lax.rsqrt((sq_ref[...] + sq2_ref[...]) * (1.0 / (NZ * NYL * NX * WROWS)) + EPSILON)
+    squares = jnp.zeros((1, ROWS), jnp.float32)
+    for ref in first:
+        part = ref[ROWS:, :ROWS].astype(jnp.float32)
+        squares = squares + part[:1] + part[EXTRA // 2 : EXTRA // 2 + 1]
+    r = lax.rsqrt(squares * (1.0 / (NZ * NYL * NX * WROWS)) + EPSILON)
     r = jnp.sum(jnp.where(i == j, r, 0.0), axis=1, keepdims=True)
     cos, sin = cos_ref[...], sin_ref[...]
 
     def head(n):
-        at = n * HEAD
-        total = p_ref[0, :, at : at + HEAD].astype(jnp.float32)
-        for k in range(1, NX):
-            total = total + p_ref[k, :, at : at + HEAD].astype(jnp.float32)
+        refs, at = (first, n * HEAD) if n * HEAD < FIRST else (second, n * HEAD - FIRST)
+        total = refs[0][:ROWS, at : at + HEAD].astype(jnp.float32)
+        for ref in refs[1:]:
+            total = total + ref[:ROWS, at : at + HEAD].astype(jnp.float32)
         return total * r + bias_ref[:, n * HEAD : (n + 1) * HEAD]
 
     def rotate(v):
@@ -143,16 +168,16 @@
 
 
 def local(states, lengths, moved, norm_gain, qkv_weight, qkv_bias):
-    yl, c = lax.axis_index("yl"), lax.axis_index("c")
-    dp = lax.axis_index(DP)
+    scalar = lambda v: v.astype(jnp.int32).reshape(1)
+    x, yl, c, dp = [scalar(lax.axis_index(name)) for name in ("x", "yl", "c", DP)]
     bf = lambda *shape: jax.ShapeDtypeStruct(shape, jnp.bfloat16)
-
     columns = qkv_weight.shape[1]
+
     sent, scaled = call(
         prepare_kernel,
-        [bf(NYH, NX, ROWS, 128), bf(WROWS, columns)],
-        (jnp.stack([yl, dp]), states, qkv_weight, norm_gain.reshape(-1, 128)),
-        1,
+        [bf(NX, ROWS, 128), bf(WROWS, columns)],
+        (yl, dp, states, qkv_weight, norm_gain.reshape(-1, 128)),
+        2,
         2,
         flops=2 * 256 * 512 * 512,
         nbytes=1 << 20,
@@ -160,18 +185,23 @@
             pltpu.VMEM((ROWS, 512), jnp.bfloat16),
             pltpu.VMEM((WROWS, columns), jnp.bfloat16),
             pltpu.VMEM((NX, ROWS, 128), jnp.bfloat16),
-            pltpu.SemaphoreType.DMA((3 + NX * NYH,)),
+            pltpu.SemaphoreType.DMA((3 + NX,)),
         ],
         vmem_bytes=60 << 20,
     )
-    raw = lax.all_to_all(sent, "yh", 0, 0, tiled=True)
-    wown = lax.all_gather(scaled, "z", axis=0, tiled=True)
-    raw, wown, lengths, moved, qkv_bias = lax.optimization_barrier((raw, wown, lengths, moved, qkv_bias))
-
-    woth = lax.ppermute(wown, "yl", [(0, 1), (1, 0)])
-    spread = lax.all_to_all(raw.transpose(1, 0, 2, 3), "x", 0, 0, tiled=True)
-
-    squares = jnp.sum(jnp.square(raw.astype(jnp.float32)), axis=(0, 1, 3))
+    mine = lax.all_to_all(sent, "x", 0, 0, tiled=True).reshape(1, NX * ROWS, 128)
+    mine, scaled = lax.optimization_barrier((mine, scaled))
+    spread = lax.all_to_all(jnp.broadcast_to(mine, (NYH, NX * ROWS, 128)), "yh", 0, 0, tiled=True)
+    held = lax.all_gather(scaled, "z", axis=0, tiled=True)
+    spread, held, lengths, qkv_bias = lax.optimization_barrier((spread, held, lengths, qkv_bias))
+
+    send = lambda v, axis, count, to: lax.ppermute(v, axis, [(i, to(i)) for i in range(count)])
+    other = send(spread, "c", NC, lambda i: 1 - i)
+    held1, held2 = held[:, :FIRST], held[:, FIRST:]
+    came1 = send(held1, "yl", NYL, lambda i: 1 - i)
+    came1, held2 = lax.optimization_barrier((came1, held2))
+    came2 = send(held2, "yl", NYL, lambda i: 1 - i)
+
     lens = lengths[0]
     ids = jnp.arange(ROWS, dtype=jnp.int32)
     starts = [jnp.sum(lens[:n]) for n in range(SAMPLES)]
@@ -185,26 +215,39 @@
     cos = jnp.concatenate([cos, cos], axis=1)
     sin = jnp.concatenate([-sin, sin], axis=1)
     bias = qkv_bias.astype(jnp.float32)[None, :]
-    spread, squares, bias, cos, sin = lax.optimization_barrier((spread, squares, bias, cos, sin))
-    others = [lax.ppermute(spread[n * 2 : n * 2 + 2], "c", [(0, 1), (1, 0)]) for n in range(2)]
-
-    partial = call(
-        matmul_kernel,
-        bf(NX, ROWS, columns),
-        (c.reshape(1), spread, *others, wown, woth),
+    came1, bias, cos, sin = lax.optimization_barrier((came1, bias, cos, sin))
+
+    def outputs(rows, count):
+        return (bf(rows, count),) * (NX - 1) + (jax.ShapeDtypeStruct((rows, count), jnp.float32),)
+
+    def spread_x(parts):
+        return [send(v, "x", NX, lambda i: (i + step) % NX) for v, step in zip(parts, STEPS[: NX - 1])] + [parts[NX - 1]]
+
+    *parts, packed = call(
+        first_kernel,
+        outputs(FULL, FIRST) + (bf(NX, ROWS, 1024),),
+        (x, c, spread, other, held1, came1),
+        2,
+        flops=2 * NX * ROWS * 1024 * FIRST,
+        nbytes=6 << 20,
+        scratch=[pltpu.VMEM((1024, FIRST), jnp.bfloat16)],
+    )
+    first = spread_x(parts)
+    came2, first[0] = lax.optimization_barrier((came2, first[0]))
+    parts = call(
+        second_kernel,
+        outputs(ROWS, columns - FIRST),
+        (c, packed, held2, came2),
         1,
-        flops=2 * NX * ROWS * 1024 * columns,
-        nbytes=6 << 20,
-        scratch=[pltpu.VMEM((1024, columns), jnp.bfloat16)],
-    )
-    partial, squares = lax.optimization_barrier((partial, squares))
-    summed = lax.all_to_all(partial, "x", 0, 0, tiled=True)
-
-    squares2 = lax.ppermute(squares, "c", [(0, 1), (1, 0)])
+        flops=2 * NX * ROWS * 1024 * (columns - FIRST),
+        nbytes=4 << 20,
+        scratch=[pltpu.VMEM((1024, columns - FIRST), jnp.bfloat16)],
+    )
+    second = spread_x(parts)
     context = call(
         attend_kernel,
-        bf(ROWS + EXTRA, PER * HEAD),
-        (lens, moved, summed, squares.reshape(1, ROWS), squares2.reshape(1, ROWS), bias, cos, sin),
+        bf(FULL, PER * HEAD),
+        (lens, moved, bias, cos, sin, *first, *second),
         2,
         flops=4 * 4 * ROWS * ROWS * HEAD,
         nbytes=3 << 20,

time: 127 us -> 132 us (1.039)
  waiting for transfers between devices: 34 us -> 19.5 us
  starting transfers between devices: 27.5 us -> 39.3 us
  blocking collectives: 46.9 us -> 57.9 us
    all_to_all x3 -> x1, waiting for transfers between devices: 22.4 us -> 0.01 us  [local(): lax.all_to_all(jnp.broadcast_to(mine, (NYH, NX * ROWS, 128)), 'yh', 0, 0,...]
    ppermute x4 -> x9, starting transfers between devices: 9.84 us -> 29.1 us  [local(): lax.ppermute(v, axis, [(i, to(i)) for i in range(count)])]
    all_to_all x0 -> x1, blocking collectives: none -> 11.1 us  [local(): lax.all_to_all(sent, 'x', 0, 0, tiled=True).reshape(1, NX * ROWS, 128)]
    ppermute x4 -> x9, waiting for transfers between devices: 1.99 us -> 11.4 us  [local(): lax.ppermute(v, axis, [(i, to(i)) for i in range(count)])]
    all_to_all x3 -> x1, starting transfers between devices: 15.2 us -> 7.33 us  [local(): lax.all_to_all(jnp.broadcast_to(mine, (NYH, NX * ROWS, 128)), 'yh', 0, 0,...]
    ppermute x1, waiting for transfers between devices: 9.64 us -> 8.14 us  [local(): lax.ppermute(context, DP, [(i, i + 1) for i in range(NZ * NYL * NX - 1)])]
    pallas_call x4 -> x5, Pallas kernels: 10.7 us -> 9.43 us  [call(): pl.pallas_call(kernel, out_shape=out_shape, in_specs=[smem] * scalars + [...]
  transfers between devices with their start and end apart: 8 -> 11, of which waited for: 5 -> 4; matrix products, arithmetic and copies ran while one was open for 4% -> 3% of each run, Pallas kernels for 0% -> 1%
where the time goes in v6:
time: 132 us; the launch traced here: 131 us
  blocking collectives  57.9 us (44%)
  starting transfers between devices  39.3 us (30%)
  waiting for transfers between devices  19.5 us (15%)
  Pallas kernels  9.43 us (7%)
  other arithmetic  3.31 us (3%)
    all_gather x1, blocking collectives, local(): held = lax.all_gather(scaled, 'z', axis=0, tiled=True)  46.7 us
    ppermute x9, starting transfers between devices, local(): lax.ppermute(v, axis, [(i, to(i)) for i in range(count)])  29.1 us
    ppermute x9, waiting for transfers between devices, local(): lax.ppermute(v, axis, [(i, to(i)) for i in range(count)])  11.4 us
    all_to_all x1, blocking collectives, local(): lax.all_to_all(sent, 'x', 0, 0, tiled=True).reshape(1, NX * ROWS, 128)  11.1 us
    pallas_call x5, Pallas kernels, call(): pl.pallas_call(kernel, out_shape=out_shape, in_specs=[smem] * scalars + [...  9.43 us
    ppermute x1, waiting for transfers between devices, local(): lax.ppermute(context, DP, [(i, i + 1) for i in range(NZ * NYL * NX - 1)])  8.14 us
    all_to_all x1, starting transfers between devices, local(): lax.all_to_all(jnp.broadcast_to(mine, (NYH, NX * ROWS, 128)), 'yh', 0, 0,...  7.33 us
    ppermute x1, starting transfers between devices, local(): lax.ppermute(context, DP, [(i, i + 1) for i in range(NZ * NYL * NX - 1)])  2.8 us
  transfers between devices with their start and end apart: 11, of which 4 were waited for; matrix products, arithmetic and copies ran while one was open for 3% of the time, Pallas kernels for 1%

profile of v6, /device:TPU:40, one launch (start us, length us, event | category | flops | bytes accessed | tf_op | source)
XLA Modules:
  0.0 131.4 jit_solution(8688209675173944899)
XLA Ops:
  0.0 2.8 %shard_map.64 = (bf16[4,256,128]{2,1,0:T(8,128)(2,1)}, bf16[32,768]{1,0:T(8,128)(2,1)}) custom-call(s32[1]{0:T(128)} %bitcast.yl_ref, s32[1]{0:T(128)} %bitcast.1.dp_ref, bf16[256,512]{1,0:T(8,128)(2,1)} %s_hbm.1, bf16[32,768]{1,0:T(8,128)(2,1)} %w_hbm.1, bf16[32,128]{1,0:T(8,128)(2,1)} %bitcast.14), custom_call_target="tpu_custom_call" | custom-call | flops 134217728 | bytes 1048576 | tf_op jit(solution)/shard_map/pallas_call | solution.py:33
  2.8 0.0 copy-start.1
  2.8 11.1 %all_to_all.10 = bf16[4,256,128]{2,1,0:T(8,128)(2,1)S(1)} all-to-all(bf16[4,256,128]{2,1,0:T(8,128)(2,1)} %get-tuple-element.30), channel_id=1, replica_groups=mesh['z'=16,'yl'=2,'x'=4,'yh'=4,'c'=2] {'x'}, dimensions={0} | all-to-all | bytes 524288 | tf_op jit(solution)/shard_map/all_to_all | solution.py:192
  13.9 1.1 broadcast_in_dim.23
  15.0 0.0 copy-start.2
  15.0 0.0 copy-start
  15.0 7.3 %all-to-all-start.1 = ((bf16[4,1024,128]{2,1,0:T(8,128)(2,1)}), bf16[4,1024,128]{2,1,0:T(8,128)(2,1)S(1)}, u32[]{:S(2)}, u32[]{:S(2)}) async-start(bf16[4,1024,128]{2,1,0:T(8,128)(2,1)} %broadcast_in_dim.23), calls=%async_computation.1 | async-start | bytes 2097152 | tf_op jit(solution)/shard_map/all_to_all | solution.py:194
  22.3 0.0 copy-done.1
  22.4 46.7 %all_gather.3 = bf16[512,768]{1,0:T(8,128)(2,1)S(1)} all-gather(bf16[32,768]{1,0:T(8,128)(2,1)S(1)} %copy-done.1), channel_id=1, replica_groups=mesh['z'=16,'yl'=2,'x'=4,'yh'=4,'c'=2] {'z'}, dimensions={0}, use_global_device_ids=true | all-gather | bytes 835584 | tf_op jit(solution)/shard_map/all_gather | solution.py:195
  69.1 0.0 all-to-all-done.1.own_ref
  69.1 1.9 %collective-permute-start.2 = (bf16[4,1024,128]{2,1,0:T(8,128)(2,1)S(1)}, bf16[4,1024,128]{2,1,0:T(8,128)(2,1)S(1)}, u32[]{:S(2)}, u32[]{:S(2)}) collective-permute-start(bf16[4,1024,128]{2,1,0:T(8,128)(2,1)S(1)} %all-to-all-done.1.own_ref), channel_id=1, source_target_pairs={{0,1},{1,0},{2,3},{3,2},{4,5},{5,4},{6,7},{7,6},{8,9},{9,8},{10,11... | collective-permute-start | bytes 3145736 | tf_op jit(solution)/shard_map/ppermute | solution.py:198
  71.1 3.3 %collective-permute-start = (bf16[512,512]{1,0:T(8,128)(2,1)S(1)}, bf16[512,512]{1,0:T(8,128)(2,1)S(1)}, u32[]{:S(2)}, u32[]{:S(2)}) collective-permute-start(bf16[512,512]{1,0:T(8,128)(2,1)S(1)} %slice.18.wown_ref), channel_id=1, source_target_pairs={{0,32},{32,0},{1,33},{33,1},{2,34},{34,2},{3,35},{35,3},{4,36},{36... | collective-permute-start | bytes 1572872 | tf_op jit(solution)/shard_map/ppermute | solution.py:198
  74.5 0.0 copy-done.2
  74.5 0.0 copy-done
  74.5 0.6 slice_reduce_fusion
  75.1 0.7 slice_reduce_fusion.1
  75.8 1.3 fusion.2
  77.1 0.5 fusion
  77.7 0.1 pad_maximum_fusion
  77.8 9.5 %collective-permute-done.woth_ref = bf16[512,512]{1,0:T(8,128)(2,1)S(1)} collective-permute-done((bf16[512,512]{1,0:T(8,128)(2,1)S(1)}, bf16[512,512]{1,0:T(8,128)(2,1)S(1)}, u32[]{:S(2)}, u32[]{:S(2)}) %collective-permute-start) | collective-permute-done | bytes 524320 | tf_op jit(solution)/shard_map/ppermute | solution.py:198
  87.3 0.0 collective-permute-done.2.oth_ref
  87.3 2.3 %shard_map.65 = (bf16[272,512]{1,0:T(8,128)(2,1)S(1)}, bf16[272,512]{1,0:T(8,128)(2,1)S(1)}, bf16[272,512]{1,0:T(8,128)(2,1)S(1)}, f32[272,512]{1,0:T(8,128)S(1)}, bf16[4,256,1024]{2,1,0:T(8,128)(2,1)S(1)}) custom-call(s32[1]{0:T(128)} %bitcast.7.x_ref, s32[1]{0:T(128)} %bitcast.8.c_ref, bf16[4,1024,128]{2,1,0:T(8,128)(2,1)S(1)} %all-to-all-done.1.own_ref, ...), custom_call_target="tpu_custom_call" | custom-call | flops 1073741824 | bytes 6291456 | tf_op jit(solution)/shard_map/pallas_call | solution.py:33
  89.6 2.5 %collective-permute-start.3 = (bf16[272,512]{1,0:T(8,128)(2,1)S(1)}, bf16[272,512]{1,0:T(8,128)(2,1)S(1)}, u32[]{:S(2)}, u32[]{:S(2)}) collective-permute-start(bf16[272,512]{1,0:T(8,128)(2,1)S(1)} %get-tuple-element.44), channel_id=1, source_target_pairs={{0,16},{8,24},{16,0},{24,8},{1,17},{9,25},{17,1},{25,9},{2,18},{10... | collective-permute-start | bytes 835592 | tf_op jit(solution)/shard_map/ppermute | solution.py:198
  92.1 3.6 %collective-permute-start.1 = (bf16[512,256]{1,0:T(8,128)(2,1)S(1)}, bf16[512,256]{1,0:T(8,128)(2,1)S(1)}, u32[]{:S(2)}, u32[]{:S(2)}) collective-permute-start(bf16[512,256]{1,0:T(8,128)(2,1)S(1)} %slice.19.wown_ref), channel_id=1, source_target_pairs={{0,32},{32,0},{1,33},{33,1},{2,34},{34,2},{3,35},{35,3},{4,36},{36... | collective-permute-start | bytes 786440 | tf_op jit(solution)/shard_map/ppermute | solution.py:198
  95.7 3.2 %collective-permute-start.4 = (bf16[272,512]{1,0:T(8,128)(2,1)S(1)}, bf16[272,512]{1,0:T(8,128)(2,1)S(1)}, u32[]{:S(2)}, u32[]{:S(2)}) collective-permute-start(bf16[272,512]{1,0:T(8,128)(2,1)S(1)} %get-tuple-element.46), channel_id=1, source_target_pairs={{0,8},{8,16},{16,24},{24,0},{1,9},{9,17},{17,25},{25,1},{2,10},{10... | collective-permute-start | bytes 835592 | tf_op jit(solution)/shard_map/ppermute | solution.py:198
  98.9 3.9 %collective-permute-start.5 = (bf16[272,512]{1,0:T(8,128)(2,1)S(1)}, bf16[272,512]{1,0:T(8,128)(2,1)S(1)}, u32[]{:S(2)}, u32[]{:S(2)}) collective-permute-start(bf16[272,512]{1,0:T(8,128)(2,1)S(1)} %get-tuple-element.47), channel_id=1, source_target_pairs={{0,24},{8,0},{16,8},{24,16},{1,25},{9,1},{17,9},{25,17},{2,26},{10... | collective-permute-start | bytes 835592 | tf_op jit(solution)/shard_map/ppermute | solution.py:198
  102.8 0.0 collective-permute-done.1.woth_ref
  102.8 0.0 collective-permute-done.3.refs_0_
  102.8 0.7 shard_map.66
  103.5 3.7 %collective-permute-start.6 = (bf16[256,256]{1,0:T(8,128)(2,1)S(1)}, bf16[256,256]{1,0:T(8,128)(2,1)S(1)}, u32[]{:S(2)}, u32[]{:S(2)}) collective-permute-start(bf16[256,256]{1,0:T(8,128)(2,1)S(1)} %get-tuple-element.51), channel_id=1, source_target_pairs={{0,16},{8,24},{16,0},{24,8},{1,17},{9,25},{17,1},{25,9},{2,18},{10... | collective-permute-start | bytes 393224 | tf_op jit(solution)/shard_map/ppermute | solution.py:198
  107.3 2.4 %collective-permute-start.7 = (bf16[256,256]{1,0:T(8,128)(2,1)S(1)}, bf16[256,256]{1,0:T(8,128)(2,1)S(1)}, u32[]{:S(2)}, u32[]{:S(2)}) collective-permute-start(bf16[256,256]{1,0:T(8,128)(2,1)S(1)} %get-tuple-element.52), channel_id=1, source_target_pairs={{0,8},{8,16},{16,24},{24,0},{1,9},{9,17},{17,25},{25,1},{2,10},{10... | collective-permute-start | bytes 393224 | tf_op jit(solution)/shard_map/ppermute | solution.py:198
  109.7 4.7 %collective-permute-start.8 = (bf16[256,256]{1,0:T(8,128)(2,1)S(1)}, bf16[256,256]{1,0:T(8,128)(2,1)S(1)}, u32[]{:S(2)}, u32[]{:S(2)}) collective-permute-start(bf16[256,256]{1,0:T(8,128)(2,1)S(1)} %get-tuple-element.53), channel_id=1, source_target_pairs={{0,24},{8,0},{16,8},{24,16},{1,25},{9,1},{17,9},{25,17},{2,26},{10... | collective-permute-start | bytes 393224 | tf_op jit(solution)/shard_map/ppermute | solution.py:198
  115.0 0.0 collective-permute-done.4.refs_1_
  115.0 0.0 collective-permute-done.5.refs_2_
  115.0 0.0 collective-permute-done.6.refs_4_
  115.0 0.3 collective-permute-done.7.refs_5_
  115.3 1.5 %collective-permute-done.8.refs_6_ = bf16[256,256]{1,0:T(8,128)(2,1)S(1)} collective-permute-done((bf16[256,256]{1,0:T(8,128)(2,1)S(1)}, bf16[256,256]{1,0:T(8,128)(2,1)S(1)}, u32[]{:S(2)}, u32[]{:S(2)}) %collective-permute-start.8) | collective-permute-done | bytes 131104 | tf_op jit(solution)/shard_map/ppermute | solution.py:198
  116.8 1.9 %shard_map.67.own_ref = bf16[272,512]{1,0:T(8,128)(2,1)S(1)} custom-call(s32[4]{0:T(128)S(1)} %bitcast.11, s32[1]{0:T(128)S(6)} %copy.7.moved_ref, f32[1,768]{1,0:T(1,128)S(1)} %reshape.50.bias_ref, f32[256,128]{1,0:T(8,128)S(1)} %get-tuple-element.39.cos_ref, f32[256,128]{1,0:T(8,128)S(1)} %get-tuple-element.40.sin_ref, ...), custom_call_target="tpu_custom_call" | custom-call | flops 134217728 | bytes 3145728 | tf_op jit(solution)/shard_map/pallas_call | solution.py:33
  118.7 2.8 %collective-permute-start.9 = (bf16[272,512]{1,0:T(8,128)(2,1)S(1)}, bf16[272,512]{1,0:T(8,128)(2,1)S(1)}, u32[]{:S(2)}, u32[]{:S(2)}) collective-permute-start(bf16[272,512]{1,0:T(8,128)(2,1)S(1)} %shard_map.67.own_ref), channel_id=1, source_target_pairs={{0,8},{8,16},{16,24},{24,32},{32,40},{40,48},{48,56},{56,64},{64,7... | collective-permute-start | bytes 835592 | tf_op jit(solution)/shard_map/ppermute | solution.py:255
  121.5 8.1 %collective-permute-done.9.prev_ref = bf16[272,512]{1,0:T(8,128)(2,1)S(1)} collective-permute-done((bf16[272,512]{1,0:T(8,128)(2,1)S(1)}, bf16[272,512]{1,0:T(8,128)(2,1)S(1)}, u32[]{:S(2)}, u32[]{:S(2)}) %collective-permute-start.9) | collective-permute-done | bytes 278560 | tf_op jit(solution)/shard_map/ppermute | solution.py:255
  129.7 1.8 %shard_map.68 = bf16[512,512]{1,0:T(8,128)(2,1)} custom-call(s32[4]{0:T(128)S(1)} %bitcast.12, s32[1]{0:T(128)S(6)} %copy.7.moved_ref, bf16[272,512]{1,0:T(8,128)(2,1)S(1)} %collective-permute-done.9.prev_ref, bf16[272,512]{1,0:T(8,128)(2,1)S(1)} %shard_map.67.own_ref), custom_call_target="tpu_custom_call" | custom-call | flops 268435456 | bytes 1048576 | tf_op jit(solution)/shard_map/pallas_call | solution.py:33
  (4 shorter events, 0.1 us)
Async XLA Ops:
  2.8 19.6 %copy-start.1 = (bf16[32,768]{1,0:T(8,128)(2,1)S(1)}, bf16[32,768]{1,0:T(8,128)(2,1)}, u32[]{:S(2)}) copy-start(bf16[32,768]{1,0:T(8,128)(2,1)} %get-tuple-element.33) | copy-start | bytes 147460
  15.0 59.4 %copy-start.2 = (bf16[768]{0:T(1024)(128)(2,1)S(1)}, bf16[768]{0:T(1024)(128)(2,1)}, u32[]{:S(2)}) copy-start(bf16[768]{0:T(1024)(128)(2,1)} %param.11) | copy-start | bytes 4612
  15.0 59.5 %copy-start = (s32[1,4]{1,0:T(1,128)S(1)}, s32[1,4]{1,0:T(1,128)}, u32[]{:S(2)}) copy-start(s32[1,4]{1,0:T(1,128)} %param.7) | copy-start | bytes 52
  15.0 54.1 %all-to-all-start.1 = ((bf16[4,1024,128]{2,1,0:T(8,128)(2,1)}), bf16[4,1024,128]{2,1,0:T(8,128)(2,1)S(1)}, u32[]{:S(2)}, u32[]{:S(2)}) async-start(bf16[4,1024,128]{2,1,0:T(8,128)(2,1)} %broadcast_in_dim.23), calls=%async_computation.1 | async-start | bytes 2097152 | tf_op jit(solution)/shard_map/all_to_all | solution.py:194
  69.1 18.2 %collective-permute-start.2 = (bf16[4,1024,128]{2,1,0:T(8,128)(2,1)S(1)}, bf16[4,1024,128]{2,1,0:T(8,128)(2,1)S(1)}, u32[]{:S(2)}, u32[]{:S(2)}) collective-permute-start(bf16[4,1024,128]{2,1,0:T(8,128)(2,1)S(1)} %all-to-all-done.1.own_ref), channel_id=1, source_target_pairs={{0,1},{1,0},{2,3},{3,2},{4,5},{5,4},{6,7},{7,6},{8,9},{9,8},{10,11... | collective-permute-start | bytes 3145736 | tf_op jit(solution)/shard_map/ppermute | solution.py:198
  71.1 16.2 %collective-permute-start = (bf16[512,512]{1,0:T(8,128)(2,1)S(1)}, bf16[512,512]{1,0:T(8,128)(2,1)S(1)}, u32[]{:S(2)}, u32[]{:S(2)}) collective-permute-start(bf16[512,512]{1,0:T(8,128)(2,1)S(1)} %slice.18.wown_ref), channel_id=1, source_target_pairs={{0,32},{32,0},{1,33},{33,1},{2,34},{34,2},{3,35},{35,3},{4,36},{36... | collective-permute-start | bytes 1572872 | tf_op jit(solution)/shard_map/ppermute | solution.py:198
  89.6 13.2 %collective-permute-start.3 = (bf16[272,512]{1,0:T(8,128)(2,1)S(1)}, bf16[272,512]{1,0:T(8,128)(2,1)S(1)}, u32[]{:S(2)}, u32[]{:S(2)}) collective-permute-start(bf16[272,512]{1,0:T(8,128)(2,1)S(1)} %get-tuple-element.44), channel_id=1, source_target_pairs={{0,16},{8,24},{16,0},{24,8},{1,17},{9,25},{17,1},{25,9},{2,18},{10... | collective-permute-start | bytes 835592 | tf_op jit(solution)/shard_map/ppermute | solution.py:198
  92.1 10.7 %collective-permute-start.1 = (bf16[512,256]{1,0:T(8,128)(2,1)S(1)}, bf16[512,256]{1,0:T(8,128)(2,1)S(1)}, u32[]{:S(2)}, u32[]{:S(2)}) collective-permute-start(bf16[512,256]{1,0:T(8,128)(2,1)S(1)} %slice.19.wown_ref), channel_id=1, source_target_pairs={{0,32},{32,0},{1,33},{33,1},{2,34},{34,2},{3,35},{35,3},{4,36},{36... | collective-permute-start | bytes 786440 | tf_op jit(solution)/shard_map/ppermute | solution.py:198
  95.7 19.3 %collective-permute-start.4 = (bf16[272,512]{1,0:T(8,128)(2,1)S(1)}, bf16[272,512]{1,0:T(8,128)(2,1)S(1)}, u32[]{:S(2)}, u32[]{:S(2)}) collective-permute-start(bf16[272,512]{1,0:T(8,128)(2,1)S(1)} %get-tuple-element.46), channel_id=1, source_target_pairs={{0,8},{8,16},{16,24},{24,0},{1,9},{9,17},{17,25},{25,1},{2,10},{10... | collective-permute-start | bytes 835592 | tf_op jit(solution)/shard_map/ppermute | solution.py:198
  98.9 16.1 %collective-permute-start.5 = (bf16[272,512]{1,0:T(8,128)(2,1)S(1)}, bf16[272,512]{1,0:T(8,128)(2,1)S(1)}, u32[]{:S(2)}, u32[]{:S(2)}) collective-permute-start(bf16[272,512]{1,0:T(8,128)(2,1)S(1)} %get-tuple-element.47), channel_id=1, source_target_pairs={{0,24},{8,0},{16,8},{24,16},{1,25},{9,1},{17,9},{25,17},{2,26},{10... | collective-permute-start | bytes 835592 | tf_op jit(solution)/shard_map/ppermute | solution.py:198
  103.5 11.5 %collective-permute-start.6 = (bf16[256,256]{1,0:T(8,128)(2,1)S(1)}, bf16[256,256]{1,0:T(8,128)(2,1)S(1)}, u32[]{:S(2)}, u32[]{:S(2)}) collective-permute-start(bf16[256,256]{1,0:T(8,128)(2,1)S(1)} %get-tuple-element.51), channel_id=1, source_target_pairs={{0,16},{8,24},{16,0},{24,8},{1,17},{9,25},{17,1},{25,9},{2,18},{10... | collective-permute-start | bytes 393224 | tf_op jit(solution)/shard_map/ppermute | solution.py:198
  107.3 8.1 %collective-permute-start.7 = (bf16[256,256]{1,0:T(8,128)(2,1)S(1)}, bf16[256,256]{1,0:T(8,128)(2,1)S(1)}, u32[]{:S(2)}, u32[]{:S(2)}) collective-permute-start(bf16[256,256]{1,0:T(8,128)(2,1)S(1)} %get-tuple-element.52), channel_id=1, source_target_pairs={{0,8},{8,16},{16,24},{24,0},{1,9},{9,17},{17,25},{25,1},{2,10},{10... | collective-permute-start | bytes 393224 | tf_op jit(solution)/shard_map/ppermute | solution.py:198
  109.7 7.2 %collective-permute-start.8 = (bf16[256,256]{1,0:T(8,128)(2,1)S(1)}, bf16[256,256]{1,0:T(8,128)(2,1)S(1)}, u32[]{:S(2)}, u32[]{:S(2)}) collective-permute-start(bf16[256,256]{1,0:T(8,128)(2,1)S(1)} %get-tuple-element.53), channel_id=1, source_target_pairs={{0,24},{8,0},{16,8},{24,16},{1,25},{9,1},{17,9},{25,17},{2,26},{10... | collective-permute-start | bytes 393224 | tf_op jit(solution)/shard_map/ppermute | solution.py:198
  118.7 10.9 %collective-permute-start.9 = (bf16[272,512]{1,0:T(8,128)(2,1)S(1)}, bf16[272,512]{1,0:T(8,128)(2,1)S(1)}, u32[]{:S(2)}, u32[]{:S(2)}) collective-permute-start(bf16[272,512]{1,0:T(8,128)(2,1)S(1)} %shard_map.67.own_ref), channel_id=1, source_target_pairs={{0,8},{8,16},{16,24},{24,32},{32,40},{40,48},{48,56},{56,64},{64,7... | collective-permute-start | bytes 835592 | tf_op jit(solution)/shard_map/ppermute | solution.py:255

commit v7 on v4

--- a/solution.py
+++ b/solution.py
@@ -18,6 +18,7 @@
 TP = ("yh", "c")
 WROWS = 32
 ROWS = 256
+HALF = 128
 SAMPLES = 4
 EXTRA = 16
 NEAR = (1, 3, 0)
@@ -39,12 +40,12 @@
     )(*args)
 
 
-def prepare_kernel(at_ref, s_hbm, w_hbm, gain_ref, o_hbm, ow_hbm, s_ref, w_ref, o_ref, sems):
+def prepare_kernel(yl_ref, dp_ref, s_hbm, w_hbm, gain_ref, o_hbm, ow_hbm, s_ref, w_ref, o_ref, sems):
     load_s = pltpu.make_async_copy(s_hbm, s_ref, sems.at[0])
     load_w = pltpu.make_async_copy(w_hbm, w_ref, sems.at[1])
     load_s.start()
     load_w.start()
-    yl, dp = at_ref[0], at_ref[1]
+    yl, dp = yl_ref[0], dp_ref[0]
     lines = gain_ref.shape[0]
     line = lax.broadcasted_iota(jnp.int32, (lines, 128), 0)
     gain = jnp.where(line == lax.shift_right_logical(dp, 2), gain_ref[...].astype(jnp.float32), 0.0)
@@ -74,27 +75,26 @@
         copy.wait()
 
 
-def first_kernel(at_ref, own_ref, oth0_ref, oth1_ref, wown_ref, woth_ref, o_ref, w_ref, x_ref):
-    far, c = at_ref[0], at_ref[1]
+def arrange_kernel(c_ref, wown_ref, woth_ref, w_ref):
+    c = c_ref[0]
     for rel in range(NC):
         for yh in range(NYH):
             row = pl.multiple_of((yh * 4 + (c ^ rel) * 2) * WROWS, 64)
             at = (rel * NYH + yh) * 128
             w_ref[at : at + 64] = wown_ref[pl.ds(row, 64)]
             w_ref[at + 64 : at + 128] = woth_ref[pl.ds(row, 64)]
-    half = NYH // 2
-
-    def states(g):
-        return jnp.concatenate(
-            [own_ref[g, yh] for yh in range(NYH)]
-            + [oth0_ref[g, yh] for yh in range(half)]
-            + [oth1_ref[g, yh] for yh in range(half)],
-            axis=1,
-        )
-
-    o_ref[...] = jnp.dot(states(far), w_ref[...], preferred_element_type=jnp.float32).astype(jnp.bfloat16)
+
+
+def first_kernel(x_at_ref, own_ref, oth_ref, w_ref, o_ref, x_ref):
+    x = x_at_ref[0]
+
+    def states(step):
+        g = (x + step) & 3
+        return jnp.concatenate([ref[g, yh] for ref in (own_ref, oth_ref) for yh in range(NYH)], axis=1)
+
+    o_ref[...] = jnp.dot(states(2), w_ref[...], preferred_element_type=jnp.float32).astype(jnp.bfloat16)
     for n, step in enumerate(NEAR):
-        x_ref[n] = states((far + 2 + step) & 3)
+        x_ref[n] = states(step)
 
 
 def second_kernel(x_ref, w_ref, o1_ref, o3_ref, own_ref):
@@ -113,7 +113,7 @@
     i = lax.broadcasted_iota(jnp.int32, (ROWS, ROWS), 0)
     j = lax.broadcasted_iota(jnp.int32, (ROWS, ROWS), 1)
     start = jnp.where(i >= s3, s3, jnp.where(i >= s2, s2, jnp.where(i >= s1, s1, 0)))
-    allowed = (j >= start) & (j <= i)
+    allowed = ((j >= start) & (j <= i)).astype(jnp.int32)
     r = lax.rsqrt((sq_ref[...] + sq2_ref[...]) * (1.0 / (NZ * NYL * NX * WROWS)) + EPSILON)
     r = jnp.sum(jnp.where(i == j, r, 0.0), axis=1, keepdims=True)
     cos, sin = cos_ref[...], sin_ref[...]
@@ -132,27 +132,39 @@
     value = head(PER + 1).astype(jnp.bfloat16)
     for h in range(PER):
         query = rotate(head(h))
-        scores = lax.dot_general(query, key, (((1,), (1,)), ((), ())), preferred_element_type=jnp.float32)
-        scores = jnp.where(allowed, scores * HEAD ** (-0.5), -1e30)
-        e = jnp.exp(scores - jnp.max(scores, axis=1, keepdims=True))
-        weights = (e / jnp.sum(e, axis=1, keepdims=True)).astype(jnp.bfloat16)
-        o_ref[:ROWS, h * HEAD : (h + 1) * HEAD] = jnp.dot(
-            weights, value, preferred_element_type=jnp.float32
-        ).astype(jnp.bfloat16)
+        for block in range(2):
+            rows, keys = slice(block * HALF, (block + 1) * HALF), slice(0, (block + 1) * HALF)
+            scores = lax.dot_general(
+                query[rows], key[keys], (((1,), (1,)), ((), ())), preferred_element_type=jnp.float32
+            )
+            scores = jnp.where(allowed[rows, keys] > 0, scores * HEAD ** (-0.5), -1e30)
+            e = jnp.exp(scores - jnp.max(scores, axis=1, keepdims=True))
+            weights = (e * (1.0 / jnp.sum(e, axis=1, keepdims=True))).astype(jnp.bfloat16)
+            o_ref[rows, h * HEAD : (h + 1) * HEAD] = jnp.dot(
+                weights, value[keys], preferred_element_type=jnp.float32
+            ).astype(jnp.bfloat16)
     tail = tail_of(len_ref, moved_ref[0]).astype(jnp.float32)
     o_ref[ROWS:] = jnp.full((EXTRA, PER * HEAD), tail, jnp.float32).astype(jnp.bfloat16)
 
 
-def pack_kernel(len_ref, moved_ref, prev_ref, own_ref, o_ref):
+def pack_kernel(len_ref, moved_ref, prev_ref, own_ref, o_hbm, o_ref, sems):
     tail = tail_of(len_ref, moved_ref[0])
     incoming = prev_ref[ROWS:, :HEAD].astype(jnp.float32)[:1, :1].astype(jnp.int32)
-    slot = lax.broadcasted_iota(jnp.int32, (2 * ROWS, ROWS), 0)
-    row = lax.broadcasted_iota(jnp.int32, (2 * ROWS, ROWS), 1)
-    first = ((slot < incoming) & (row == slot + (ROWS - incoming))).astype(jnp.bfloat16)
-    second = ((row == slot - incoming) & (row < ROWS - tail)).astype(jnp.bfloat16)
-    picked = jnp.dot(first, prev_ref[:ROWS], preferred_element_type=jnp.float32)
-    picked = picked + jnp.dot(second, own_ref[:ROWS], preferred_element_type=jnp.float32)
-    o_ref[...] = picked.astype(jnp.bfloat16)
+    row = lax.broadcasted_iota(jnp.int32, (ROWS, ROWS), 1)
+    copies = []
+    for block in range(2):
+        slot = lax.broadcasted_iota(jnp.int32, (ROWS, ROWS), 0) + block * ROWS
+        pick = ((row == slot - incoming) & (row < ROWS - tail)).astype(jnp.bfloat16)
+        picked = jnp.dot(pick, own_ref[:ROWS], preferred_element_type=jnp.float32)
+        if block == 0:
+            pick = ((slot < incoming) & (row == slot + (ROWS - incoming))).astype(jnp.bfloat16)
+            picked = picked + jnp.dot(pick, prev_ref[:ROWS], preferred_element_type=jnp.float32)
+        o_ref[block] = picked.astype(jnp.bfloat16)
+        copy = pltpu.make_async_copy(o_ref.at[block], o_hbm.at[pl.ds(block * ROWS, ROWS)], sems.at[block])
+        copy.start()
+        copies.append(copy)
+    for copy in copies:
+        copy.wait()
 
 
 def local(states, lengths, moved, norm_gain, qkv_weight, qkv_bias):
@@ -164,8 +176,8 @@
     sent, scaled = call(
         prepare_kernel,
         [bf(NYH, NX, ROWS, 128), bf(WROWS, columns)],
-        (jnp.stack([yl, dp]), states, qkv_weight, norm_gain.reshape(-1, 128)),
-        1,
+        (yl.reshape(1), dp.reshape(1), states, qkv_weight, norm_gain.reshape(-1, 128)),
+        2,
         2,
         flops=2 * 256 * 512 * 512,
         nbytes=1 << 20,
@@ -182,7 +194,8 @@
     raw, wown, lengths, moved, qkv_bias = lax.optimization_barrier((raw, wown, lengths, moved, qkv_bias))
 
     woth = lax.ppermute(wown, "yl", [(0, 1), (1, 0)])
-    spread = lax.all_to_all(raw.transpose(1, 0, 2, 3), "x", 0, 0, tiled=True)
+    raw = lax.optimization_barrier(raw.transpose(1, 0, 2, 3))
+    spread = lax.all_to_all(raw, "x", 0, 0, tiled=True)
 
     squares = jnp.sum(jnp.square(raw.astype(jnp.float32)), axis=(0, 1, 3))
     lens = lengths[0]
@@ -199,15 +212,18 @@
     sin = jnp.concatenate([-sin, sin], axis=1)
     bias = qkv_bias.astype(jnp.float32)[None, :]
     spread, squares, bias, cos, sin = lax.optimization_barrier((spread, squares, bias, cos, sin))
-    others = [lax.ppermute(spread[:, n * 2 : n * 2 + 2], "c", [(0, 1), (1, 0)]) for n in range(2)]
+    other = lax.ppermute(spread, "c", [(0, 1), (1, 0)])
 
     x = lax.axis_index("x")
     whole = lambda step, v: lax.ppermute(v, "x", [(i, (i + step) % NX) for i in range(NX)])
     flops = 2 * ROWS * 1024 * columns
-    far, weights, near = call(
+    weights = call(
+        arrange_kernel, bf(1024, columns), (c.reshape(1), wown, woth), 1, flops=20 * 10**9, nbytes=3 << 20
+    )
+    far, near = call(
         first_kernel,
-        (bf(ROWS, columns), bf(1024, columns), bf(3, ROWS, 1024)),
-        (jnp.stack([(x + 2) & 3, c]), spread, *others, wown, woth),
+        (bf(ROWS, columns), bf(3, ROWS, 1024)),
+        (x.reshape(1), spread, other, weights),
         1,
         flops=flops,
         nbytes=6 << 20,
@@ -235,12 +251,13 @@
     previous = lax.ppermute(context, DP, [(i, i + 1) for i in range(NZ * NYL * NX - 1)])
     return call(
         pack_kernel,
-        bf(2 * ROWS, PER * HEAD),
+        [bf(2 * ROWS, PER * HEAD)],
         (lens, moved, previous, context),
         2,
         flops=4 * 512 * 256 * 512,
         nbytes=1 << 20,
-    )
+        scratch=[pltpu.VMEM((2, ROWS, PER * HEAD), jnp.bfloat16), pltpu.SemaphoreType.DMA((2,))],
+    )[0]
 
 
 def solution(mesh):

time: 124 us -> 120 us (0.968)
  waiting for transfers between devices: 25.6 us -> 22.6 us
  local copies, waits for them, and re-layouts: 2.39 us -> 1.07 us
    ppermute x3, waiting for transfers between devices: 9.61 us -> 6.28 us  [local(): lax.ppermute(v, 'x', [(i, (i + step) % NX) for i in range(NX)])]
    ppermute x2 -> x1, starting transfers between devices: 4.32 us -> 1.91 us  [local(): other = lax.ppermute(spread, 'c', [(0, 1), (1, 0)])]
    ppermute x3, starting transfers between devices: 9.54 us -> 11.6 us  [local(): lax.ppermute(v, 'x', [(i, (i + step) % NX) for i in range(NX)])]
    ppermute x1, waiting for transfers between devices: 0.01 us -> 1.89 us  [local(): woth = lax.ppermute(wown, 'yl', [(0, 1), (1, 0)])]
    all_to_all x1, waiting for transfers between devices: 4.06 us -> 2.71 us  [local(): spread = lax.all_to_all(raw, 'x', 0, 0, tiled=True)]
    pallas_call x5 -> x6, Pallas kernels: 9.92 us -> 9.69 us  [call(): pl.pallas_call(kernel, out_shape=out_shape, in_specs=[smem] * scalars + [...]
  transfers between devices with their start and end apart: 10 -> 9, of which waited for: 5 -> 6; matrix products, arithmetic and copies ran while one was open for 4% -> 4% of each run, Pallas kernels for 1% -> 1%
where the time goes in v7:
time: 120 us; the launch traced here: 119 us
  blocking collectives  46.9 us (39%)
  starting transfers between devices  32.9 us (27%)
  waiting for transfers between devices  22.6 us (19%)
  Pallas kernels  9.69 us (8%)
  other arithmetic  4.97 us (4%)
    all_gather x1, blocking collectives, local(): wown = lax.all_gather(scaled, 'z', axis=0, tiled=True)  46.9 us
    ppermute x3, starting transfers between devices, local(): lax.ppermute(v, 'x', [(i, (i + step) % NX) for i in range(NX)])  11.6 us
    ppermute x1, waiting for transfers between devices, local(): lax.ppermute(context, DP, [(i, i + 1) for i in range(NZ * NYL * NX - 1)])  10.1 us
    pallas_call x6, Pallas kernels, call(): pl.pallas_call(kernel, out_shape=out_shape, in_specs=[smem] * scalars + [...  9.69 us
    all_to_all x1, starting transfers between devices, local(): raw = lax.all_to_all(sent, 'yh', 0, 0, tiled=True)  7.34 us
    ppermute x3, waiting for transfers between devices, local(): lax.ppermute(v, 'x', [(i, (i + step) % NX) for i in range(NX)])  6.28 us
    all_to_all x1, starting transfers between devices, local(): spread = lax.all_to_all(raw, 'x', 0, 0, tiled=True)  4.42 us
    ppermute x1, starting transfers between devices, local(): woth = lax.ppermute(wown, 'yl', [(0, 1), (1, 0)])  3.24 us
  transfers between devices with their start and end apart: 9, of which 6 were waited for; matrix products, arithmetic and copies ran while one was open for 4% of the time, Pallas kernels for 1%

profile of v7, /device:TPU:40, one launch (start us, length us, event | category | flops | bytes accessed | tf_op | source)
XLA Modules:
  0.0 119.0 jit_solution(13597293448462009148)
XLA Ops:
  0.0 3.0 %shard_map.64 = (bf16[4,4,256,128]{3,2,1,0:T(8,128)(2,1)}, bf16[32,768]{1,0:T(8,128)(2,1)}) custom-call(s32[1]{0:T(128)} %bitcast.yl_ref, s32[1]{0:T(128)} %bitcast.1.dp_ref, bf16[256,512]{1,0:T(8,128)(2,1)} %s_hbm.1, bf16[32,768]{1,0:T(8,128)(2,1)} %w_hbm.1, bf16[32,128]{1,0:T(8,128)(2,1)} %bitcast.18), custom_call_target="tpu_custom_call" | custom-call | flops 134217728 | bytes 1048576 | tf_op jit(solution)/shard_map/pallas_call | solution.py:32
  3.0 0.0 copy-start.1
  3.0 7.3 %all-to-all-start = ((bf16[4,4,256,128]{3,2,1,0:T(8,128)(2,1)}), bf16[4,4,256,128]{3,2,1,0:T(8,128)(2,1)S(1)}, u32[]{:S(2)}, u32[]{:S(2)}) async-start(bf16[4,4,256,128]{3,2,1,0:T(8,128)(2,1)} %get-tuple-element.24), calls=%async_computation | async-start | bytes 2097152 | tf_op jit(solution)/shard_map/all_to_all | solution.py:192
  10.4 0.0 copy-done.1
  10.4 46.9 %all_gather.3.wown_ref = bf16[512,768]{1,0:T(8,128)(2,1)S(1)} all-gather(bf16[32,768]{1,0:T(8,128)(2,1)S(1)} %copy-done.1), channel_id=1, replica_groups=mesh['z'=16,'yl'=2,'x'=4,'yh'=4,'c'=2] {'z'}, dimensions={0}, use_global_device_ids=true | all-gather | bytes 835584 | tf_op jit(solution)/shard_map/all_gather | solution.py:193
  57.3 0.0 all-to-all-done
  57.3 1.1 copy.10
  58.4 0.0 copy-start
  58.4 0.0 copy-start.2
  58.4 4.4 %all-to-all-start.1 = ((bf16[4,4,256,128]{3,2,1,0:T(8,128)(2,1)}), bf16[4,4,256,128]{3,2,1,0:T(8,128)(2,1)S(1)}, u32[]{:S(2)}, u32[]{:S(2)}) async-start(bf16[4,4,256,128]{3,2,1,0:T(8,128)(2,1)} %bitcast.11), calls=%async_computation.1 | async-start | bytes 2097152 | tf_op jit(solution)/shard_map/all_to_all | solution.py:198
  62.8 3.2 %collective-permute-start.1 = (bf16[512,768]{1,0:T(8,128)(2,1)S(1)}, bf16[512,768]{1,0:T(8,128)(2,1)S(1)}, u32[]{:S(2)}, u32[]{:S(2)}) collective-permute-start(bf16[512,768]{1,0:T(8,128)(2,1)S(1)} %all_gather.3.wown_ref), channel_id=1, source_target_pairs={{0,32},{32,0},{1,33},{33,1},{2,34},{34,2},{3,35},{35,3},{4,36},{36... | collective-permute-start | bytes 2359304 | tf_op jit(solution)/shard_map/ppermute | solution.py:196
  66.0 0.0 copy-done
  66.1 0.6 slice_reduce_fusion
  66.7 0.0 copy-done.2
  66.7 0.7 slice_reduce_fusion.1
  67.4 1.4 %fusion.2 = f32[256]{0:T(256)S(1)} fusion(s32[]{:T(128)S(1)} %bitcast.13, s32[]{:T(128)} %slice_reduce_fusion, s32[]{:T(128)} %slice_reduce_fusion.1), kind=kLoop, calls=%fused_computation.12 | loop fusion | flops 2048 | bytes 1036 | tf_op jit(solution)/shard_map/convert_element_type | solution.py:207
  68.8 0.5 fusion
  69.3 0.1 pad_maximum_fusion
  69.5 1.5 %multiply_reduce_fusion = f32[256]{0:T(256)S(1)} fusion(bf16[4,4,256,128]{3,2,1,0:T(8,128)(2,1)} %bitcast.11), kind=kLoop, calls=%fused_computation | loop fusion | flops 1572608 | bytes 1049600 | tf_op jit(solution)/shard_map/reduce_sum | solution.py:200
  71.0 2.7 %all-to-all-done.1.own_ref = bf16[4,4,256,128]{3,2,1,0:T(8,128)(2,1)S(1)} async-done(((bf16[4,4,256,128]{3,2,1,0:T(8,128)(2,1)}), bf16[4,4,256,128]{3,2,1,0:T(8,128)(2,1)S(1)}, u32[]{:S(2)}, u32[]{:S(2)}) %all-to-all-start.1) | async-done | bytes 1048608 | tf_op jit(solution)/shard_map/all_to_all | solution.py:198
  73.7 1.9 %collective-permute-start = (bf16[4,4,256,128]{3,2,1,0:T(8,128)(2,1)S(1)}, bf16[4,4,256,128]{3,2,1,0:T(8,128)(2,1)S(1)}, u32[]{:S(2)}, u32[]{:S(2)}) collective-permute-start(bf16[4,4,256,128]{3,2,1,0:T(8,128)(2,1)S(1)} %all-to-all-done.1.own_ref), channel_id=1, source_target_pairs={{0,1},{1,0},{2,3},{3,2},{4,5},{5,4},{6,7},{7,6},{8,9},{9,8},{10,11... | collective-permute-start | bytes 3145736 | tf_op jit(solution)/shard_map/ppermute | solution.py:215
  75.6 1.9 %collective-permute-done.1.woth_ref = bf16[512,768]{1,0:T(8,128)(2,1)S(1)} collective-permute-done((bf16[512,768]{1,0:T(8,128)(2,1)S(1)}, bf16[512,768]{1,0:T(8,128)(2,1)S(1)}, u32[]{:S(2)}, u32[]{:S(2)}) %collective-permute-start.1) | collective-permute-done | bytes 786464 | tf_op jit(solution)/shard_map/ppermute | solution.py:196
  77.5 0.1 shard_map.65.w_ref
  77.6 0.6 collective-permute-done.oth_ref
  78.2 0.8 shard_map.66
  79.0 4.5 %collective-permute-start.2 = (bf16[256,768]{1,0:T(8,128)(2,1)S(1)}, bf16[256,768]{1,0:T(8,128)(2,1)S(1)}, u32[]{:S(2)}, u32[]{:S(2)}) collective-permute-start(bf16[256,768]{1,0:T(8,128)(2,1)S(1)} %get-tuple-element.36), channel_id=1, source_target_pairs={{0,16},{8,24},{16,0},{24,8},{1,17},{9,25},{17,1},{25,9},{2,18},{10... | collective-permute-start | bytes 1179656 | tf_op jit(solution)/shard_map/ppermute | solution.py:218
  83.6 1.4 %shard_map.67 = (bf16[256,768]{1,0:T(8,128)(2,1)S(1)}, bf16[256,768]{1,0:T(8,128)(2,1)S(1)}, f32[256,768]{1,0:T(8,128)S(1)}) custom-call(bf16[3,256,1024]{2,1,0:T(8,128)(2,1)S(1)} %get-tuple-element.32.x_ref, bf16[1024,768]{1,0:T(8,128)(2,1)S(1)} %shard_map.65.w_ref), custom_call_target="tpu_custom_call" | custom-call | flops 1207959552 | bytes 4194304 | tf_op jit(solution)/shard_map/pallas_call | solution.py:32
  85.0 2.5 %collective-permute-start.3 = (bf16[256,768]{1,0:T(8,128)(2,1)S(1)}, bf16[256,768]{1,0:T(8,128)(2,1)S(1)}, u32[]{:S(2)}, u32[]{:S(2)}) collective-permute-start(bf16[256,768]{1,0:T(8,128)(2,1)S(1)} %get-tuple-element.37), channel_id=1, source_target_pairs={{0,8},{8,16},{16,24},{24,0},{1,9},{9,17},{17,25},{25,1},{2,10},{10... | collective-permute-start | bytes 1179656 | tf_op jit(solution)/shard_map/ppermute | solution.py:218
  87.5 4.6 %collective-permute-start.4 = (bf16[256,768]{1,0:T(8,128)(2,1)S(1)}, bf16[256,768]{1,0:T(8,128)(2,1)S(1)}, u32[]{:S(2)}, u32[]{:S(2)}) collective-permute-start(bf16[256,768]{1,0:T(8,128)(2,1)S(1)} %get-tuple-element.38), channel_id=1, source_target_pairs={{0,24},{8,0},{16,8},{24,16},{1,25},{9,1},{17,9},{25,17},{2,26},{10... | collective-permute-start | bytes 1179656 | tf_op jit(solution)/shard_map/ppermute | solution.py:218
  92.7 1.9 %collective-permute-start.5 = (f32[256]{0:T(256)S(1)}, f32[256]{0:T(256)S(1)}, u32[]{:S(2)}, u32[]{:S(2)}) collective-permute-start(f32[256]{0:T(256)S(1)} %multiply_reduce_fusion), channel_id=1, source_target_pairs={{0,1},{1,0},{2,3},{3,2},{4,5},{5,4},{6,7},{7,6},{8,9},{9,8},{10,11... | collective-permute-start | bytes 3080 | tf_op jit(solution)/shard_map/ppermute | solution.py:242
  94.6 0.0 collective-permute-done.2
  94.7 0.1 convert_add_fusion.p0_ref
  94.7 1.0 collective-permute-done.5
  95.7 6.3 %collective-permute-done.3.p1_ref = bf16[256,768]{1,0:T(8,128)(2,1)S(1)} collective-permute-done((bf16[256,768]{1,0:T(8,128)(2,1)S(1)}, bf16[256,768]{1,0:T(8,128)(2,1)S(1)}, u32[]{:S(2)}, u32[]{:S(2)}) %collective-permute-start.3) | collective-permute-done | bytes 393248 | tf_op jit(solution)/shard_map/ppermute | solution.py:218
  102.0 0.0 collective-permute-done.4.p2_ref
  102.0 2.7 %shard_map.68.own_ref = bf16[272,512]{1,0:T(8,128)(2,1)S(1)} custom-call(s32[4]{0:T(128)S(1)} %bitcast.14, s32[1]{0:T(128)S(6)} %copy.11.moved_ref, f32[256,768]{1,0:T(8,128)S(1)} %convert_add_fusion.p0_ref, bf16[256,768]{1,0:T(8,128)(2,1)S(1)} %collective-permute-done.3.p1_ref, bf16[256,768]{1,0:T(8,128)(2,1)S(1)} %collective-permute-done.4.p2_ref, ...), custom_call_target="tpu_custom_call" | custom-call | flops 134217728 | bytes 3145728 | tf_op jit(solution)/shard_map/pallas_call | solution.py:32
  104.7 2.5 %collective-permute-start.6 = (bf16[272,512]{1,0:T(8,128)(2,1)S(1)}, bf16[272,512]{1,0:T(8,128)(2,1)S(1)}, u32[]{:S(2)}, u32[]{:S(2)}) collective-permute-start(bf16[272,512]{1,0:T(8,128)(2,1)S(1)} %shard_map.68.own_ref), channel_id=1, source_target_pairs={{0,8},{8,16},{16,24},{24,32},{32,40},{40,48},{48,56},{56,64},{64,7... | collective-permute-start | bytes 835592 | tf_op jit(solution)/shard_map/ppermute | solution.py:251
  107.2 10.1 %collective-permute-done.6.prev_ref = bf16[272,512]{1,0:T(8,128)(2,1)S(1)} collective-permute-done((bf16[272,512]{1,0:T(8,128)(2,1)S(1)}, bf16[272,512]{1,0:T(8,128)(2,1)S(1)}, u32[]{:S(2)}, u32[]{:S(2)}) %collective-permute-start.6) | collective-permute-done | bytes 278560 | tf_op jit(solution)/shard_map/ppermute | solution.py:251
  117.3 1.7 %shard_map.69 = bf16[512,512]{1,0:T(8,128)(2,1)} custom-call(s32[4]{0:T(128)S(1)} %bitcast.15, s32[1]{0:T(128)S(6)} %copy.11.moved_ref, bf16[272,512]{1,0:T(8,128)(2,1)S(1)} %collective-permute-done.6.prev_ref, bf16[272,512]{1,0:T(8,128)(2,1)S(1)} %shard_map.68.own_ref), custom_call_target="tpu_custom_call" | custom-call | flops 268435456 | bytes 1048576 | tf_op jit(solution)/shard_map/pallas_call | solution.py:32
  (2 shorter events, 0.0 us)
Async XLA Ops:
  3.0 7.4 %copy-start.1 = (bf16[32,768]{1,0:T(8,128)(2,1)S(1)}, bf16[32,768]{1,0:T(8,128)(2,1)}, u32[]{:S(2)}) copy-start(bf16[32,768]{1,0:T(8,128)(2,1)} %get-tuple-element.25) | copy-start | bytes 147460
  3.0 54.3 %all-to-all-start = ((bf16[4,4,256,128]{3,2,1,0:T(8,128)(2,1)}), bf16[4,4,256,128]{3,2,1,0:T(8,128)(2,1)S(1)}, u32[]{:S(2)}, u32[]{:S(2)}) async-start(bf16[4,4,256,128]{3,2,1,0:T(8,128)(2,1)} %get-tuple-element.24), calls=%async_computation | async-start | bytes 2097152 | tf_op jit(solution)/shard_map/all_to_all | solution.py:192
  58.4 7.7 %copy-start = (s32[1,4]{1,0:T(1,128)S(1)}, s32[1,4]{1,0:T(1,128)}, u32[]{:S(2)}) copy-start(s32[1,4]{1,0:T(1,128)} %param.7) | copy-start | bytes 52
  58.4 8.3 %copy-start.2 = (bf16[768]{0:T(1024)(128)(2,1)S(1)}, bf16[768]{0:T(1024)(128)(2,1)}, u32[]{:S(2)}) copy-start(bf16[768]{0:T(1024)(128)(2,1)} %param.11) | copy-start | bytes 4612
  58.4 15.3 %all-to-all-start.1 = ((bf16[4,4,256,128]{3,2,1,0:T(8,128)(2,1)}), bf16[4,4,256,128]{3,2,1,0:T(8,128)(2,1)S(1)}, u32[]{:S(2)}, u32[]{:S(2)}) async-start(bf16[4,4,256,128]{3,2,1,0:T(8,128)(2,1)} %bitcast.11), calls=%async_computation.1 | async-start | bytes 2097152 | tf_op jit(solution)/shard_map/all_to_all | solution.py:198
  62.8 14.7 %collective-permute-start.1 = (bf16[512,768]{1,0:T(8,128)(2,1)S(1)}, bf16[512,768]{1,0:T(8,128)(2,1)S(1)}, u32[]{:S(2)}, u32[]{:S(2)}) collective-permute-start(bf16[512,768]{1,0:T(8,128)(2,1)S(1)} %all_gather.3.wown_ref), channel_id=1, source_target_pairs={{0,32},{32,0},{1,33},{33,1},{2,34},{34,2},{3,35},{35,3},{4,36},{36... | collective-permute-start | bytes 2359304 | tf_op jit(solution)/shard_map/ppermute | solution.py:196
  73.7 4.5 %collective-permute-start = (bf16[4,4,256,128]{3,2,1,0:T(8,128)(2,1)S(1)}, bf16[4,4,256,128]{3,2,1,0:T(8,128)(2,1)S(1)}, u32[]{:S(2)}, u32[]{:S(2)}) collective-permute-start(bf16[4,4,256,128]{3,2,1,0:T(8,128)(2,1)S(1)} %all-to-all-done.1.own_ref), channel_id=1, source_target_pairs={{0,1},{1,0},{2,3},{3,2},{4,5},{5,4},{6,7},{7,6},{8,9},{9,8},{10,11... | collective-permute-start | bytes 3145736 | tf_op jit(solution)/shard_map/ppermute | solution.py:215
  79.0 15.6 %collective-permute-start.2 = (bf16[256,768]{1,0:T(8,128)(2,1)S(1)}, bf16[256,768]{1,0:T(8,128)(2,1)S(1)}, u32[]{:S(2)}, u32[]{:S(2)}) collective-permute-start(bf16[256,768]{1,0:T(8,128)(2,1)S(1)} %get-tuple-element.36), channel_id=1, source_target_pairs={{0,16},{8,24},{16,0},{24,8},{1,17},{9,25},{17,1},{25,9},{2,18},{10... | collective-permute-start | bytes 1179656 | tf_op jit(solution)/shard_map/ppermute | solution.py:218
  85.0 17.0 %collective-permute-start.3 = (bf16[256,768]{1,0:T(8,128)(2,1)S(1)}, bf16[256,768]{1,0:T(8,128)(2,1)S(1)}, u32[]{:S(2)}, u32[]{:S(2)}) collective-permute-start(bf16[256,768]{1,0:T(8,128)(2,1)S(1)} %get-tuple-element.37), channel_id=1, source_target_pairs={{0,8},{8,16},{16,24},{24,0},{1,9},{9,17},{17,25},{25,1},{2,10},{10... | collective-permute-start | bytes 1179656 | tf_op jit(solution)/shard_map/ppermute | solution.py:218
  87.5 14.5 %collective-permute-start.4 = (bf16[256,768]{1,0:T(8,128)(2,1)S(1)}, bf16[256,768]{1,0:T(8,128)(2,1)S(1)}, u32[]{:S(2)}, u32[]{:S(2)}) collective-permute-start(bf16[256,768]{1,0:T(8,128)(2,1)S(1)} %get-tuple-element.38), channel_id=1, source_target_pairs={{0,24},{8,0},{16,8},{24,16},{1,25},{9,1},{17,9},{25,17},{2,26},{10... | collective-permute-start | bytes 1179656 | tf_op jit(solution)/shard_map/ppermute | solution.py:218
  92.7 3.0 %collective-permute-start.5 = (f32[256]{0:T(256)S(1)}, f32[256]{0:T(256)S(1)}, u32[]{:S(2)}, u32[]{:S(2)}) collective-permute-start(f32[256]{0:T(256)S(1)} %multiply_reduce_fusion), channel_id=1, source_target_pairs={{0,1},{1,0},{2,3},{3,2},{4,5},{5,4},{6,7},{7,6},{8,9},{9,8},{10,11... | collective-permute-start | bytes 3080 | tf_op jit(solution)/shard_map/ppermute | solution.py:242
  104.7 12.6 %collective-permute-start.6 = (bf16[272,512]{1,0:T(8,128)(2,1)S(1)}, bf16[272,512]{1,0:T(8,128)(2,1)S(1)}, u32[]{:S(2)}, u32[]{:S(2)}) collective-permute-start(bf16[272,512]{1,0:T(8,128)(2,1)S(1)} %shard_map.68.own_ref), channel_id=1, source_target_pairs={{0,8},{8,16},{16,24},{24,32},{32,40},{40,48},{48,56},{56,64},{64,7... | collective-permute-start | bytes 835592 | tf_op jit(solution)/shard_map/ppermute | solution.py:251

commit v8 on v7

--- a/solution.py
+++ b/solution.py
@@ -41,13 +41,13 @@
 
 
 def prepare_kernel(yl_ref, dp_ref, s_hbm, w_hbm, gain_ref, o_hbm, ow_hbm, s_ref, w_ref, o_ref, sems):
-    load_s = pltpu.make_async_copy(s_hbm, s_ref, sems.at[0])
-    load_w = pltpu.make_async_copy(w_hbm, w_ref, sems.at[1])
-    load_s.start()
-    load_w.start()
+    halves = [pl.ds(n * HALF, HALF) for n in range(2)]
+    loads = [pltpu.make_async_copy(s_hbm.at[rows], s_ref.at[rows], sems.at[n]) for n, rows in enumerate(halves)]
+    load_w = pltpu.make_async_copy(w_hbm, w_ref, sems.at[2])
+    for copy in (loads[0], load_w, loads[1]):
+        copy.start()
     yl, dp = yl_ref[0], dp_ref[0]
-    lines = gain_ref.shape[0]
-    line = lax.broadcasted_iota(jnp.int32, (lines, 128), 0)
+    line = lax.broadcasted_iota(jnp.int32, (gain_ref.shape[0], 128), 0)
     gain = jnp.where(line == lax.shift_right_logical(dp, 2), gain_ref[...].astype(jnp.float32), 0.0)
     gain = jnp.sum(gain, axis=0, keepdims=True)
     row = lax.broadcasted_iota(jnp.int32, (WROWS, 128), 0)
@@ -57,20 +57,20 @@
     r = lax.broadcasted_iota(jnp.int32, (512, 128), 1)
     rel, zz, k = lax.shift_right_logical(r, 6), lax.shift_right_logical(r, 5) & 1, r & 31
     base = zz * 256 + (rel ^ yl) * 128 + k
-    load_s.wait()
+    perms = [(source == base + x * 32).astype(jnp.bfloat16) for x in range(NX)]
     stores = []
-    for x in range(NX):
-        perm = (source == base + x * 32).astype(jnp.bfloat16)
-        o_ref[x] = jnp.dot(s_ref[...], perm, preferred_element_type=jnp.float32).astype(jnp.bfloat16)
+    for n, rows in enumerate(halves):
+        loads[n].wait()
+        for x in range(NX):
+            o_ref[x, rows] = jnp.dot(s_ref[rows], perms[x], preferred_element_type=jnp.float32).astype(jnp.bfloat16)
         for yh in range(NYH):
-            copy = pltpu.make_async_copy(o_ref.at[x], o_hbm.at[yh, x], sems.at[3 + x * NYH + yh])
-            copy.start()
-            stores.append(copy)
-    load_w.wait()
-    w_ref[...] = (w_ref[...].astype(jnp.float32) * gain).astype(jnp.bfloat16)
-    copy = pltpu.make_async_copy(w_ref, ow_hbm, sems.at[2])
-    copy.start()
-    stores.append(copy)
+            stores.append(pltpu.make_async_copy(o_ref.at[:, rows], o_hbm.at[yh, :, rows], sems.at[4 + n * NYH + yh]))
+            stores[-1].start()
+        if n == 0:
+            load_w.wait()
+            w_ref[...] = (w_ref[...].astype(jnp.float32) * gain).astype(jnp.bfloat16)
+            stores.append(pltpu.make_async_copy(w_ref, ow_hbm, sems.at[3]))
+            stores[-1].start()
     for copy in stores:
         copy.wait()
 
@@ -113,7 +113,7 @@
     i = lax.broadcasted_iota(jnp.int32, (ROWS, ROWS), 0)
     j = lax.broadcasted_iota(jnp.int32, (ROWS, ROWS), 1)
     start = jnp.where(i >= s3, s3, jnp.where(i >= s2, s2, jnp.where(i >= s1, s1, 0)))
-    allowed = ((j >= start) & (j <= i)).astype(jnp.int32)
+    allowed = (j >= start) & (j <= i)
     r = lax.rsqrt((sq_ref[...] + sq2_ref[...]) * (1.0 / (NZ * NYL * NX * WROWS)) + EPSILON)
     r = jnp.sum(jnp.where(i == j, r, 0.0), axis=1, keepdims=True)
     cos, sin = cos_ref[...], sin_ref[...]
@@ -132,17 +132,13 @@
     value = head(PER + 1).astype(jnp.bfloat16)
     for h in range(PER):
         query = rotate(head(h))
-        for block in range(2):
-            rows, keys = slice(block * HALF, (block + 1) * HALF), slice(0, (block + 1) * HALF)
-            scores = lax.dot_general(
-                query[rows], key[keys], (((1,), (1,)), ((), ())), preferred_element_type=jnp.float32
-            )
-            scores = jnp.where(allowed[rows, keys] > 0, scores * HEAD ** (-0.5), -1e30)
-            e = jnp.exp(scores - jnp.max(scores, axis=1, keepdims=True))
-            weights = (e * (1.0 / jnp.sum(e, axis=1, keepdims=True))).astype(jnp.bfloat16)
-            o_ref[rows, h * HEAD : (h + 1) * HEAD] = jnp.dot(
-                weights, value[keys], preferred_element_type=jnp.float32
-            ).astype(jnp.bfloat16)
+        scores = lax.dot_general(query, key, (((1,), (1,)), ((), ())), preferred_element_type=jnp.float32)
+        scores = jnp.where(allowed, scores * HEAD ** (-0.5), -1e30)
+        e = jnp.exp(scores - jnp.max(scores, axis=1, keepdims=True))
+        weights = (e * (1.0 / jnp.sum(e, axis=1, keepdims=True))).astype(jnp.bfloat16)
+        o_ref[:ROWS, h * HEAD : (h + 1) * HEAD] = jnp.dot(
+            weights, value, preferred_element_type=jnp.float32
+        ).astype(jnp.bfloat16)
     tail = tail_of(len_ref, moved_ref[0]).astype(jnp.float32)
     o_ref[ROWS:] = jnp.full((EXTRA, PER * HEAD), tail, jnp.float32).astype(jnp.bfloat16)
 
@@ -185,7 +181,7 @@
             pltpu.VMEM((ROWS, 512), jnp.bfloat16),
             pltpu.VMEM((WROWS, columns), jnp.bfloat16),
             pltpu.VMEM((NX, ROWS, 128), jnp.bfloat16),
-            pltpu.SemaphoreType.DMA((3 + NX * NYH,)),
+            pltpu.SemaphoreType.DMA((4 + 2 * NYH,)),
         ],
         vmem_bytes=60 << 20,
     )

time: 120 us -> 119 us (level)
  no operation moved by 1% of the time
where the time goes in v8:
time: 119 us; the launch traced here: 118 us
  blocking collectives  46.9 us (39%)
  starting transfers between devices  32.9 us (28%)
  waiting for transfers between devices  22.6 us (19%)
  Pallas kernels  8.94 us (8%)
  other arithmetic  4.97 us (4%)
    all_gather x1, blocking collectives, local(): wown = lax.all_gather(scaled, 'z', axis=0, tiled=True)  46.9 us
    ppermute x3, starting transfers between devices, local(): lax.ppermute(v, 'x', [(i, (i + step) % NX) for i in range(NX)])  11.6 us
    ppermute x1, waiting for transfers between devices, local(): lax.ppermute(context, DP, [(i, i + 1) for i in range(NZ * NYL * NX - 1)])  10.1 us
    pallas_call x6, Pallas kernels, call(): pl.pallas_call(kernel, out_shape=out_shape, in_specs=[smem] * scalars + [...  8.94 us
    all_to_all x1, starting transfers between devices, local(): raw = lax.all_to_all(sent, 'yh', 0, 0, tiled=True)  7.34 us
    ppermute x3, waiting for transfers between devices, local(): lax.ppermute(v, 'x', [(i, (i + step) % NX) for i in range(NX)])  6.28 us
    all_to_all x1, starting transfers between devices, local(): spread = lax.all_to_all(raw, 'x', 0, 0, tiled=True)  4.43 us
    ppermute x1, starting transfers between devices, local(): woth = lax.ppermute(wown, 'yl', [(0, 1), (1, 0)])  3.24 us
  transfers between devices with their start and end apart: 9, of which 6 were waited for; matrix products, arithmetic and copies ran while one was open for 4% of the time, Pallas kernels for 1%

profile of v8, /device:TPU:40, one launch (start us, length us, event | category | flops | bytes accessed | tf_op | source)
XLA Modules:
  0.0 118.2 jit_solution(14717640660858608421)
XLA Ops:
  0.0 3.1 %shard_map.64 = (bf16[4,4,256,128]{3,2,1,0:T(8,128)(2,1)}, bf16[32,768]{1,0:T(8,128)(2,1)}) custom-call(s32[1]{0:T(128)} %bitcast.yl_ref, s32[1]{0:T(128)} %bitcast.1.dp_ref, bf16[256,512]{1,0:T(8,128)(2,1)} %s_hbm.1, bf16[32,768]{1,0:T(8,128)(2,1)} %w_hbm.1, bf16[32,128]{1,0:T(8,128)(2,1)} %bitcast.18), custom_call_target="tpu_custom_call" | custom-call | flops 134217728 | bytes 1048576 | tf_op jit(solution)/shard_map/pallas_call | solution.py:32
  3.1 0.0 copy-start.1
  3.1 7.3 %all-to-all-start = ((bf16[4,4,256,128]{3,2,1,0:T(8,128)(2,1)}), bf16[4,4,256,128]{3,2,1,0:T(8,128)(2,1)S(1)}, u32[]{:S(2)}, u32[]{:S(2)}) async-start(bf16[4,4,256,128]{3,2,1,0:T(8,128)(2,1)} %get-tuple-element.24), calls=%async_computation | async-start | bytes 2097152 | tf_op jit(solution)/shard_map/all_to_all | solution.py:188
  10.5 0.0 copy-done.1
  10.5 46.9 %all_gather.3.wown_ref = bf16[512,768]{1,0:T(8,128)(2,1)S(1)} all-gather(bf16[32,768]{1,0:T(8,128)(2,1)S(1)} %copy-done.1), channel_id=1, replica_groups=mesh['z'=16,'yl'=2,'x'=4,'yh'=4,'c'=2] {'z'}, dimensions={0}, use_global_device_ids=true | all-gather | bytes 835584 | tf_op jit(solution)/shard_map/all_gather | solution.py:189
  57.4 0.0 all-to-all-done
  57.4 1.1 copy.10
  58.4 0.0 copy-start
  58.4 0.0 copy-start.2
  58.4 4.4 %all-to-all-start.1 = ((bf16[4,4,256,128]{3,2,1,0:T(8,128)(2,1)}), bf16[4,4,256,128]{3,2,1,0:T(8,128)(2,1)S(1)}, u32[]{:S(2)}, u32[]{:S(2)}) async-start(bf16[4,4,256,128]{3,2,1,0:T(8,128)(2,1)} %bitcast.11), calls=%async_computation.1 | async-start | bytes 2097152 | tf_op jit(solution)/shard_map/all_to_all | solution.py:194
  62.8 3.2 %collective-permute-start.1 = (bf16[512,768]{1,0:T(8,128)(2,1)S(1)}, bf16[512,768]{1,0:T(8,128)(2,1)S(1)}, u32[]{:S(2)}, u32[]{:S(2)}) collective-permute-start(bf16[512,768]{1,0:T(8,128)(2,1)S(1)} %all_gather.3.wown_ref), channel_id=1, source_target_pairs={{0,32},{32,0},{1,33},{33,1},{2,34},{34,2},{3,35},{35,3},{4,36},{36... | collective-permute-start | bytes 2359304 | tf_op jit(solution)/shard_map/ppermute | solution.py:192
  66.1 0.0 copy-done
  66.1 0.6 slice_reduce_fusion
  66.7 0.0 copy-done.2
  66.7 0.7 slice_reduce_fusion.1
  67.5 1.4 %fusion.2 = f32[256]{0:T(256)S(1)} fusion(s32[]{:T(128)S(1)} %bitcast.13, s32[]{:T(128)} %slice_reduce_fusion, s32[]{:T(128)} %slice_reduce_fusion.1), kind=kLoop, calls=%fused_computation.12 | loop fusion | flops 2048 | bytes 1036 | tf_op jit(solution)/shard_map/convert_element_type | solution.py:203
  68.8 0.5 fusion
  69.4 0.1 pad_maximum_fusion
  69.5 1.5 %multiply_reduce_fusion = f32[256]{0:T(256)S(1)} fusion(bf16[4,4,256,128]{3,2,1,0:T(8,128)(2,1)} %bitcast.11), kind=kLoop, calls=%fused_computation | loop fusion | flops 1572608 | bytes 1049600 | tf_op jit(solution)/shard_map/reduce_sum | solution.py:196
  71.0 2.7 %all-to-all-done.1.own_ref = bf16[4,4,256,128]{3,2,1,0:T(8,128)(2,1)S(1)} async-done(((bf16[4,4,256,128]{3,2,1,0:T(8,128)(2,1)}), bf16[4,4,256,128]{3,2,1,0:T(8,128)(2,1)S(1)}, u32[]{:S(2)}, u32[]{:S(2)}) %all-to-all-start.1) | async-done | bytes 1048608 | tf_op jit(solution)/shard_map/all_to_all | solution.py:194
  73.7 1.9 %collective-permute-start = (bf16[4,4,256,128]{3,2,1,0:T(8,128)(2,1)S(1)}, bf16[4,4,256,128]{3,2,1,0:T(8,128)(2,1)S(1)}, u32[]{:S(2)}, u32[]{:S(2)}) collective-permute-start(bf16[4,4,256,128]{3,2,1,0:T(8,128)(2,1)S(1)} %all-to-all-done.1.own_ref), channel_id=1, source_target_pairs={{0,1},{1,0},{2,3},{3,2},{4,5},{5,4},{6,7},{7,6},{8,9},{9,8},{10,11... | collective-permute-start | bytes 3145736 | tf_op jit(solution)/shard_map/ppermute | solution.py:211
  75.7 1.9 %collective-permute-done.1.woth_ref = bf16[512,768]{1,0:T(8,128)(2,1)S(1)} collective-permute-done((bf16[512,768]{1,0:T(8,128)(2,1)S(1)}, bf16[512,768]{1,0:T(8,128)(2,1)S(1)}, u32[]{:S(2)}, u32[]{:S(2)}) %collective-permute-start.1) | collective-permute-done | bytes 786464 | tf_op jit(solution)/shard_map/ppermute | solution.py:192
  77.5 0.1 shard_map.65.w_ref
  77.7 0.6 collective-permute-done.oth_ref
  78.3 0.8 shard_map.66
  79.1 4.5 %collective-permute-start.2 = (bf16[256,768]{1,0:T(8,128)(2,1)S(1)}, bf16[256,768]{1,0:T(8,128)(2,1)S(1)}, u32[]{:S(2)}, u32[]{:S(2)}) collective-permute-start(bf16[256,768]{1,0:T(8,128)(2,1)S(1)} %get-tuple-element.36), channel_id=1, source_target_pairs={{0,16},{8,24},{16,0},{24,8},{1,17},{9,25},{17,1},{25,9},{2,18},{10... | collective-permute-start | bytes 1179656 | tf_op jit(solution)/shard_map/ppermute | solution.py:214
  83.6 1.4 %shard_map.67 = (bf16[256,768]{1,0:T(8,128)(2,1)S(1)}, bf16[256,768]{1,0:T(8,128)(2,1)S(1)}, f32[256,768]{1,0:T(8,128)S(1)}) custom-call(bf16[3,256,1024]{2,1,0:T(8,128)(2,1)S(1)} %get-tuple-element.32.x_ref, bf16[1024,768]{1,0:T(8,128)(2,1)S(1)} %shard_map.65.w_ref), custom_call_target="tpu_custom_call" | custom-call | flops 1207959552 | bytes 4194304 | tf_op jit(solution)/shard_map/pallas_call | solution.py:32
  85.1 2.5 %collective-permute-start.3 = (bf16[256,768]{1,0:T(8,128)(2,1)S(1)}, bf16[256,768]{1,0:T(8,128)(2,1)S(1)}, u32[]{:S(2)}, u32[]{:S(2)}) collective-permute-start(bf16[256,768]{1,0:T(8,128)(2,1)S(1)} %get-tuple-element.37), channel_id=1, source_target_pairs={{0,8},{8,16},{16,24},{24,0},{1,9},{9,17},{17,25},{25,1},{2,10},{10... | collective-permute-start | bytes 1179656 | tf_op jit(solution)/shard_map/ppermute | solution.py:214
  87.5 4.6 %collective-permute-start.4 = (bf16[256,768]{1,0:T(8,128)(2,1)S(1)}, bf16[256,768]{1,0:T(8,128)(2,1)S(1)}, u32[]{:S(2)}, u32[]{:S(2)}) collective-permute-start(bf16[256,768]{1,0:T(8,128)(2,1)S(1)} %get-tuple-element.38), channel_id=1, source_target_pairs={{0,24},{8,0},{16,8},{24,16},{1,25},{9,1},{17,9},{25,17},{2,26},{10... | collective-permute-start | bytes 1179656 | tf_op jit(solution)/shard_map/ppermute | solution.py:214
  92.8 1.9 %collective-permute-start.5 = (f32[256]{0:T(256)S(1)}, f32[256]{0:T(256)S(1)}, u32[]{:S(2)}, u32[]{:S(2)}) collective-permute-start(f32[256]{0:T(256)S(1)} %multiply_reduce_fusion), channel_id=1, source_target_pairs={{0,1},{1,0},{2,3},{3,2},{4,5},{5,4},{6,7},{7,6},{8,9},{9,8},{10,11... | collective-permute-start | bytes 3080 | tf_op jit(solution)/shard_map/ppermute | solution.py:238
  94.7 0.0 collective-permute-done.2
  94.7 0.1 convert_add_fusion.p0_ref
  94.8 1.0 collective-permute-done.5
  95.8 6.3 %collective-permute-done.3.p1_ref = bf16[256,768]{1,0:T(8,128)(2,1)S(1)} collective-permute-done((bf16[256,768]{1,0:T(8,128)(2,1)S(1)}, bf16[256,768]{1,0:T(8,128)(2,1)S(1)}, u32[]{:S(2)}, u32[]{:S(2)}) %collective-permute-start.3) | collective-permute-done | bytes 393248 | tf_op jit(solution)/shard_map/ppermute | solution.py:214
  102.1 0.0 collective-permute-done.4.p2_ref
  102.1 1.9 %shard_map.68.own_ref = bf16[272,512]{1,0:T(8,128)(2,1)S(1)} custom-call(s32[4]{0:T(128)S(1)} %bitcast.14, s32[1]{0:T(128)S(6)} %copy.11.moved_ref, f32[256,768]{1,0:T(8,128)S(1)} %convert_add_fusion.p0_ref, bf16[256,768]{1,0:T(8,128)(2,1)S(1)} %collective-permute-done.3.p1_ref, bf16[256,768]{1,0:T(8,128)(2,1)S(1)} %collective-permute-done.4.p2_ref, ...), custom_call_target="tpu_custom_call" | custom-call | flops 134217728 | bytes 3145728 | tf_op jit(solution)/shard_map/pallas_call | solution.py:32
  104.0 2.5 %collective-permute-start.6 = (bf16[272,512]{1,0:T(8,128)(2,1)S(1)}, bf16[272,512]{1,0:T(8,128)(2,1)S(1)}, u32[]{:S(2)}, u32[]{:S(2)}) collective-permute-start(bf16[272,512]{1,0:T(8,128)(2,1)S(1)} %shard_map.68.own_ref), channel_id=1, source_target_pairs={{0,8},{8,16},{16,24},{24,32},{32,40},{40,48},{48,56},{56,64},{64,7... | collective-permute-start | bytes 835592 | tf_op jit(solution)/shard_map/ppermute | solution.py:247
  106.5 10.1 %collective-permute-done.6.prev_ref = bf16[272,512]{1,0:T(8,128)(2,1)S(1)} collective-permute-done((bf16[272,512]{1,0:T(8,128)(2,1)S(1)}, bf16[272,512]{1,0:T(8,128)(2,1)S(1)}, u32[]{:S(2)}, u32[]{:S(2)}) %collective-permute-start.6) | collective-permute-done | bytes 278560 | tf_op jit(solution)/shard_map/ppermute | solution.py:247
  116.6 1.7 %shard_map.69 = bf16[512,512]{1,0:T(8,128)(2,1)} custom-call(s32[4]{0:T(128)S(1)} %bitcast.15, s32[1]{0:T(128)S(6)} %copy.11.moved_ref, bf16[272,512]{1,0:T(8,128)(2,1)S(1)} %collective-permute-done.6.prev_ref, bf16[272,512]{1,0:T(8,128)(2,1)S(1)} %shard_map.68.own_ref), custom_call_target="tpu_custom_call" | custom-call | flops 268435456 | bytes 1048576 | tf_op jit(solution)/shard_map/pallas_call | solution.py:32
  (2 shorter events, 0.0 us)
Async XLA Ops:
  3.1 7.4 %copy-start.1 = (bf16[32,768]{1,0:T(8,128)(2,1)S(1)}, bf16[32,768]{1,0:T(8,128)(2,1)}, u32[]{:S(2)}) copy-start(bf16[32,768]{1,0:T(8,128)(2,1)} %get-tuple-element.25) | copy-start | bytes 147460
  3.1 54.3 %all-to-all-start = ((bf16[4,4,256,128]{3,2,1,0:T(8,128)(2,1)}), bf16[4,4,256,128]{3,2,1,0:T(8,128)(2,1)S(1)}, u32[]{:S(2)}, u32[]{:S(2)}) async-start(bf16[4,4,256,128]{3,2,1,0:T(8,128)(2,1)} %get-tuple-element.24), calls=%async_computation | async-start | bytes 2097152 | tf_op jit(solution)/shard_map/all_to_all | solution.py:188
  58.4 7.7 %copy-start = (s32[1,4]{1,0:T(1,128)S(1)}, s32[1,4]{1,0:T(1,128)}, u32[]{:S(2)}) copy-start(s32[1,4]{1,0:T(1,128)} %param.7) | copy-start | bytes 52
  58.4 8.3 %copy-start.2 = (bf16[768]{0:T(1024)(128)(2,1)S(1)}, bf16[768]{0:T(1024)(128)(2,1)}, u32[]{:S(2)}) copy-start(bf16[768]{0:T(1024)(128)(2,1)} %param.11) | copy-start | bytes 4612
  58.4 15.3 %all-to-all-start.1 = ((bf16[4,4,256,128]{3,2,1,0:T(8,128)(2,1)}), bf16[4,4,256,128]{3,2,1,0:T(8,128)(2,1)S(1)}, u32[]{:S(2)}, u32[]{:S(2)}) async-start(bf16[4,4,256,128]{3,2,1,0:T(8,128)(2,1)} %bitcast.11), calls=%async_computation.1 | async-start | bytes 2097152 | tf_op jit(solution)/shard_map/all_to_all | solution.py:194
  62.8 14.7 %collective-permute-start.1 = (bf16[512,768]{1,0:T(8,128)(2,1)S(1)}, bf16[512,768]{1,0:T(8,128)(2,1)S(1)}, u32[]{:S(2)}, u32[]{:S(2)}) collective-permute-start(bf16[512,768]{1,0:T(8,128)(2,1)S(1)} %all_gather.3.wown_ref), channel_id=1, source_target_pairs={{0,32},{32,0},{1,33},{33,1},{2,34},{34,2},{3,35},{35,3},{4,36},{36... | collective-permute-start | bytes 2359304 | tf_op jit(solution)/shard_map/ppermute | solution.py:192
  73.7 4.5 %collective-permute-start = (bf16[4,4,256,128]{3,2,1,0:T(8,128)(2,1)S(1)}, bf16[4,4,256,128]{3,2,1,0:T(8,128)(2,1)S(1)}, u32[]{:S(2)}, u32[]{:S(2)}) collective-permute-start(bf16[4,4,256,128]{3,2,1,0:T(8,128)(2,1)S(1)} %all-to-all-done.1.own_ref), channel_id=1, source_target_pairs={{0,1},{1,0},{2,3},{3,2},{4,5},{5,4},{6,7},{7,6},{8,9},{9,8},{10,11... | collective-permute-start | bytes 3145736 | tf_op jit(solution)/shard_map/ppermute | solution.py:211
  79.1 15.6 %collective-permute-start.2 = (bf16[256,768]{1,0:T(8,128)(2,1)S(1)}, bf16[256,768]{1,0:T(8,128)(2,1)S(1)}, u32[]{:S(2)}, u32[]{:S(2)}) collective-permute-start(bf16[256,768]{1,0:T(8,128)(2,1)S(1)} %get-tuple-element.36), channel_id=1, source_target_pairs={{0,16},{8,24},{16,0},{24,8},{1,17},{9,25},{17,1},{25,9},{2,18},{10... | collective-permute-start | bytes 1179656 | tf_op jit(solution)/shard_map/ppermute | solution.py:214
  85.1 17.0 %collective-permute-start.3 = (bf16[256,768]{1,0:T(8,128)(2,1)S(1)}, bf16[256,768]{1,0:T(8,128)(2,1)S(1)}, u32[]{:S(2)}, u32[]{:S(2)}) collective-permute-start(bf16[256,768]{1,0:T(8,128)(2,1)S(1)} %get-tuple-element.37), channel_id=1, source_target_pairs={{0,8},{8,16},{16,24},{24,0},{1,9},{9,17},{17,25},{25,1},{2,10},{10... | collective-permute-start | bytes 1179656 | tf_op jit(solution)/shard_map/ppermute | solution.py:214
  87.5 14.6 %collective-permute-start.4 = (bf16[256,768]{1,0:T(8,128)(2,1)S(1)}, bf16[256,768]{1,0:T(8,128)(2,1)S(1)}, u32[]{:S(2)}, u32[]{:S(2)}) collective-permute-start(bf16[256,768]{1,0:T(8,128)(2,1)S(1)} %get-tuple-element.38), channel_id=1, source_target_pairs={{0,24},{8,0},{16,8},{24,16},{1,25},{9,1},{17,9},{25,17},{2,26},{10... | collective-permute-start | bytes 1179656 | tf_op jit(solution)/shard_map/ppermute | solution.py:214
  92.8 3.0 %collective-permute-start.5 = (f32[256]{0:T(256)S(1)}, f32[256]{0:T(256)S(1)}, u32[]{:S(2)}, u32[]{:S(2)}) collective-permute-start(f32[256]{0:T(256)S(1)} %multiply_reduce_fusion), channel_id=1, source_target_pairs={{0,1},{1,0},{2,3},{3,2},{4,5},{5,4},{6,7},{7,6},{8,9},{9,8},{10,11... | collective-permute-start | bytes 3080 | tf_op jit(solution)/shard_map/ppermute | solution.py:238
  104.0 12.6 %collective-permute-start.6 = (bf16[272,512]{1,0:T(8,128)(2,1)S(1)}, bf16[272,512]{1,0:T(8,128)(2,1)S(1)}, u32[]{:S(2)}, u32[]{:S(2)}) collective-permute-start(bf16[272,512]{1,0:T(8,128)(2,1)S(1)} %shard_map.68.own_ref), channel_id=1, source_target_pairs={{0,8},{8,16},{16,24},{24,32},{32,40},{40,48},{48,56},{56,64},{64,7... | collective-permute-start | bytes 835592 | tf_op jit(solution)/shard_map/ppermute | solution.py:247

commit v9 on v8

--- a/solution.py
+++ b/solution.py
@@ -53,16 +53,18 @@
     row = lax.broadcasted_iota(jnp.int32, (WROWS, 128), 0)
     lane = lax.broadcasted_iota(jnp.int32, (WROWS, 128), 1)
     gain = jnp.sum(jnp.where(lane == (dp & 3) * WROWS + row, gain, 0.0), axis=1, keepdims=True)
-    source = lax.broadcasted_iota(jnp.int32, (512, 128), 0)
-    r = lax.broadcasted_iota(jnp.int32, (512, 128), 1)
-    rel, zz, k = lax.shift_right_logical(r, 6), lax.shift_right_logical(r, 5) & 1, r & 31
-    base = zz * 256 + (rel ^ yl) * 128 + k
-    perms = [(source == base + x * 32).astype(jnp.bfloat16) for x in range(NX)]
+    source = lax.broadcasted_iota(jnp.int32, (512, 256), 0)
+    r = lax.broadcasted_iota(jnp.int32, (512, 256), 1)
+    odd, rel, zz, k = [lax.shift_right_logical(r, n) & mask for n, mask in ((7, 1), (6, 1), (5, 1), (0, 31))]
+    base = zz * 256 + (rel ^ yl) * 128 + odd * 32 + k
+    perms = [(source == base + x * 32).astype(jnp.bfloat16) for x in range(0, NX, 2)]
     stores = []
     for n, rows in enumerate(halves):
         loads[n].wait()
-        for x in range(NX):
-            o_ref[x, rows] = jnp.dot(s_ref[rows], perms[x], preferred_element_type=jnp.float32).astype(jnp.bfloat16)
+        for x in range(0, NX, 2):
+            pair = jnp.dot(s_ref[rows], perms[x // 2], preferred_element_type=jnp.float32).astype(jnp.bfloat16)
+            o_ref[x, rows] = pair[:, :128]
+            o_ref[x + 1, rows] = pair[:, 128:]
         for yh in range(NYH):
             stores.append(pltpu.make_async_copy(o_ref.at[:, rows], o_hbm.at[yh, :, rows], sems.at[4 + n * NYH + yh]))
             stores[-1].start()
@@ -97,16 +99,20 @@
         x_ref[n] = states(step)
 
 
-def second_kernel(x_ref, w_ref, o1_ref, o3_ref, own_ref):
-    for n, ref in enumerate((o1_ref, o3_ref, own_ref)):
+def second_kernel(x_ref, w_ref, o1_ref, o3_ref):
+    for n, ref in enumerate((o1_ref, o3_ref)):
         ref[...] = jnp.dot(x_ref[n], w_ref[...], preferred_element_type=jnp.float32).astype(ref.dtype)
+
+
+def own_kernel(x_ref, w_ref, o_ref):
+    o_ref[...] = jnp.dot(x_ref[2], w_ref[...], preferred_element_type=jnp.float32)
 
 
 def tail_of(lens, moved):
     return sum(jnp.where(n >= SAMPLES - moved, lens[n], 0) for n in range(SAMPLES))
 
 
-def attend_kernel(len_ref, moved_ref, p0_ref, p1_ref, p2_ref, sq_ref, sq2_ref, bias_ref, cos_ref, sin_ref, o_ref):
+def attend_kernel(len_ref, moved_ref, p0_ref, p1_ref, p2_ref, sq_ref, sq2_ref, bias_ref, cos_ref, sin_ref, o_ref, sent_ref):
     s1 = len_ref[0]
     s2 = s1 + len_ref[1]
     s3 = s2 + len_ref[2]
@@ -136,25 +142,28 @@
         scores = jnp.where(allowed, scores * HEAD ** (-0.5), -1e30)
         e = jnp.exp(scores - jnp.max(scores, axis=1, keepdims=True))
         weights = (e * (1.0 / jnp.sum(e, axis=1, keepdims=True))).astype(jnp.bfloat16)
-        o_ref[:ROWS, h * HEAD : (h + 1) * HEAD] = jnp.dot(
+        o_ref[:, h * HEAD : (h + 1) * HEAD] = jnp.dot(
             weights, value, preferred_element_type=jnp.float32
         ).astype(jnp.bfloat16)
     tail = tail_of(len_ref, moved_ref[0]).astype(jnp.float32)
-    o_ref[ROWS:] = jnp.full((EXTRA, PER * HEAD), tail, jnp.float32).astype(jnp.bfloat16)
+    sent_ref[EXTRA:] = o_ref[EXTRA:]
+    top = o_ref[:EXTRA].astype(jnp.float32)
+    row = lax.broadcasted_iota(jnp.int32, top.shape, 0)
+    sent_ref[:EXTRA] = jnp.where(row == 0, tail, top).astype(jnp.bfloat16)
 
 
 def pack_kernel(len_ref, moved_ref, prev_ref, own_ref, o_hbm, o_ref, sems):
     tail = tail_of(len_ref, moved_ref[0])
-    incoming = prev_ref[ROWS:, :HEAD].astype(jnp.float32)[:1, :1].astype(jnp.int32)
+    incoming = prev_ref[:EXTRA, :HEAD].astype(jnp.float32)[:1, :1].astype(jnp.int32)
     row = lax.broadcasted_iota(jnp.int32, (ROWS, ROWS), 1)
     copies = []
     for block in range(2):
         slot = lax.broadcasted_iota(jnp.int32, (ROWS, ROWS), 0) + block * ROWS
         pick = ((row == slot - incoming) & (row < ROWS - tail)).astype(jnp.bfloat16)
-        picked = jnp.dot(pick, own_ref[:ROWS], preferred_element_type=jnp.float32)
+        picked = jnp.dot(pick, own_ref[...], preferred_element_type=jnp.float32)
         if block == 0:
             pick = ((slot < incoming) & (row == slot + (ROWS - incoming))).astype(jnp.bfloat16)
-            picked = picked + jnp.dot(pick, prev_ref[:ROWS], preferred_element_type=jnp.float32)
+            picked = picked + jnp.dot(pick, prev_ref[...], preferred_element_type=jnp.float32)
         o_ref[block] = picked.astype(jnp.bfloat16)
         copy = pltpu.make_async_copy(o_ref.at[block], o_hbm.at[pl.ds(block * ROWS, ROWS)], sems.at[block])
         copy.start()
@@ -225,26 +234,29 @@
         nbytes=6 << 20,
     )
     far = whole(2, far)
-    right, left, own = call(
+    right, left = call(
         second_kernel,
-        (bf(ROWS, columns), bf(ROWS, columns), jax.ShapeDtypeStruct((ROWS, columns), jnp.float32)),
+        (bf(ROWS, columns), bf(ROWS, columns)),
         (near, weights),
-        flops=3 * flops,
+        flops=2 * flops,
         nbytes=4 << 20,
+    )
+    own = call(
+        own_kernel, jax.ShapeDtypeStruct((ROWS, columns), jnp.float32), (near, weights), flops=flops, nbytes=3 << 20
     )
     right, left = whole(1, right), whole(3, left)
     own, squares = lax.optimization_barrier((own, squares))
     own = own + far.astype(jnp.float32)
     squares2 = lax.ppermute(squares, "c", [(0, 1), (1, 0)])
-    context = call(
+    context, sent = call(
         attend_kernel,
-        bf(ROWS + EXTRA, PER * HEAD),
+        (bf(ROWS, PER * HEAD), bf(ROWS, PER * HEAD)),
         (lens, moved, own, right, left, squares.reshape(1, ROWS), squares2.reshape(1, ROWS), bias, cos, sin),
         2,
         flops=4 * 4 * ROWS * ROWS * HEAD,
         nbytes=3 << 20,
     )
-    previous = lax.ppermute(context, DP, [(i, i + 1) for i in range(NZ * NYL * NX - 1)])
+    previous = lax.ppermute(sent, DP, [(i, i + 1) for i in range(NZ * NYL * NX - 1)])
     return call(
         pack_kernel,
         [bf(2 * ROWS, PER * HEAD)],

time: 119 us -> 118 us (level)
    pallas_call x6 -> x7, Pallas kernels: 8.94 us -> 9.02 us  [call(): pl.pallas_call(kernel, out_shape=out_shape, in_specs=[smem] * scalars + [...]
where the time goes in v9:
time: 118 us
  blocking collectives  46.9 us (40%)
  starting transfers between devices  32.9 us (28%)
  waiting for transfers between devices  22.3 us (19%)
  Pallas kernels  9.02 us (8%)
  other arithmetic  4.77 us (4%)
    all_gather x1, blocking collectives, local(): wown = lax.all_gather(scaled, 'z', axis=0, tiled=True)  46.9 us
    ppermute x3, starting transfers between devices, local(): lax.ppermute(v, 'x', [(i, (i + step) % NX) for i in range(NX)])  11.6 us
    ppermute x1, waiting for transfers between devices, local(): lax.ppermute(sent, DP, [(i, i + 1) for i in range(NZ * NYL * NX - 1)])  9.75 us
    pallas_call x7, Pallas kernels, call(): pl.pallas_call(kernel, out_shape=out_shape, in_specs=[smem] * scalars + [...  9.02 us
    all_to_all x1, starting transfers between devices, local(): raw = lax.all_to_all(sent, 'yh', 0, 0, tiled=True)  7.34 us
    ppermute x3, waiting for transfers between devices, local(): lax.ppermute(v, 'x', [(i, (i + step) % NX) for i in range(NX)])  6.11 us
    all_to_all x1, starting transfers between devices, local(): spread = lax.all_to_all(raw, 'x', 0, 0, tiled=True)  4.42 us
    ppermute x1, starting transfers between devices, local(): woth = lax.ppermute(wown, 'yl', [(0, 1), (1, 0)])  3.25 us
  transfers between devices with their start and end apart: 9, of which 6 were waited for; matrix products, arithmetic and copies ran while one was open for 4% of the time, Pallas kernels for 1%

profile of v9, /device:TPU:40, one launch (start us, length us, event | category | flops | bytes accessed | tf_op | source)
XLA Modules:
  0.0 117.8 jit_solution(17443763365412535381)
XLA Ops:
  0.0 3.0 %shard_map.64 = (bf16[4,4,256,128]{3,2,1,0:T(8,128)(2,1)}, bf16[32,768]{1,0:T(8,128)(2,1)}) custom-call(s32[1]{0:T(128)} %bitcast.yl_ref, s32[1]{0:T(128)} %bitcast.1.dp_ref, bf16[256,512]{1,0:T(8,128)(2,1)} %s_hbm.1, bf16[32,768]{1,0:T(8,128)(2,1)} %w_hbm.1, bf16[32,128]{1,0:T(8,128)(2,1)} %bitcast.18), custom_call_target="tpu_custom_call" | custom-call | flops 134217728 | bytes 1048576 | tf_op jit(solution)/shard_map/pallas_call | solution.py:32
  3.0 0.0 copy-start.1
  3.0 7.3 %all-to-all-start = ((bf16[4,4,256,128]{3,2,1,0:T(8,128)(2,1)}), bf16[4,4,256,128]{3,2,1,0:T(8,128)(2,1)S(1)}, u32[]{:S(2)}, u32[]{:S(2)}) async-start(bf16[4,4,256,128]{3,2,1,0:T(8,128)(2,1)} %get-tuple-element.25), calls=%async_computation | async-start | bytes 2097152 | tf_op jit(solution)/shard_map/all_to_all | solution.py:197
  10.3 0.0 copy-done.1
  10.3 46.9 %all_gather.3.wown_ref = bf16[512,768]{1,0:T(8,128)(2,1)S(1)} all-gather(bf16[32,768]{1,0:T(8,128)(2,1)S(1)} %copy-done.1), channel_id=1, replica_groups=mesh['z'=16,'yl'=2,'x'=4,'yh'=4,'c'=2] {'z'}, dimensions={0}, use_global_device_ids=true | all-gather | bytes 835584 | tf_op jit(solution)/shard_map/all_gather | solution.py:198
  57.2 0.0 all-to-all-done
  57.2 1.0 copy.10
  58.3 0.0 copy-start
  58.3 0.0 copy-start.2
  58.3 4.4 %all-to-all-start.1 = ((bf16[4,4,256,128]{3,2,1,0:T(8,128)(2,1)}), bf16[4,4,256,128]{3,2,1,0:T(8,128)(2,1)S(1)}, u32[]{:S(2)}, u32[]{:S(2)}) async-start(bf16[4,4,256,128]{3,2,1,0:T(8,128)(2,1)} %bitcast.11), calls=%async_computation.1 | async-start | bytes 2097152 | tf_op jit(solution)/shard_map/all_to_all | solution.py:203
  62.7 3.2 %collective-permute-start.1 = (bf16[512,768]{1,0:T(8,128)(2,1)S(1)}, bf16[512,768]{1,0:T(8,128)(2,1)S(1)}, u32[]{:S(2)}, u32[]{:S(2)}) collective-permute-start(bf16[512,768]{1,0:T(8,128)(2,1)S(1)} %all_gather.3.wown_ref), channel_id=1, source_target_pairs={{0,32},{32,0},{1,33},{33,1},{2,34},{34,2},{3,35},{35,3},{4,36},{36... | collective-permute-start | bytes 2359304 | tf_op jit(solution)/shard_map/ppermute | solution.py:201
  66.0 0.0 copy-done
  66.0 0.6 slice_reduce_fusion
  66.6 0.0 copy-done.2
  66.6 0.6 slice_reduce_fusion.1
  67.2 1.3 %fusion.2 = f32[256]{0:T(256)S(1)} fusion(s32[]{:T(128)S(1)} %bitcast.13, s32[]{:T(128)} %slice_reduce_fusion, s32[]{:T(128)} %slice_reduce_fusion.1), kind=kLoop, calls=%fused_computation.12 | loop fusion | flops 2048 | bytes 1036 | tf_op jit(solution)/shard_map/convert_element_type | solution.py:212
  68.5 0.5 fusion
  69.0 0.1 pad_maximum_fusion
  69.2 1.5 %multiply_reduce_fusion = f32[256]{0:T(256)S(1)} fusion(bf16[4,4,256,128]{3,2,1,0:T(8,128)(2,1)} %bitcast.11), kind=kLoop, calls=%fused_computation | loop fusion | flops 1572608 | bytes 1049600 | tf_op jit(solution)/shard_map/reduce_sum | solution.py:205
  70.7 2.9 %all-to-all-done.1.own_ref = bf16[4,4,256,128]{3,2,1,0:T(8,128)(2,1)S(1)} async-done(((bf16[4,4,256,128]{3,2,1,0:T(8,128)(2,1)}), bf16[4,4,256,128]{3,2,1,0:T(8,128)(2,1)S(1)}, u32[]{:S(2)}, u32[]{:S(2)}) %all-to-all-start.1) | async-done | bytes 1048608 | tf_op jit(solution)/shard_map/all_to_all | solution.py:203
  73.6 1.9 %collective-permute-start = (bf16[4,4,256,128]{3,2,1,0:T(8,128)(2,1)S(1)}, bf16[4,4,256,128]{3,2,1,0:T(8,128)(2,1)S(1)}, u32[]{:S(2)}, u32[]{:S(2)}) collective-permute-start(bf16[4,4,256,128]{3,2,1,0:T(8,128)(2,1)S(1)} %all-to-all-done.1.own_ref), channel_id=1, source_target_pairs={{0,1},{1,0},{2,3},{3,2},{4,5},{5,4},{6,7},{7,6},{8,9},{9,8},{10,11... | collective-permute-start | bytes 3145736 | tf_op jit(solution)/shard_map/ppermute | solution.py:220
  75.5 1.9 %collective-permute-done.1.woth_ref = bf16[512,768]{1,0:T(8,128)(2,1)S(1)} collective-permute-done((bf16[512,768]{1,0:T(8,128)(2,1)S(1)}, bf16[512,768]{1,0:T(8,128)(2,1)S(1)}, u32[]{:S(2)}, u32[]{:S(2)}) %collective-permute-start.1) | collective-permute-done | bytes 786464 | tf_op jit(solution)/shard_map/ppermute | solution.py:201
  77.4 0.1 shard_map.65.w_ref
  77.5 0.6 collective-permute-done.oth_ref
  78.2 0.8 shard_map.66
  79.0 4.5 %collective-permute-start.2 = (bf16[256,768]{1,0:T(8,128)(2,1)S(1)}, bf16[256,768]{1,0:T(8,128)(2,1)S(1)}, u32[]{:S(2)}, u32[]{:S(2)}) collective-permute-start(bf16[256,768]{1,0:T(8,128)(2,1)S(1)} %get-tuple-element.36), channel_id=1, source_target_pairs={{0,16},{8,24},{16,0},{24,8},{1,17},{9,25},{17,1},{25,9},{2,18},{10... | collective-permute-start | bytes 1179656 | tf_op jit(solution)/shard_map/ppermute | solution.py:223
  83.5 1.0 shard_map.68
  84.5 2.5 %collective-permute-start.3 = (bf16[256,768]{1,0:T(8,128)(2,1)S(1)}, bf16[256,768]{1,0:T(8,128)(2,1)S(1)}, u32[]{:S(2)}, u32[]{:S(2)}) collective-permute-start(bf16[256,768]{1,0:T(8,128)(2,1)S(1)} %get-tuple-element.37), channel_id=1, source_target_pairs={{0,8},{8,16},{16,24},{24,0},{1,9},{9,17},{17,25},{25,1},{2,10},{10... | collective-permute-start | bytes 1179656 | tf_op jit(solution)/shard_map/ppermute | solution.py:223
  87.0 4.6 %collective-permute-start.4 = (bf16[256,768]{1,0:T(8,128)(2,1)S(1)}, bf16[256,768]{1,0:T(8,128)(2,1)S(1)}, u32[]{:S(2)}, u32[]{:S(2)}) collective-permute-start(bf16[256,768]{1,0:T(8,128)(2,1)S(1)} %get-tuple-element.38), channel_id=1, source_target_pairs={{0,24},{8,0},{16,8},{24,16},{1,25},{9,1},{17,9},{25,17},{2,26},{10... | collective-permute-start | bytes 1179656 | tf_op jit(solution)/shard_map/ppermute | solution.py:223
  92.2 0.6 shard_map.67
  92.8 1.9 %collective-permute-start.5 = (f32[256]{0:T(256)S(1)}, f32[256]{0:T(256)S(1)}, u32[]{:S(2)}, u32[]{:S(2)}) collective-permute-start(f32[256]{0:T(256)S(1)} %multiply_reduce_fusion), channel_id=1, source_target_pairs={{0,1},{1,0},{2,3},{3,2},{4,5},{5,4},{6,7},{7,6},{8,9},{9,8},{10,11... | collective-permute-start | bytes 3080 | tf_op jit(solution)/shard_map/ppermute | solution.py:250
  94.7 0.0 collective-permute-done.2
  94.7 0.1 convert_add_fusion.p0_ref
  94.8 1.0 collective-permute-done.5
  95.8 6.1 %collective-permute-done.3.p1_ref = bf16[256,768]{1,0:T(8,128)(2,1)S(1)} collective-permute-done((bf16[256,768]{1,0:T(8,128)(2,1)S(1)}, bf16[256,768]{1,0:T(8,128)(2,1)S(1)}, u32[]{:S(2)}, u32[]{:S(2)}) %collective-permute-start.3) | collective-permute-done | bytes 393248 | tf_op jit(solution)/shard_map/ppermute | solution.py:223
  102.0 0.0 collective-permute-done.4.p2_ref
  102.0 1.9 %shard_map.69 = (bf16[256,512]{1,0:T(8,128)(2,1)S(1)}, bf16[256,512]{1,0:T(8,128)(2,1)S(1)}) custom-call(s32[4]{0:T(128)S(1)} %bitcast.14, s32[1]{0:T(128)S(6)} %copy.11.moved_ref, f32[256,768]{1,0:T(8,128)S(1)} %convert_add_fusion.p0_ref, bf16[256,768]{1,0:T(8,128)(2,1)S(1)} %collective-permute-done.3.p1_ref, ...), custom_call_target="tpu_custom_call" | custom-call | flops 134217728 | bytes 3145728 | tf_op jit(solution)/shard_map/pallas_call | solution.py:32
  103.9 2.5 %collective-permute-start.6 = (bf16[256,512]{1,0:T(8,128)(2,1)S(1)}, bf16[256,512]{1,0:T(8,128)(2,1)S(1)}, u32[]{:S(2)}, u32[]{:S(2)}) collective-permute-start(bf16[256,512]{1,0:T(8,128)(2,1)S(1)} %get-tuple-element.43), channel_id=1, source_target_pairs={{0,8},{8,16},{16,24},{24,32},{32,40},{40,48},{48,56},{56,64},{64,7... | collective-permute-start | bytes 786440 | tf_op jit(solution)/shard_map/ppermute | solution.py:259
  106.4 9.8 %collective-permute-done.6.prev_ref = bf16[256,512]{1,0:T(8,128)(2,1)S(1)} collective-permute-done((bf16[256,512]{1,0:T(8,128)(2,1)S(1)}, bf16[256,512]{1,0:T(8,128)(2,1)S(1)}, u32[]{:S(2)}, u32[]{:S(2)}) %collective-permute-start.6) | collective-permute-done | bytes 262176 | tf_op jit(solution)/shard_map/ppermute | solution.py:259
  116.1 1.7 %shard_map.70 = bf16[512,512]{1,0:T(8,128)(2,1)} custom-call(s32[4]{0:T(128)S(1)} %bitcast.15, s32[1]{0:T(128)S(6)} %copy.11.moved_ref, bf16[256,512]{1,0:T(8,128)(2,1)S(1)} %collective-permute-done.6.prev_ref, bf16[256,512]{1,0:T(8,128)(2,1)S(1)} %get-tuple-element.44.own_ref), custom_call_target="tpu_custom_call" | custom-call | flops 268435456 | bytes 1048576 | tf_op jit(solution)/shard_map/pallas_call | solution.py:32
  (2 shorter events, 0.0 us)
Async XLA Ops:
  3.0 7.4 %copy-start.1 = (bf16[32,768]{1,0:T(8,128)(2,1)S(1)}, bf16[32,768]{1,0:T(8,128)(2,1)}, u32[]{:S(2)}) copy-start(bf16[32,768]{1,0:T(8,128)(2,1)} %get-tuple-element.26) | copy-start | bytes 147460
  3.0 54.3 %all-to-all-start = ((bf16[4,4,256,128]{3,2,1,0:T(8,128)(2,1)}), bf16[4,4,256,128]{3,2,1,0:T(8,128)(2,1)S(1)}, u32[]{:S(2)}, u32[]{:S(2)}) async-start(bf16[4,4,256,128]{3,2,1,0:T(8,128)(2,1)} %get-tuple-element.25), calls=%async_computation | async-start | bytes 2097152 | tf_op jit(solution)/shard_map/all_to_all | solution.py:197
  58.3 7.7 %copy-start = (s32[1,4]{1,0:T(1,128)S(1)}, s32[1,4]{1,0:T(1,128)}, u32[]{:S(2)}) copy-start(s32[1,4]{1,0:T(1,128)} %param.7) | copy-start | bytes 52
  58.3 8.3 %copy-start.2 = (bf16[768]{0:T(1024)(128)(2,1)S(1)}, bf16[768]{0:T(1024)(128)(2,1)}, u32[]{:S(2)}) copy-start(bf16[768]{0:T(1024)(128)(2,1)} %param.11) | copy-start | bytes 4612
  58.3 15.3 %all-to-all-start.1 = ((bf16[4,4,256,128]{3,2,1,0:T(8,128)(2,1)}), bf16[4,4,256,128]{3,2,1,0:T(8,128)(2,1)S(1)}, u32[]{:S(2)}, u32[]{:S(2)}) async-start(bf16[4,4,256,128]{3,2,1,0:T(8,128)(2,1)} %bitcast.11), calls=%async_computation.1 | async-start | bytes 2097152 | tf_op jit(solution)/shard_map/all_to_all | solution.py:203
  62.7 14.7 %collective-permute-start.1 = (bf16[512,768]{1,0:T(8,128)(2,1)S(1)}, bf16[512,768]{1,0:T(8,128)(2,1)S(1)}, u32[]{:S(2)}, u32[]{:S(2)}) collective-permute-start(bf16[512,768]{1,0:T(8,128)(2,1)S(1)} %all_gather.3.wown_ref), channel_id=1, source_target_pairs={{0,32},{32,0},{1,33},{33,1},{2,34},{34,2},{3,35},{35,3},{4,36},{36... | collective-permute-start | bytes 2359304 | tf_op jit(solution)/shard_map/ppermute | solution.py:201
  73.6 4.5 %collective-permute-start = (bf16[4,4,256,128]{3,2,1,0:T(8,128)(2,1)S(1)}, bf16[4,4,256,128]{3,2,1,0:T(8,128)(2,1)S(1)}, u32[]{:S(2)}, u32[]{:S(2)}) collective-permute-start(bf16[4,4,256,128]{3,2,1,0:T(8,128)(2,1)S(1)} %all-to-all-done.1.own_ref), channel_id=1, source_target_pairs={{0,1},{1,0},{2,3},{3,2},{4,5},{5,4},{6,7},{7,6},{8,9},{9,8},{10,11... | collective-permute-start | bytes 3145736 | tf_op jit(solution)/shard_map/ppermute | solution.py:220
  79.0 15.8 %collective-permute-start.2 = (bf16[256,768]{1,0:T(8,128)(2,1)S(1)}, bf16[256,768]{1,0:T(8,128)(2,1)S(1)}, u32[]{:S(2)}, u32[]{:S(2)}) collective-permute-start(bf16[256,768]{1,0:T(8,128)(2,1)S(1)} %get-tuple-element.36), channel_id=1, source_target_pairs={{0,16},{8,24},{16,0},{24,8},{1,17},{9,25},{17,1},{25,9},{2,18},{10... | collective-permute-start | bytes 1179656 | tf_op jit(solution)/shard_map/ppermute | solution.py:223
  84.5 17.4 %collective-permute-start.3 = (bf16[256,768]{1,0:T(8,128)(2,1)S(1)}, bf16[256,768]{1,0:T(8,128)(2,1)S(1)}, u32[]{:S(2)}, u32[]{:S(2)}) collective-permute-start(bf16[256,768]{1,0:T(8,128)(2,1)S(1)} %get-tuple-element.37), channel_id=1, source_target_pairs={{0,8},{8,16},{16,24},{24,0},{1,9},{9,17},{17,25},{25,1},{2,10},{10... | collective-permute-start | bytes 1179656 | tf_op jit(solution)/shard_map/ppermute | solution.py:223
  87.0 15.0 %collective-permute-start.4 = (bf16[256,768]{1,0:T(8,128)(2,1)S(1)}, bf16[256,768]{1,0:T(8,128)(2,1)S(1)}, u32[]{:S(2)}, u32[]{:S(2)}) collective-permute-start(bf16[256,768]{1,0:T(8,128)(2,1)S(1)} %get-tuple-element.38), channel_id=1, source_target_pairs={{0,24},{8,0},{16,8},{24,16},{1,25},{9,1},{17,9},{25,17},{2,26},{10... | collective-permute-start | bytes 1179656 | tf_op jit(solution)/shard_map/ppermute | solution.py:223
  92.8 3.0 %collective-permute-start.5 = (f32[256]{0:T(256)S(1)}, f32[256]{0:T(256)S(1)}, u32[]{:S(2)}, u32[]{:S(2)}) collective-permute-start(f32[256]{0:T(256)S(1)} %multiply_reduce_fusion), channel_id=1, source_target_pairs={{0,1},{1,0},{2,3},{3,2},{4,5},{5,4},{6,7},{7,6},{8,9},{9,8},{10,11... | collective-permute-start | bytes 3080 | tf_op jit(solution)/shard_map/ppermute | solution.py:250
  103.9 12.2 %collective-permute-start.6 = (bf16[256,512]{1,0:T(8,128)(2,1)S(1)}, bf16[256,512]{1,0:T(8,128)(2,1)S(1)}, u32[]{:S(2)}, u32[]{:S(2)}) collective-permute-start(bf16[256,512]{1,0:T(8,128)(2,1)S(1)} %get-tuple-element.43), channel_id=1, source_target_pairs={{0,8},{8,16},{16,24},{24,32},{32,40},{40,48},{48,56},{56,64},{64,7... | collective-permute-start | bytes 786440 | tf_op jit(solution)/shard_map/ppermute | solution.py:259

commit v10 on v9

--- a/solution.py
+++ b/solution.py
@@ -21,7 +21,6 @@
 HALF = 128
 SAMPLES = 4
 EXTRA = 16
-NEAR = (1, 3, 0)
 VMEM = 16 << 20
 
 
@@ -87,32 +86,22 @@
             w_ref[at + 64 : at + 128] = woth_ref[pl.ds(row, 64)]
 
 
-def first_kernel(x_at_ref, own_ref, oth_ref, w_ref, o_ref, x_ref):
-    x = x_at_ref[0]
-
-    def states(step):
-        g = (x + step) & 3
-        return jnp.concatenate([ref[g, yh] for ref in (own_ref, oth_ref) for yh in range(NYH)], axis=1)
-
-    o_ref[...] = jnp.dot(states(2), w_ref[...], preferred_element_type=jnp.float32).astype(jnp.bfloat16)
-    for n, step in enumerate(NEAR):
-        x_ref[n] = states(step)
-
-
-def second_kernel(x_ref, w_ref, o1_ref, o3_ref):
-    for n, ref in enumerate((o1_ref, o3_ref)):
-        ref[...] = jnp.dot(x_ref[n], w_ref[...], preferred_element_type=jnp.float32).astype(ref.dtype)
-
-
-def own_kernel(x_ref, w_ref, o_ref):
-    o_ref[...] = jnp.dot(x_ref[2], w_ref[...], preferred_element_type=jnp.float32)
+def product_kernel(own_ref, oth_ref, w_ref, o_hbm, o_ref, sems):
+    copies = []
+    for g in range(NX):
+        x = jnp.concatenate([ref[g, yh] for ref in (own_ref, oth_ref) for yh in range(NYH)], axis=1)
+        o_ref[g] = jnp.dot(x, w_ref[...], preferred_element_type=jnp.float32).astype(jnp.bfloat16)
+        copies.append(pltpu.make_async_copy(o_ref.at[g], o_hbm.at[g], sems.at[g]))
+        copies[-1].start()
+    for copy in copies:
+        copy.wait()
 
 
 def tail_of(lens, moved):
     return sum(jnp.where(n >= SAMPLES - moved, lens[n], 0) for n in range(SAMPLES))
 
 
-def attend_kernel(len_ref, moved_ref, p0_ref, p1_ref, p2_ref, sq_ref, sq2_ref, bias_ref, cos_ref, sin_ref, o_ref, sent_ref):
+def attend_kernel(len_ref, moved_ref, p_ref, sq_ref, sq2_ref, bias_ref, cos_ref, sin_ref, o_ref, sent_ref):
     s1 = len_ref[0]
     s2 = s1 + len_ref[1]
     s3 = s2 + len_ref[2]
@@ -126,9 +115,9 @@
 
     def head(n):
         at = n * HEAD
-        total = p0_ref[:, at : at + HEAD]
-        for ref in (p1_ref, p2_ref):
-            total = total + ref[:, at : at + HEAD].astype(jnp.float32)
+        total = p_ref[0, :, at : at + HEAD].astype(jnp.float32)
+        for k in range(1, NX):
+            total = total + p_ref[k, :, at : at + HEAD].astype(jnp.float32)
         return total * r + bias_ref[:, n * HEAD : (n + 1) * HEAD]
 
     def rotate(v):
@@ -219,39 +208,24 @@
     spread, squares, bias, cos, sin = lax.optimization_barrier((spread, squares, bias, cos, sin))
     other = lax.ppermute(spread, "c", [(0, 1), (1, 0)])
 
-    x = lax.axis_index("x")
-    whole = lambda step, v: lax.ppermute(v, "x", [(i, (i + step) % NX) for i in range(NX)])
-    flops = 2 * ROWS * 1024 * columns
     weights = call(
         arrange_kernel, bf(1024, columns), (c.reshape(1), wown, woth), 1, flops=20 * 10**9, nbytes=3 << 20
     )
-    far, near = call(
-        first_kernel,
-        (bf(ROWS, columns), bf(3, ROWS, 1024)),
-        (x.reshape(1), spread, other, weights),
-        1,
-        flops=flops,
+    partial = call(
+        product_kernel,
+        [bf(NX, ROWS, columns)],
+        (spread, other, weights),
+        flops=2 * NX * ROWS * 1024 * columns,
         nbytes=6 << 20,
-    )
-    far = whole(2, far)
-    right, left = call(
-        second_kernel,
-        (bf(ROWS, columns), bf(ROWS, columns)),
-        (near, weights),
-        flops=2 * flops,
-        nbytes=4 << 20,
-    )
-    own = call(
-        own_kernel, jax.ShapeDtypeStruct((ROWS, columns), jnp.float32), (near, weights), flops=flops, nbytes=3 << 20
-    )
-    right, left = whole(1, right), whole(3, left)
-    own, squares = lax.optimization_barrier((own, squares))
-    own = own + far.astype(jnp.float32)
+        scratch=[pltpu.VMEM((NX, ROWS, columns), jnp.bfloat16), pltpu.SemaphoreType.DMA((NX,))],
+    )[0]
+    partial, squares = lax.optimization_barrier((partial, squares))
+    summed = lax.all_to_all(partial, "x", 0, 0, tiled=True)
     squares2 = lax.ppermute(squares, "c", [(0, 1), (1, 0)])
     context, sent = call(
         attend_kernel,
         (bf(ROWS, PER * HEAD), bf(ROWS, PER * HEAD)),
-        (lens, moved, own, right, left, squares.reshape(1, ROWS), squares2.reshape(1, ROWS), bias, cos, sin),
+        (lens, moved, summed, squares.reshape(1, ROWS), squares2.reshape(1, ROWS), bias, cos, sin),
         2,
         flops=4 * 4 * ROWS * ROWS * HEAD,
         nbytes=3 << 20,

time: 118 us -> 121 us (1.025)
  waiting for transfers between devices: 22.3 us -> 32.3 us
  starting transfers between devices: 32.9 us -> 25.2 us
    all_to_all x0 -> x1, waiting for transfers between devices: none -> 17.9 us  [local(): summed = lax.all_to_all(partial, 'x', 0, 0, tiled=True)]
    ppermute x3 -> x0, starting transfers between devices: 11.6 us -> none  [local(): lax.ppermute(v, 'x', [(i, (i + step) % NX) for i in range(NX)])]
    ppermute x3 -> x0, waiting for transfers between devices: 6.11 us -> none  [local(): lax.ppermute(v, 'x', [(i, (i + step) % NX) for i in range(NX)])]
    all_to_all x0 -> x1, starting transfers between devices: none -> 3.92 us  [local(): summed = lax.all_to_all(partial, 'x', 0, 0, tiled=True)]
    pallas_call x7 -> x5, Pallas kernels: 9.02 us -> 9.29 us  [call(): pl.pallas_call(kernel, out_shape=out_shape, in_specs=[smem] * scalars + [...]
  transfers between devices with their start and end apart: 9 -> 7, of which waited for: 6 -> 6; matrix products, arithmetic and copies ran while one was open for 4% -> 4% of each run, Pallas kernels for 1% -> 0%
where the time goes in v10:
time: 121 us; the launch traced here: 120 us
  blocking collectives  46.9 us (39%)
  waiting for transfers between devices  32.3 us (27%)
  starting transfers between devices  25.2 us (21%)
  Pallas kernels  9.29 us (8%)
  other arithmetic  4.77 us (4%)
    all_gather x1, blocking collectives, local(): wown = lax.all_gather(scaled, 'z', axis=0, tiled=True)  46.9 us
    all_to_all x1, waiting for transfers between devices, local(): summed = lax.all_to_all(partial, 'x', 0, 0, tiled=True)  17.9 us
    pallas_call x5, Pallas kernels, call(): pl.pallas_call(kernel, out_shape=out_shape, in_specs=[smem] * scalars + [...  9.29 us
    ppermute x1, waiting for transfers between devices, local(): lax.ppermute(sent, DP, [(i, i + 1) for i in range(NZ * NYL * NX - 1)])  8.61 us
    all_to_all x1, starting transfers between devices, local(): raw = lax.all_to_all(sent, 'yh', 0, 0, tiled=True)  7.34 us
    all_to_all x1, starting transfers between devices, local(): spread = lax.all_to_all(raw, 'x', 0, 0, tiled=True)  4.42 us
    all_to_all x1, starting transfers between devices, local(): summed = lax.all_to_all(partial, 'x', 0, 0, tiled=True)  3.92 us
    ppermute x1, starting transfers between devices, local(): woth = lax.ppermute(wown, 'yl', [(0, 1), (1, 0)])  3.25 us
  transfers between devices with their start and end apart: 7, of which 6 were waited for; matrix products, arithmetic and copies ran while one was open for 4% of the time, Pallas kernels for 0%

profile of v10, /device:TPU:40, one launch (start us, length us, event | category | flops | bytes accessed | tf_op | source)
XLA Modules:
  0.0 120.3 jit_solution(10063117737318750411)
XLA Ops:
  0.0 3.0 %shard_map.64 = (bf16[4,4,256,128]{3,2,1,0:T(8,128)(2,1)}, bf16[32,768]{1,0:T(8,128)(2,1)}) custom-call(s32[1]{0:T(128)} %bitcast.yl_ref, s32[1]{0:T(128)} %bitcast.1.dp_ref, bf16[256,512]{1,0:T(8,128)(2,1)} %s_hbm.1, bf16[32,768]{1,0:T(8,128)(2,1)} %w_hbm.1, bf16[32,128]{1,0:T(8,128)(2,1)} %bitcast.17), custom_call_target="tpu_custom_call" | custom-call | flops 134217728 | bytes 1048576 | tf_op jit(solution)/shard_map/pallas_call | solution.py:31
  3.0 0.0 copy-start.1
  3.0 7.3 %all-to-all-start = ((bf16[4,4,256,128]{3,2,1,0:T(8,128)(2,1)}), bf16[4,4,256,128]{3,2,1,0:T(8,128)(2,1)S(1)}, u32[]{:S(2)}, u32[]{:S(2)}) async-start(bf16[4,4,256,128]{3,2,1,0:T(8,128)(2,1)} %get-tuple-element.21), calls=%async_computation | async-start | bytes 2097152 | tf_op jit(solution)/shard_map/all_to_all | solution.py:186
  10.3 0.0 copy-done.1
  10.4 46.9 %all_gather.3.wown_ref = bf16[512,768]{1,0:T(8,128)(2,1)S(1)} all-gather(bf16[32,768]{1,0:T(8,128)(2,1)S(1)} %copy-done.1), channel_id=1, replica_groups=mesh['z'=16,'yl'=2,'x'=4,'yh'=4,'c'=2] {'z'}, dimensions={0}, use_global_device_ids=true | all-gather | bytes 835584 | tf_op jit(solution)/shard_map/all_gather | solution.py:187
  57.3 0.0 all-to-all-done
  57.3 1.0 copy.10
  58.3 0.0 copy-start
  58.3 0.0 copy-start.2
  58.3 4.4 %all-to-all-start.1 = ((bf16[4,4,256,128]{3,2,1,0:T(8,128)(2,1)}), bf16[4,4,256,128]{3,2,1,0:T(8,128)(2,1)S(1)}, u32[]{:S(2)}, u32[]{:S(2)}) async-start(bf16[4,4,256,128]{3,2,1,0:T(8,128)(2,1)} %bitcast.10), calls=%async_computation.1 | async-start | bytes 2097152 | tf_op jit(solution)/shard_map/all_to_all | solution.py:192
  62.7 3.2 %collective-permute-start.1 = (bf16[512,768]{1,0:T(8,128)(2,1)S(1)}, bf16[512,768]{1,0:T(8,128)(2,1)S(1)}, u32[]{:S(2)}, u32[]{:S(2)}) collective-permute-start(bf16[512,768]{1,0:T(8,128)(2,1)S(1)} %all_gather.3.wown_ref), channel_id=1, source_target_pairs={{0,32},{32,0},{1,33},{33,1},{2,34},{34,2},{3,35},{35,3},{4,36},{36... | collective-permute-start | bytes 2359304 | tf_op jit(solution)/shard_map/ppermute | solution.py:190
  66.0 0.0 copy-done
  66.0 0.6 slice_reduce_fusion
  66.6 0.0 copy-done.2
  66.6 0.7 slice_reduce_fusion.1
  67.3 1.3 %fusion.2 = f32[256]{0:T(256)S(1)} fusion(s32[]{:T(128)S(1)} %bitcast.12, s32[]{:T(128)} %slice_reduce_fusion, s32[]{:T(128)} %slice_reduce_fusion.1), kind=kLoop, calls=%fused_computation.11 | loop fusion | flops 2048 | bytes 1036 | tf_op jit(solution)/shard_map/convert_element_type | solution.py:201
  68.6 0.5 fusion
  69.1 0.1 pad_maximum_fusion
  69.3 1.5 %multiply_reduce_fusion = f32[256]{0:T(256)S(1)} fusion(bf16[4,4,256,128]{3,2,1,0:T(8,128)(2,1)} %bitcast.10), kind=kLoop, calls=%fused_computation | loop fusion | flops 1572608 | bytes 1049600 | tf_op jit(solution)/shard_map/reduce_sum | solution.py:194
  70.8 2.8 %all-to-all-done.1.own_ref = bf16[4,4,256,128]{3,2,1,0:T(8,128)(2,1)S(1)} async-done(((bf16[4,4,256,128]{3,2,1,0:T(8,128)(2,1)}), bf16[4,4,256,128]{3,2,1,0:T(8,128)(2,1)S(1)}, u32[]{:S(2)}, u32[]{:S(2)}) %all-to-all-start.1) | async-done | bytes 1048608 | tf_op jit(solution)/shard_map/all_to_all | solution.py:192
  73.6 1.9 %collective-permute-start = (bf16[4,4,256,128]{3,2,1,0:T(8,128)(2,1)S(1)}, bf16[4,4,256,128]{3,2,1,0:T(8,128)(2,1)S(1)}, u32[]{:S(2)}, u32[]{:S(2)}) collective-permute-start(bf16[4,4,256,128]{3,2,1,0:T(8,128)(2,1)S(1)} %all-to-all-done.1.own_ref), channel_id=1, source_target_pairs={{0,1},{1,0},{2,3},{3,2},{4,5},{5,4},{6,7},{7,6},{8,9},{9,8},{10,11... | collective-permute-start | bytes 3145736 | tf_op jit(solution)/shard_map/ppermute | solution.py:209
  75.5 1.9 %collective-permute-done.1.woth_ref = bf16[512,768]{1,0:T(8,128)(2,1)S(1)} collective-permute-done((bf16[512,768]{1,0:T(8,128)(2,1)S(1)}, bf16[512,768]{1,0:T(8,128)(2,1)S(1)}, u32[]{:S(2)}, u32[]{:S(2)}) %collective-permute-start.1) | collective-permute-done | bytes 786464 | tf_op jit(solution)/shard_map/ppermute | solution.py:190
  77.4 0.1 shard_map.65.w_ref
  77.5 0.6 collective-permute-done.oth_ref
  78.2 2.6 %shard_map.66 = bf16[4,256,768]{2,1,0:T(8,128)(2,1)} custom-call(bf16[4,4,256,128]{3,2,1,0:T(8,128)(2,1)S(1)} %all-to-all-done.1.own_ref, bf16[4,4,256,128]{3,2,1,0:T(8,128)(2,1)S(1)} %collective-permute-done.oth_ref, bf16[1024,768]{1,0:T(8,128)(2,1)S(1)} %shard_map.65.w_ref), custom_call_target="tpu_custom_call" | custom-call | flops 1610612736 | bytes 6291456 | tf_op jit(solution)/shard_map/pallas_call | solution.py:31
  80.8 3.9 %all-to-all-start.2 = ((bf16[4,256,768]{2,1,0:T(8,128)(2,1)}), bf16[4,256,768]{2,1,0:T(8,128)(2,1)S(1)}, u32[]{:S(2)}, u32[]{:S(2)}) async-start(bf16[4,256,768]{2,1,0:T(8,128)(2,1)} %shard_map.66), calls=%async_computation.2 | async-start | bytes 3145728 | tf_op jit(solution)/shard_map/all_to_all | solution.py:223
  84.7 1.9 %collective-permute-start.2 = (f32[256]{0:T(256)S(1)}, f32[256]{0:T(256)S(1)}, u32[]{:S(2)}, u32[]{:S(2)}) collective-permute-start(f32[256]{0:T(256)S(1)} %multiply_reduce_fusion), channel_id=1, source_target_pairs={{0,1},{1,0},{2,3},{3,2},{4,5},{5,4},{6,7},{7,6},{8,9},{9,8},{10,11... | collective-permute-start | bytes 3080 | tf_op jit(solution)/shard_map/ppermute | solution.py:224
  87.3 0.5 collective-permute-done.2
  87.7 17.9 %all-to-all-done.2.p_ref = bf16[4,256,768]{2,1,0:T(8,128)(2,1)S(1)} async-done(((bf16[4,256,768]{2,1,0:T(8,128)(2,1)}), bf16[4,256,768]{2,1,0:T(8,128)(2,1)S(1)}, u32[]{:S(2)}, u32[]{:S(2)}) %all-to-all-start.2) | async-done | bytes 1572896 | tf_op jit(solution)/shard_map/all_to_all | solution.py:223
  105.6 1.9 %shard_map.67 = (bf16[256,512]{1,0:T(8,128)(2,1)S(1)}, bf16[256,512]{1,0:T(8,128)(2,1)S(1)}) custom-call(s32[4]{0:T(128)S(1)} %bitcast.13, s32[1]{0:T(128)S(6)} %copy.11.moved_ref, bf16[4,256,768]{2,1,0:T(8,128)(2,1)S(1)} %all-to-all-done.2.p_ref, f32[1,256]{1,0:T(1,128)S(1)} %bitcast.15, f32[1,256]{1,0:T(1,128)S(1)} %bitcast.16, ...), custom_call_target="tpu_custom_call" | custom-call | flops 134217728 | bytes 3145728 | tf_op jit(solution)/shard_map/pallas_call | solution.py:31
  107.6 2.5 %collective-permute-start.3 = (bf16[256,512]{1,0:T(8,128)(2,1)S(1)}, bf16[256,512]{1,0:T(8,128)(2,1)S(1)}, u32[]{:S(2)}, u32[]{:S(2)}) collective-permute-start(bf16[256,512]{1,0:T(8,128)(2,1)S(1)} %get-tuple-element.35), channel_id=1, source_target_pairs={{0,8},{8,16},{16,24},{24,32},{32,40},{40,48},{48,56},{56,64},{64,7... | collective-permute-start | bytes 786440 | tf_op jit(solution)/shard_map/ppermute | solution.py:233
  110.1 8.6 %collective-permute-done.3.prev_ref = bf16[256,512]{1,0:T(8,128)(2,1)S(1)} collective-permute-done((bf16[256,512]{1,0:T(8,128)(2,1)S(1)}, bf16[256,512]{1,0:T(8,128)(2,1)S(1)}, u32[]{:S(2)}, u32[]{:S(2)}) %collective-permute-start.3) | collective-permute-done | bytes 262176 | tf_op jit(solution)/shard_map/ppermute | solution.py:233
  118.7 1.7 %shard_map.68 = bf16[512,512]{1,0:T(8,128)(2,1)} custom-call(s32[4]{0:T(128)S(1)} %bitcast.14, s32[1]{0:T(128)S(6)} %copy.11.moved_ref, bf16[256,512]{1,0:T(8,128)(2,1)S(1)} %collective-permute-done.3.prev_ref, bf16[256,512]{1,0:T(8,128)(2,1)S(1)} %get-tuple-element.36.own_ref), custom_call_target="tpu_custom_call" | custom-call | flops 268435456 | bytes 1048576 | tf_op jit(solution)/shard_map/pallas_call | solution.py:31
  (2 shorter events, 0.0 us)
Async XLA Ops:
  3.0 7.4 %copy-start.1 = (bf16[32,768]{1,0:T(8,128)(2,1)S(1)}, bf16[32,768]{1,0:T(8,128)(2,1)}, u32[]{:S(2)}) copy-start(bf16[32,768]{1,0:T(8,128)(2,1)} %get-tuple-element.22) | copy-start | bytes 147460
  3.0 54.3 %all-to-all-start = ((bf16[4,4,256,128]{3,2,1,0:T(8,128)(2,1)}), bf16[4,4,256,128]{3,2,1,0:T(8,128)(2,1)S(1)}, u32[]{:S(2)}, u32[]{:S(2)}) async-start(bf16[4,4,256,128]{3,2,1,0:T(8,128)(2,1)} %get-tuple-element.21), calls=%async_computation | async-start | bytes 2097152 | tf_op jit(solution)/shard_map/all_to_all | solution.py:186
  58.3 7.7 %copy-start = (s32[1,4]{1,0:T(1,128)S(1)}, s32[1,4]{1,0:T(1,128)}, u32[]{:S(2)}) copy-start(s32[1,4]{1,0:T(1,128)} %param.7) | copy-start | bytes 52
  58.3 8.3 %copy-start.2 = (bf16[768]{0:T(1024)(128)(2,1)S(1)}, bf16[768]{0:T(1024)(128)(2,1)}, u32[]{:S(2)}) copy-start(bf16[768]{0:T(1024)(128)(2,1)} %param.11) | copy-start | bytes 4612
  58.3 15.3 %all-to-all-start.1 = ((bf16[4,4,256,128]{3,2,1,0:T(8,128)(2,1)}), bf16[4,4,256,128]{3,2,1,0:T(8,128)(2,1)S(1)}, u32[]{:S(2)}, u32[]{:S(2)}) async-start(bf16[4,4,256,128]{3,2,1,0:T(8,128)(2,1)} %bitcast.10), calls=%async_computation.1 | async-start | bytes 2097152 | tf_op jit(solution)/shard_map/all_to_all | solution.py:192
  62.7 14.7 %collective-permute-start.1 = (bf16[512,768]{1,0:T(8,128)(2,1)S(1)}, bf16[512,768]{1,0:T(8,128)(2,1)S(1)}, u32[]{:S(2)}, u32[]{:S(2)}) collective-permute-start(bf16[512,768]{1,0:T(8,128)(2,1)S(1)} %all_gather.3.wown_ref), channel_id=1, source_target_pairs={{0,32},{32,0},{1,33},{33,1},{2,34},{34,2},{3,35},{35,3},{4,36},{36... | collective-permute-start | bytes 2359304 | tf_op jit(solution)/shard_map/ppermute | solution.py:190
  73.6 4.5 %collective-permute-start = (bf16[4,4,256,128]{3,2,1,0:T(8,128)(2,1)S(1)}, bf16[4,4,256,128]{3,2,1,0:T(8,128)(2,1)S(1)}, u32[]{:S(2)}, u32[]{:S(2)}) collective-permute-start(bf16[4,4,256,128]{3,2,1,0:T(8,128)(2,1)S(1)} %all-to-all-done.1.own_ref), channel_id=1, source_target_pairs={{0,1},{1,0},{2,3},{3,2},{4,5},{5,4},{6,7},{7,6},{8,9},{9,8},{10,11... | collective-permute-start | bytes 3145736 | tf_op jit(solution)/shard_map/ppermute | solution.py:209
  80.8 24.8 %all-to-all-start.2 = ((bf16[4,256,768]{2,1,0:T(8,128)(2,1)}), bf16[4,256,768]{2,1,0:T(8,128)(2,1)S(1)}, u32[]{:S(2)}, u32[]{:S(2)}) async-start(bf16[4,256,768]{2,1,0:T(8,128)(2,1)} %shard_map.66), calls=%async_computation.2 | async-start | bytes 3145728 | tf_op jit(solution)/shard_map/all_to_all | solution.py:223
  84.7 3.0 %collective-permute-start.2 = (f32[256]{0:T(256)S(1)}, f32[256]{0:T(256)S(1)}, u32[]{:S(2)}, u32[]{:S(2)}) collective-permute-start(f32[256]{0:T(256)S(1)} %multiply_reduce_fusion), channel_id=1, source_target_pairs={{0,1},{1,0},{2,3},{3,2},{4,5},{5,4},{6,7},{7,6},{8,9},{9,8},{10,11... | collective-permute-start | bytes 3080 | tf_op jit(solution)/shard_map/ppermute | solution.py:224
  107.6 11.1 %collective-permute-start.3 = (bf16[256,512]{1,0:T(8,128)(2,1)S(1)}, bf16[256,512]{1,0:T(8,128)(2,1)S(1)}, u32[]{:S(2)}, u32[]{:S(2)}) collective-permute-start(bf16[256,512]{1,0:T(8,128)(2,1)S(1)} %get-tuple-element.35), channel_id=1, source_target_pairs={{0,8},{8,16},{16,24},{24,32},{32,40},{40,48},{48,56},{56,64},{64,7... | collective-permute-start | bytes 786440 | tf_op jit(solution)/shard_map/ppermute | solution.py:233

commit v11 on v9

--- a/solution.py
+++ b/solution.py
@@ -21,7 +21,6 @@
 HALF = 128
 SAMPLES = 4
 EXTRA = 16
-NEAR = (1, 3, 0)
 VMEM = 16 << 20
 
 
@@ -87,25 +86,18 @@
             w_ref[at + 64 : at + 128] = woth_ref[pl.ds(row, 64)]
 
 
-def first_kernel(x_at_ref, own_ref, oth_ref, w_ref, o_ref, x_ref):
-    x = x_at_ref[0]
-
-    def states(step):
-        g = (x + step) & 3
-        return jnp.concatenate([ref[g, yh] for ref in (own_ref, oth_ref) for yh in range(NYH)], axis=1)
-
-    o_ref[...] = jnp.dot(states(2), w_ref[...], preferred_element_type=jnp.float32).astype(jnp.bfloat16)
-    for n, step in enumerate(NEAR):
-        x_ref[n] = states(step)
-
-
-def second_kernel(x_ref, w_ref, o1_ref, o3_ref):
-    for n, ref in enumerate((o1_ref, o3_ref)):
-        ref[...] = jnp.dot(x_ref[n], w_ref[...], preferred_element_type=jnp.float32).astype(ref.dtype)
+def product_kernel(x_at_ref, own_ref, oth_ref, w_ref, o2_ref, o1_ref, o3_ref, x_ref):
+    for step, o_ref in ((2, o2_ref), (1, o1_ref), (3, o3_ref), (0, x_ref)):
+        g = (x_at_ref[0] + step) & 3
+        x = jnp.concatenate([ref[g, yh] for ref in (own_ref, oth_ref) for yh in range(NYH)], axis=1)
+        if step == 0:
+            o_ref[...] = x
+        else:
+            o_ref[...] = jnp.dot(x, w_ref[...], preferred_element_type=jnp.float32).astype(jnp.bfloat16)
 
 
 def own_kernel(x_ref, w_ref, o_ref):
-    o_ref[...] = jnp.dot(x_ref[2], w_ref[...], preferred_element_type=jnp.float32)
+    o_ref[...] = jnp.dot(x_ref[...], w_ref[...], preferred_element_type=jnp.float32)
 
 
 def tail_of(lens, moved):
@@ -225,22 +217,15 @@
     weights = call(
         arrange_kernel, bf(1024, columns), (c.reshape(1), wown, woth), 1, flops=20 * 10**9, nbytes=3 << 20
     )
-    far, near = call(
-        first_kernel,
-        (bf(ROWS, columns), bf(3, ROWS, 1024)),
+    far, right, left, near = call(
+        product_kernel,
+        (bf(ROWS, columns),) * 3 + (bf(ROWS, 1024),),
         (x.reshape(1), spread, other, weights),
         1,
-        flops=flops,
+        flops=3 * flops,
         nbytes=6 << 20,
     )
     far = whole(2, far)
-    right, left = call(
-        second_kernel,
-        (bf(ROWS, columns), bf(ROWS, columns)),
-        (near, weights),
-        flops=2 * flops,
-        nbytes=4 << 20,
-    )
     own = call(
         own_kernel, jax.ShapeDtypeStruct((ROWS, columns), jnp.float32), (near, weights), flops=flops, nbytes=3 << 20
     )

time: 118 us -> 119 us (level)
    ppermute x3, waiting for transfers between devices: 6.11 us -> 7.73 us  [local(): lax.ppermute(v, 'x', [(i, (i + step) % NX) for i in range(NX)])]
    pallas_call x7 -> x6, Pallas kernels: 9.02 us -> 8.72 us  [call(): pl.pallas_call(kernel, out_shape=out_shape, in_specs=[smem] * scalars + [...]
  transfers between devices with their start and end apart: 9 -> 9, of which waited for: 6 -> 7; matrix products, arithmetic and copies ran while one was open for 4% -> 4% of each run, Pallas kernels for 1% -> 1%
where the time goes in v11:
time: 119 us; the launch traced here: 118 us
  blocking collectives  46.9 us (39%)
  starting transfers between devices  32.9 us (28%)
  waiting for transfers between devices  23.1 us (19%)
  Pallas kernels  8.72 us (7%)
  other arithmetic  4.97 us (4%)
    all_gather x1, blocking collectives, local(): wown = lax.all_gather(scaled, 'z', axis=0, tiled=True)  46.9 us
    ppermute x3, starting transfers between devices, local(): lax.ppermute(v, 'x', [(i, (i + step) % NX) for i in range(NX)])  11.6 us
    ppermute x1, waiting for transfers between devices, local(): lax.ppermute(sent, DP, [(i, i + 1) for i in range(NZ * NYL * NX - 1)])  9.75 us
    pallas_call x6, Pallas kernels, call(): pl.pallas_call(kernel, out_shape=out_shape, in_specs=[smem] * scalars + [...  8.72 us
    ppermute x3, waiting for transfers between devices, local(): lax.ppermute(v, 'x', [(i, (i + step) % NX) for i in range(NX)])  7.73 us
    all_to_all x1, starting transfers between devices, local(): raw = lax.all_to_all(sent, 'yh', 0, 0, tiled=True)  7.34 us
    all_to_all x1, starting transfers between devices, local(): spread = lax.all_to_all(raw, 'x', 0, 0, tiled=True)  4.42 us
    ppermute x1, starting transfers between devices, local(): woth = lax.ppermute(wown, 'yl', [(0, 1), (1, 0)])  3.25 us
  transfers between devices with their start and end apart: 9, of which 7 were waited for; matrix products, arithmetic and copies ran while one was open for 4% of the time, Pallas kernels for 1%

profile of v11, /device:TPU:40, one launch (start us, length us, event | category | flops | bytes accessed | tf_op | source)
XLA Modules:
  0.0 118.5 jit_solution(12660643656592943258)
XLA Ops:
  0.0 3.0 %shard_map.64 = (bf16[4,4,256,128]{3,2,1,0:T(8,128)(2,1)}, bf16[32,768]{1,0:T(8,128)(2,1)}) custom-call(s32[1]{0:T(128)} %bitcast.yl_ref, s32[1]{0:T(128)} %bitcast.1.dp_ref, bf16[256,512]{1,0:T(8,128)(2,1)} %s_hbm.1, bf16[32,768]{1,0:T(8,128)(2,1)} %w_hbm.1, bf16[32,128]{1,0:T(8,128)(2,1)} %bitcast.18), custom_call_target="tpu_custom_call" | custom-call | flops 134217728 | bytes 1048576 | tf_op jit(solution)/shard_map/pallas_call | solution.py:31
  3.0 0.0 copy-start.1
  3.0 7.3 %all-to-all-start = ((bf16[4,4,256,128]{3,2,1,0:T(8,128)(2,1)}), bf16[4,4,256,128]{3,2,1,0:T(8,128)(2,1)S(1)}, u32[]{:S(2)}, u32[]{:S(2)}) async-start(bf16[4,4,256,128]{3,2,1,0:T(8,128)(2,1)} %get-tuple-element.25), calls=%async_computation | async-start | bytes 2097152 | tf_op jit(solution)/shard_map/all_to_all | solution.py:189
  10.3 0.0 copy-done.1
  10.3 46.9 %all_gather.3.wown_ref = bf16[512,768]{1,0:T(8,128)(2,1)S(1)} all-gather(bf16[32,768]{1,0:T(8,128)(2,1)S(1)} %copy-done.1), channel_id=1, replica_groups=mesh['z'=16,'yl'=2,'x'=4,'yh'=4,'c'=2] {'z'}, dimensions={0}, use_global_device_ids=true | all-gather | bytes 835584 | tf_op jit(solution)/shard_map/all_gather | solution.py:190
  57.2 0.0 all-to-all-done
  57.2 1.1 copy.10
  58.3 0.0 copy-start
  58.3 0.0 copy-start.2
  58.3 4.4 %all-to-all-start.1 = ((bf16[4,4,256,128]{3,2,1,0:T(8,128)(2,1)}), bf16[4,4,256,128]{3,2,1,0:T(8,128)(2,1)S(1)}, u32[]{:S(2)}, u32[]{:S(2)}) async-start(bf16[4,4,256,128]{3,2,1,0:T(8,128)(2,1)} %bitcast.11), calls=%async_computation.1 | async-start | bytes 2097152 | tf_op jit(solution)/shard_map/all_to_all | solution.py:195
  62.7 3.2 %collective-permute-start.1 = (bf16[512,768]{1,0:T(8,128)(2,1)S(1)}, bf16[512,768]{1,0:T(8,128)(2,1)S(1)}, u32[]{:S(2)}, u32[]{:S(2)}) collective-permute-start(bf16[512,768]{1,0:T(8,128)(2,1)S(1)} %all_gather.3.wown_ref), channel_id=1, source_target_pairs={{0,32},{32,0},{1,33},{33,1},{2,34},{34,2},{3,35},{35,3},{4,36},{36... | collective-permute-start | bytes 2359304 | tf_op jit(solution)/shard_map/ppermute | solution.py:193
  66.0 0.0 copy-done
  66.0 0.6 slice_reduce_fusion
  66.6 0.0 copy-done.2
  66.6 0.7 slice_reduce_fusion.1
  67.3 1.4 %fusion.2 = f32[256]{0:T(256)S(1)} fusion(s32[]{:T(128)S(1)} %bitcast.13, s32[]{:T(128)} %slice_reduce_fusion, s32[]{:T(128)} %slice_reduce_fusion.1), kind=kLoop, calls=%fused_computation.12 | loop fusion | flops 2048 | bytes 1036 | tf_op jit(solution)/shard_map/convert_element_type | solution.py:204
  68.7 0.5 fusion
  69.3 0.1 pad_maximum_fusion
  69.4 1.5 %multiply_reduce_fusion = f32[256]{0:T(256)S(1)} fusion(bf16[4,4,256,128]{3,2,1,0:T(8,128)(2,1)} %bitcast.11), kind=kLoop, calls=%fused_computation | loop fusion | flops 1572608 | bytes 1049600 | tf_op jit(solution)/shard_map/reduce_sum | solution.py:197
  70.9 2.7 %all-to-all-done.1.own_ref = bf16[4,4,256,128]{3,2,1,0:T(8,128)(2,1)S(1)} async-done(((bf16[4,4,256,128]{3,2,1,0:T(8,128)(2,1)}), bf16[4,4,256,128]{3,2,1,0:T(8,128)(2,1)S(1)}, u32[]{:S(2)}, u32[]{:S(2)}) %all-to-all-start.1) | async-done | bytes 1048608 | tf_op jit(solution)/shard_map/all_to_all | solution.py:195
  73.6 1.9 %collective-permute-start = (bf16[4,4,256,128]{3,2,1,0:T(8,128)(2,1)S(1)}, bf16[4,4,256,128]{3,2,1,0:T(8,128)(2,1)S(1)}, u32[]{:S(2)}, u32[]{:S(2)}) collective-permute-start(bf16[4,4,256,128]{3,2,1,0:T(8,128)(2,1)S(1)} %all-to-all-done.1.own_ref), channel_id=1, source_target_pairs={{0,1},{1,0},{2,3},{3,2},{4,5},{5,4},{6,7},{7,6},{8,9},{9,8},{10,11... | collective-permute-start | bytes 3145736 | tf_op jit(solution)/shard_map/ppermute | solution.py:212
  75.5 1.9 %collective-permute-done.1.woth_ref = bf16[512,768]{1,0:T(8,128)(2,1)S(1)} collective-permute-done((bf16[512,768]{1,0:T(8,128)(2,1)S(1)}, bf16[512,768]{1,0:T(8,128)(2,1)S(1)}, u32[]{:S(2)}, u32[]{:S(2)}) %collective-permute-start.1) | collective-permute-done | bytes 786464 | tf_op jit(solution)/shard_map/ppermute | solution.py:193
  77.4 0.1 shard_map.65.w_ref
  77.5 0.6 collective-permute-done.oth_ref
  78.2 1.5 %shard_map.66 = (bf16[256,768]{1,0:T(8,128)(2,1)S(1)}, bf16[256,768]{1,0:T(8,128)(2,1)S(1)}, bf16[256,768]{1,0:T(8,128)(2,1)S(1)}, bf16[256,1024]{1,0:T(8,128)(2,1)S(1)}) custom-call(s32[1]{0:T(128)} %bitcast.4.x_at_ref, bf16[4,4,256,128]{3,2,1,0:T(8,128)(2,1)S(1)} %all-to-all-done.1.own_ref, bf16[4,4,256,128]{3,2,1,0:T(8,128)(2,1)S(1)} %collective-permute-done.oth_ref, ...), custom_call_target="tpu_custom_call" | custom-call | flops 1207959552 | bytes 6291456 | tf_op jit(solution)/shard_map/pallas_call | solution.py:31
  79.7 4.5 %collective-permute-start.2 = (bf16[256,768]{1,0:T(8,128)(2,1)S(1)}, bf16[256,768]{1,0:T(8,128)(2,1)S(1)}, u32[]{:S(2)}, u32[]{:S(2)}) collective-permute-start(bf16[256,768]{1,0:T(8,128)(2,1)S(1)} %get-tuple-element.36), channel_id=1, source_target_pairs={{0,16},{8,24},{16,0},{24,8},{1,17},{9,25},{17,1},{25,9},{2,18},{10... | collective-permute-start | bytes 1179656 | tf_op jit(solution)/shard_map/ppermute | solution.py:215
  84.2 2.5 %collective-permute-start.3 = (bf16[256,768]{1,0:T(8,128)(2,1)S(1)}, bf16[256,768]{1,0:T(8,128)(2,1)S(1)}, u32[]{:S(2)}, u32[]{:S(2)}) collective-permute-start(bf16[256,768]{1,0:T(8,128)(2,1)S(1)} %get-tuple-element.37), channel_id=1, source_target_pairs={{0,8},{8,16},{16,24},{24,0},{1,9},{9,17},{17,25},{25,1},{2,10},{10... | collective-permute-start | bytes 1179656 | tf_op jit(solution)/shard_map/ppermute | solution.py:215
  86.7 4.6 %collective-permute-start.4 = (bf16[256,768]{1,0:T(8,128)(2,1)S(1)}, bf16[256,768]{1,0:T(8,128)(2,1)S(1)}, u32[]{:S(2)}, u32[]{:S(2)}) collective-permute-start(bf16[256,768]{1,0:T(8,128)(2,1)S(1)} %get-tuple-element.38), channel_id=1, source_target_pairs={{0,24},{8,0},{16,8},{24,16},{1,25},{9,1},{17,9},{25,17},{2,26},{10... | collective-permute-start | bytes 1179656 | tf_op jit(solution)/shard_map/ppermute | solution.py:215
  91.9 0.6 shard_map.67
  92.5 1.9 %collective-permute-start.5 = (f32[256]{0:T(256)S(1)}, f32[256]{0:T(256)S(1)}, u32[]{:S(2)}, u32[]{:S(2)}) collective-permute-start(f32[256]{0:T(256)S(1)} %multiply_reduce_fusion), channel_id=1, source_target_pairs={{0,1},{1,0},{2,3},{3,2},{4,5},{5,4},{6,7},{7,6},{8,9},{9,8},{10,11... | collective-permute-start | bytes 3080 | tf_op jit(solution)/shard_map/ppermute | solution.py:235
  94.4 0.6 collective-permute-done.2
  95.1 0.1 convert_add_fusion.p0_ref
  95.1 0.4 collective-permute-done.5
  95.5 7.1 %collective-permute-done.3.p1_ref = bf16[256,768]{1,0:T(8,128)(2,1)S(1)} collective-permute-done((bf16[256,768]{1,0:T(8,128)(2,1)S(1)}, bf16[256,768]{1,0:T(8,128)(2,1)S(1)}, u32[]{:S(2)}, u32[]{:S(2)}) %collective-permute-start.3) | collective-permute-done | bytes 393248 | tf_op jit(solution)/shard_map/ppermute | solution.py:215
  102.6 0.0 collective-permute-done.4.p2_ref
  102.6 1.9 %shard_map.68 = (bf16[256,512]{1,0:T(8,128)(2,1)S(1)}, bf16[256,512]{1,0:T(8,128)(2,1)S(1)}) custom-call(s32[4]{0:T(128)S(1)} %bitcast.14, s32[1]{0:T(128)S(6)} %copy.11.moved_ref, f32[256,768]{1,0:T(8,128)S(1)} %convert_add_fusion.p0_ref, bf16[256,768]{1,0:T(8,128)(2,1)S(1)} %collective-permute-done.3.p1_ref, ...), custom_call_target="tpu_custom_call" | custom-call | flops 134217728 | bytes 3145728 | tf_op jit(solution)/shard_map/pallas_call | solution.py:31
  104.6 2.5 %collective-permute-start.6 = (bf16[256,512]{1,0:T(8,128)(2,1)S(1)}, bf16[256,512]{1,0:T(8,128)(2,1)S(1)}, u32[]{:S(2)}, u32[]{:S(2)}) collective-permute-start(bf16[256,512]{1,0:T(8,128)(2,1)S(1)} %get-tuple-element.43), channel_id=1, source_target_pairs={{0,8},{8,16},{16,24},{24,32},{32,40},{40,48},{48,56},{56,64},{64,7... | collective-permute-start | bytes 786440 | tf_op jit(solution)/shard_map/ppermute | solution.py:244
  107.0 9.8 %collective-permute-done.6.prev_ref = bf16[256,512]{1,0:T(8,128)(2,1)S(1)} collective-permute-done((bf16[256,512]{1,0:T(8,128)(2,1)S(1)}, bf16[256,512]{1,0:T(8,128)(2,1)S(1)}, u32[]{:S(2)}, u32[]{:S(2)}) %collective-permute-start.6) | collective-permute-done | bytes 262176 | tf_op jit(solution)/shard_map/ppermute | solution.py:244
  116.8 1.7 %shard_map.69 = bf16[512,512]{1,0:T(8,128)(2,1)} custom-call(s32[4]{0:T(128)S(1)} %bitcast.15, s32[1]{0:T(128)S(6)} %copy.11.moved_ref, bf16[256,512]{1,0:T(8,128)(2,1)S(1)} %collective-permute-done.6.prev_ref, bf16[256,512]{1,0:T(8,128)(2,1)S(1)} %get-tuple-element.44.own_ref), custom_call_target="tpu_custom_call" | custom-call | flops 268435456 | bytes 1048576 | tf_op jit(solution)/shard_map/pallas_call | solution.py:31
  (2 shorter events, 0.0 us)
Async XLA Ops:
  3.0 7.4 %copy-start.1 = (bf16[32,768]{1,0:T(8,128)(2,1)S(1)}, bf16[32,768]{1,0:T(8,128)(2,1)}, u32[]{:S(2)}) copy-start(bf16[32,768]{1,0:T(8,128)(2,1)} %get-tuple-element.26) | copy-start | bytes 147460
  3.0 54.3 %all-to-all-start = ((bf16[4,4,256,128]{3,2,1,0:T(8,128)(2,1)}), bf16[4,4,256,128]{3,2,1,0:T(8,128)(2,1)S(1)}, u32[]{:S(2)}, u32[]{:S(2)}) async-start(bf16[4,4,256,128]{3,2,1,0:T(8,128)(2,1)} %get-tuple-element.25), calls=%async_computation | async-start | bytes 2097152 | tf_op jit(solution)/shard_map/all_to_all | solution.py:189
  58.3 7.7 %copy-start = (s32[1,4]{1,0:T(1,128)S(1)}, s32[1,4]{1,0:T(1,128)}, u32[]{:S(2)}) copy-start(s32[1,4]{1,0:T(1,128)} %param.7) | copy-start | bytes 52
  58.3 8.3 %copy-start.2 = (bf16[768]{0:T(1024)(128)(2,1)S(1)}, bf16[768]{0:T(1024)(128)(2,1)}, u32[]{:S(2)}) copy-start(bf16[768]{0:T(1024)(128)(2,1)} %param.11) | copy-start | bytes 4612
  58.3 15.3 %all-to-all-start.1 = ((bf16[4,4,256,128]{3,2,1,0:T(8,128)(2,1)}), bf16[4,4,256,128]{3,2,1,0:T(8,128)(2,1)S(1)}, u32[]{:S(2)}, u32[]{:S(2)}) async-start(bf16[4,4,256,128]{3,2,1,0:T(8,128)(2,1)} %bitcast.11), calls=%async_computation.1 | async-start | bytes 2097152 | tf_op jit(solution)/shard_map/all_to_all | solution.py:195
  62.7 14.7 %collective-permute-start.1 = (bf16[512,768]{1,0:T(8,128)(2,1)S(1)}, bf16[512,768]{1,0:T(8,128)(2,1)S(1)}, u32[]{:S(2)}, u32[]{:S(2)}) collective-permute-start(bf16[512,768]{1,0:T(8,128)(2,1)S(1)} %all_gather.3.wown_ref), channel_id=1, source_target_pairs={{0,32},{32,0},{1,33},{33,1},{2,34},{34,2},{3,35},{35,3},{4,36},{36... | collective-permute-start | bytes 2359304 | tf_op jit(solution)/shard_map/ppermute | solution.py:193
  73.6 4.5 %collective-permute-start = (bf16[4,4,256,128]{3,2,1,0:T(8,128)(2,1)S(1)}, bf16[4,4,256,128]{3,2,1,0:T(8,128)(2,1)S(1)}, u32[]{:S(2)}, u32[]{:S(2)}) collective-permute-start(bf16[4,4,256,128]{3,2,1,0:T(8,128)(2,1)S(1)} %all-to-all-done.1.own_ref), channel_id=1, source_target_pairs={{0,1},{1,0},{2,3},{3,2},{4,5},{5,4},{6,7},{7,6},{8,9},{9,8},{10,11... | collective-permute-start | bytes 3145736 | tf_op jit(solution)/shard_map/ppermute | solution.py:212
  79.7 15.4 %collective-permute-start.2 = (bf16[256,768]{1,0:T(8,128)(2,1)S(1)}, bf16[256,768]{1,0:T(8,128)(2,1)S(1)}, u32[]{:S(2)}, u32[]{:S(2)}) collective-permute-start(bf16[256,768]{1,0:T(8,128)(2,1)S(1)} %get-tuple-element.36), channel_id=1, source_target_pairs={{0,16},{8,24},{16,0},{24,8},{1,17},{9,25},{17,1},{25,9},{2,18},{10... | collective-permute-start | bytes 1179656 | tf_op jit(solution)/shard_map/ppermute | solution.py:215
  84.2 18.4 %collective-permute-start.3 = (bf16[256,768]{1,0:T(8,128)(2,1)S(1)}, bf16[256,768]{1,0:T(8,128)(2,1)S(1)}, u32[]{:S(2)}, u32[]{:S(2)}) collective-permute-start(bf16[256,768]{1,0:T(8,128)(2,1)S(1)} %get-tuple-element.37), channel_id=1, source_target_pairs={{0,8},{8,16},{16,24},{24,0},{1,9},{9,17},{17,25},{25,1},{2,10},{10... | collective-permute-start | bytes 1179656 | tf_op jit(solution)/shard_map/ppermute | solution.py:215
  86.7 16.0 %collective-permute-start.4 = (bf16[256,768]{1,0:T(8,128)(2,1)S(1)}, bf16[256,768]{1,0:T(8,128)(2,1)S(1)}, u32[]{:S(2)}, u32[]{:S(2)}) collective-permute-start(bf16[256,768]{1,0:T(8,128)(2,1)S(1)} %get-tuple-element.38), channel_id=1, source_target_pairs={{0,24},{8,0},{16,8},{24,16},{1,25},{9,1},{17,9},{25,17},{2,26},{10... | collective-permute-start | bytes 1179656 | tf_op jit(solution)/shard_map/ppermute | solution.py:215
  92.5 3.0 %collective-permute-start.5 = (f32[256]{0:T(256)S(1)}, f32[256]{0:T(256)S(1)}, u32[]{:S(2)}, u32[]{:S(2)}) collective-permute-start(f32[256]{0:T(256)S(1)} %multiply_reduce_fusion), channel_id=1, source_target_pairs={{0,1},{1,0},{2,3},{3,2},{4,5},{5,4},{6,7},{7,6},{8,9},{9,8},{10,11... | collective-permute-start | bytes 3080 | tf_op jit(solution)/shard_map/ppermute | solution.py:235
  104.6 12.2 %collective-permute-start.6 = (bf16[256,512]{1,0:T(8,128)(2,1)S(1)}, bf16[256,512]{1,0:T(8,128)(2,1)S(1)}, u32[]{:S(2)}, u32[]{:S(2)}) collective-permute-start(bf16[256,512]{1,0:T(8,128)(2,1)S(1)} %get-tuple-element.43), channel_id=1, source_target_pairs={{0,8},{8,16},{16,24},{24,32},{32,40},{40,48},{48,56},{56,64},{64,7... | collective-permute-start | bytes 786440 | tf_op jit(solution)/shard_map/ppermute | solution.py:244

commit v12 on v9

--- a/solution.py
+++ b/solution.py
@@ -21,7 +21,7 @@
 HALF = 128
 SAMPLES = 4
 EXTRA = 16
-NEAR = (1, 3, 0)
+NEAR = (3, 2, 0)
 VMEM = 16 << 20
 
 
@@ -94,7 +94,7 @@
         g = (x + step) & 3
         return jnp.concatenate([ref[g, yh] for ref in (own_ref, oth_ref) for yh in range(NYH)], axis=1)
 
-    o_ref[...] = jnp.dot(states(2), w_ref[...], preferred_element_type=jnp.float32).astype(jnp.bfloat16)
+    o_ref[...] = jnp.dot(states(1), w_ref[...], preferred_element_type=jnp.float32).astype(jnp.bfloat16)
     for n, step in enumerate(NEAR):
         x_ref[n] = states(step)
 
@@ -225,7 +225,7 @@
     weights = call(
         arrange_kernel, bf(1024, columns), (c.reshape(1), wown, woth), 1, flops=20 * 10**9, nbytes=3 << 20
     )
-    far, near = call(
+    right, near = call(
         first_kernel,
         (bf(ROWS, columns), bf(3, ROWS, 1024)),
         (x.reshape(1), spread, other, weights),
@@ -233,8 +233,8 @@
         flops=flops,
         nbytes=6 << 20,
     )
-    far = whole(2, far)
-    right, left = call(
+    right = whole(1, right)
+    left, far = call(
         second_kernel,
         (bf(ROWS, columns), bf(ROWS, columns)),
         (near, weights),
@@ -244,14 +244,14 @@
     own = call(
         own_kernel, jax.ShapeDtypeStruct((ROWS, columns), jnp.float32), (near, weights), flops=flops, nbytes=3 << 20
     )
-    right, left = whole(1, right), whole(3, left)
+    left, far = whole(3, left), whole(2, far)
     own, squares = lax.optimization_barrier((own, squares))
-    own = own + far.astype(jnp.float32)
+    own = own + right.astype(jnp.float32)
     squares2 = lax.ppermute(squares, "c", [(0, 1), (1, 0)])
     context, sent = call(
         attend_kernel,
         (bf(ROWS, PER * HEAD), bf(ROWS, PER * HEAD)),
-        (lens, moved, own, right, left, squares.reshape(1, ROWS), squares2.reshape(1, ROWS), bias, cos, sin),
+        (lens, moved, own, left, far, squares.reshape(1, ROWS), squares2.reshape(1, ROWS), bias, cos, sin),
         2,
         flops=4 * 4 * ROWS * ROWS * HEAD,
         nbytes=3 << 20,

time: 118 us -> 119 us (level)
    ppermute x3, waiting for transfers between devices: 6.11 us -> 10.3 us  [local(): lax.ppermute(v, 'x', [(i, (i + step) % NX) for i in range(NX)])]
    ppermute x1, waiting for transfers between devices: 9.75 us -> 7.21 us  [local(): lax.ppermute(sent, DP, [(i, i + 1) for i in range(NZ * NYL * NX - 1)])]
    ppermute x3, starting transfers between devices: 11.6 us -> 10.4 us  [local(): lax.ppermute(v, 'x', [(i, (i + step) % NX) for i in range(NX)])]
where the time goes in v12:
time: 119 us; the launch traced here: 118 us
  blocking collectives  46.9 us (39%)
  starting transfers between devices  32.7 us (27%)
  waiting for transfers between devices  22.9 us (19%)
  Pallas kernels  9.02 us (8%)
  other arithmetic  4.77 us (4%)
    all_gather x1, blocking collectives, local(): wown = lax.all_gather(scaled, 'z', axis=0, tiled=True)  46.9 us
    ppermute x3, starting transfers between devices, local(): lax.ppermute(v, 'x', [(i, (i + step) % NX) for i in range(NX)])  10.4 us
    ppermute x3, waiting for transfers between devices, local(): lax.ppermute(v, 'x', [(i, (i + step) % NX) for i in range(NX)])  10.3 us
    pallas_call x7, Pallas kernels, call(): pl.pallas_call(kernel, out_shape=out_shape, in_specs=[smem] * scalars + [...  9.02 us
    all_to_all x1, starting transfers between devices, local(): raw = lax.all_to_all(sent, 'yh', 0, 0, tiled=True)  7.34 us
    ppermute x1, waiting for transfers between devices, local(): lax.ppermute(sent, DP, [(i, i + 1) for i in range(NZ * NYL * NX - 1)])  7.21 us
    all_to_all x1, starting transfers between devices, local(): spread = lax.all_to_all(raw, 'x', 0, 0, tiled=True)  4.42 us
    ppermute x1, starting transfers between devices, local(): lax.ppermute(sent, DP, [(i, i + 1) for i in range(NZ * NYL * NX - 1)])  3.48 us
  transfers between devices with their start and end apart: 9, of which 6 were waited for; matrix products, arithmetic and copies ran while one was open for 4% of the time, Pallas kernels for 1%

profile of v12, /device:TPU:40, one launch (start us, length us, event | category | flops | bytes accessed | tf_op | source)
XLA Modules:
  0.0 118.2 jit_solution(16560336784607084100)
XLA Ops:
  0.0 3.0 %shard_map.64 = (bf16[4,4,256,128]{3,2,1,0:T(8,128)(2,1)}, bf16[32,768]{1,0:T(8,128)(2,1)}) custom-call(s32[1]{0:T(128)} %bitcast.yl_ref, s32[1]{0:T(128)} %bitcast.1.dp_ref, bf16[256,512]{1,0:T(8,128)(2,1)} %s_hbm.1, bf16[32,768]{1,0:T(8,128)(2,1)} %w_hbm.1, bf16[32,128]{1,0:T(8,128)(2,1)} %bitcast.18), custom_call_target="tpu_custom_call" | custom-call | flops 134217728 | bytes 1048576 | tf_op jit(solution)/shard_map/pallas_call | solution.py:32
  3.0 0.0 copy-start.1
  3.0 7.3 %all-to-all-start = ((bf16[4,4,256,128]{3,2,1,0:T(8,128)(2,1)}), bf16[4,4,256,128]{3,2,1,0:T(8,128)(2,1)S(1)}, u32[]{:S(2)}, u32[]{:S(2)}) async-start(bf16[4,4,256,128]{3,2,1,0:T(8,128)(2,1)} %get-tuple-element.25), calls=%async_computation | async-start | bytes 2097152 | tf_op jit(solution)/shard_map/all_to_all | solution.py:197
  10.3 0.0 copy-done.1
  10.3 46.9 %all_gather.3.wown_ref = bf16[512,768]{1,0:T(8,128)(2,1)S(1)} all-gather(bf16[32,768]{1,0:T(8,128)(2,1)S(1)} %copy-done.1), channel_id=1, replica_groups=mesh['z'=16,'yl'=2,'x'=4,'yh'=4,'c'=2] {'z'}, dimensions={0}, use_global_device_ids=true | all-gather | bytes 835584 | tf_op jit(solution)/shard_map/all_gather | solution.py:198
  57.2 0.0 all-to-all-done
  57.2 1.0 copy.10
  58.3 0.0 copy-start
  58.3 0.0 copy-start.2
  58.3 4.4 %all-to-all-start.1 = ((bf16[4,4,256,128]{3,2,1,0:T(8,128)(2,1)}), bf16[4,4,256,128]{3,2,1,0:T(8,128)(2,1)S(1)}, u32[]{:S(2)}, u32[]{:S(2)}) async-start(bf16[4,4,256,128]{3,2,1,0:T(8,128)(2,1)} %bitcast.11), calls=%async_computation.1 | async-start | bytes 2097152 | tf_op jit(solution)/shard_map/all_to_all | solution.py:203
  62.7 3.2 %collective-permute-start.1 = (bf16[512,768]{1,0:T(8,128)(2,1)S(1)}, bf16[512,768]{1,0:T(8,128)(2,1)S(1)}, u32[]{:S(2)}, u32[]{:S(2)}) collective-permute-start(bf16[512,768]{1,0:T(8,128)(2,1)S(1)} %all_gather.3.wown_ref), channel_id=1, source_target_pairs={{0,32},{32,0},{1,33},{33,1},{2,34},{34,2},{3,35},{35,3},{4,36},{36... | collective-permute-start | bytes 2359304 | tf_op jit(solution)/shard_map/ppermute | solution.py:201
  66.0 0.0 copy-done
  66.0 0.6 slice_reduce_fusion
  66.6 0.0 copy-done.2
  66.6 0.6 slice_reduce_fusion.1
  67.2 1.3 %fusion.2 = f32[256]{0:T(256)S(1)} fusion(s32[]{:T(128)S(1)} %bitcast.13, s32[]{:T(128)} %slice_reduce_fusion, s32[]{:T(128)} %slice_reduce_fusion.1), kind=kLoop, calls=%fused_computation.12 | loop fusion | flops 2048 | bytes 1036 | tf_op jit(solution)/shard_map/convert_element_type | solution.py:212
  68.5 0.5 fusion
  69.0 0.1 pad_maximum_fusion
  69.2 1.5 %multiply_reduce_fusion = f32[256]{0:T(256)S(1)} fusion(bf16[4,4,256,128]{3,2,1,0:T(8,128)(2,1)} %bitcast.11), kind=kLoop, calls=%fused_computation | loop fusion | flops 1572608 | bytes 1049600 | tf_op jit(solution)/shard_map/reduce_sum | solution.py:205
  70.7 2.9 %all-to-all-done.1.own_ref = bf16[4,4,256,128]{3,2,1,0:T(8,128)(2,1)S(1)} async-done(((bf16[4,4,256,128]{3,2,1,0:T(8,128)(2,1)}), bf16[4,4,256,128]{3,2,1,0:T(8,128)(2,1)S(1)}, u32[]{:S(2)}, u32[]{:S(2)}) %all-to-all-start.1) | async-done | bytes 1048608 | tf_op jit(solution)/shard_map/all_to_all | solution.py:203
  73.6 1.9 %collective-permute-start = (bf16[4,4,256,128]{3,2,1,0:T(8,128)(2,1)S(1)}, bf16[4,4,256,128]{3,2,1,0:T(8,128)(2,1)S(1)}, u32[]{:S(2)}, u32[]{:S(2)}) collective-permute-start(bf16[4,4,256,128]{3,2,1,0:T(8,128)(2,1)S(1)} %all-to-all-done.1.own_ref), channel_id=1, source_target_pairs={{0,1},{1,0},{2,3},{3,2},{4,5},{5,4},{6,7},{7,6},{8,9},{9,8},{10,11... | collective-permute-start | bytes 3145736 | tf_op jit(solution)/shard_map/ppermute | solution.py:220
  75.5 1.9 %collective-permute-done.1.woth_ref = bf16[512,768]{1,0:T(8,128)(2,1)S(1)} collective-permute-done((bf16[512,768]{1,0:T(8,128)(2,1)S(1)}, bf16[512,768]{1,0:T(8,128)(2,1)S(1)}, u32[]{:S(2)}, u32[]{:S(2)}) %collective-permute-start.1) | collective-permute-done | bytes 786464 | tf_op jit(solution)/shard_map/ppermute | solution.py:201
  77.4 0.1 shard_map.65.w_ref
  77.5 0.6 collective-permute-done.oth_ref
  78.2 0.8 shard_map.66
  79.0 3.0 %collective-permute-start.2 = (bf16[256,768]{1,0:T(8,128)(2,1)S(1)}, bf16[256,768]{1,0:T(8,128)(2,1)S(1)}, u32[]{:S(2)}, u32[]{:S(2)}) collective-permute-start(bf16[256,768]{1,0:T(8,128)(2,1)S(1)} %get-tuple-element.36), channel_id=1, source_target_pairs={{0,8},{8,16},{16,24},{24,0},{1,9},{9,17},{17,25},{25,1},{2,10},{10... | collective-permute-start | bytes 1179656 | tf_op jit(solution)/shard_map/ppermute | solution.py:223
  82.0 1.0 shard_map.68
  83.0 4.0 %collective-permute-start.3 = (bf16[256,768]{1,0:T(8,128)(2,1)S(1)}, bf16[256,768]{1,0:T(8,128)(2,1)S(1)}, u32[]{:S(2)}, u32[]{:S(2)}) collective-permute-start(bf16[256,768]{1,0:T(8,128)(2,1)S(1)} %get-tuple-element.37), channel_id=1, source_target_pairs={{0,24},{8,0},{16,8},{24,16},{1,25},{9,1},{17,9},{25,17},{2,26},{10... | collective-permute-start | bytes 1179656 | tf_op jit(solution)/shard_map/ppermute | solution.py:223
  87.0 3.3 %collective-permute-start.4 = (bf16[256,768]{1,0:T(8,128)(2,1)S(1)}, bf16[256,768]{1,0:T(8,128)(2,1)S(1)}, u32[]{:S(2)}, u32[]{:S(2)}) collective-permute-start(bf16[256,768]{1,0:T(8,128)(2,1)S(1)} %get-tuple-element.38), channel_id=1, source_target_pairs={{0,16},{8,24},{16,0},{24,8},{1,17},{9,25},{17,1},{25,9},{2,18},{10... | collective-permute-start | bytes 1179656 | tf_op jit(solution)/shard_map/ppermute | solution.py:223
  91.0 0.6 shard_map.67
  91.6 1.9 %collective-permute-start.5 = (f32[256]{0:T(256)S(1)}, f32[256]{0:T(256)S(1)}, u32[]{:S(2)}, u32[]{:S(2)}) collective-permute-start(f32[256]{0:T(256)S(1)} %multiply_reduce_fusion), channel_id=1, source_target_pairs={{0,1},{1,0},{2,3},{3,2},{4,5},{5,4},{6,7},{7,6},{8,9},{9,8},{10,11... | collective-permute-start | bytes 3080 | tf_op jit(solution)/shard_map/ppermute | solution.py:250
  93.5 8.1 %collective-permute-done.2 = bf16[256,768]{1,0:T(8,128)(2,1)S(1)} collective-permute-done((bf16[256,768]{1,0:T(8,128)(2,1)S(1)}, bf16[256,768]{1,0:T(8,128)(2,1)S(1)}, u32[]{:S(2)}, u32[]{:S(2)}) %collective-permute-start.2) | collective-permute-done | bytes 393248 | tf_op jit(solution)/shard_map/ppermute | solution.py:223
  101.7 0.1 convert_add_fusion.p0_ref
  101.7 0.0 collective-permute-done.5
  101.7 2.1 %collective-permute-done.3.p1_ref = bf16[256,768]{1,0:T(8,128)(2,1)S(1)} collective-permute-done((bf16[256,768]{1,0:T(8,128)(2,1)S(1)}, bf16[256,768]{1,0:T(8,128)(2,1)S(1)}, u32[]{:S(2)}, u32[]{:S(2)}) %collective-permute-start.3) | collective-permute-done | bytes 393248 | tf_op jit(solution)/shard_map/ppermute | solution.py:223
  103.9 0.0 collective-permute-done.4.p2_ref
  103.9 1.9 %shard_map.69 = (bf16[256,512]{1,0:T(8,128)(2,1)S(1)}, bf16[256,512]{1,0:T(8,128)(2,1)S(1)}) custom-call(s32[4]{0:T(128)S(1)} %bitcast.14, s32[1]{0:T(128)S(6)} %copy.11.moved_ref, f32[256,768]{1,0:T(8,128)S(1)} %convert_add_fusion.p0_ref, bf16[256,768]{1,0:T(8,128)(2,1)S(1)} %collective-permute-done.3.p1_ref, ...), custom_call_target="tpu_custom_call" | custom-call | flops 134217728 | bytes 3145728 | tf_op jit(solution)/shard_map/pallas_call | solution.py:32
  105.8 3.5 %collective-permute-start.6 = (bf16[256,512]{1,0:T(8,128)(2,1)S(1)}, bf16[256,512]{1,0:T(8,128)(2,1)S(1)}, u32[]{:S(2)}, u32[]{:S(2)}) collective-permute-start(bf16[256,512]{1,0:T(8,128)(2,1)S(1)} %get-tuple-element.43), channel_id=1, source_target_pairs={{0,8},{8,16},{16,24},{24,32},{32,40},{40,48},{48,56},{56,64},{64,7... | collective-permute-start | bytes 786440 | tf_op jit(solution)/shard_map/ppermute | solution.py:259
  109.3 7.2 %collective-permute-done.6.prev_ref = bf16[256,512]{1,0:T(8,128)(2,1)S(1)} collective-permute-done((bf16[256,512]{1,0:T(8,128)(2,1)S(1)}, bf16[256,512]{1,0:T(8,128)(2,1)S(1)}, u32[]{:S(2)}, u32[]{:S(2)}) %collective-permute-start.6) | collective-permute-done | bytes 262176 | tf_op jit(solution)/shard_map/ppermute | solution.py:259
  116.5 1.7 %shard_map.70 = bf16[512,512]{1,0:T(8,128)(2,1)} custom-call(s32[4]{0:T(128)S(1)} %bitcast.15, s32[1]{0:T(128)S(6)} %copy.11.moved_ref, bf16[256,512]{1,0:T(8,128)(2,1)S(1)} %collective-permute-done.6.prev_ref, bf16[256,512]{1,0:T(8,128)(2,1)S(1)} %get-tuple-element.44.own_ref), custom_call_target="tpu_custom_call" | custom-call | flops 268435456 | bytes 1048576 | tf_op jit(solution)/shard_map/pallas_call | solution.py:32
  (2 shorter events, 0.0 us)
Async XLA Ops:
  3.0 7.4 %copy-start.1 = (bf16[32,768]{1,0:T(8,128)(2,1)S(1)}, bf16[32,768]{1,0:T(8,128)(2,1)}, u32[]{:S(2)}) copy-start(bf16[32,768]{1,0:T(8,128)(2,1)} %get-tuple-element.26) | copy-start | bytes 147460
  3.0 54.3 %all-to-all-start = ((bf16[4,4,256,128]{3,2,1,0:T(8,128)(2,1)}), bf16[4,4,256,128]{3,2,1,0:T(8,128)(2,1)S(1)}, u32[]{:S(2)}, u32[]{:S(2)}) async-start(bf16[4,4,256,128]{3,2,1,0:T(8,128)(2,1)} %get-tuple-element.25), calls=%async_computation | async-start | bytes 2097152 | tf_op jit(solution)/shard_map/all_to_all | solution.py:197
  58.3 7.7 %copy-start = (s32[1,4]{1,0:T(1,128)S(1)}, s32[1,4]{1,0:T(1,128)}, u32[]{:S(2)}) copy-start(s32[1,4]{1,0:T(1,128)} %param.7) | copy-start | bytes 52
  58.3 8.3 %copy-start.2 = (bf16[768]{0:T(1024)(128)(2,1)S(1)}, bf16[768]{0:T(1024)(128)(2,1)}, u32[]{:S(2)}) copy-start(bf16[768]{0:T(1024)(128)(2,1)} %param.11) | copy-start | bytes 4612
  58.3 15.3 %all-to-all-start.1 = ((bf16[4,4,256,128]{3,2,1,0:T(8,128)(2,1)}), bf16[4,4,256,128]{3,2,1,0:T(8,128)(2,1)S(1)}, u32[]{:S(2)}, u32[]{:S(2)}) async-start(bf16[4,4,256,128]{3,2,1,0:T(8,128)(2,1)} %bitcast.11), calls=%async_computation.1 | async-start | bytes 2097152 | tf_op jit(solution)/shard_map/all_to_all | solution.py:203
  62.7 14.7 %collective-permute-start.1 = (bf16[512,768]{1,0:T(8,128)(2,1)S(1)}, bf16[512,768]{1,0:T(8,128)(2,1)S(1)}, u32[]{:S(2)}, u32[]{:S(2)}) collective-permute-start(bf16[512,768]{1,0:T(8,128)(2,1)S(1)} %all_gather.3.wown_ref), channel_id=1, source_target_pairs={{0,32},{32,0},{1,33},{33,1},{2,34},{34,2},{3,35},{35,3},{4,36},{36... | collective-permute-start | bytes 2359304 | tf_op jit(solution)/shard_map/ppermute | solution.py:201
  73.6 4.5 %collective-permute-start = (bf16[4,4,256,128]{3,2,1,0:T(8,128)(2,1)S(1)}, bf16[4,4,256,128]{3,2,1,0:T(8,128)(2,1)S(1)}, u32[]{:S(2)}, u32[]{:S(2)}) collective-permute-start(bf16[4,4,256,128]{3,2,1,0:T(8,128)(2,1)S(1)} %all-to-all-done.1.own_ref), channel_id=1, source_target_pairs={{0,1},{1,0},{2,3},{3,2},{4,5},{5,4},{6,7},{7,6},{8,9},{9,8},{10,11... | collective-permute-start | bytes 3145736 | tf_op jit(solution)/shard_map/ppermute | solution.py:220
  79.0 22.7 %collective-permute-start.2 = (bf16[256,768]{1,0:T(8,128)(2,1)S(1)}, bf16[256,768]{1,0:T(8,128)(2,1)S(1)}, u32[]{:S(2)}, u32[]{:S(2)}) collective-permute-start(bf16[256,768]{1,0:T(8,128)(2,1)S(1)} %get-tuple-element.36), channel_id=1, source_target_pairs={{0,8},{8,16},{16,24},{24,0},{1,9},{9,17},{17,25},{25,1},{2,10},{10... | collective-permute-start | bytes 1179656 | tf_op jit(solution)/shard_map/ppermute | solution.py:223
  83.0 20.9 %collective-permute-start.3 = (bf16[256,768]{1,0:T(8,128)(2,1)S(1)}, bf16[256,768]{1,0:T(8,128)(2,1)S(1)}, u32[]{:S(2)}, u32[]{:S(2)}) collective-permute-start(bf16[256,768]{1,0:T(8,128)(2,1)S(1)} %get-tuple-element.37), channel_id=1, source_target_pairs={{0,24},{8,0},{16,8},{24,16},{1,25},{9,1},{17,9},{25,17},{2,26},{10... | collective-permute-start | bytes 1179656 | tf_op jit(solution)/shard_map/ppermute | solution.py:223
  87.0 16.8 %collective-permute-start.4 = (bf16[256,768]{1,0:T(8,128)(2,1)S(1)}, bf16[256,768]{1,0:T(8,128)(2,1)S(1)}, u32[]{:S(2)}, u32[]{:S(2)}) collective-permute-start(bf16[256,768]{1,0:T(8,128)(2,1)S(1)} %get-tuple-element.38), channel_id=1, source_target_pairs={{0,16},{8,24},{16,0},{24,8},{1,17},{9,25},{17,1},{25,9},{2,18},{10... | collective-permute-start | bytes 1179656 | tf_op jit(solution)/shard_map/ppermute | solution.py:223
  91.6 10.1 %collective-permute-start.5 = (f32[256]{0:T(256)S(1)}, f32[256]{0:T(256)S(1)}, u32[]{:S(2)}, u32[]{:S(2)}) collective-permute-start(f32[256]{0:T(256)S(1)} %multiply_reduce_fusion), channel_id=1, source_target_pairs={{0,1},{1,0},{2,3},{3,2},{4,5},{5,4},{6,7},{7,6},{8,9},{9,8},{10,11... | collective-permute-start | bytes 3080 | tf_op jit(solution)/shard_map/ppermute | solution.py:250
  105.8 10.7 %collective-permute-start.6 = (bf16[256,512]{1,0:T(8,128)(2,1)S(1)}, bf16[256,512]{1,0:T(8,128)(2,1)S(1)}, u32[]{:S(2)}, u32[]{:S(2)}) collective-permute-start(bf16[256,512]{1,0:T(8,128)(2,1)S(1)} %get-tuple-element.43), channel_id=1, source_target_pairs={{0,8},{8,16},{16,24},{24,32},{32,40},{40,48},{48,56},{56,64},{64,7... | collective-permute-start | bytes 786440 | tf_op jit(solution)/shard_map/ppermute | solution.py:259

commit v13 on v11

--- a/solution.py
+++ b/solution.py
@@ -1,3 +1,5 @@
+import functools
+
 import jax
 import jax.numpy as jnp
 from jax import lax
@@ -86,18 +88,11 @@
             w_ref[at + 64 : at + 128] = woth_ref[pl.ds(row, 64)]
 
 
-def product_kernel(x_at_ref, own_ref, oth_ref, w_ref, o2_ref, o1_ref, o3_ref, x_ref):
-    for step, o_ref in ((2, o2_ref), (1, o1_ref), (3, o3_ref), (0, x_ref)):
+def product_kernel(steps, x_at_ref, own_ref, oth_ref, w_ref, *o_refs):
+    for step, o_ref in zip(steps, o_refs):
         g = (x_at_ref[0] + step) & 3
         x = jnp.concatenate([ref[g, yh] for ref in (own_ref, oth_ref) for yh in range(NYH)], axis=1)
-        if step == 0:
-            o_ref[...] = x
-        else:
-            o_ref[...] = jnp.dot(x, w_ref[...], preferred_element_type=jnp.float32).astype(jnp.bfloat16)
-
-
-def own_kernel(x_ref, w_ref, o_ref):
-    o_ref[...] = jnp.dot(x_ref[...], w_ref[...], preferred_element_type=jnp.float32)
+        o_ref[...] = jnp.dot(x, w_ref[...], preferred_element_type=jnp.float32).astype(o_ref.dtype)
 
 
 def tail_of(lens, moved):
@@ -217,18 +212,21 @@
     weights = call(
         arrange_kernel, bf(1024, columns), (c.reshape(1), wown, woth), 1, flops=20 * 10**9, nbytes=3 << 20
     )
-    far, right, left, near = call(
-        product_kernel,
-        (bf(ROWS, columns),) * 3 + (bf(ROWS, 1024),),
-        (x.reshape(1), spread, other, weights),
-        1,
-        flops=3 * flops,
-        nbytes=6 << 20,
-    )
+
+    def products(dtype, *steps):
+        return call(
+            functools.partial(product_kernel, steps),
+            (jax.ShapeDtypeStruct((ROWS, columns), dtype),) * len(steps),
+            (x.reshape(1), spread, other, weights),
+            1,
+            flops=len(steps) * flops,
+            nbytes=4 << 20,
+        )
+
+    (far,) = products(jnp.bfloat16, 2)
     far = whole(2, far)
-    own = call(
-        own_kernel, jax.ShapeDtypeStruct((ROWS, columns), jnp.float32), (near, weights), flops=flops, nbytes=3 << 20
-    )
+    right, left = products(jnp.bfloat16, 1, 3)
+    (own,) = products(jnp.float32, 0)
     right, left = whole(1, right), whole(3, left)
     own, squares = lax.optimization_barrier((own, squares))
     own = own + far.astype(jnp.float32)

time: 119 us -> 118 us (level)
    ppermute x3, waiting for transfers between devices: 7.73 us -> 6.1 us  [local(): lax.ppermute(v, 'x', [(i, (i + step) % NX) for i in range(NX)])]
    pallas_call x6 -> x7, Pallas kernels: 8.72 us -> 8.81 us  [call(): pl.pallas_call(kernel, out_shape=out_shape, in_specs=[smem] * scalars + [...]
  transfers between devices with their start and end apart: 9 -> 9, of which waited for: 7 -> 6; matrix products, arithmetic and copies ran while one was open for 4% -> 4% of each run, Pallas kernels for 1% -> 1%
where the time goes in v13:
time: 118 us
  blocking collectives  46.9 us (40%)
  starting transfers between devices  32.9 us (28%)
  waiting for transfers between devices  22.1 us (19%)
  Pallas kernels  8.81 us (7%)
  other arithmetic  4.98 us (4%)
    all_gather x1, blocking collectives, local(): wown = lax.all_gather(scaled, 'z', axis=0, tiled=True)  46.9 us
    ppermute x3, starting transfers between devices, local(): lax.ppermute(v, 'x', [(i, (i + step) % NX) for i in range(NX)])  11.6 us
    ppermute x1, waiting for transfers between devices, local(): lax.ppermute(sent, DP, [(i, i + 1) for i in range(NZ * NYL * NX - 1)])  9.75 us
    pallas_call x7, Pallas kernels, call(): pl.pallas_call(kernel, out_shape=out_shape, in_specs=[smem] * scalars + [...  8.81 us
    all_to_all x1, starting transfers between devices, local(): raw = lax.all_to_all(sent, 'yh', 0, 0, tiled=True)  7.34 us
    ppermute x3, waiting for transfers between devices, local(): lax.ppermute(v, 'x', [(i, (i + step) % NX) for i in range(NX)])  6.1 us
    all_to_all x1, starting transfers between devices, local(): spread = lax.all_to_all(raw, 'x', 0, 0, tiled=True)  4.42 us
    ppermute x1, starting transfers between devices, local(): woth = lax.ppermute(wown, 'yl', [(0, 1), (1, 0)])  3.25 us
  transfers between devices with their start and end apart: 9, of which 6 were waited for; matrix products, arithmetic and copies ran while one was open for 4% of the time, Pallas kernels for 1%

profile of v13, /device:TPU:40, one launch (start us, length us, event | category | flops | bytes accessed | tf_op | source)
XLA Modules:
  0.0 117.6 jit_solution(10577915844028056874)
XLA Ops:
  0.0 3.0 %shard_map.64 = (bf16[4,4,256,128]{3,2,1,0:T(8,128)(2,1)}, bf16[32,768]{1,0:T(8,128)(2,1)}) custom-call(s32[1]{0:T(128)} %bitcast.yl_ref, s32[1]{0:T(128)} %bitcast.1.dp_ref, bf16[256,512]{1,0:T(8,128)(2,1)} %s_hbm.1, bf16[32,768]{1,0:T(8,128)(2,1)} %w_hbm.1, bf16[32,128]{1,0:T(8,128)(2,1)} %bitcast.18), custom_call_target="tpu_custom_call" | custom-call | flops 134217728 | bytes 1048576 | tf_op jit(solution)/shard_map/pallas_call | solution.py:33
  3.0 0.0 copy-start.1
  3.0 7.3 %all-to-all-start = ((bf16[4,4,256,128]{3,2,1,0:T(8,128)(2,1)}), bf16[4,4,256,128]{3,2,1,0:T(8,128)(2,1)S(1)}, u32[]{:S(2)}, u32[]{:S(2)}) async-start(bf16[4,4,256,128]{3,2,1,0:T(8,128)(2,1)} %get-tuple-element.23), calls=%async_computation | async-start | bytes 2097152 | tf_op jit(solution)/shard_map/all_to_all | solution.py:184
  10.3 0.0 copy-done.1
  10.3 46.9 %all_gather.3.wown_ref = bf16[512,768]{1,0:T(8,128)(2,1)S(1)} all-gather(bf16[32,768]{1,0:T(8,128)(2,1)S(1)} %copy-done.1), channel_id=1, replica_groups=mesh['z'=16,'yl'=2,'x'=4,'yh'=4,'c'=2] {'z'}, dimensions={0}, use_global_device_ids=true | all-gather | bytes 835584 | tf_op jit(solution)/shard_map/all_gather | solution.py:185
  57.2 0.0 all-to-all-done
  57.2 1.0 copy.10
  58.3 0.0 copy-start
  58.3 0.0 copy-start.2
  58.3 4.4 %all-to-all-start.1 = ((bf16[4,4,256,128]{3,2,1,0:T(8,128)(2,1)}), bf16[4,4,256,128]{3,2,1,0:T(8,128)(2,1)S(1)}, u32[]{:S(2)}, u32[]{:S(2)}) async-start(bf16[4,4,256,128]{3,2,1,0:T(8,128)(2,1)} %bitcast.11), calls=%async_computation.1 | async-start | bytes 2097152 | tf_op jit(solution)/shard_map/all_to_all | solution.py:190
  62.7 3.2 %collective-permute-start.1 = (bf16[512,768]{1,0:T(8,128)(2,1)S(1)}, bf16[512,768]{1,0:T(8,128)(2,1)S(1)}, u32[]{:S(2)}, u32[]{:S(2)}) collective-permute-start(bf16[512,768]{1,0:T(8,128)(2,1)S(1)} %all_gather.3.wown_ref), channel_id=1, source_target_pairs={{0,32},{32,0},{1,33},{33,1},{2,34},{34,2},{3,35},{35,3},{4,36},{36... | collective-permute-start | bytes 2359304 | tf_op jit(solution)/shard_map/ppermute | solution.py:188
  66.0 0.0 copy-done
  66.0 0.6 slice_reduce_fusion
  66.6 0.0 copy-done.2
  66.6 0.7 slice_reduce_fusion.1
  67.3 1.4 %fusion.2 = f32[256]{0:T(256)S(1)} fusion(s32[]{:T(128)S(1)} %bitcast.13, s32[]{:T(128)} %slice_reduce_fusion, s32[]{:T(128)} %slice_reduce_fusion.1), kind=kLoop, calls=%fused_computation.12 | loop fusion | flops 2048 | bytes 1036 | tf_op jit(solution)/shard_map/convert_element_type | solution.py:199
  68.7 0.5 fusion
  69.3 0.1 pad_maximum_fusion
  69.4 1.5 %multiply_reduce_fusion = f32[256]{0:T(256)S(1)} fusion(bf16[4,4,256,128]{3,2,1,0:T(8,128)(2,1)} %bitcast.11), kind=kLoop, calls=%fused_computation | loop fusion | flops 1572608 | bytes 1049600 | tf_op jit(solution)/shard_map/reduce_sum | solution.py:192
  70.9 2.7 %all-to-all-done.1.own_ref = bf16[4,4,256,128]{3,2,1,0:T(8,128)(2,1)S(1)} async-done(((bf16[4,4,256,128]{3,2,1,0:T(8,128)(2,1)}), bf16[4,4,256,128]{3,2,1,0:T(8,128)(2,1)S(1)}, u32[]{:S(2)}, u32[]{:S(2)}) %all-to-all-start.1) | async-done | bytes 1048608 | tf_op jit(solution)/shard_map/all_to_all | solution.py:190
  73.6 1.9 %collective-permute-start = (bf16[4,4,256,128]{3,2,1,0:T(8,128)(2,1)S(1)}, bf16[4,4,256,128]{3,2,1,0:T(8,128)(2,1)S(1)}, u32[]{:S(2)}, u32[]{:S(2)}) collective-permute-start(bf16[4,4,256,128]{3,2,1,0:T(8,128)(2,1)S(1)} %all-to-all-done.1.own_ref), channel_id=1, source_target_pairs={{0,1},{1,0},{2,3},{3,2},{4,5},{5,4},{6,7},{7,6},{8,9},{9,8},{10,11... | collective-permute-start | bytes 3145736 | tf_op jit(solution)/shard_map/ppermute | solution.py:207
  75.5 1.9 %collective-permute-done.1.woth_ref = bf16[512,768]{1,0:T(8,128)(2,1)S(1)} collective-permute-done((bf16[512,768]{1,0:T(8,128)(2,1)S(1)}, bf16[512,768]{1,0:T(8,128)(2,1)S(1)}, u32[]{:S(2)}, u32[]{:S(2)}) %collective-permute-start.1) | collective-permute-done | bytes 786464 | tf_op jit(solution)/shard_map/ppermute | solution.py:188
  77.4 0.1 shard_map.65.w_ref
  77.5 0.6 collective-permute-done.oth_ref
  78.2 0.6 shard_map.67
  78.7 4.5 %collective-permute-start.2 = (bf16[256,768]{1,0:T(8,128)(2,1)S(1)}, bf16[256,768]{1,0:T(8,128)(2,1)S(1)}, u32[]{:S(2)}, u32[]{:S(2)}) collective-permute-start(bf16[256,768]{1,0:T(8,128)(2,1)S(1)} %shard_map.67), channel_id=1, source_target_pairs={{0,16},{8,24},{16,0},{24,8},{1,17},{9,25},{17,1},{25,9},{2,18},{10... | collective-permute-start | bytes 1179656 | tf_op jit(solution)/shard_map/ppermute | solution.py:210
  83.3 1.0 shard_map.68
  84.3 2.5 %collective-permute-start.3 = (bf16[256,768]{1,0:T(8,128)(2,1)S(1)}, bf16[256,768]{1,0:T(8,128)(2,1)S(1)}, u32[]{:S(2)}, u32[]{:S(2)}) collective-permute-start(bf16[256,768]{1,0:T(8,128)(2,1)S(1)} %get-tuple-element.33), channel_id=1, source_target_pairs={{0,8},{8,16},{16,24},{24,0},{1,9},{9,17},{17,25},{25,1},{2,10},{10... | collective-permute-start | bytes 1179656 | tf_op jit(solution)/shard_map/ppermute | solution.py:210
  86.8 4.6 %collective-permute-start.4 = (bf16[256,768]{1,0:T(8,128)(2,1)S(1)}, bf16[256,768]{1,0:T(8,128)(2,1)S(1)}, u32[]{:S(2)}, u32[]{:S(2)}) collective-permute-start(bf16[256,768]{1,0:T(8,128)(2,1)S(1)} %get-tuple-element.34), channel_id=1, source_target_pairs={{0,24},{8,0},{16,8},{24,16},{1,25},{9,1},{17,9},{25,17},{2,26},{10... | collective-permute-start | bytes 1179656 | tf_op jit(solution)/shard_map/ppermute | solution.py:210
  92.0 0.6 shard_map.66
  92.6 1.9 %collective-permute-start.5 = (f32[256]{0:T(256)S(1)}, f32[256]{0:T(256)S(1)}, u32[]{:S(2)}, u32[]{:S(2)}) collective-permute-start(f32[256]{0:T(256)S(1)} %multiply_reduce_fusion), channel_id=1, source_target_pairs={{0,1},{1,0},{2,3},{3,2},{4,5},{5,4},{6,7},{7,6},{8,9},{9,8},{10,11... | collective-permute-start | bytes 3080 | tf_op jit(solution)/shard_map/ppermute | solution.py:233
  94.5 0.0 collective-permute-done.2
  94.5 0.1 convert_add_fusion.p0_ref
  94.6 1.0 collective-permute-done.5
  95.6 6.1 %collective-permute-done.3.p1_ref = bf16[256,768]{1,0:T(8,128)(2,1)S(1)} collective-permute-done((bf16[256,768]{1,0:T(8,128)(2,1)S(1)}, bf16[256,768]{1,0:T(8,128)(2,1)S(1)}, u32[]{:S(2)}, u32[]{:S(2)}) %collective-permute-start.3) | collective-permute-done | bytes 393248 | tf_op jit(solution)/shard_map/ppermute | solution.py:210
  101.7 0.0 collective-permute-done.4.p2_ref
  101.7 1.9 %shard_map.69 = (bf16[256,512]{1,0:T(8,128)(2,1)S(1)}, bf16[256,512]{1,0:T(8,128)(2,1)S(1)}) custom-call(s32[4]{0:T(128)S(1)} %bitcast.14, s32[1]{0:T(128)S(6)} %copy.11.moved_ref, f32[256,768]{1,0:T(8,128)S(1)} %convert_add_fusion.p0_ref, bf16[256,768]{1,0:T(8,128)(2,1)S(1)} %collective-permute-done.3.p1_ref, ...), custom_call_target="tpu_custom_call" | custom-call | flops 134217728 | bytes 3145728 | tf_op jit(solution)/shard_map/pallas_call | solution.py:33
  103.7 2.5 %collective-permute-start.6 = (bf16[256,512]{1,0:T(8,128)(2,1)S(1)}, bf16[256,512]{1,0:T(8,128)(2,1)S(1)}, u32[]{:S(2)}, u32[]{:S(2)}) collective-permute-start(bf16[256,512]{1,0:T(8,128)(2,1)S(1)} %get-tuple-element.39), channel_id=1, source_target_pairs={{0,8},{8,16},{16,24},{24,32},{32,40},{40,48},{48,56},{56,64},{64,7... | collective-permute-start | bytes 786440 | tf_op jit(solution)/shard_map/ppermute | solution.py:242
  106.1 9.8 %collective-permute-done.6.prev_ref = bf16[256,512]{1,0:T(8,128)(2,1)S(1)} collective-permute-done((bf16[256,512]{1,0:T(8,128)(2,1)S(1)}, bf16[256,512]{1,0:T(8,128)(2,1)S(1)}, u32[]{:S(2)}, u32[]{:S(2)}) %collective-permute-start.6) | collective-permute-done | bytes 262176 | tf_op jit(solution)/shard_map/ppermute | solution.py:242
  115.9 1.7 %shard_map.70 = bf16[512,512]{1,0:T(8,128)(2,1)} custom-call(s32[4]{0:T(128)S(1)} %bitcast.15, s32[1]{0:T(128)S(6)} %copy.11.moved_ref, bf16[256,512]{1,0:T(8,128)(2,1)S(1)} %collective-permute-done.6.prev_ref, bf16[256,512]{1,0:T(8,128)(2,1)S(1)} %get-tuple-element.40.own_ref), custom_call_target="tpu_custom_call" | custom-call | flops 268435456 | bytes 1048576 | tf_op jit(solution)/shard_map/pallas_call | solution.py:33
  (2 shorter events, 0.0 us)
Async XLA Ops:
  3.0 7.4 %copy-start.1 = (bf16[32,768]{1,0:T(8,128)(2,1)S(1)}, bf16[32,768]{1,0:T(8,128)(2,1)}, u32[]{:S(2)}) copy-start(bf16[32,768]{1,0:T(8,128)(2,1)} %get-tuple-element.24) | copy-start | bytes 147460
  3.0 54.3 %all-to-all-start = ((bf16[4,4,256,128]{3,2,1,0:T(8,128)(2,1)}), bf16[4,4,256,128]{3,2,1,0:T(8,128)(2,1)S(1)}, u32[]{:S(2)}, u32[]{:S(2)}) async-start(bf16[4,4,256,128]{3,2,1,0:T(8,128)(2,1)} %get-tuple-element.23), calls=%async_computation | async-start | bytes 2097152 | tf_op jit(solution)/shard_map/all_to_all | solution.py:184
  58.3 7.7 %copy-start = (s32[1,4]{1,0:T(1,128)S(1)}, s32[1,4]{1,0:T(1,128)}, u32[]{:S(2)}) copy-start(s32[1,4]{1,0:T(1,128)} %param.7) | copy-start | bytes 52
  58.3 8.3 %copy-start.2 = (bf16[768]{0:T(1024)(128)(2,1)S(1)}, bf16[768]{0:T(1024)(128)(2,1)}, u32[]{:S(2)}) copy-start(bf16[768]{0:T(1024)(128)(2,1)} %param.11) | copy-start | bytes 4612
  58.3 15.3 %all-to-all-start.1 = ((bf16[4,4,256,128]{3,2,1,0:T(8,128)(2,1)}), bf16[4,4,256,128]{3,2,1,0:T(8,128)(2,1)S(1)}, u32[]{:S(2)}, u32[]{:S(2)}) async-start(bf16[4,4,256,128]{3,2,1,0:T(8,128)(2,1)} %bitcast.11), calls=%async_computation.1 | async-start | bytes 2097152 | tf_op jit(solution)/shard_map/all_to_all | solution.py:190
  62.7 14.7 %collective-permute-start.1 = (bf16[512,768]{1,0:T(8,128)(2,1)S(1)}, bf16[512,768]{1,0:T(8,128)(2,1)S(1)}, u32[]{:S(2)}, u32[]{:S(2)}) collective-permute-start(bf16[512,768]{1,0:T(8,128)(2,1)S(1)} %all_gather.3.wown_ref), channel_id=1, source_target_pairs={{0,32},{32,0},{1,33},{33,1},{2,34},{34,2},{3,35},{35,3},{4,36},{36... | collective-permute-start | bytes 2359304 | tf_op jit(solution)/shard_map/ppermute | solution.py:188
  73.6 4.5 %collective-permute-start = (bf16[4,4,256,128]{3,2,1,0:T(8,128)(2,1)S(1)}, bf16[4,4,256,128]{3,2,1,0:T(8,128)(2,1)S(1)}, u32[]{:S(2)}, u32[]{:S(2)}) collective-permute-start(bf16[4,4,256,128]{3,2,1,0:T(8,128)(2,1)S(1)} %all-to-all-done.1.own_ref), channel_id=1, source_target_pairs={{0,1},{1,0},{2,3},{3,2},{4,5},{5,4},{6,7},{7,6},{8,9},{9,8},{10,11... | collective-permute-start | bytes 3145736 | tf_op jit(solution)/shard_map/ppermute | solution.py:207
  78.7 15.8 %collective-permute-start.2 = (bf16[256,768]{1,0:T(8,128)(2,1)S(1)}, bf16[256,768]{1,0:T(8,128)(2,1)S(1)}, u32[]{:S(2)}, u32[]{:S(2)}) collective-permute-start(bf16[256,768]{1,0:T(8,128)(2,1)S(1)} %shard_map.67), channel_id=1, source_target_pairs={{0,16},{8,24},{16,0},{24,8},{1,17},{9,25},{17,1},{25,9},{2,18},{10... | collective-permute-start | bytes 1179656 | tf_op jit(solution)/shard_map/ppermute | solution.py:210
  84.3 17.4 %collective-permute-start.3 = (bf16[256,768]{1,0:T(8,128)(2,1)S(1)}, bf16[256,768]{1,0:T(8,128)(2,1)S(1)}, u32[]{:S(2)}, u32[]{:S(2)}) collective-permute-start(bf16[256,768]{1,0:T(8,128)(2,1)S(1)} %get-tuple-element.33), channel_id=1, source_target_pairs={{0,8},{8,16},{16,24},{24,0},{1,9},{9,17},{17,25},{25,1},{2,10},{10... | collective-permute-start | bytes 1179656 | tf_op jit(solution)/shard_map/ppermute | solution.py:210
  86.8 14.9 %collective-permute-start.4 = (bf16[256,768]{1,0:T(8,128)(2,1)S(1)}, bf16[256,768]{1,0:T(8,128)(2,1)S(1)}, u32[]{:S(2)}, u32[]{:S(2)}) collective-permute-start(bf16[256,768]{1,0:T(8,128)(2,1)S(1)} %get-tuple-element.34), channel_id=1, source_target_pairs={{0,24},{8,0},{16,8},{24,16},{1,25},{9,1},{17,9},{25,17},{2,26},{10... | collective-permute-start | bytes 1179656 | tf_op jit(solution)/shard_map/ppermute | solution.py:210
  92.6 3.0 %collective-permute-start.5 = (f32[256]{0:T(256)S(1)}, f32[256]{0:T(256)S(1)}, u32[]{:S(2)}, u32[]{:S(2)}) collective-permute-start(f32[256]{0:T(256)S(1)} %multiply_reduce_fusion), channel_id=1, source_target_pairs={{0,1},{1,0},{2,3},{3,2},{4,5},{5,4},{6,7},{7,6},{8,9},{9,8},{10,11... | collective-permute-start | bytes 3080 | tf_op jit(solution)/shard_map/ppermute | solution.py:233
  103.7 12.2 %collective-permute-start.6 = (bf16[256,512]{1,0:T(8,128)(2,1)S(1)}, bf16[256,512]{1,0:T(8,128)(2,1)S(1)}, u32[]{:S(2)}, u32[]{:S(2)}) collective-permute-start(bf16[256,512]{1,0:T(8,128)(2,1)S(1)} %get-tuple-element.39), channel_id=1, source_target_pairs={{0,8},{8,16},{16,24},{24,32},{32,40},{40,48},{48,56},{56,64},{64,7... | collective-permute-start | bytes 786440 | tf_op jit(solution)/shard_map/ppermute | solution.py:242

commit v14 on v9

--- a/solution.py
+++ b/solution.py
@@ -131,15 +131,16 @@
             total = total + ref[:, at : at + HEAD].astype(jnp.float32)
         return total * r + bias_ref[:, n * HEAD : (n + 1) * HEAD]
 
-    def rotate(v):
+    def rotate(v, cos, sin):
         return (v * cos + pltpu.roll(v, HEAD // 2, 1) * sin).astype(jnp.bfloat16)
 
-    key = rotate(head(PER))
+    key = rotate(head(PER), cos, sin)
+    cos, sin = cos * HEAD ** (-0.5), sin * HEAD ** (-0.5)
     value = head(PER + 1).astype(jnp.bfloat16)
     for h in range(PER):
-        query = rotate(head(h))
+        query = rotate(head(h), cos, sin)
         scores = lax.dot_general(query, key, (((1,), (1,)), ((), ())), preferred_element_type=jnp.float32)
-        scores = jnp.where(allowed, scores * HEAD ** (-0.5), -1e30)
+        scores = jnp.where(allowed, scores, -1e30)
         e = jnp.exp(scores - jnp.max(scores, axis=1, keepdims=True))
         weights = (e * (1.0 / jnp.sum(e, axis=1, keepdims=True))).astype(jnp.bfloat16)
         o_ref[:, h * HEAD : (h + 1) * HEAD] = jnp.dot(

time: 118 us -> 118 us (level)
  no operation moved by 1% of the time
where the time goes in v14:
time: 118 us
  blocking collectives  46.9 us (40%)
  starting transfers between devices  32.9 us (28%)
  waiting for transfers between devices  22.3 us (19%)
  Pallas kernels  9.01 us (8%)
  other arithmetic  4.77 us (4%)
    all_gather x1, blocking collectives, local(): wown = lax.all_gather(scaled, 'z', axis=0, tiled=True)  46.9 us
    ppermute x3, starting transfers between devices, local(): lax.ppermute(v, 'x', [(i, (i + step) % NX) for i in range(NX)])  11.6 us
    ppermute x1, waiting for transfers between devices, local(): lax.ppermute(sent, DP, [(i, i + 1) for i in range(NZ * NYL * NX - 1)])  9.75 us
    pallas_call x7, Pallas kernels, call(): pl.pallas_call(kernel, out_shape=out_shape, in_specs=[smem] * scalars + [...  9.01 us
    all_to_all x1, starting transfers between devices, local(): raw = lax.all_to_all(sent, 'yh', 0, 0, tiled=True)  7.34 us
    ppermute x3, waiting for transfers between devices, local(): lax.ppermute(v, 'x', [(i, (i + step) % NX) for i in range(NX)])  6.11 us
    all_to_all x1, starting transfers between devices, local(): spread = lax.all_to_all(raw, 'x', 0, 0, tiled=True)  4.42 us
    ppermute x1, starting transfers between devices, local(): woth = lax.ppermute(wown, 'yl', [(0, 1), (1, 0)])  3.25 us
  transfers between devices with their start and end apart: 9, of which 6 were waited for; matrix products, arithmetic and copies ran while one was open for 4% of the time, Pallas kernels for 1%

profile of v14, /device:TPU:40, one launch (start us, length us, event | category | flops | bytes accessed | tf_op | source)
XLA Modules:
  0.0 117.8 jit_solution(8001789600347993603)
XLA Ops:
  0.0 3.0 %shard_map.64 = (bf16[4,4,256,128]{3,2,1,0:T(8,128)(2,1)}, bf16[32,768]{1,0:T(8,128)(2,1)}) custom-call(s32[1]{0:T(128)} %bitcast.yl_ref, s32[1]{0:T(128)} %bitcast.1.dp_ref, bf16[256,512]{1,0:T(8,128)(2,1)} %s_hbm.1, bf16[32,768]{1,0:T(8,128)(2,1)} %w_hbm.1, bf16[32,128]{1,0:T(8,128)(2,1)} %bitcast.18), custom_call_target="tpu_custom_call" | custom-call | flops 134217728 | bytes 1048576 | tf_op jit(solution)/shard_map/pallas_call | solution.py:32
  3.0 0.0 copy-start.1
  3.0 7.3 %all-to-all-start = ((bf16[4,4,256,128]{3,2,1,0:T(8,128)(2,1)}), bf16[4,4,256,128]{3,2,1,0:T(8,128)(2,1)S(1)}, u32[]{:S(2)}, u32[]{:S(2)}) async-start(bf16[4,4,256,128]{3,2,1,0:T(8,128)(2,1)} %get-tuple-element.25), calls=%async_computation | async-start | bytes 2097152 | tf_op jit(solution)/shard_map/all_to_all | solution.py:198
  10.3 0.0 copy-done.1
  10.3 46.9 %all_gather.3.wown_ref = bf16[512,768]{1,0:T(8,128)(2,1)S(1)} all-gather(bf16[32,768]{1,0:T(8,128)(2,1)S(1)} %copy-done.1), channel_id=1, replica_groups=mesh['z'=16,'yl'=2,'x'=4,'yh'=4,'c'=2] {'z'}, dimensions={0}, use_global_device_ids=true | all-gather | bytes 835584 | tf_op jit(solution)/shard_map/all_gather | solution.py:199
  57.2 0.0 all-to-all-done
  57.2 1.0 copy.10
  58.3 0.0 copy-start
  58.3 0.0 copy-start.2
  58.3 4.4 %all-to-all-start.1 = ((bf16[4,4,256,128]{3,2,1,0:T(8,128)(2,1)}), bf16[4,4,256,128]{3,2,1,0:T(8,128)(2,1)S(1)}, u32[]{:S(2)}, u32[]{:S(2)}) async-start(bf16[4,4,256,128]{3,2,1,0:T(8,128)(2,1)} %bitcast.11), calls=%async_computation.1 | async-start | bytes 2097152 | tf_op jit(solution)/shard_map/all_to_all | solution.py:204
  62.7 3.2 %collective-permute-start.1 = (bf16[512,768]{1,0:T(8,128)(2,1)S(1)}, bf16[512,768]{1,0:T(8,128)(2,1)S(1)}, u32[]{:S(2)}, u32[]{:S(2)}) collective-permute-start(bf16[512,768]{1,0:T(8,128)(2,1)S(1)} %all_gather.3.wown_ref), channel_id=1, source_target_pairs={{0,32},{32,0},{1,33},{33,1},{2,34},{34,2},{3,35},{35,3},{4,36},{36... | collective-permute-start | bytes 2359304 | tf_op jit(solution)/shard_map/ppermute | solution.py:202
  66.0 0.0 copy-done
  66.0 0.6 slice_reduce_fusion
  66.6 0.0 copy-done.2
  66.6 0.6 slice_reduce_fusion.1
  67.2 1.3 %fusion.2 = f32[256]{0:T(256)S(1)} fusion(s32[]{:T(128)S(1)} %bitcast.13, s32[]{:T(128)} %slice_reduce_fusion, s32[]{:T(128)} %slice_reduce_fusion.1), kind=kLoop, calls=%fused_computation.12 | loop fusion | flops 2048 | bytes 1036 | tf_op jit(solution)/shard_map/convert_element_type | solution.py:213
  68.5 0.5 fusion
  69.0 0.1 pad_maximum_fusion
  69.2 1.5 %multiply_reduce_fusion = f32[256]{0:T(256)S(1)} fusion(bf16[4,4,256,128]{3,2,1,0:T(8,128)(2,1)} %bitcast.11), kind=kLoop, calls=%fused_computation | loop fusion | flops 1572608 | bytes 1049600 | tf_op jit(solution)/shard_map/reduce_sum | solution.py:206
  70.7 2.9 %all-to-all-done.1.own_ref = bf16[4,4,256,128]{3,2,1,0:T(8,128)(2,1)S(1)} async-done(((bf16[4,4,256,128]{3,2,1,0:T(8,128)(2,1)}), bf16[4,4,256,128]{3,2,1,0:T(8,128)(2,1)S(1)}, u32[]{:S(2)}, u32[]{:S(2)}) %all-to-all-start.1) | async-done | bytes 1048608 | tf_op jit(solution)/shard_map/all_to_all | solution.py:204
  73.6 1.9 %collective-permute-start = (bf16[4,4,256,128]{3,2,1,0:T(8,128)(2,1)S(1)}, bf16[4,4,256,128]{3,2,1,0:T(8,128)(2,1)S(1)}, u32[]{:S(2)}, u32[]{:S(2)}) collective-permute-start(bf16[4,4,256,128]{3,2,1,0:T(8,128)(2,1)S(1)} %all-to-all-done.1.own_ref), channel_id=1, source_target_pairs={{0,1},{1,0},{2,3},{3,2},{4,5},{5,4},{6,7},{7,6},{8,9},{9,8},{10,11... | collective-permute-start | bytes 3145736 | tf_op jit(solution)/shard_map/ppermute | solution.py:221
  75.5 1.9 %collective-permute-done.1.woth_ref = bf16[512,768]{1,0:T(8,128)(2,1)S(1)} collective-permute-done((bf16[512,768]{1,0:T(8,128)(2,1)S(1)}, bf16[512,768]{1,0:T(8,128)(2,1)S(1)}, u32[]{:S(2)}, u32[]{:S(2)}) %collective-permute-start.1) | collective-permute-done | bytes 786464 | tf_op jit(solution)/shard_map/ppermute | solution.py:202
  77.4 0.1 shard_map.65.w_ref
  77.5 0.6 collective-permute-done.oth_ref
  78.2 0.8 shard_map.66
  79.0 4.5 %collective-permute-start.2 = (bf16[256,768]{1,0:T(8,128)(2,1)S(1)}, bf16[256,768]{1,0:T(8,128)(2,1)S(1)}, u32[]{:S(2)}, u32[]{:S(2)}) collective-permute-start(bf16[256,768]{1,0:T(8,128)(2,1)S(1)} %get-tuple-element.36), channel_id=1, source_target_pairs={{0,16},{8,24},{16,0},{24,8},{1,17},{9,25},{17,1},{25,9},{2,18},{10... | collective-permute-start | bytes 1179656 | tf_op jit(solution)/shard_map/ppermute | solution.py:224
  83.5 1.0 shard_map.68
  84.5 2.5 %collective-permute-start.3 = (bf16[256,768]{1,0:T(8,128)(2,1)S(1)}, bf16[256,768]{1,0:T(8,128)(2,1)S(1)}, u32[]{:S(2)}, u32[]{:S(2)}) collective-permute-start(bf16[256,768]{1,0:T(8,128)(2,1)S(1)} %get-tuple-element.37), channel_id=1, source_target_pairs={{0,8},{8,16},{16,24},{24,0},{1,9},{9,17},{17,25},{25,1},{2,10},{10... | collective-permute-start | bytes 1179656 | tf_op jit(solution)/shard_map/ppermute | solution.py:224
  87.0 4.6 %collective-permute-start.4 = (bf16[256,768]{1,0:T(8,128)(2,1)S(1)}, bf16[256,768]{1,0:T(8,128)(2,1)S(1)}, u32[]{:S(2)}, u32[]{:S(2)}) collective-permute-start(bf16[256,768]{1,0:T(8,128)(2,1)S(1)} %get-tuple-element.38), channel_id=1, source_target_pairs={{0,24},{8,0},{16,8},{24,16},{1,25},{9,1},{17,9},{25,17},{2,26},{10... | collective-permute-start | bytes 1179656 | tf_op jit(solution)/shard_map/ppermute | solution.py:224
  92.2 0.6 shard_map.67
  92.8 1.9 %collective-permute-start.5 = (f32[256]{0:T(256)S(1)}, f32[256]{0:T(256)S(1)}, u32[]{:S(2)}, u32[]{:S(2)}) collective-permute-start(f32[256]{0:T(256)S(1)} %multiply_reduce_fusion), channel_id=1, source_target_pairs={{0,1},{1,0},{2,3},{3,2},{4,5},{5,4},{6,7},{7,6},{8,9},{9,8},{10,11... | collective-permute-start | bytes 3080 | tf_op jit(solution)/shard_map/ppermute | solution.py:251
  94.7 0.0 collective-permute-done.2
  94.7 0.1 convert_add_fusion.p0_ref
  94.8 1.0 collective-permute-done.5
  95.8 6.1 %collective-permute-done.3.p1_ref = bf16[256,768]{1,0:T(8,128)(2,1)S(1)} collective-permute-done((bf16[256,768]{1,0:T(8,128)(2,1)S(1)}, bf16[256,768]{1,0:T(8,128)(2,1)S(1)}, u32[]{:S(2)}, u32[]{:S(2)}) %collective-permute-start.3) | collective-permute-done | bytes 393248 | tf_op jit(solution)/shard_map/ppermute | solution.py:224
  102.0 0.0 collective-permute-done.4.p2_ref
  102.0 1.9 %shard_map.69 = (bf16[256,512]{1,0:T(8,128)(2,1)S(1)}, bf16[256,512]{1,0:T(8,128)(2,1)S(1)}) custom-call(s32[4]{0:T(128)S(1)} %bitcast.14, s32[1]{0:T(128)S(6)} %copy.11.moved_ref, f32[256,768]{1,0:T(8,128)S(1)} %convert_add_fusion.p0_ref, bf16[256,768]{1,0:T(8,128)(2,1)S(1)} %collective-permute-done.3.p1_ref, ...), custom_call_target="tpu_custom_call" | custom-call | flops 134217728 | bytes 3145728 | tf_op jit(solution)/shard_map/pallas_call | solution.py:32
  103.9 2.5 %collective-permute-start.6 = (bf16[256,512]{1,0:T(8,128)(2,1)S(1)}, bf16[256,512]{1,0:T(8,128)(2,1)S(1)}, u32[]{:S(2)}, u32[]{:S(2)}) collective-permute-start(bf16[256,512]{1,0:T(8,128)(2,1)S(1)} %get-tuple-element.43), channel_id=1, source_target_pairs={{0,8},{8,16},{16,24},{24,32},{32,40},{40,48},{48,56},{56,64},{64,7... | collective-permute-start | bytes 786440 | tf_op jit(solution)/shard_map/ppermute | solution.py:260
  106.4 9.7 %collective-permute-done.6.prev_ref = bf16[256,512]{1,0:T(8,128)(2,1)S(1)} collective-permute-done((bf16[256,512]{1,0:T(8,128)(2,1)S(1)}, bf16[256,512]{1,0:T(8,128)(2,1)S(1)}, u32[]{:S(2)}, u32[]{:S(2)}) %collective-permute-start.6) | collective-permute-done | bytes 262176 | tf_op jit(solution)/shard_map/ppermute | solution.py:260
  116.1 1.7 %shard_map.70 = bf16[512,512]{1,0:T(8,128)(2,1)} custom-call(s32[4]{0:T(128)S(1)} %bitcast.15, s32[1]{0:T(128)S(6)} %copy.11.moved_ref, bf16[256,512]{1,0:T(8,128)(2,1)S(1)} %collective-permute-done.6.prev_ref, bf16[256,512]{1,0:T(8,128)(2,1)S(1)} %get-tuple-element.44.own_ref), custom_call_target="tpu_custom_call" | custom-call | flops 268435456 | bytes 1048576 | tf_op jit(solution)/shard_map/pallas_call | solution.py:32
  (2 shorter events, 0.0 us)
Async XLA Ops:
  3.0 7.4 %copy-start.1 = (bf16[32,768]{1,0:T(8,128)(2,1)S(1)}, bf16[32,768]{1,0:T(8,128)(2,1)}, u32[]{:S(2)}) copy-start(bf16[32,768]{1,0:T(8,128)(2,1)} %get-tuple-element.26) | copy-start | bytes 147460
  3.0 54.3 %all-to-all-start = ((bf16[4,4,256,128]{3,2,1,0:T(8,128)(2,1)}), bf16[4,4,256,128]{3,2,1,0:T(8,128)(2,1)S(1)}, u32[]{:S(2)}, u32[]{:S(2)}) async-start(bf16[4,4,256,128]{3,2,1,0:T(8,128)(2,1)} %get-tuple-element.25), calls=%async_computation | async-start | bytes 2097152 | tf_op jit(solution)/shard_map/all_to_all | solution.py:198
  58.3 7.7 %copy-start = (s32[1,4]{1,0:T(1,128)S(1)}, s32[1,4]{1,0:T(1,128)}, u32[]{:S(2)}) copy-start(s32[1,4]{1,0:T(1,128)} %param.7) | copy-start | bytes 52
  58.3 8.3 %copy-start.2 = (bf16[768]{0:T(1024)(128)(2,1)S(1)}, bf16[768]{0:T(1024)(128)(2,1)}, u32[]{:S(2)}) copy-start(bf16[768]{0:T(1024)(128)(2,1)} %param.11) | copy-start | bytes 4612
  58.3 15.3 %all-to-all-start.1 = ((bf16[4,4,256,128]{3,2,1,0:T(8,128)(2,1)}), bf16[4,4,256,128]{3,2,1,0:T(8,128)(2,1)S(1)}, u32[]{:S(2)}, u32[]{:S(2)}) async-start(bf16[4,4,256,128]{3,2,1,0:T(8,128)(2,1)} %bitcast.11), calls=%async_computation.1 | async-start | bytes 2097152 | tf_op jit(solution)/shard_map/all_to_all | solution.py:204
  62.7 14.7 %collective-permute-start.1 = (bf16[512,768]{1,0:T(8,128)(2,1)S(1)}, bf16[512,768]{1,0:T(8,128)(2,1)S(1)}, u32[]{:S(2)}, u32[]{:S(2)}) collective-permute-start(bf16[512,768]{1,0:T(8,128)(2,1)S(1)} %all_gather.3.wown_ref), channel_id=1, source_target_pairs={{0,32},{32,0},{1,33},{33,1},{2,34},{34,2},{3,35},{35,3},{4,36},{36... | collective-permute-start | bytes 2359304 | tf_op jit(solution)/shard_map/ppermute | solution.py:202
  73.6 4.5 %collective-permute-start = (bf16[4,4,256,128]{3,2,1,0:T(8,128)(2,1)S(1)}, bf16[4,4,256,128]{3,2,1,0:T(8,128)(2,1)S(1)}, u32[]{:S(2)}, u32[]{:S(2)}) collective-permute-start(bf16[4,4,256,128]{3,2,1,0:T(8,128)(2,1)S(1)} %all-to-all-done.1.own_ref), channel_id=1, source_target_pairs={{0,1},{1,0},{2,3},{3,2},{4,5},{5,4},{6,7},{7,6},{8,9},{9,8},{10,11... | collective-permute-start | bytes 3145736 | tf_op jit(solution)/shard_map/ppermute | solution.py:221
  79.0 15.8 %collective-permute-start.2 = (bf16[256,768]{1,0:T(8,128)(2,1)S(1)}, bf16[256,768]{1,0:T(8,128)(2,1)S(1)}, u32[]{:S(2)}, u32[]{:S(2)}) collective-permute-start(bf16[256,768]{1,0:T(8,128)(2,1)S(1)} %get-tuple-element.36), channel_id=1, source_target_pairs={{0,16},{8,24},{16,0},{24,8},{1,17},{9,25},{17,1},{25,9},{2,18},{10... | collective-permute-start | bytes 1179656 | tf_op jit(solution)/shard_map/ppermute | solution.py:224
  84.5 17.4 %collective-permute-start.3 = (bf16[256,768]{1,0:T(8,128)(2,1)S(1)}, bf16[256,768]{1,0:T(8,128)(2,1)S(1)}, u32[]{:S(2)}, u32[]{:S(2)}) collective-permute-start(bf16[256,768]{1,0:T(8,128)(2,1)S(1)} %get-tuple-element.37), channel_id=1, source_target_pairs={{0,8},{8,16},{16,24},{24,0},{1,9},{9,17},{17,25},{25,1},{2,10},{10... | collective-permute-start | bytes 1179656 | tf_op jit(solution)/shard_map/ppermute | solution.py:224
  87.0 15.0 %collective-permute-start.4 = (bf16[256,768]{1,0:T(8,128)(2,1)S(1)}, bf16[256,768]{1,0:T(8,128)(2,1)S(1)}, u32[]{:S(2)}, u32[]{:S(2)}) collective-permute-start(bf16[256,768]{1,0:T(8,128)(2,1)S(1)} %get-tuple-element.38), channel_id=1, source_target_pairs={{0,24},{8,0},{16,8},{24,16},{1,25},{9,1},{17,9},{25,17},{2,26},{10... | collective-permute-start | bytes 1179656 | tf_op jit(solution)/shard_map/ppermute | solution.py:224
  92.8 3.0 %collective-permute-start.5 = (f32[256]{0:T(256)S(1)}, f32[256]{0:T(256)S(1)}, u32[]{:S(2)}, u32[]{:S(2)}) collective-permute-start(f32[256]{0:T(256)S(1)} %multiply_reduce_fusion), channel_id=1, source_target_pairs={{0,1},{1,0},{2,3},{3,2},{4,5},{5,4},{6,7},{7,6},{8,9},{9,8},{10,11... | collective-permute-start | bytes 3080 | tf_op jit(solution)/shard_map/ppermute | solution.py:251
  103.9 12.2 %collective-permute-start.6 = (bf16[256,512]{1,0:T(8,128)(2,1)S(1)}, bf16[256,512]{1,0:T(8,128)(2,1)S(1)}, u32[]{:S(2)}, u32[]{:S(2)}) collective-permute-start(bf16[256,512]{1,0:T(8,128)(2,1)S(1)} %get-tuple-element.43), channel_id=1, source_target_pairs={{0,8},{8,16},{16,24},{24,32},{32,40},{40,48},{48,56},{56,64},{64,7... | collective-permute-start | bytes 786440 | tf_op jit(solution)/shard_map/ppermute | solution.py:260
